TPU v7x, 256 devices: a whole 4x4x8 slice. The times are simulated.
256 devices in a mesh: ch: 8 (over z), seq: 32 (over y, x, core).
Axes of the slice: x: 4, y: 4, z: 8, core: 2. Of those that a mesh axis runs over, the one named last changes fastest.
Arguments:
- inputs: bfloat16 [4096, 4096], P('seq', 'ch'), may hold values from -6 to 6
- in_weight: bfloat16 [4096, 3, 4096], P('seq'), may hold values from -0.09375 to 0.09375
- out_weight: bfloat16 [4096, 4096], P('seq', 'ch'), may hold values from -0.09375 to 0.09375
- short_filter: float32 [3, 3, 4096], P(None, None, 'ch'), may hold values from -3 to 3
- decay: float32 [4096, 2], P('ch'), may hold values from 7.324219e-05 to 0.025
- angle: float32 [4096, 2], P('ch'), may hold values from 0 to 0.5
- residue: float32 [2, 4096, 2], P(None, 'ch'), may hold values from -4 to 4
- bias: float32 [4096], P('ch'), may hold values from -4 to 4
Outputs:
- mixed: bfloat16 [4096, 4096], P('seq', 'ch')
All inputs are finite; a program needn't handle non-finite values.
Results may differ from a plain program's by a relative error of at most 0.007.
Values may be sent and summed in bfloat16 or wider, within the bound.
No kernel may reach another device: no remote copies, remote signals or barrier semaphores. Data moves between devices by JAX's collectives and lax.ppermute only.
A program may use at most 64 MiB of HBM per device.

v0:
```python
import jax
import jax.numpy as jnp
from jax import lax
from jax.sharding import PartitionSpec as P

BLOCK = 32


highest = lax.Precision.HIGHEST


def shifted(x, axis, by):
    length = lax.axis_size(axis)
    pairs = [(i, i + by) for i in range(length) if 0 <= i + by < length]
    return lax.ppermute(x, axis, pairs)


def prefix_2(part, axis, combine, identity):
    place = lax.axis_index(axis)
    gathered = jax.tree.map(lambda a: lax.all_gather(a, axis), part)
    state = jax.tree.map(lambda a, e: jnp.zeros_like(a) + jnp.asarray(e, a.dtype), part, identity)

    def one(step, state):
        return combine(
            state, jax.tree.map(lambda a: lax.dynamic_index_in_dim(a, step, 0, False), gathered)
        )

    return lax.fori_loop(0, place, one, state)


def body(inputs, in_weight, out_weight, short_filter, decay, angle, residue, bias):
    rows = inputs.shape[0]
    chans = inputs.shape[1]
    blocks = rows // BLOCK
    features = lax.all_gather(inputs, "ch", axis=1, tiled=True)
    col_start = lax.axis_index("ch") * chans
    own_weight = lax.dynamic_slice_in_dim(in_weight, col_start, chans, 2)
    piece = lax.all_gather(own_weight, "seq", axis=0, tiled=True)
    cols = features
    projected = jnp.dot(cols, piece.reshape(piece.shape[0], -1), preferred_element_type=jnp.float32)
    projected = projected.astype(jnp.bfloat16)
    rim = shifted(projected[-2:], "seq", 1)
    extended = (
        jnp.concatenate([rim, projected], axis=0).astype(jnp.float32).reshape(rows + 2, 3, chans)
    )
    filtered = (
        short_filter[0] * extended[2:]
        + short_filter[1] * extended[1:-1]
        + short_filter[2] * extended[:-2]
    )
    query = filtered[:, 0, :]
    mixin = filtered[:, 1, :] * filtered[:, 2, :]
    rate = decay.T
    turn = angle.T
    real_part = residue[0].T
    imag_part = residue[1].T

    def powers(exponent):
        mag = jnp.exp(-exponent[:, None, None] * rate[None])
        phase = exponent[:, None, None] * turn[None]
        return (mag * jnp.cos(phase), mag * jnp.sin(phase))

    lags = jnp.arange(BLOCK).astype(jnp.float32)
    lag_re, lag_im = powers(lags)
    kernel = jnp.sum(lag_re * real_part[None] - lag_im * imag_part[None], axis=1)
    offsets = jnp.arange(BLOCK)[:, None] - jnp.arange(BLOCK)[None, :]
    toeplitz = jnp.where((offsets >= 0)[:, :, None], kernel[jnp.clip(offsets, 0, BLOCK - 1)], 0.0)
    blocked = mixin.reshape(blocks, BLOCK, chans)
    inner = jnp.einsum("tsc,ksc->ktc", toeplitz, blocked, precision=highest)
    end_re, end_im = powers(BLOCK - 1 - lags)
    state_re = jnp.einsum("snc,ksc->knc", end_re, blocked, precision=highest)
    state_im = jnp.einsum("snc,ksc->knc", end_im, blocked, precision=highest)
    step_re, step_im = powers(jnp.full((1,), BLOCK, jnp.float32))
    step_re = step_re[0]
    step_im = step_im[0]

    def advance(carry, fresh):
        old_re, old_im = carry
        new_re = step_re * old_re - step_im * old_im + fresh[0]
        new_im = step_re * old_im + step_im * old_re + fresh[1]
        return ((new_re, new_im), (old_re, old_im))

    zero_state = jnp.zeros(rate.shape, jnp.float32)
    (final_re, final_im), (before_re, before_im) = lax.scan(
        advance, (zero_state, zero_state), (state_re, state_im)
    )
    jump_re, jump_im = powers(jnp.full((1,), rows, jnp.float32))

    def combine(early, late):
        ar1, ai1, sr1, si1 = early
        ar2, ai2, sr2, si2 = late
        return (
            ar1 * ar2 - ai1 * ai2,
            ar1 * ai2 + ai1 * ar2,
            ar2 * sr1 - ai2 * si1 + sr2,
            ar2 * si1 + ai2 * sr1 + si2,
        )

    identity = (jnp.ones_like(zero_state), zero_state, zero_state, zero_state)
    prefix = prefix_2((jump_re[0], jump_im[0], final_re, final_im), "seq", combine, identity)
    entry_re = prefix[2]
    entry_im = prefix[3]
    shift_re, shift_im = powers((jnp.arange(blocks) * BLOCK).astype(jnp.float32))
    total_re = before_re + shift_re * entry_re[None] - shift_im * entry_im[None]
    total_im = before_im + shift_re * entry_im[None] + shift_im * entry_re[None]
    out_re, out_im = powers(lags + 1.0)
    weighted_re = out_re * real_part[None] - out_im * imag_part[None]
    weighted_im = out_re * imag_part[None] + out_im * real_part[None]
    carried = jnp.einsum("unc,knc->kuc", weighted_re, total_re, precision=highest)
    carried = carried - jnp.einsum("unc,knc->kuc", weighted_im, total_im, precision=highest)
    long_term = (inner + carried).reshape(rows, chans) + bias[None, :] * mixin
    gated = (query * long_term).astype(jnp.bfloat16)
    gathered = lax.all_gather(gated, "ch", axis=1, tiled=True)
    cols = gathered
    result = jnp.dot(
        cols,
        lax.all_gather(out_weight, "seq", axis=0, tiled=True),
        preferred_element_type=jnp.float32,
    )
    return result.astype(jnp.bfloat16)


def solution(mesh):
    placed = (
        P("seq", "ch"),
        P("seq", None, None),
        P("seq", "ch"),
        P(None, None, "ch"),
        P("ch", None),
        P("ch", None),
        P(None, "ch", None),
        P("ch"),
    )
    return jax.shard_map(
        body, mesh=mesh, in_specs=placed, out_specs=P("seq", "ch"), check_vma=False
    )
```

profile of v0, /device:TPU:2, one launch (start us, length us, event | category | flops | bytes accessed | tf_op | source)
XLA Modules:
  0.0 365.2 jit_solution(17970752399903277085)
XLA Ops:
  6.5 0.7 all-gather.15.cloned.1.call-update
  7.3 0.0 all-gather.13.cloned.1.call-start
  7.3 1.1 copy-done
  8.5 0.9 copy.82
  9.4 0.0 all-gather.13.cloned.1.call-update
  9.4 0.0 all-gather.19.cloned.1.call-start
  9.5 0.7 all-gather.19.cloned.1.call-update
  10.2 0.0 all-gather.17.cloned.1.call-start
  10.2 0.5 fusion.27
  10.8 0.7 slice_bitcast_fusion.5
  11.5 0.1 reshape.111
  11.6 0.8 multiply_bitcast_fusion
  12.4 0.6 multiply_convert_fusion
  13.0 26.5 %all-gather.4 = f32[32,2,512]{2,1,0:T(2,128)} all-gather(f32[1,2,512]{2,1,0:T(2,128)S(1)} %get-tuple-element.254), channel_id=2, replica_groups=mesh['ch'=8,'seq'=32] {'seq'}, dimensions={0}, use_global_device_ids=true | all-gather | bytes 135168 | tf_op jit(solution)/shard_map/all_gather | solution.py:20
  39.5 0.7 slice_bitcast_fusion.3
  40.3 3.0 multiply_add_fusion.1
  43.3 7.6 %all-gather.15.cloned.1.call-done = bf16[128,4096]{1,0:T(8,128)(2,1)} async-done(((bf16[128,512]{1,0:T(8,128)(2,1)}), bf16[128,4096]{1,0:T(8,128)(2,1)}) %all-gather.15.cloned.1.call-update) | async-done | bytes 1048592 | tf_op jit(solution)/shard_map/all_gather | solution.py:35
  50.9 75.7 %all-gather.13.cloned.1.call-done = bf16[4096,3,512]{0,2,1:T(8,128)(2,1)} async-done(((bf16[128,3,512]{0,2,1:T(8,128)(2,1)}), bf16[4096,3,512]{0,2,1:T(8,128)(2,1)}) %all-gather.13.cloned.1.call-update) | async-done | bytes 12582928 | tf_op jit(solution)/shard_map/all_gather | solution.py:38
  126.6 9.1 %fusion.6 = bf16[128,1536]{1,0:T(8,128)(2,1)S(1)} fusion(bf16[4096,1536]{0,1:T(8,128)(2,1)} %bitcast.124, bf16[128,4096]{1,0:T(8,128)(2,1)} %all-gather.15.cloned.1.call-done), kind=kOutput, calls=%fused_computation.20 | convolution fusion | flops 1610809344 | bytes 14024704 | tf_op jit(solution)/shard_map/dot_general | solution.py:40
  135.6 0.7 copy-done.4
  136.4 0.6 slice.62
  137.0 2.2 collective-permute-start
  139.2 24.9 %all-gather.5 = f32[32,2,512]{2,1,0:T(2,128)} all-gather(f32[1,2,512]{2,1,0:T(2,128)S(1)} %get-tuple-element.252), channel_id=3, replica_groups=mesh['ch'=8,'seq'=32] {'seq'}, dimensions={0}, use_global_device_ids=true | all-gather | bytes 135168 | tf_op jit(solution)/shard_map/all_gather | solution.py:20
  164.1 2.0 copy.70
  166.1 1.9 copy.72
  168.0 1.0 copy.76
  169.0 4.9 %gather_fusion = f32[1024,512]{1,0:T(8,128)} fusion(f32[32,512]{1,0:T(8,128)S(1)} %get-tuple-element.247, s32[1024]{0:T(1024)S(1)} %broadcast_clamp_fusion), kind=kCustom, calls=%fused_computation | custom fusion | bytes 4198400 | tf_op jit(solution)/shard_map/gather | solution.py:67
  173.9 8.5 %copy.67 = f32[32,32,512]{1,0,2:T(8,128)} copy(f32[32,32,512]{2,1,0:T(8,128)} %bitcast.112) | data formatting | bytes 4194304 | tf_op jit(solution)/shard_map/gather | solution.py:67
  182.4 1.0 copy.78
  183.4 0.0 collective-permute-done
  183.4 1.1 maximum_convert_fusion
  184.5 1.6 fusion.29
  186.1 2.3 copy.63
  188.4 2.3 copy.61
  190.6 2.3 copy.62
  192.9 2.0 multiply_add_fusion
  195.0 0.9 copy-done.1
  195.9 0.7 slice_multiply_fusion
  196.6 1.1 copy.64
  197.7 1.4 copy.68
  199.1 5.7 %convolution_bitcast_fusion.1 = f32[4,2,512]{0,1,2:T(2,128)} fusion(f32[4,32,512]{1,0,2:T(4,128)} %copy.68, f32[32,2,512]{0,1,2:T(2,128)} %copy.70), kind=kOutput, calls=%fused_computation.25 | convolution fusion | flops 1572864 | bytes 409600 | tf_op jit(solution)/shard_map/snc,ksc->knc/dot_general | solution.py:71
  204.8 1.2 copy.73
  206.1 5.7 %convolution_bitcast_fusion = f32[4,2,512]{0,1,2:T(2,128)} fusion(f32[4,32,512]{1,0,2:T(4,128)} %copy.68, f32[32,2,512]{0,1,2:T(2,128)} %copy.72), kind=kOutput, calls=%fused_computation.24 | convolution fusion | flops 1572864 | bytes 409600 | tf_op jit(solution)/shard_map/snc,ksc->knc/dot_general | solution.py:72
  211.8 1.2 copy.74
  213.0 0.2 while.33
  213.3 23.7 %all-gather.6 = f32[32,2,512]{2,1,0:T(2,128)S(1)} all-gather(f32[1,2,512]{2,1,0:T(2,128)S(1)} %bitcast.118), channel_id=4, replica_groups=mesh['ch'=8,'seq'=32] {'seq'}, dimensions={0}, use_global_device_ids=true | all-gather | bytes 135168 | tf_op jit(solution)/shard_map/all_gather | solution.py:20
  236.9 23.0 %all-gather.7 = f32[32,2,512]{2,1,0:T(2,128)S(1)} all-gather(f32[1,2,512]{2,1,0:T(2,128)S(1)} %bitcast.119), channel_id=5, replica_groups=mesh['ch'=8,'seq'=32] {'seq'}, dimensions={0}, use_global_device_ids=true | all-gather | bytes 135168 | tf_op jit(solution)/shard_map/all_gather | solution.py:20
  259.9 1.4 while.32
  259.9 0.7 bitcast_add_fusion.6
  260.7 0.7 bitcast_add_fusion.6
  261.4 0.3 multiply_add_fusion.2
  261.7 1.0 copy.75
  262.8 1.0 copy.77
  263.8 5.4 %fusion.30 = f32[512,4,32]{2,1,0:T(4,128)S(1)} fusion(f32[4,2,512]{0,1,2:T(2,128)} %copy.75, f32[32,2,512]{0,1,2:T(2,128)} %copy.76), kind=kOutput, calls=%fused_computation.87 | convolution fusion | flops 1572864 | bytes 409600 | tf_op jit(solution)/shard_map/unc,knc->kuc/dot_general | solution.py:109
  269.3 15.9 %fusion.2 = f32[512,4,32]{2,1,0:T(4,128)S(1)} fusion(f32[4,32,512]{1,0,2:T(4,128)} %copy.68, f32[32,32,512]{1,0,2:T(8,128)} %copy.67, pred[32,32]{1,0:T(8,128)(4,1)S(1)} %subtract_compare_fusion), kind=kOutput, calls=%fused_computation.15 | convolution fusion | flops 25690112 | bytes 2622464 | tf_op jit(solution)/shard_map/tsc,ksc->ktc/dot_general | solution.py:69
  285.2 0.0 copy-start.7
  285.2 5.4 %fusion.8 = f32[4,32,512]{1,0,2:T(4,128)} fusion(f32[512,4,32]{2,1,0:T(4,128)S(1)} %fusion.2, f32[512,4,32]{2,1,0:T(4,128)S(1)} %fusion.30, f32[4,2,512]{0,1,2:T(2,128)S(1)} %copy-done.3, f32[32,2,512]{0,1,2:T(2,128)S(1)} %copy-done.2), kind=kOutput, calls=%fused_computation.23 | convolution fusion | flops 1703936 | bytes 933888 | tf_op jit(solution)/shard_map/unc,knc->kuc/dot_general | solution.py:110
  290.6 1.5 copy.79
  292.1 0.9 copy.80
  293.0 2.0 fusion.10
  295.0 0.0 all-gather.17.cloned.1.call-update
  295.0 0.0 all-gather.19.cloned.1.call-done
  295.0 59.8 %all-gather.17.cloned.1.call-done = bf16[128,4096]{0,1:T(8,128)(2,1)} async-done(((bf16[128,512]{0,1:T(8,128)(2,1)}), bf16[128,4096]{0,1:T(8,128)(2,1)}) %all-gather.17.cloned.1.call-update) | async-done | bytes 1048592 | tf_op jit(solution)/shard_map/all_gather | solution.py:113
  354.8 3.9 %convolution_convert_fusion.1 = bf16[128,512]{1,0:T(8,128)(2,1)} fusion(bf16[128,4096]{0,1:T(8,128)(2,1)} %all-gather.17.cloned.1.call-done, bf16[4096,512]{1,0:T(8,128)(2,1)} %all-gather.19.cloned.1.call-done), kind=kOutput, calls=%fused_computation.26 | convolution fusion | flops 536936448 | bytes 5373952 | tf_op jit(solution)/shard_map/dot_general | solution.py:115
  (39 shorter events, 0.3 us)
Async XLA Ops:
  6.5 1.9 copy-start
  6.5 44.3 %all-gather.15.cloned.1.call-start = ((), (), s32[]{:S(2)}) async-start(), calls=%async_computation.1 | async-start | bytes 1179648 | tf_op jit(solution)/shard_map/all_gather | solution.py:35
  7.3 119.3 %all-gather.13.cloned.1.call-start = ((), (), s32[]{:S(2)}) async-start(), calls=%async_computation | async-start | bytes 12976128 | tf_op jit(solution)/shard_map/all_gather | solution.py:38
  9.4 285.6 %all-gather.19.cloned.1.call-start = ((), (), s32[]{:S(2)}) async-start(), calls=%async_computation.3 | async-start | bytes 4325376 | tf_op jit(solution)/shard_map/all_gather | solution.py:117
  10.2 344.6 %all-gather.17.cloned.1.call-start = ((), (), s32[]{:S(2)}) async-start(), calls=%async_computation.2 | async-start | bytes 1179648 | tf_op jit(solution)/shard_map/all_gather | solution.py:113
  135.6 0.8 copy-start.4
  137.0 46.4 %collective-permute-start = (bf16[2,1536]{1,0:T(2,128)(2,1)}, bf16[2,1536]{1,0:T(2,128)(2,1)}, u32[]{:S(2)}, u32[]{:S(2)}) collective-permute-start(bf16[2,1536]{1,0:T(2,128)(2,1)} %slice.62), channel_id=1, source_target_pairs={{0,1},{1,2},{2,3},{3,4},{4,5},{5,6},{6,7},{7,8},{8,9},{9,10},{10,1... | collective-permute-start | bytes 18440 | tf_op jit(solution)/shard_map/ppermute | solution.py:15
  195.0 0.9 copy-start.1
  196.6 64.8 %copy-start.5 = (f32[512,2]{0,1:T(2,128)S(1)}, f32[512,2]{0,1:T(2,128)}, u32[]{:S(2)}) copy-start(f32[512,2]{0,1:T(2,128)} %param.17) | copy-start | bytes 12292
  196.6 64.8 %copy-start.6 = (f32[512,2]{0,1:T(2,128)S(1)}, f32[512,2]{0,1:T(2,128)}, u32[]{:S(2)}) copy-start(f32[512,2]{0,1:T(2,128)} %param.16) | copy-start | bytes 12292
  196.6 64.8 %copy-start.8 = (f32[4]{0:T(128)S(1)}, f32[4]{0:T(128)}, u32[]{:S(2)}) copy-start(f32[4]{0:T(128)} %fusion.27) | copy-start | bytes 52
  196.6 64.8 %copy-start.9 = (f32[4]{0:T(128)S(1)}, f32[4]{0:T(128)}, u32[]{:S(2)}) copy-start(f32[4]{0:T(128)} %multiply_convert_fusion) | copy-start | bytes 52
  269.3 15.9 %copy-start.2 = (f32[32,2,512]{0,1,2:T(2,128)S(1)}, f32[32,2,512]{0,1,2:T(2,128)}, u32[]{:S(2)}) copy-start(f32[32,2,512]{0,1,2:T(2,128)} %copy.78) | copy-start | bytes 393220
  269.3 15.9 %copy-start.3 = (f32[4,2,512]{0,1,2:T(2,128)S(1)}, f32[4,2,512]{0,1,2:T(2,128)}, u32[]{:S(2)}) copy-start(f32[4,2,512]{0,1,2:T(2,128)} %copy.77) | copy-start | bytes 49156
  285.2 7.8 %copy-start.7 = (f32[512]{0:T(512)S(1)}, f32[512]{0:T(512)}, u32[]{:S(2)}) copy-start(f32[512]{0:T(512)} %param.19) | copy-start | bytes 6148
Sparse Core Ops, SparseCore 0:
  9.2 41.6 all-gather.14
  53.3 73.1 all-gather.12
  129.1 51.0 all-gather.18
  295.1 59.6 all-gather.16
where the time goes:
time: 368 us; the launch traced here: 365 us
  waiting for transfers between devices  144 us (39%)
  blocking collectives  98.1 us (27%)
  matrix products  51.2 us (14%)
  local copies, waits for them, and re-layouts  42.9 us (12%)
  between operations  13.4 us (4%)
  other arithmetic  12.8 us (3%)
    all_gather x4, blocking collectives, prefix_2(): gathered = jax.tree.map(lambda a: lax.all_gather(a, axis), part)  98.1 us
    all_gather x1, waiting for transfers between devices, body(): piece = lax.all_gather(own_weight, 'seq', axis=0, tiled=True)  75.7 us
    all_gather x1, waiting for transfers between devices, body(): gathered = lax.all_gather(gated, 'ch', axis=1, tiled=True)  59.8 us
    dot_general x1, matrix products, body(): inner = jnp.einsum('tsc,ksc->ktc', toeplitz, blocked, precision=highest)  15.9 us
    gather x2, local copies, waits for them, and re-layouts, body(): kernel[jnp.clip(offsets, 0, BLOCK - 1)]  13.4 us
    dot_general x1, matrix products, body(): jnp.dot(cols, piece.reshape(piece.shape[0], -1), preferred_element_type=j...  9.08 us
    all_gather x1, waiting for transfers between devices, body(): features = lax.all_gather(inputs, 'ch', axis=1, tiled=True)  7.56 us
  transfers between devices with their start and end apart: 5, of which 3 were waited for; matrix products, arithmetic and copies ran while one was open for 27% of the time, Pallas kernels for 0%

commit v1 on v0

v1 whole, which is shorter than its diff:
```python
import functools

import jax
import jax.numpy as jnp
from jax import lax
from jax.experimental import pallas as pl
from jax.experimental.pallas import tpu as pltpu
from jax.sharding import PartitionSpec as P

HALO = 16
LANES = 128
SUB = 8
VMEM = 58 * 1024 * 1024


def spread(x, axis):
    count = lax.axis_size(axis)
    return lax.all_to_all(
        jnp.broadcast_to(x[None], (count,) + x.shape), axis, 0, 0, tiled=True
    )


def powers(exponent, rate, turn):
    mag = jnp.exp(-exponent[:, None, None] * rate[None])
    phase = exponent[:, None, None] * turn[None]
    return mag * jnp.cos(phase), mag * jnp.sin(phase)


def project_kernel(
    rows, chans, x_ref, w_ref, taps_ref, step_ref, join_ref, mixin_ref, query_ref, begin_ref, final_ref, acc
):
    place = pl.program_id(0)

    @pl.when(place == 0)
    def _():
        acc[...] = jnp.zeros_like(acc)

    acc[...] += jnp.dot(x_ref[0], w_ref[...], preferred_element_type=jnp.float32)

    @pl.when(place == pl.num_programs(0) - 1)
    def _():
        length = rows // SUB

        def filtered(branch):
            cols = slice(branch * chans, (branch + 1) * chans)
            now = acc[:rows, cols].astype(jnp.bfloat16).astype(jnp.float32)
            past = acc[rows : rows + 8, cols].astype(jnp.bfloat16).astype(jnp.float32)
            one = jnp.concatenate([past[1:2], now[:-1]], axis=0)
            two = jnp.concatenate([past[0:2], now[:-2]], axis=0)
            tap = [taps_ref[3 * j + branch : 3 * j + branch + 1, :] for j in range(3)]
            return tap[0] * now + tap[1] * one + tap[2] * two

        query = filtered(0)
        mixin = filtered(1) * filtered(2)
        for q in range(chans // LANES):
            cols = slice(q * LANES, (q + 1) * LANES)
            query_ref[q] = query[:, cols]
            mixin_ref[q] = mixin[:, cols]
        for q in range(chans // LANES):
            cols = slice(q * LANES, (q + 1) * LANES)
            wide = lambda row: jnp.broadcast_to(row, (SUB, LANES))
            ar = [wide(step_ref[n : n + 1, cols]) for n in range(2)]
            ai = [wide(step_ref[2 + n : 3 + n, cols]) for n in range(2)]
            re = [jnp.zeros((SUB, LANES), jnp.float32)] * 2
            im = [jnp.zeros((SUB, LANES), jnp.float32)] * 2
            for i in range(length):
                u = mixin_ref[q, pl.ds(i, SUB, stride=length), :]
                for n in range(2):
                    re[n], im[n] = ar[n] * re[n] - ai[n] * im[n] + u, ar[n] * im[n] + ai[n] * re[n]
            for n in range(2):
                jr = join_ref[n : n + 1, cols]
                ji = join_ref[2 + n : 3 + n, cols]
                er = jnp.zeros((1, LANES), jnp.float32)
                ei = jnp.zeros((1, LANES), jnp.float32)
                for b in range(SUB):
                    begin_ref[n, b : b + 1, cols] = er
                    begin_ref[2 + n, b : b + 1, cols] = ei
                    er, ei = (
                        jr * er - ji * ei + re[n][b : b + 1],
                        jr * ei + ji * er + im[n][b : b + 1],
                    )
                final_ref[n : n + 1, cols] = er
                final_ref[2 + n : 3 + n, cols] = ei


def gate_kernel(
    rows, chans, all_ref, jump_ref, begin_ref, reach_ref, step_ref, residue_ref, bias_ref, mixin_ref, query_ref, out_ref, long
):
    length = rows // SUB
    entry = []
    for n in range(2):
        fr, fi = all_ref[:, n, :], all_ref[:, 2 + n, :]
        cr, ci = jump_ref[n], jump_ref[2 + n]
        gr = jnp.sum(cr * fr - ci * fi, axis=0, keepdims=True)
        gi = jnp.sum(cr * fi + ci * fr, axis=0, keepdims=True)
        rr, ri = reach_ref[n], reach_ref[2 + n]
        entry.append((begin_ref[n] + rr * gr - ri * gi, begin_ref[2 + n] + rr * gi + ri * gr))
    for q in range(chans // LANES):
        cols = slice(q * LANES, (q + 1) * LANES)
        wide = lambda row: jnp.broadcast_to(row, (SUB, LANES))
        ar = [wide(step_ref[n : n + 1, cols]) for n in range(2)]
        ai = [wide(step_ref[2 + n : 3 + n, cols]) for n in range(2)]
        pr = [wide(residue_ref[n : n + 1, cols]) for n in range(2)]
        pi = [wide(residue_ref[2 + n : 3 + n, cols]) for n in range(2)]
        direct = wide(bias_ref[:, cols])
        re = [entry[n][0][:, cols] for n in range(2)]
        im = [entry[n][1][:, cols] for n in range(2)]
        for i in range(length):
            u = mixin_ref[q, pl.ds(i, SUB, stride=length), :]
            y = direct * u
            for n in range(2):
                re[n], im[n] = ar[n] * re[n] - ai[n] * im[n] + u, ar[n] * im[n] + ai[n] * re[n]
                y = y + (pr[n] * re[n] - pi[n] * im[n])
            long[q, pl.ds(i, SUB, stride=length), :] = y
        out_ref[:, cols] = (query_ref[q] * long[q]).astype(out_ref.dtype)


def mix_kernel(x_ref, w_ref, out_ref, acc):
    place = pl.program_id(0)

    @pl.when(place == 0)
    def _():
        acc[...] = jnp.zeros_like(acc)

    acc[...] += jnp.dot(x_ref[0], w_ref[...], preferred_element_type=jnp.float32)

    @pl.when(place == pl.num_programs(0) - 1)
    def _():
        out_ref[...] = acc[...].astype(out_ref.dtype)


def body(inputs, in_weight, out_weight, short_filter, decay, angle, residue, bias):
    rows, chans = inputs.shape
    place, blocks = lax.axis_index("seq"), lax.axis_size("seq")
    count = lax.axis_size("ch")
    col_start = lax.axis_index("ch") * chans
    own_weight = jnp.concatenate(
        [lax.dynamic_slice(in_weight[:, g, :], (0, col_start), (in_weight.shape[0], chans)) for g in range(3)],
        axis=1,
    )
    weight = lax.all_gather(own_weight, "seq", axis=0, tiled=True)
    second = lax.all_gather(out_weight, "seq", axis=0, tiled=True)

    rim = lax.ppermute(inputs[-2:], "seq", [(i, i + 1) for i in range(blocks - 1)])
    tokens = jnp.concatenate([inputs, rim, jnp.zeros((HALO - 2, chans), inputs.dtype)], axis=0)
    features = spread(tokens, "ch")

    rate, turn = decay.T, angle.T
    length = rows // SUB
    pack = lambda pair: jnp.concatenate(pair, axis=1)
    step = pack(powers(jnp.ones((1,), jnp.float32), rate, turn))[0]
    join = pack(powers(jnp.full((1,), length, jnp.float32), rate, turn))[0]
    reach = pack(powers((jnp.arange(SUB) * length).astype(jnp.float32), rate, turn))
    reach = reach.transpose(1, 0, 2)
    gap = place - 1 - jnp.arange(blocks)
    jump = pack(powers((jnp.maximum(gap, 0) * rows).astype(jnp.float32), rate, turn))
    jump = jnp.where((gap >= 0)[:, None, None], jump, 0.0).transpose(1, 0, 2)
    poles = jnp.concatenate([residue[0].T, residue[1].T], axis=0)

    f32 = jnp.float32
    whole = lambda shape: pl.BlockSpec(shape, lambda k: (0,) * len(shape))
    mixin, query, begin, final = pl.pallas_call(
        functools.partial(project_kernel, rows, chans),
        grid=(count,),
        in_specs=[
            pl.BlockSpec((1, rows + HALO, chans), lambda k: (k, 0, 0)),
            pl.BlockSpec((chans, 3 * chans), lambda k: (k, 0)),
            whole((9, chans)),
            whole((4, chans)),
            whole((4, chans)),
        ],
        out_specs=[
            whole((chans // LANES, rows, LANES)),
            whole((chans // LANES, rows, LANES)),
            whole((4, SUB, chans)),
            whole((4, chans)),
        ],
        out_shape=[
            jax.ShapeDtypeStruct((chans // LANES, rows, LANES), f32),
            jax.ShapeDtypeStruct((chans // LANES, rows, LANES), f32),
            jax.ShapeDtypeStruct((4, SUB, chans), f32),
            jax.ShapeDtypeStruct((4, chans), f32),
        ],
        scratch_shapes=[pltpu.VMEM((rows + HALO, 3 * chans), f32)],
        compiler_params=pltpu.CompilerParams(vmem_limit_bytes=VMEM),
        name="project",
    )(features, weight, short_filter.reshape(9, chans), step, join)

    states = spread(final, "seq")
    gated = pl.pallas_call(
        functools.partial(gate_kernel, rows, chans),
        out_shape=jax.ShapeDtypeStruct((rows, chans), jnp.bfloat16),
        scratch_shapes=[pltpu.VMEM((chans // LANES, rows, LANES), f32)],
        compiler_params=pltpu.CompilerParams(vmem_limit_bytes=VMEM),
        name="gate",
    )(states, jump, begin, reach, step, poles, bias[None, :], mixin, query)

    gathered = spread(gated, "ch")
    return pl.pallas_call(
        mix_kernel,
        grid=(count,),
        in_specs=[
            pl.BlockSpec((1, rows, chans), lambda k: (k, 0, 0)),
            pl.BlockSpec((chans, chans), lambda k: (k, 0)),
        ],
        out_specs=pl.BlockSpec((rows, chans), lambda k: (0, 0)),
        out_shape=jax.ShapeDtypeStruct((rows, chans), jnp.bfloat16),
        scratch_shapes=[pltpu.VMEM((rows, chans), f32)],
        compiler_params=pltpu.CompilerParams(vmem_limit_bytes=VMEM),
        name="mix",
    )(gathered, second)


def solution(mesh):
    placed = (
        P("seq", "ch"),
        P("seq", None, None),
        P("seq", "ch"),
        P(None, None, "ch"),
        P("ch", None),
        P("ch", None),
        P(None, "ch", None),
        P("ch"),
    )
    return jax.shard_map(
        body, mesh=mesh, in_specs=placed, out_specs=P("seq", "ch"), check_vma=False
    )
```

time: 368 us -> 164 us (0.45)
  blocking collectives: 98.1 us -> 0 us
  matrix products: 51.2 us -> 0 us
  waiting for transfers between devices: 144 us -> 92.8 us
  local copies, waits for them, and re-layouts: 42.9 us -> 9.15 us
  starting transfers between devices: 2.28 us -> 23.2 us
  Pallas kernels: 0 us -> 18.7 us
  other arithmetic: 12.8 us -> 4.44 us
    all_gather x4 -> x2, waiting for transfers between devices: 143 us -> 40.6 us  [the longest x1 24.7 us: body(): weight = lax.all_gather(own_weight, 'seq', axis=0, tiled=True)]
    all_gather x4 -> x0, blocking collectives: 98.1 us -> none  [prefix_2(): gathered = jax.tree.map(lambda a: lax.all_gather(a, axis), part)]
    dot_general x7 -> x0, matrix products: 51.2 us -> none  [the longest x1 15.9 us: body(): inner = jnp.einsum('tsc,ksc->ktc', toeplitz, blocked, precision=highest)]
    all_to_all x0 -> x3, waiting for transfers between devices: none -> 48.6 us  [spread(): lax.all_to_all(jnp.broadcast_to(x[None], (count,) + x.shape), axis, 0, 0,...]
    all_to_all x0 -> x3, starting transfers between devices: none -> 21.2 us  [spread(): lax.all_to_all(jnp.broadcast_to(x[None], (count,) + x.shape), axis, 0, 0,...]
    pallas_call x0 -> x3, Pallas kernels: none -> 18.7 us  [the longest x1 9.99 us: body(): pl.pallas_call(functools.partial(project_kernel, rows, chans), grid=(coun...]
    gather x2 -> x0, local copies, waits for them, and re-layouts: 13.4 us -> none  [body(): kernel[jnp.clip(offsets, 0, BLOCK - 1)]]
    mul x5 -> x0, local copies, waits for them, and re-layouts: 7.08 us -> none  [the longest x2 3.88 us: powers(): return (mag * jnp.cos(phase), mag * jnp.sin(phase))]
  transfers between devices with their start and end apart: 5 -> 6, of which waited for: 3 -> 6; matrix products, arithmetic and copies ran while one was open for 27% -> 6% of each run, Pallas kernels for 0% -> 8%
where the time goes in v1:
time: 164 us; the launch traced here: 162 us
  waiting for transfers between devices  92.8 us (57%)
  starting transfers between devices  23.2 us (14%)
  Pallas kernels  18.7 us (11%)
  between operations  13.6 us (8%)
  local copies, waits for them, and re-layouts  9.15 us (6%)
  other arithmetic  4.44 us (3%)
    all_to_all x3, waiting for transfers between devices, spread(): lax.all_to_all(jnp.broadcast_to(x[None], (count,) + x.shape), axis, 0, 0,...  48.6 us
    all_gather x1, waiting for transfers between devices, body(): weight = lax.all_gather(own_weight, 'seq', axis=0, tiled=True)  24.7 us
    all_to_all x3, starting transfers between devices, spread(): lax.all_to_all(jnp.broadcast_to(x[None], (count,) + x.shape), axis, 0, 0,...  21.2 us
    all_gather x1, waiting for transfers between devices, body(): second = lax.all_gather(out_weight, 'seq', axis=0, tiled=True)  15.9 us
    pallas_call x1, Pallas kernels, body(): pl.pallas_call(functools.partial(project_kernel, rows, chans), grid=(coun...  9.99 us
    pallas_call x1, Pallas kernels, body(): pl.pallas_call(mix_kernel, grid=(count,), in_specs=[pl.BlockSpec((1, rows...  6.41 us
    broadcast_in_dim x3, local copies, waits for them, and re-layouts, spread(): jnp.broadcast_to(x[None], (count,) + x.shape)  4.56 us
  transfers between devices with their start and end apart: 6, of which 6 were waited for; matrix products, arithmetic and copies ran while one was open for 6% of the time, Pallas kernels for 8%

profile of v1, /device:TPU:2, one launch (start us, length us, event | category | flops | bytes accessed | tf_op | source)
XLA Modules:
  0.0 161.9 jit_solution(3576276766910194526)
XLA Ops:
  6.5 0.0 all-gather.3.cloned.1.call-start
  6.5 0.0 copy-start.3
  6.5 2.1 %fusion.8 = (bf16[128,1,4096]{2,0,1:T(8,128)(2,1)S(1)}, bf16[128,1,4096]{2,0,1:T(8,128)(2,1)S(1)}, bf16[128,1,4096]{2,0,1:T(8,128)(2,1)S(1)}) fusion(bf16[128,3,4096]{2,0,1:T(8,128)(2,1)} %param.9), kind=kLoop, calls=%fused_computation.35 | loop fusion | bytes 6291456 | tf_op jit(solution)/shard_map/slice | solution.py:138
  8.6 0.0 copy-start.6
  8.6 0.0 copy-start.7
  8.7 0.0 copy-start.4
  8.7 0.0 copy-start.5
  8.8 0.8 pad_maximum_fusion
  9.5 0.0 all-gather.3.cloned.1.call-update
  9.6 0.0 all-gather.5.cloned.1.call-start
  9.6 0.7 all-gather.5.cloned.1.call-update
  10.3 0.0 copy-done.3
  10.3 1.9 %collective-permute-start = (bf16[2,512]{1,0:T(2,128)(2,1)S(1)}, bf16[2,512]{1,0:T(2,128)(2,1)S(1)}, u32[]{:S(2)}, u32[]{:S(2)}) collective-permute-start(bf16[2,512]{1,0:T(2,128)(2,1)S(1)} %slice.18), channel_id=1, source_target_pairs={{0,1},{1,2},{2,3},{3,4},{4,5},{5,6},{6,7},{7,8},{8,9},{9,10},{10,1... | collective-permute-start | bytes 6152 | tf_op jit(solution)/shard_map/ppermute | solution.py:144
  12.3 0.1 pad.15.clone
  12.3 2.9 %collective-permute-done = bf16[2,512]{1,0:T(2,128)(2,1)S(1)} collective-permute-done((bf16[2,512]{1,0:T(2,128)(2,1)S(1)}, bf16[2,512]{1,0:T(2,128)(2,1)S(1)}, u32[]{:S(2)}, u32[]{:S(2)}) %collective-permute-start) | collective-permute-done | bytes 2080 | tf_op jit(solution)/shard_map/ppermute | solution.py:144
  15.2 0.1 maximum_maximum_fusion
  15.3 1.1 broadcast_in_dim.19
  16.5 8.5 %all-to-all-start = ((bf16[8,144,512]{2,1,0:T(8,128)(2,1)}), bf16[8,144,512]{2,1,0:T(8,128)(2,1)S(1)}, u32[]{:S(2)}, u32[]{:S(2)}) async-start(bf16[8,144,512]{2,1,0:T(8,128)(2,1)} %broadcast_in_dim.19), calls=%async_computation | async-start | bytes 2359296 | tf_op jit(solution)/shard_map/all_to_all | solution.py:18
  24.9 0.0 copy-done.6
  24.9 0.6 reshape.47.taps_ref
  25.6 0.0 copy-done.7
  25.6 0.6 pad_maximum_fusion.1.residue_ref
  26.2 0.0 copy-done.4
  26.2 0.0 copy-done.5
  26.2 0.1 multiply_bitcast_fusion.1
  26.4 0.6 maximum_bitcast_fusion.1
  27.0 0.2 fusion.3
  27.2 0.6 maximum_bitcast_fusion.reach_ref
  27.8 0.6 fusion.1
  28.4 27.6 %all-to-all-done.x_ref = bf16[8,144,512]{2,1,0:T(8,128)(2,1)S(1)} async-done(((bf16[8,144,512]{2,1,0:T(8,128)(2,1)}), bf16[8,144,512]{2,1,0:T(8,128)(2,1)S(1)}, u32[]{:S(2)}, u32[]{:S(2)}) %all-to-all-start) | async-done | bytes 1179680 | tf_op jit(solution)/shard_map/all_to_all | solution.py:18
  56.0 0.0 copy-start
  56.0 24.7 %all-gather.3.cloned.1.call-done.w_ref = bf16[4096,1536]{1,0:T(8,128)(2,1)} async-done(((bf16[128,1536]{1,0:T(8,128)(2,1)}), bf16[4096,1536]{1,0:T(8,128)(2,1)}) %all-gather.3.cloned.1.call-update) | async-done | bytes 12582928 | tf_op jit(solution)/shard_map/all_gather | solution.py:141
  80.7 0.0 copy-done
  80.7 10.0 %project.1 = (f32[4,128,128]{2,1,0:T(8,128)}, f32[4,128,128]{2,1,0:T(8,128)}, f32[4,8,512]{2,1,0:T(8,128)}, f32[4,512]{1,0:T(4,128)}) custom-call(bf16[8,144,512]{2,1,0:T(8,128)(2,1)} %copy-done, bf16[4096,1536]{1,0:T(8,128)(2,1)} %all-gather.3.cloned.1.call-done.w_ref, f32[9,512]{1,0:T(8,128)} %reshape.47.taps_ref, f32[4,512]{1,0:T(4,128)} %get-tuple-element.28.step_ref, ...), custom_call_target="tpu_custom_call" | custom-call | tf_op jit(solution)/shard_map/project/pallas_call | solution.py:162
  90.7 1.4 broadcast_in_dim.20
  92.1 5.7 %all-to-all-start.1 = ((f32[32,4,512]{2,1,0:T(4,128)}), f32[32,4,512]{2,1,0:T(4,128)S(1)}, u32[]{:S(2)}, u32[]{:S(2)}) async-start(f32[32,4,512]{2,1,0:T(4,128)} %broadcast_in_dim.20), calls=%async_computation.1 | async-start | bytes 524288 | tf_op jit(solution)/shard_map/all_to_all | solution.py:18
  97.9 0.8 fusion.jump_ref
  98.7 7.7 %all-to-all-done.1.all_ref = f32[32,4,512]{2,1,0:T(4,128)S(1)} async-done(((f32[32,4,512]{2,1,0:T(4,128)}), f32[32,4,512]{2,1,0:T(4,128)S(1)}, u32[]{:S(2)}, u32[]{:S(2)}) %all-to-all-start.1) | async-done | bytes 262176 | tf_op jit(solution)/shard_map/all_to_all | solution.py:18
  106.4 0.0 copy-start.2
  106.4 0.7 copy-done.2
  107.1 2.3 %gate.1 = bf16[128,512]{1,0:T(8,128)(2,1)} custom-call(f32[32,4,512]{2,1,0:T(4,128)} %copy-done.2, f32[4,32,512]{2,1,0:T(8,128)} %fusion.jump_ref, f32[4,8,512]{2,1,0:T(8,128)} %get-tuple-element.10.begin_ref, f32[4,8,512]{2,1,0:T(8,128)} %maximum_bitcast_fusion.reach_ref, f32[4,512]{1,0:T(4,128)} %get-tuple-element.28.step_ref, ...), custom_call_target="tpu_custom_call" | custom-call | tf_op jit(solution)/shard_map/gate/pallas_call | solution.py:190
  109.4 2.0 %broadcast_in_dim.28 = bf16[8,128,512]{2,1,0:T(8,128)(2,1)} broadcast(bf16[128,512]{1,0:T(8,128)(2,1)} %gate.1), dimensions={1,2} | broadcast | bytes 1179648 | tf_op jit(solution)/shard_map/broadcast_in_dim | solution.py:19
  111.4 7.0 %all-to-all-start.2 = ((bf16[8,128,512]{2,1,0:T(8,128)(2,1)}), bf16[8,128,512]{2,1,0:T(8,128)(2,1)S(1)}, u32[]{:S(2)}, u32[]{:S(2)}) async-start(bf16[8,128,512]{2,1,0:T(8,128)(2,1)} %broadcast_in_dim.28), calls=%async_computation.2 | async-start | bytes 2097152 | tf_op jit(solution)/shard_map/all_to_all | solution.py:18
  118.4 15.9 %all-gather.5.cloned.1.call-done.w_ref = bf16[4096,512]{1,0:T(8,128)(2,1)} async-done(((bf16[128,512]{1,0:T(8,128)(2,1)}), bf16[4096,512]{1,0:T(8,128)(2,1)}) %all-gather.5.cloned.1.call-update) | async-done | bytes 4194320 | tf_op jit(solution)/shard_map/all_gather | solution.py:142
  134.3 13.3 %all-to-all-done.2.x_ref = bf16[8,128,512]{2,1,0:T(8,128)(2,1)S(1)} async-done(((bf16[8,128,512]{2,1,0:T(8,128)(2,1)}), bf16[8,128,512]{2,1,0:T(8,128)(2,1)S(1)}, u32[]{:S(2)}, u32[]{:S(2)}) %all-to-all-start.2) | async-done | bytes 1048608 | tf_op jit(solution)/shard_map/all_to_all | solution.py:18
  147.6 0.0 copy-start.1
  147.6 1.0 copy-done.1
  148.6 6.4 %mix.1 = bf16[128,512]{1,0:T(8,128)(2,1)} custom-call(bf16[8,128,512]{2,1,0:T(8,128)(2,1)} %copy-done.1, bf16[4096,512]{1,0:T(8,128)(2,1)} %all-gather.5.cloned.1.call-done.w_ref), custom_call_target="tpu_custom_call" | custom-call | tf_op jit(solution)/shard_map/mix/pallas_call | solution.py:199
  (10 shorter events, 0.1 us)
Async XLA Ops:
  6.5 74.2 %all-gather.3.cloned.1.call-start = ((), (), s32[]{:S(2)}) async-start(), calls=%async_computation.3 | async-start | bytes 12976128 | tf_op jit(solution)/shard_map/all_gather | solution.py:141
  6.5 3.8 %copy-start.3 = (bf16[128,512]{1,0:T(8,128)(2,1)S(1)}, bf16[128,512]{1,0:T(8,128)(2,1)}, u32[]{:S(2)}) copy-start(bf16[128,512]{1,0:T(8,128)(2,1)} %param.8) | copy-start | bytes 393220
  8.6 16.3 %copy-start.6 = (f32[3,3,512]{2,1,0:T(4,128)S(1)}, f32[3,3,512]{2,1,0:T(4,128)}, u32[]{:S(2)}) copy-start(f32[3,3,512]{2,1,0:T(4,128)} %param.11) | copy-start | bytes 55300
  8.6 17.0 %copy-start.7 = (f32[2,512,2]{1,2,0:T(2,128)S(1)}, f32[2,512,2]{1,2,0:T(2,128)}, u32[]{:S(2)}) copy-start(f32[2,512,2]{1,2,0:T(2,128)} %param.14) | copy-start | bytes 24580
  8.7 17.6 %copy-start.4 = (f32[512,2]{0,1:T(2,128)S(1)}, f32[512,2]{0,1:T(2,128)}, u32[]{:S(2)}) copy-start(f32[512,2]{0,1:T(2,128)} %param.13) | copy-start | bytes 12292
  8.7 17.6 %copy-start.5 = (f32[512,2]{0,1:T(2,128)S(1)}, f32[512,2]{0,1:T(2,128)}, u32[]{:S(2)}) copy-start(f32[512,2]{0,1:T(2,128)} %param.12) | copy-start | bytes 12292
  9.6 124.7 %all-gather.5.cloned.1.call-start = ((), (), s32[]{:S(2)}) async-start(), calls=%async_computation.4 | async-start | bytes 4325376 | tf_op jit(solution)/shard_map/all_gather | solution.py:142
  10.3 4.9 %collective-permute-start = (bf16[2,512]{1,0:T(2,128)(2,1)S(1)}, bf16[2,512]{1,0:T(2,128)(2,1)S(1)}, u32[]{:S(2)}, u32[]{:S(2)}) collective-permute-start(bf16[2,512]{1,0:T(2,128)(2,1)S(1)} %slice.18), channel_id=1, source_target_pairs={{0,1},{1,2},{2,3},{3,4},{4,5},{5,6},{6,7},{7,8},{8,9},{9,10},{10,1... | collective-permute-start | bytes 6152 | tf_op jit(solution)/shard_map/ppermute | solution.py:144
  16.5 39.5 %all-to-all-start = ((bf16[8,144,512]{2,1,0:T(8,128)(2,1)}), bf16[8,144,512]{2,1,0:T(8,128)(2,1)S(1)}, u32[]{:S(2)}, u32[]{:S(2)}) async-start(bf16[8,144,512]{2,1,0:T(8,128)(2,1)} %broadcast_in_dim.19), calls=%async_computation | async-start | bytes 2359296 | tf_op jit(solution)/shard_map/all_to_all | solution.py:18
  56.0 24.8 %copy-start = (bf16[8,144,512]{2,1,0:T(8,128)(2,1)}, bf16[8,144,512]{2,1,0:T(8,128)(2,1)S(1)}, u32[]{:S(2)}) copy-start(bf16[8,144,512]{2,1,0:T(8,128)(2,1)S(1)} %all-to-all-done.x_ref) | copy-start | bytes 3538948
  92.1 14.2 %all-to-all-start.1 = ((f32[32,4,512]{2,1,0:T(4,128)}), f32[32,4,512]{2,1,0:T(4,128)S(1)}, u32[]{:S(2)}, u32[]{:S(2)}) async-start(f32[32,4,512]{2,1,0:T(4,128)} %broadcast_in_dim.20), calls=%async_computation.1 | async-start | bytes 524288 | tf_op jit(solution)/shard_map/all_to_all | solution.py:18
  106.4 0.7 copy-start.2
  111.4 36.2 %all-to-all-start.2 = ((bf16[8,128,512]{2,1,0:T(8,128)(2,1)}), bf16[8,128,512]{2,1,0:T(8,128)(2,1)S(1)}, u32[]{:S(2)}, u32[]{:S(2)}) async-start(bf16[8,128,512]{2,1,0:T(8,128)(2,1)} %broadcast_in_dim.28), calls=%async_computation.2 | async-start | bytes 2097152 | tf_op jit(solution)/shard_map/all_to_all | solution.py:18
  147.6 1.0 copy-start.1
Sparse Core Ops, SparseCore 0:
  9.9 70.7 all-gather.2
  83.3 50.9 all-gather.4

commit v2 on v1

v2 whole, which is shorter than its diff:
```python
import functools

import jax
import jax.numpy as jnp
from jax import lax
from jax.experimental import pallas as pl
from jax.experimental.pallas import tpu as pltpu
from jax.sharding import PartitionSpec as P

HALO = 16
LANES = 128
SUB = 8
VMEM = 58 * 1024 * 1024
SMALL = 16 * 1024 * 1024


def spread(x, axis):
    count = lax.axis_size(axis)
    return lax.all_to_all(
        jnp.broadcast_to(x[None], (count,) + x.shape), axis, 0, 0, tiled=True
    )


def powers(exponent, rate, turn):
    mag = jnp.exp(-exponent[:, None, None] * rate[None])
    phase = exponent[:, None, None] * turn[None]
    return mag * jnp.cos(phase), mag * jnp.sin(phase)


def project_kernel(half_ref, own_ref, other_ref, w_ref, keep_ref, send_ref, acc):
    place = pl.program_id(0)
    rows = own_ref.shape[1]

    @pl.when(place == 0)
    def _():
        acc[...] = jnp.zeros_like(acc)

    both = jnp.concatenate([own_ref[0], other_ref[0]], axis=0)
    acc[...] += jnp.dot(both, w_ref[...], preferred_element_type=jnp.float32)

    @pl.when(place == pl.num_programs(0) - 1)
    def _():
        keep_ref[...] = acc[:rows]
        send_ref[...] = acc[rows:].astype(send_ref.dtype)


def scan_kernel(
    rows, chans, keep_ref, more_ref, taps_ref, step_ref, join_ref, mixin_ref, query_ref, begin_ref, final_ref
):
    length = rows // SUB

    def filtered(branch):
        cols = slice(branch * chans, (branch + 1) * chans)
        total = keep_ref[:, cols] + more_ref[:, cols].astype(jnp.float32)
        total = total.astype(jnp.bfloat16).astype(jnp.float32)
        now = total[:rows]
        past = total[rows : rows + 8]
        one = jnp.concatenate([past[1:2], now[:-1]], axis=0)
        two = jnp.concatenate([past[0:2], now[:-2]], axis=0)
        tap = [taps_ref[3 * j + branch : 3 * j + branch + 1, :] for j in range(3)]
        return tap[0] * now + tap[1] * one + tap[2] * two

    query = filtered(0)
    mixin = filtered(1) * filtered(2)
    for q in range(chans // LANES):
        cols = slice(q * LANES, (q + 1) * LANES)
        query_ref[q] = query[:, cols]
        mixin_ref[q] = mixin[:, cols]
    for q in range(chans // LANES):
        cols = slice(q * LANES, (q + 1) * LANES)
        wide = lambda row: jnp.broadcast_to(row, (SUB, LANES))
        ar = [wide(step_ref[n : n + 1, cols]) for n in range(2)]
        ai = [wide(step_ref[2 + n : 3 + n, cols]) for n in range(2)]
        re = [jnp.zeros((SUB, LANES), jnp.float32)] * 2
        im = [jnp.zeros((SUB, LANES), jnp.float32)] * 2
        for i in range(length):
            u = mixin_ref[q, pl.ds(i, SUB, stride=length), :]
            for n in range(2):
                re[n], im[n] = ar[n] * re[n] - ai[n] * im[n] + u, ar[n] * im[n] + ai[n] * re[n]
        for n in range(2):
            jr = join_ref[n : n + 1, cols]
            ji = join_ref[2 + n : 3 + n, cols]
            er = jnp.zeros((1, LANES), jnp.float32)
            ei = jnp.zeros((1, LANES), jnp.float32)
            for b in range(SUB):
                begin_ref[n, b : b + 1, cols] = er
                begin_ref[2 + n, b : b + 1, cols] = ei
                er, ei = (
                    jr * er - ji * ei + re[n][b : b + 1],
                    jr * ei + ji * er + im[n][b : b + 1],
                )
            final_ref[n : n + 1, cols] = er
            final_ref[2 + n : 3 + n, cols] = ei


def gate_kernel(
    rows, chans, all_ref, jump_ref, begin_ref, reach_ref, step_ref, residue_ref, bias_ref, mixin_ref, query_ref, out_ref, long
):
    length = rows // SUB
    entry = []
    for n in range(2):
        fr, fi = all_ref[:, n, :], all_ref[:, 2 + n, :]
        cr, ci = jump_ref[n], jump_ref[2 + n]
        gr = jnp.sum(cr * fr - ci * fi, axis=0, keepdims=True)
        gi = jnp.sum(cr * fi + ci * fr, axis=0, keepdims=True)
        rr, ri = reach_ref[n], reach_ref[2 + n]
        entry.append((begin_ref[n] + rr * gr - ri * gi, begin_ref[2 + n] + rr * gi + ri * gr))
    for q in range(chans // LANES):
        cols = slice(q * LANES, (q + 1) * LANES)
        wide = lambda row: jnp.broadcast_to(row, (SUB, LANES))
        ar = [wide(step_ref[n : n + 1, cols]) for n in range(2)]
        ai = [wide(step_ref[2 + n : 3 + n, cols]) for n in range(2)]
        pr = [wide(residue_ref[n : n + 1, cols]) for n in range(2)]
        pi = [wide(residue_ref[2 + n : 3 + n, cols]) for n in range(2)]
        direct = wide(bias_ref[:, cols])
        re = [entry[n][0][:, cols] for n in range(2)]
        im = [entry[n][1][:, cols] for n in range(2)]
        for i in range(length):
            u = mixin_ref[q, pl.ds(i, SUB, stride=length), :]
            y = direct * u
            for n in range(2):
                re[n], im[n] = ar[n] * re[n] - ai[n] * im[n] + u, ar[n] * im[n] + ai[n] * re[n]
                y = y + (pr[n] * re[n] - pi[n] * im[n])
            long[q, pl.ds(i, SUB, stride=length), :] = y
        out_ref[:, cols] = (query_ref[q] * long[q]).astype(out_ref.dtype)


def mix_kernel(count, which_ref, *refs):
    x_refs, (w_ref, base_ref, out_ref, acc) = refs[:count], refs[count:]
    place = pl.program_id(0)

    @pl.when(place == 0)
    def _():
        acc[...] = base_ref[...].astype(jnp.float32)

    for j in range(count):

        @pl.when(place == j)
        def _(j=j):
            acc[...] += jnp.dot(x_refs[j][...], w_ref[...], preferred_element_type=jnp.float32)

    @pl.when(place == count - 1)
    def _():
        out_ref[...] = acc[...].astype(out_ref.dtype)


def mix(blocks, which, weight, base, dtype):
    rows, chans = blocks[0].shape
    cols = weight.shape[1]
    whole = lambda shape: pl.BlockSpec(shape, lambda k, w: (0,) * len(shape))
    return pl.pallas_call(
        functools.partial(mix_kernel, len(blocks)),
        grid_spec=pltpu.PrefetchScalarGridSpec(
            num_scalar_prefetch=1,
            grid=(len(blocks),),
            in_specs=[whole((rows, chans)) for _ in blocks]
            + [pl.BlockSpec((chans, cols), lambda k, w: (w[k], 0)), whole((rows, cols))],
            out_specs=whole((rows, cols)),
            scratch_shapes=[pltpu.VMEM((rows, cols), jnp.float32)],
        ),
        out_shape=jax.ShapeDtypeStruct((rows, cols), dtype),
        compiler_params=pltpu.CompilerParams(vmem_limit_bytes=SMALL),
        cost_estimate=pl.CostEstimate(
            flops=2 * len(blocks) * rows * chans * cols,
            bytes_accessed=2 * len(blocks) * chans * cols,
            transcendentals=0,
        ),
        name="mix",
    )(which, *blocks, weight, base)


def body(inputs, in_weight, out_weight, short_filter, decay, angle, residue, bias):
    rows, chans = inputs.shape
    place, blocks = lax.axis_index("seq"), lax.axis_size("seq")
    count = lax.axis_size("ch")
    col_start = lax.axis_index("ch") * chans
    own_weight = jnp.concatenate(
        [lax.dynamic_slice(in_weight[:, g, :], (0, col_start), (in_weight.shape[0], chans)) for g in range(3)],
        axis=1,
    )
    half = blocks // 2
    weight = lax.all_gather(
        own_weight,
        "seq",
        axis=0,
        tiled=True,
        axis_index_groups=[list(range(half)), list(range(half, blocks))],
    )
    second = lax.all_gather(out_weight, "seq", axis=0, tiled=True)

    rim = lax.ppermute(inputs[-2:], "seq", [(i, i + 1) for i in range(blocks - 1)])
    tokens = jnp.concatenate([inputs, rim, jnp.zeros((HALO - 2, chans), inputs.dtype)], axis=0)
    group = blocks // 4
    mirror = lambda s: (3 - s // group) * group + s % group
    swaps = []
    for c in range(count):
        for s in range(blocks):
            near = c // (count // 2) == s // half
            to = (c, s) if near else (count - 1 - c, mirror(s))
            swaps.append((c * blocks + s, to[0] * blocks + to[1]))
    features = spread(lax.ppermute(tokens, ("ch", "seq"), swaps), "ch")

    rate, turn = decay.T, angle.T
    length = rows // SUB
    pack = lambda pair: jnp.concatenate(pair, axis=1)
    step = pack(powers(jnp.ones((1,), jnp.float32), rate, turn))[0]
    join = pack(powers(jnp.full((1,), length, jnp.float32), rate, turn))[0]
    reach = pack(powers((jnp.arange(SUB) * length).astype(jnp.float32), rate, turn))
    reach = reach.transpose(1, 0, 2)
    gap = place - 1 - jnp.arange(blocks)
    jump = pack(powers((jnp.maximum(gap, 0) * rows).astype(jnp.float32), rate, turn))
    jump = jnp.where((gap >= 0)[:, None, None], jump, 0.0).transpose(1, 0, 2)
    poles = jnp.concatenate([residue[0].T, residue[1].T], axis=0)

    f32 = jnp.float32
    whole = lambda shape: pl.BlockSpec(shape, lambda k: (0,) * len(shape))
    quarter = count // 2
    padded = rows + HALO
    keep, send = pl.pallas_call(
        project_kernel,
        grid_spec=pltpu.PrefetchScalarGridSpec(
            num_scalar_prefetch=1,
            grid=(quarter,),
            in_specs=[
                pl.BlockSpec((1, padded, chans), lambda k, h: (h[0] * quarter + k, 0, 0)),
                pl.BlockSpec((1, padded, chans), lambda k, h: (count - 1 - h[0] * quarter - k, 0, 0)),
                pl.BlockSpec((chans, 3 * chans), lambda k, h: (k, 0)),
            ],
            out_specs=[
                pl.BlockSpec((padded, 3 * chans), lambda k, h: (0, 0)),
                pl.BlockSpec((padded, 3 * chans), lambda k, h: (0, 0)),
            ],
            scratch_shapes=[pltpu.VMEM((2 * padded, 3 * chans), f32)],
        ),
        out_shape=[
            jax.ShapeDtypeStruct((padded, 3 * chans), f32),
            jax.ShapeDtypeStruct((padded, 3 * chans), jnp.bfloat16),
        ],
        compiler_params=pltpu.CompilerParams(vmem_limit_bytes=VMEM),
        name="project",
    )((place // half).reshape(1).astype(jnp.int32), features, features, weight)
    more = lax.ppermute(send, "seq", [(s, mirror(s)) for s in range(blocks)])
    mixin, query, begin, final = pl.pallas_call(
        functools.partial(scan_kernel, rows, chans),
        out_shape=[
            jax.ShapeDtypeStruct((chans // LANES, rows, LANES), f32),
            jax.ShapeDtypeStruct((chans // LANES, rows, LANES), f32),
            jax.ShapeDtypeStruct((4, SUB, chans), f32),
            jax.ShapeDtypeStruct((4, chans), f32),
        ],
        compiler_params=pltpu.CompilerParams(vmem_limit_bytes=SMALL),
        name="scan",
    )(keep, more, short_filter.reshape(9, chans), step, join)

    states = spread(final, "seq")
    gated = pl.pallas_call(
        functools.partial(gate_kernel, rows, chans),
        out_shape=jax.ShapeDtypeStruct((rows, chans), jnp.bfloat16),
        scratch_shapes=[pltpu.VMEM((chans // LANES, rows, LANES), f32)],
        compiler_params=pltpu.CompilerParams(vmem_limit_bytes=SMALL),
        name="gate",
    )(states, jump, begin, reach, step, poles, bias[None, :], mixin, query)

    here = lax.axis_index("ch")
    up = [(c, (c + 1) % count) for c in range(count)]
    down = [(c, (c - 1) % count) for c in range(count)]
    arrived, origin = [gated], [here]
    below = above = gated
    for hop in range(1, count // 2 + 1):
        below = lax.ppermute(below, "ch", up)
        arrived.append(below)
        origin.append(here - hop)
        if 2 * hop < count:
            above = lax.ppermute(above, "ch", down)
            arrived.append(above)
            origin.append(here + hop)
    which = jnp.stack([lax.rem(o + count, count) for o in origin]).astype(jnp.int32)
    base = jnp.zeros((rows, chans), f32)
    first = mix(arrived[:5], which[:5], second, base, f32)
    return mix(arrived[5:], which[5:], second, first, jnp.bfloat16)


def solution(mesh):
    placed = (
        P("seq", "ch"),
        P("seq", None, None),
        P("seq", "ch"),
        P(None, None, "ch"),
        P("ch", None),
        P("ch", None),
        P(None, "ch", None),
        P("ch"),
    )
    return jax.shard_map(
        body, mesh=mesh, in_specs=placed, out_specs=P("seq", "ch"), check_vma=False
    )
```

time: 164 us -> 145 us (0.88); the launches traced: 162 us -> 145 us
  waiting for transfers between devices: 92.8 us -> 68.1 us
  starting transfers between devices: 23.2 us -> 40.5 us
  Pallas kernels: 18.7 us -> 11.5 us
  other arithmetic: 4.44 us -> 2 us
    all_gather x1, waiting for transfers between devices: 24.7 us -> 0.01 us  [body(): lax.all_gather(own_weight, 'seq', axis=0, tiled=True, axis_index_groups=[...]
    ppermute x0 -> x9, waiting for transfers between devices: none -> 24.2 us  [the longest x1 12.9 us: body(): more = lax.ppermute(send, 'seq', [(s, mirror(s)) for s in range(blocks)])]
    all_gather x1, waiting for transfers between devices: 15.9 us -> 0.01 us  [body(): second = lax.all_gather(out_weight, 'seq', axis=0, tiled=True)]
    ppermute x0 -> x9, starting transfers between devices: none -> 11.8 us  [the longest x3 9.7 us: body(): above = lax.ppermute(above, 'ch', down)]
    all_to_all x3 -> x2, waiting for transfers between devices: 48.6 us -> 40.4 us  [spread(): lax.all_to_all(jnp.broadcast_to(x[None], (count,) + x.shape), axis, 0, 0,...]
    all_to_all x3 -> x2, starting transfers between devices: 21.2 us -> 26.8 us  [spread(): lax.all_to_all(jnp.broadcast_to(x[None], (count,) + x.shape), axis, 0, 0,...]
    pallas_call x2 -> x4, Pallas kernels: 16.4 us -> 11.1 us  [the longest x1 6.56 us: body(): pl.pallas_call(project_kernel, grid_spec=pltpu.PrefetchScalarGridSpec(num...]
    broadcast_in_dim x3 -> x2, local copies, waits for them, and re-layouts: 4.56 us -> 1.85 us  [spread(): jnp.broadcast_to(x[None], (count,) + x.shape)]
  transfers between devices with their start and end apart: 6 -> 14, of which waited for: 6 -> 8; matrix products, arithmetic and copies ran while one was open for 6% -> 2% of each run, Pallas kernels for 8% -> 7%
where the time goes in v2:
time: 145 us
  waiting for transfers between devices  68.1 us (47%)
  starting transfers between devices  40.5 us (28%)
  between operations  13.7 us (9%)
  Pallas kernels  11.5 us (8%)
  local copies, waits for them, and re-layouts  8.61 us (6%)
  other arithmetic  2 us (1%)
    all_to_all x2, waiting for transfers between devices, spread(): lax.all_to_all(jnp.broadcast_to(x[None], (count,) + x.shape), axis, 0, 0,...  40.4 us
    all_to_all x2, starting transfers between devices, spread(): lax.all_to_all(jnp.broadcast_to(x[None], (count,) + x.shape), axis, 0, 0,...  26.8 us
    ppermute x1, waiting for transfers between devices, body(): more = lax.ppermute(send, 'seq', [(s, mirror(s)) for s in range(blocks)])  12.9 us
    ppermute x4, waiting for transfers between devices, body(): below = lax.ppermute(below, 'ch', up)  11.2 us
    ppermute x3, starting transfers between devices, body(): above = lax.ppermute(above, 'ch', down)  9.7 us
    pallas_call x1, Pallas kernels, body(): pl.pallas_call(project_kernel, grid_spec=pltpu.PrefetchScalarGridSpec(num...  6.56 us
    unnamed x20, local copies, waits for them, and re-layouts  4.41 us
    pallas_call x2, Pallas kernels, mix(): pl.pallas_call(functools.partial(mix_kernel, len(blocks)), grid_spec=pltp...  3.84 us
  transfers between devices with their start and end apart: 14, of which 8 were waited for; matrix products, arithmetic and copies ran while one was open for 2% of the time, Pallas kernels for 7%

profile of v2, /device:TPU:2, one launch (start us, length us, event | category | flops | bytes accessed | tf_op | source)
XLA Modules:
  0.0 144.5 jit_solution(6471464492474269118)
XLA Ops:
  6.5 0.0 all-gather.3.cloned.1.call-start
  6.5 0.0 copy-start.5
  6.5 2.1 %fusion.8 = (bf16[128,1,4096]{2,0,1:T(8,128)(2,1)S(1)}, bf16[128,1,4096]{2,0,1:T(8,128)(2,1)S(1)}, bf16[128,1,4096]{2,0,1:T(8,128)(2,1)S(1)}) fusion(bf16[128,3,4096]{2,0,1:T(8,128)(2,1)} %param.9), kind=kLoop, calls=%fused_computation.36 | loop fusion | bytes 6291456 | tf_op jit(solution)/shard_map/slice | solution.py:178
  8.6 0.0 copy-start.8
  8.6 0.0 copy-start.6
  8.7 0.0 copy-start.7
  8.7 0.0 copy-start.9
  8.7 0.8 pad_maximum_fusion
  9.5 0.0 all-gather.3.cloned.1.call-update
  9.6 0.0 all-gather.5.cloned.1.call-start
  9.6 0.7 all-gather.5.cloned.1.call-update
  10.3 0.0 copy-done.5
  10.3 1.9 %collective-permute-start = (bf16[2,512]{1,0:T(2,128)(2,1)S(1)}, bf16[2,512]{1,0:T(2,128)(2,1)S(1)}, u32[]{:S(2)}, u32[]{:S(2)}) collective-permute-start(bf16[2,512]{1,0:T(2,128)(2,1)S(1)} %slice.22), channel_id=1, source_target_pairs={{0,1},{1,2},{2,3},{3,4},{4,5},{5,6},{6,7},{7,8},{8,9},{9,10},{10,1... | collective-permute-start | bytes 6152 | tf_op jit(solution)/shard_map/ppermute | solution.py:191
  12.3 0.1 pad.15.clone
  12.4 2.9 %collective-permute-done = bf16[2,512]{1,0:T(2,128)(2,1)S(1)} collective-permute-done((bf16[2,512]{1,0:T(2,128)(2,1)S(1)}, bf16[2,512]{1,0:T(2,128)(2,1)S(1)}, u32[]{:S(2)}, u32[]{:S(2)}) %collective-permute-start) | collective-permute-done | bytes 2080 | tf_op jit(solution)/shard_map/ppermute | solution.py:191
  15.2 0.1 maximum_maximum_fusion
  15.3 0.7 collective-permute-start.1
  16.0 0.0 collective-permute-done.1
  16.0 1.1 broadcast_in_dim.19
  17.2 21.2 %all-to-all-start = ((bf16[8,144,512]{2,1,0:T(8,128)(2,1)}), bf16[8,144,512]{2,1,0:T(8,128)(2,1)S(1)}, u32[]{:S(2)}, u32[]{:S(2)}) async-start(bf16[8,144,512]{2,1,0:T(8,128)(2,1)} %broadcast_in_dim.19), calls=%async_computation | async-start | bytes 2359296 | tf_op jit(solution)/shard_map/all_to_all | solution.py:19
  38.4 0.0 copy-done.8
  38.5 0.0 copy-done.6
  38.5 0.0 copy-done.7
  38.5 0.1 multiply_bitcast_fusion.1
  38.7 0.0 copy-done.9
  38.7 0.2 fusion.3
  38.9 29.8 %all-to-all-done.own_ref.other_ref = bf16[8,144,512]{2,1,0:T(8,128)(2,1)S(1)} async-done(((bf16[8,144,512]{2,1,0:T(8,128)(2,1)}), bf16[8,144,512]{2,1,0:T(8,128)(2,1)S(1)}, u32[]{:S(2)}, u32[]{:S(2)}) %all-to-all-start) | async-done | bytes 1179680 | tf_op jit(solution)/shard_map/all_to_all | solution.py:19
  68.7 0.0 copy-start.4
  68.7 0.0 all-gather.3.cloned.1.call-done.w_ref
  68.7 1.0 copy-done.4
  69.7 0.0 copy-start.3
  69.7 6.6 %project.1 = (f32[144,1536]{1,0:T(8,128)}, bf16[144,1536]{1,0:T(8,128)(2,1)}) custom-call(s32[1]{0:T(128)} %bitcast.3.half_ref, bf16[8,144,512]{2,1,0:T(8,128)(2,1)} %copy-done.4, bf16[8,144,512]{2,1,0:T(8,128)(2,1)} %copy-done.4, bf16[2048,1536]{1,0:T(8,128)(2,1)} %all-gather.3.cloned.1.call-done.w_ref), custom_call_target="tpu_custom_call" | custom-call | tf_op jit(solution)/shard_map/project/pallas_call | solution.py:219
  76.3 1.3 collective-permute-start.2
  77.6 0.6 fusion.1
  78.2 12.9 %collective-permute-done.2.more_ref = bf16[144,1536]{1,0:T(8,128)(2,1)S(1)} collective-permute-done((bf16[144,1536]{1,0:T(8,128)(2,1)}, bf16[144,1536]{1,0:T(8,128)(2,1)S(1)}, u32[]{:S(2)}, u32[]{:S(2)}) %collective-permute-start.2) | collective-permute-done | bytes 442400 | tf_op jit(solution)/shard_map/ppermute | solution.py:242
  91.1 1.2 copy-done.2
  92.3 0.7 scan.1
  93.0 0.7 broadcast_in_dim.20
  93.7 5.5 %all-to-all-start.1 = ((f32[32,4,512]{2,1,0:T(4,128)}), f32[32,4,512]{2,1,0:T(4,128)S(1)}, u32[]{:S(2)}, u32[]{:S(2)}) async-start(f32[32,4,512]{2,1,0:T(4,128)} %broadcast_in_dim.20), calls=%async_computation.1 | async-start | bytes 524288 | tf_op jit(solution)/shard_map/all_to_all | solution.py:19
  99.3 0.1 fusion.jump_ref
  99.4 10.6 %all-to-all-done.1.all_ref = f32[32,4,512]{2,1,0:T(4,128)S(1)} async-done(((f32[32,4,512]{2,1,0:T(4,128)}), f32[32,4,512]{2,1,0:T(4,128)S(1)}, u32[]{:S(2)}, u32[]{:S(2)}) %all-to-all-start.1) | async-done | bytes 262176 | tf_op jit(solution)/shard_map/all_to_all | solution.py:19
  110.0 0.0 copy-done.3
  110.0 0.4 gate.1.refs_0_
  110.4 0.1 collective-permute-start.3
  110.5 3.2 %collective-permute-start.6 = (bf16[128,512]{1,0:T(8,128)(2,1)S(1)}, bf16[128,512]{1,0:T(8,128)(2,1)S(1)}, u32[]{:S(2)}, u32[]{:S(2)}) collective-permute-start(bf16[128,512]{1,0:T(8,128)(2,1)S(1)} %gate.1.refs_0_), channel_id=1, source_target_pairs={{0,224},{32,0},{64,32},{96,64},{128,96},{160,128},{192,160},{224,1... | collective-permute-start | bytes 393224 | tf_op jit(solution)/shard_map/ppermute | solution.py:274
  113.7 3.5 %collective-permute-done.3.refs_1_ = bf16[128,512]{1,0:T(8,128)(2,1)S(1)} collective-permute-done((bf16[128,512]{1,0:T(8,128)(2,1)S(1)}, bf16[128,512]{1,0:T(8,128)(2,1)S(1)}, u32[]{:S(2)}, u32[]{:S(2)}) %collective-permute-start.3) | collective-permute-done | bytes 131104 | tf_op jit(solution)/shard_map/ppermute | solution.py:270
  117.2 0.0 collective-permute-start.4
  117.2 0.0 collective-permute-done.6.refs_2_
  117.2 3.2 %collective-permute-start.7 = (bf16[128,512]{1,0:T(8,128)(2,1)S(1)}, bf16[128,512]{1,0:T(8,128)(2,1)S(1)}, u32[]{:S(2)}, u32[]{:S(2)}) collective-permute-start(bf16[128,512]{1,0:T(8,128)(2,1)S(1)} %collective-permute-done.6.refs_2_), channel_id=1, source_target_pairs={{0,224},{32,0},{64,32},{96,64},{128,96},{160,128},{192,160},{224,1... | collective-permute-start | bytes 393224 | tf_op jit(solution)/shard_map/ppermute | solution.py:274
  120.4 2.9 %collective-permute-done.4.refs_3_ = bf16[128,512]{1,0:T(8,128)(2,1)S(1)} collective-permute-done((bf16[128,512]{1,0:T(8,128)(2,1)S(1)}, bf16[128,512]{1,0:T(8,128)(2,1)S(1)}, u32[]{:S(2)}, u32[]{:S(2)}) %collective-permute-start.4) | collective-permute-done | bytes 131104 | tf_op jit(solution)/shard_map/ppermute | solution.py:270
  123.3 0.0 collective-permute-start.5
  123.3 0.1 stack.38.which_ref
  123.4 0.0 collective-permute-done.7.refs_4_
  123.4 3.2 %collective-permute-start.8 = (bf16[128,512]{1,0:T(8,128)(2,1)S(1)}, bf16[128,512]{1,0:T(8,128)(2,1)S(1)}, u32[]{:S(2)}, u32[]{:S(2)}) collective-permute-start(bf16[128,512]{1,0:T(8,128)(2,1)S(1)} %collective-permute-done.7.refs_4_), channel_id=1, source_target_pairs={{0,224},{32,0},{64,32},{96,64},{128,96},{160,128},{192,160},{224,1... | collective-permute-start | bytes 393224 | tf_op jit(solution)/shard_map/ppermute | solution.py:274
  126.7 2.8 %collective-permute-done.5.refs_0_ = bf16[128,512]{1,0:T(8,128)(2,1)S(1)} collective-permute-done((bf16[128,512]{1,0:T(8,128)(2,1)S(1)}, bf16[128,512]{1,0:T(8,128)(2,1)S(1)}, u32[]{:S(2)}, u32[]{:S(2)}) %collective-permute-start.5) | collective-permute-done | bytes 131104 | tf_op jit(solution)/shard_map/ppermute | solution.py:270
  129.5 0.0 collective-permute-start.9
  129.5 0.1 pad_add_fusion.which_ref
  129.6 0.0 copy-start
  129.6 2.2 %copy-done = bf16[4096,512]{1,0:T(8,128)(2,1)S(1)} copy-done((bf16[4096,512]{1,0:T(8,128)(2,1)S(1)}, bf16[4096,512]{1,0:T(8,128)(2,1)}, u32[]{:S(2)}) %copy-start) | copy-done | bytes 4194328
  131.8 1.9 %mix.2.refs_4_ = f32[128,512]{1,0:T(8,128)S(1)} custom-call(s32[5]{0:T(128)S(1)} %stack.38.which_ref, bf16[128,512]{1,0:T(8,128)(2,1)S(1)} %gate.1.refs_0_, bf16[128,512]{1,0:T(8,128)(2,1)S(1)} %collective-permute-done.3.refs_1_, bf16[128,512]{1,0:T(8,128)(2,1)S(1)} %collective-permute-done.6.refs_2_, bf16[128,512]{1,0:T(8,128)(2,1)S(1)} %collective-permute-done.4.refs_3_, ...), custom_call_target="tpu_custom_call" | custom-call | flops 335544320 | bytes 2621440 | tf_op jit(solution)/shard_map/mix/pallas_call | solution.py:151
  133.7 0.0 collective-permute-done.8.refs_1_
  133.7 2.0 %collective-permute-done.9.refs_2_ = bf16[128,512]{1,0:T(8,128)(2,1)S(1)} collective-permute-done((bf16[128,512]{1,0:T(8,128)(2,1)S(1)}, bf16[128,512]{1,0:T(8,128)(2,1)S(1)}, u32[]{:S(2)}, u32[]{:S(2)}) %collective-permute-start.9) | collective-permute-done | bytes 131104 | tf_op jit(solution)/shard_map/ppermute | solution.py:270
  135.7 0.0 copy-done.1
  135.7 2.0 %mix.3 = bf16[128,512]{1,0:T(8,128)(2,1)} custom-call(s32[3]{0:T(128)S(1)} %pad_add_fusion.which_ref, bf16[128,512]{1,0:T(8,128)(2,1)S(1)} %collective-permute-done.5.refs_0_, bf16[128,512]{1,0:T(8,128)(2,1)S(1)} %collective-permute-done.8.refs_1_, bf16[128,512]{1,0:T(8,128)(2,1)S(1)} %collective-permute-done.9.refs_2_, bf16[4096,512]{1,0:T(8,128)(2,1)S(1)} %copy-done.1, ...), custom_call_target="tpu_custom_call" | custom-call | flops 201326592 | bytes 1572864 | tf_op jit(solution)/shard_map/mix/pallas_call | solution.py:151
  (19 shorter events, 0.2 us)
Async XLA Ops:
  6.5 62.2 %all-gather.3.cloned.1.call-start = ((), (), s32[]{:S(2)}) async-start(), calls=%async_computation.2 | async-start | bytes 6684672 | tf_op jit(solution)/shard_map/all_gather | solution.py:182
  6.5 3.8 %copy-start.5 = (bf16[128,512]{1,0:T(8,128)(2,1)S(1)}, bf16[128,512]{1,0:T(8,128)(2,1)}, u32[]{:S(2)}) copy-start(bf16[128,512]{1,0:T(8,128)(2,1)} %param.8) | copy-start | bytes 393220
  8.6 29.8 %copy-start.8 = (f32[3,3,512]{2,1,0:T(4,128)S(1)}, f32[3,3,512]{2,1,0:T(4,128)}, u32[]{:S(2)}) copy-start(f32[3,3,512]{2,1,0:T(4,128)} %param.11) | copy-start | bytes 55300
  8.6 29.8 %copy-start.6 = (f32[512,2]{0,1:T(2,128)S(1)}, f32[512,2]{0,1:T(2,128)}, u32[]{:S(2)}) copy-start(f32[512,2]{0,1:T(2,128)} %param.13) | copy-start | bytes 12292
  8.7 29.8 %copy-start.7 = (f32[512,2]{0,1:T(2,128)S(1)}, f32[512,2]{0,1:T(2,128)}, u32[]{:S(2)}) copy-start(f32[512,2]{0,1:T(2,128)} %param.12) | copy-start | bytes 12292
  8.7 30.0 %copy-start.9 = (f32[2,512,2]{1,2,0:T(2,128)S(1)}, f32[2,512,2]{1,2,0:T(2,128)}, u32[]{:S(2)}) copy-start(f32[2,512,2]{1,2,0:T(2,128)} %param.14) | copy-start | bytes 24580
  9.6 120.0 %all-gather.5.cloned.1.call-start = ((), (), s32[]{:S(2)}) async-start(), calls=%async_computation.3 | async-start | bytes 4325376 | tf_op jit(solution)/shard_map/all_gather | solution.py:189
  10.3 4.9 %collective-permute-start = (bf16[2,512]{1,0:T(2,128)(2,1)S(1)}, bf16[2,512]{1,0:T(2,128)(2,1)S(1)}, u32[]{:S(2)}, u32[]{:S(2)}) collective-permute-start(bf16[2,512]{1,0:T(2,128)(2,1)S(1)} %slice.22), channel_id=1, source_target_pairs={{0,1},{1,2},{2,3},{3,4},{4,5},{5,6},{6,7},{7,8},{8,9},{9,10},{10,1... | collective-permute-start | bytes 6152 | tf_op jit(solution)/shard_map/ppermute | solution.py:191
  15.3 0.7 collective-permute-start.1
  17.2 51.5 %all-to-all-start = ((bf16[8,144,512]{2,1,0:T(8,128)(2,1)}), bf16[8,144,512]{2,1,0:T(8,128)(2,1)S(1)}, u32[]{:S(2)}, u32[]{:S(2)}) async-start(bf16[8,144,512]{2,1,0:T(8,128)(2,1)} %broadcast_in_dim.19), calls=%async_computation | async-start | bytes 2359296 | tf_op jit(solution)/shard_map/all_to_all | solution.py:19
  68.7 1.0 copy-start.4
  69.7 40.3 %copy-start.3 = (f32[512]{0:T(512)S(1)}, f32[512]{0:T(512)}, u32[]{:S(2)}) copy-start(f32[512]{0:T(512)} %param.15) | copy-start | bytes 6148
  76.3 14.8 %collective-permute-start.2 = (bf16[144,1536]{1,0:T(8,128)(2,1)}, bf16[144,1536]{1,0:T(8,128)(2,1)S(1)}, u32[]{:S(2)}, u32[]{:S(2)}) collective-permute-start(bf16[144,1536]{1,0:T(8,128)(2,1)} %get-tuple-element.12), channel_id=1, source_target_pairs={{0,24},{1,25},{2,26},{3,27},{4,28},{5,29},{6,30},{7,31},{8,16},{9,... | collective-permute-start | bytes 1327112 | tf_op jit(solution)/shard_map/ppermute | solution.py:242
  91.1 1.2 copy-start.2
  93.7 16.2 %all-to-all-start.1 = ((f32[32,4,512]{2,1,0:T(4,128)}), f32[32,4,512]{2,1,0:T(4,128)S(1)}, u32[]{:S(2)}, u32[]{:S(2)}) async-start(f32[32,4,512]{2,1,0:T(4,128)} %broadcast_in_dim.20), calls=%async_computation.1 | async-start | bytes 524288 | tf_op jit(solution)/shard_map/all_to_all | solution.py:19
  110.4 6.8 %collective-permute-start.3 = (bf16[128,512]{1,0:T(8,128)(2,1)S(1)}, bf16[128,512]{1,0:T(8,128)(2,1)S(1)}, u32[]{:S(2)}, u32[]{:S(2)}) collective-permute-start(bf16[128,512]{1,0:T(8,128)(2,1)S(1)} %gate.1.refs_0_), channel_id=1, source_target_pairs={{0,32},{32,64},{64,96},{96,128},{128,160},{160,192},{192,224},{224... | collective-permute-start | bytes 393224 | tf_op jit(solution)/shard_map/ppermute | solution.py:270
  110.5 6.7 %collective-permute-start.6 = (bf16[128,512]{1,0:T(8,128)(2,1)S(1)}, bf16[128,512]{1,0:T(8,128)(2,1)S(1)}, u32[]{:S(2)}, u32[]{:S(2)}) collective-permute-start(bf16[128,512]{1,0:T(8,128)(2,1)S(1)} %gate.1.refs_0_), channel_id=1, source_target_pairs={{0,224},{32,0},{64,32},{96,64},{128,96},{160,128},{192,160},{224,1... | collective-permute-start | bytes 393224 | tf_op jit(solution)/shard_map/ppermute | solution.py:274
  117.2 6.2 %collective-permute-start.4 = (bf16[128,512]{1,0:T(8,128)(2,1)S(1)}, bf16[128,512]{1,0:T(8,128)(2,1)S(1)}, u32[]{:S(2)}, u32[]{:S(2)}) collective-permute-start(bf16[128,512]{1,0:T(8,128)(2,1)S(1)} %collective-permute-done.3.refs_1_), channel_id=1, source_target_pairs={{0,32},{32,64},{64,96},{96,128},{128,160},{160,192},{192,224},{224... | collective-permute-start | bytes 393224 | tf_op jit(solution)/shard_map/ppermute | solution.py:270
  117.2 6.3 %collective-permute-start.7 = (bf16[128,512]{1,0:T(8,128)(2,1)S(1)}, bf16[128,512]{1,0:T(8,128)(2,1)S(1)}, u32[]{:S(2)}, u32[]{:S(2)}) collective-permute-start(bf16[128,512]{1,0:T(8,128)(2,1)S(1)} %collective-permute-done.6.refs_2_), channel_id=1, source_target_pairs={{0,224},{32,0},{64,32},{96,64},{128,96},{160,128},{192,160},{224,1... | collective-permute-start | bytes 393224 | tf_op jit(solution)/shard_map/ppermute | solution.py:274
  123.3 6.2 %collective-permute-start.5 = (bf16[128,512]{1,0:T(8,128)(2,1)S(1)}, bf16[128,512]{1,0:T(8,128)(2,1)S(1)}, u32[]{:S(2)}, u32[]{:S(2)}) collective-permute-start(bf16[128,512]{1,0:T(8,128)(2,1)S(1)} %collective-permute-done.4.refs_3_), channel_id=1, source_target_pairs={{0,32},{32,64},{64,96},{96,128},{128,160},{160,192},{192,224},{224... | collective-permute-start | bytes 393224 | tf_op jit(solution)/shard_map/ppermute | solution.py:270
  123.4 10.3 %collective-permute-start.8 = (bf16[128,512]{1,0:T(8,128)(2,1)S(1)}, bf16[128,512]{1,0:T(8,128)(2,1)S(1)}, u32[]{:S(2)}, u32[]{:S(2)}) collective-permute-start(bf16[128,512]{1,0:T(8,128)(2,1)S(1)} %collective-permute-done.7.refs_4_), channel_id=1, source_target_pairs={{0,224},{32,0},{64,32},{96,64},{128,96},{160,128},{192,160},{224,1... | collective-permute-start | bytes 393224 | tf_op jit(solution)/shard_map/ppermute | solution.py:274
  129.5 6.2 %collective-permute-start.9 = (bf16[128,512]{1,0:T(8,128)(2,1)S(1)}, bf16[128,512]{1,0:T(8,128)(2,1)S(1)}, u32[]{:S(2)}, u32[]{:S(2)}) collective-permute-start(bf16[128,512]{1,0:T(8,128)(2,1)S(1)} %collective-permute-done.5.refs_0_), channel_id=1, source_target_pairs={{0,32},{32,64},{64,96},{96,128},{128,160},{160,192},{192,224},{224... | collective-permute-start | bytes 393224 | tf_op jit(solution)/shard_map/ppermute | solution.py:270
  129.6 2.2 %copy-start = (bf16[4096,512]{1,0:T(8,128)(2,1)S(1)}, bf16[4096,512]{1,0:T(8,128)(2,1)}, u32[]{:S(2)}) copy-start(bf16[4096,512]{1,0:T(8,128)(2,1)} %all-gather.5.cloned.1.call-done.refs_5_.refs_3_) | copy-start | bytes 12582916
  131.8 3.9 %copy-start.1 = (bf16[4096,512]{1,0:T(8,128)(2,1)S(1)}, bf16[4096,512]{1,0:T(8,128)(2,1)}, u32[]{:S(2)}) copy-start(bf16[4096,512]{1,0:T(8,128)(2,1)} %all-gather.5.cloned.1.call-done.refs_5_.refs_3_) | copy-start | bytes 12582916
Sparse Core Ops, SparseCore 0:
  9.7 47.6 all-gather.2
  59.9 53.7 all-gather.4

commit v3 on v2

--- a/solution.py
+++ b/solution.py
@@ -21,24 +21,53 @@
     )
 
 
+def ring_hops(count):
+    hops = [0]
+    for hop in range(1, count // 2 + 1):
+        hops += [-hop, hop] if 2 * hop < count else [-hop]
+    return hops
+
+
+def ring(x, axis):
+    count = lax.axis_size(axis)
+    up = [(c, (c + 1) % count) for c in range(count)]
+    down = [(c, (c - 1) % count) for c in range(count)]
+    arrived = [x]
+    below = above = x
+    for hop in range(1, count // 2 + 1):
+        below = lax.ppermute(below, axis, up)
+        arrived.append(below)
+        if 2 * hop < count:
+            above = lax.ppermute(above, axis, down)
+            arrived.append(above)
+    return arrived
+
+
 def powers(exponent, rate, turn):
     mag = jnp.exp(-exponent[:, None, None] * rate[None])
     phase = exponent[:, None, None] * turn[None]
     return mag * jnp.cos(phase), mag * jnp.sin(phase)
 
 
-def project_kernel(half_ref, own_ref, other_ref, w_ref, keep_ref, send_ref, acc):
-    place = pl.program_id(0)
-    rows = own_ref.shape[1]
-
-    @pl.when(place == 0)
+def project_kernel(count, place_ref, *refs):
+    x_refs, (w_ref, keep_ref, send_ref, features, acc) = refs[:count], refs[count:]
+    step = pl.program_id(0)
+    quarter = pl.num_programs(0)
+    rows = x_refs[0].shape[0]
+    half, here = place_ref[0], place_ref[1]
+
+    @pl.when(step == 0)
     def _():
+        for x_ref, hop in zip(x_refs, ring_hops(count)):
+            features[lax.rem(here + hop + count, count)] = x_ref[...]
         acc[...] = jnp.zeros_like(acc)
 
-    both = jnp.concatenate([own_ref[0], other_ref[0]], axis=0)
+    own = features[half * quarter + step]
+    other = features[count - 1 - half * quarter - step]
+    both = jnp.concatenate([own, other], axis=0)
     acc[...] += jnp.dot(both, w_ref[...], preferred_element_type=jnp.float32)
 
-    @pl.when(place == pl.num_programs(0) - 1)
+    @pl.when(step == quarter - 1)
     def _():
         keep_ref[...] = acc[:rows]
         send_ref[...] = acc[rows:].astype(send_ref.dtype)
@@ -52,7 +81,6 @@
     def filtered(branch):
         cols = slice(branch * chans, (branch + 1) * chans)
         total = keep_ref[:, cols] + more_ref[:, cols].astype(jnp.float32)
-        total = total.astype(jnp.bfloat16).astype(jnp.float32)
         now = total[:rows]
         past = total[rows : rows + 8]
         one = jnp.concatenate([past[1:2], now[:-1]], axis=0)
@@ -126,12 +154,12 @@
 
 
 def mix_kernel(count, which_ref, *refs):
-    x_refs, (w_ref, base_ref, out_ref, acc) = refs[:count], refs[count:]
+    x_refs, (w_ref, out_ref, acc) = refs[:count], refs[count:]
     place = pl.program_id(0)
 
     @pl.when(place == 0)
     def _():
-        acc[...] = base_ref[...].astype(jnp.float32)
+        acc[...] = jnp.zeros_like(acc)
 
     for j in range(count):
 
@@ -144,7 +172,7 @@
         out_ref[...] = acc[...].astype(out_ref.dtype)
 
 
-def mix(blocks, which, weight, base, dtype):
+def mix(blocks, which, weight):
     rows, chans = blocks[0].shape
     cols = weight.shape[1]
     whole = lambda shape: pl.BlockSpec(shape, lambda k, w: (0,) * len(shape))
@@ -154,19 +182,14 @@
             num_scalar_prefetch=1,
             grid=(len(blocks),),
             in_specs=[whole((rows, chans)) for _ in blocks]
-            + [pl.BlockSpec((chans, cols), lambda k, w: (w[k], 0)), whole((rows, cols))],
+            + [pl.BlockSpec((chans, cols), lambda k, w: (w[k], 0))],
             out_specs=whole((rows, cols)),
             scratch_shapes=[pltpu.VMEM((rows, cols), jnp.float32)],
         ),
-        out_shape=jax.ShapeDtypeStruct((rows, cols), dtype),
-        compiler_params=pltpu.CompilerParams(vmem_limit_bytes=SMALL),
-        cost_estimate=pl.CostEstimate(
-            flops=2 * len(blocks) * rows * chans * cols,
-            bytes_accessed=2 * len(blocks) * chans * cols,
-            transcendentals=0,
-        ),
+        out_shape=jax.ShapeDtypeStruct((rows, cols), jnp.bfloat16),
+        compiler_params=pltpu.CompilerParams(vmem_limit_bytes=VMEM),
         name="mix",
-    )(which, *blocks, weight, base)
+    )(which, *blocks, weight)
 
 
 def body(inputs, in_weight, out_weight, short_filter, decay, angle, residue, bias):
@@ -198,7 +221,8 @@
             near = c // (count // 2) == s // half
             to = (c, s) if near else (count - 1 - c, mirror(s))
             swaps.append((c * blocks + s, to[0] * blocks + to[1]))
-    features = spread(lax.ppermute(tokens, ("ch", "seq"), swaps), "ch")
+    features = ring(lax.ppermute(tokens, ("ch", "seq"), swaps), "ch")
+    here = lax.axis_index("ch")
 
     rate, turn = decay.T, angle.T
     length = rows // SUB
@@ -217,20 +241,20 @@
     quarter = count // 2
     padded = rows + HALO
     keep, send = pl.pallas_call(
-        project_kernel,
+        functools.partial(project_kernel, count),
         grid_spec=pltpu.PrefetchScalarGridSpec(
             num_scalar_prefetch=1,
             grid=(quarter,),
-            in_specs=[
-                pl.BlockSpec((1, padded, chans), lambda k, h: (h[0] * quarter + k, 0, 0)),
-                pl.BlockSpec((1, padded, chans), lambda k, h: (count - 1 - h[0] * quarter - k, 0, 0)),
-                pl.BlockSpec((chans, 3 * chans), lambda k, h: (k, 0)),
-            ],
+            in_specs=[pl.BlockSpec((padded, chans), lambda k, h: (0, 0))] * count
+            + [pl.BlockSpec((chans, 3 * chans), lambda k, h: (k, 0))],
             out_specs=[
                 pl.BlockSpec((padded, 3 * chans), lambda k, h: (0, 0)),
                 pl.BlockSpec((padded, 3 * chans), lambda k, h: (0, 0)),
             ],
-            scratch_shapes=[pltpu.VMEM((2 * padded, 3 * chans), f32)],
+            scratch_shapes=[
+                pltpu.VMEM((count, padded, chans), jnp.bfloat16),
+                pltpu.VMEM((2 * padded, 3 * chans), f32),
+            ],
         ),
         out_shape=[
             jax.ShapeDtypeStruct((padded, 3 * chans), f32),
@@ -238,7 +262,7 @@
         ],
         compiler_params=pltpu.CompilerParams(vmem_limit_bytes=VMEM),
         name="project",
-    )((place // half).reshape(1).astype(jnp.int32), features, features, weight)
+    )(jnp.stack([place // half, here]).astype(jnp.int32), *features, weight)
     more = lax.ppermute(send, "seq", [(s, mirror(s)) for s in range(blocks)])
     mixin, query, begin, final = pl.pallas_call(
         functools.partial(scan_kernel, rows, chans),
@@ -261,23 +285,8 @@
         name="gate",
     )(states, jump, begin, reach, step, poles, bias[None, :], mixin, query)
 
-    here = lax.axis_index("ch")
-    up = [(c, (c + 1) % count) for c in range(count)]
-    down = [(c, (c - 1) % count) for c in range(count)]
-    arrived, origin = [gated], [here]
-    below = above = gated
-    for hop in range(1, count // 2 + 1):
-        below = lax.ppermute(below, "ch", up)
-        arrived.append(below)
-        origin.append(here - hop)
-        if 2 * hop < count:
-            above = lax.ppermute(above, "ch", down)
-            arrived.append(above)
-            origin.append(here + hop)
-    which = jnp.stack([lax.rem(o + count, count) for o in origin]).astype(jnp.int32)
-    base = jnp.zeros((rows, chans), f32)
-    first = mix(arrived[:5], which[:5], second, base, f32)
-    return mix(arrived[5:], which[5:], second, first, jnp.bfloat16)
+    which = jnp.stack([lax.rem(here + hop + count, count) for hop in ring_hops(count)])
+    return mix(ring(gated, "ch"), which.astype(jnp.int32), second)
 
 
 def solution(mesh):

time: 145 us -> 138 us (0.952)
  waiting for transfers between devices: 68.1 us -> 53.5 us
  starting transfers between devices: 40.5 us -> 46.5 us
  Pallas kernels: 11.5 us -> 15.6 us
  local copies, waits for them, and re-layouts: 8.61 us -> 6.08 us
    all_to_all x2 -> x1, waiting for transfers between devices: 40.4 us -> 7.58 us  [spread(): lax.all_to_all(jnp.broadcast_to(x[None], (count,) + x.shape), axis, 0, 0,...]
    ppermute x8 -> x15, starting transfers between devices: 10.5 us -> 36.4 us  [the longest x6 32.1 us: ring(): above = lax.ppermute(above, axis, down)]
    ppermute x8 -> x15, waiting for transfers between devices: 11.3 us -> 31.3 us  [the longest x8 31.3 us: ring(): below = lax.ppermute(below, axis, up)]
    all_to_all x2 -> x1, starting transfers between devices: 26.8 us -> 6.92 us  [spread(): lax.all_to_all(jnp.broadcast_to(x[None], (count,) + x.shape), axis, 0, 0,...]
    pallas_call x2 -> x1, Pallas kernels: 3.84 us -> 7.28 us  [mix(): pl.pallas_call(functools.partial(mix_kernel, len(blocks)), grid_spec=pltp...]
    unnamed x20 -> x46, local copies, waits for them, and re-layouts: 4.41 us -> 2.48 us
    ppermute x1, waiting for transfers between devices: 12.9 us -> 11.1 us  [body(): more = lax.ppermute(send, 'seq', [(s, mirror(s)) for s in range(blocks)])]
  transfers between devices with their start and end apart: 14 -> 20, of which waited for: 8 -> 11; matrix products, arithmetic and copies ran while one was open for 2% -> 2% of each run, Pallas kernels for 7% -> 6%
where the time goes in v3:
time: 138 us
  waiting for transfers between devices  53.5 us (39%)
  starting transfers between devices  46.5 us (34%)
  Pallas kernels  15.6 us (11%)
  between operations  13.8 us (10%)
  local copies, waits for them, and re-layouts  6.08 us (4%)
  other arithmetic  2.47 us (2%)
    ppermute x6, starting transfers between devices, ring(): above = lax.ppermute(above, axis, down)  32.1 us
    ppermute x8, waiting for transfers between devices, ring(): below = lax.ppermute(below, axis, up)  31.3 us
    ppermute x1, waiting for transfers between devices, body(): more = lax.ppermute(send, 'seq', [(s, mirror(s)) for s in range(blocks)])  11.1 us
    all_to_all x1, waiting for transfers between devices, spread(): lax.all_to_all(jnp.broadcast_to(x[None], (count,) + x.shape), axis, 0, 0,...  7.58 us
    pallas_call x1, Pallas kernels, mix(): pl.pallas_call(functools.partial(mix_kernel, len(blocks)), grid_spec=pltp...  7.28 us
    pallas_call x1, Pallas kernels, body(): pl.pallas_call(functools.partial(project_kernel, count), grid_spec=pltpu....  7.21 us
    all_to_all x1, starting transfers between devices, spread(): lax.all_to_all(jnp.broadcast_to(x[None], (count,) + x.shape), axis, 0, 0,...  6.92 us
    ppermute x8, starting transfers between devices, ring(): below = lax.ppermute(below, axis, up)  3.64 us
  transfers between devices with their start and end apart: 20, of which 11 were waited for; matrix products, arithmetic and copies ran while one was open for 2% of the time, Pallas kernels for 6%

profile of v3, /device:TPU:2, one launch (start us, length us, event | category | flops | bytes accessed | tf_op | source)
XLA Modules:
  0.0 137.9 jit_solution(13758891468223307313)
XLA Ops:
  6.5 0.0 copy-start.21
  6.6 2.1 %fusion.8 = (bf16[128,1,4096]{2,0,1:T(8,128)(2,1)S(1)}, bf16[128,1,4096]{2,0,1:T(8,128)(2,1)S(1)}, bf16[128,1,4096]{2,0,1:T(8,128)(2,1)S(1)}) fusion(bf16[128,3,4096]{2,0,1:T(8,128)(2,1)} %param.9), kind=kLoop, calls=%fused_computation.36 | loop fusion | bytes 6291456 | tf_op jit(solution)/shard_map/slice | solution.py:201
  8.7 0.8 pad_maximum_fusion
  9.5 0.0 all-gather.3.cloned.1.call-update
  9.5 0.0 all-gather.5.cloned.1.call-start
  9.6 0.7 all-gather.5.cloned.1.call-update
  10.3 1.9 %collective-permute-start = (bf16[2,512]{1,0:T(2,128)(2,1)S(1)}, bf16[2,512]{1,0:T(2,128)(2,1)S(1)}, u32[]{:S(2)}, u32[]{:S(2)}) collective-permute-start(bf16[2,512]{1,0:T(2,128)(2,1)S(1)} %slice.18), channel_id=1, source_target_pairs={{0,1},{1,2},{2,3},{3,4},{4,5},{5,6},{6,7},{7,8},{8,9},{9,10},{10,1... | collective-permute-start | bytes 6152 | tf_op jit(solution)/shard_map/ppermute | solution.py:214
  12.3 0.1 pad.15.clone
  12.3 2.9 %collective-permute-done = bf16[2,512]{1,0:T(2,128)(2,1)S(1)} collective-permute-done((bf16[2,512]{1,0:T(2,128)(2,1)S(1)}, bf16[2,512]{1,0:T(2,128)(2,1)S(1)}, u32[]{:S(2)}, u32[]{:S(2)}) %collective-permute-start) | collective-permute-done | bytes 2080 | tf_op jit(solution)/shard_map/ppermute | solution.py:214
  15.2 0.1 maximum_maximum_fusion
  15.3 0.7 collective-permute-start.1
  16.0 0.2 fusion.3
  16.2 0.0 collective-permute-done.1.refs_0_
  16.2 2.0 %collective-permute-start.2 = (bf16[144,512]{1,0:T(8,128)(2,1)S(1)}, bf16[144,512]{1,0:T(8,128)(2,1)S(1)}, u32[]{:S(2)}, u32[]{:S(2)}) collective-permute-start(bf16[144,512]{1,0:T(8,128)(2,1)S(1)} %collective-permute-done.1.refs_0_), channel_id=1, source_target_pairs={{0,32},{32,64},{64,96},{96,128},{128,160},{160,192},{192,224},{224... | collective-permute-start | bytes 442376 | tf_op jit(solution)/shard_map/ppermute | solution.py:38
  18.2 0.1 multiply_bitcast_fusion.1
  18.3 16.8 %collective-permute-start.3 = (bf16[144,512]{1,0:T(8,128)(2,1)S(1)}, bf16[144,512]{1,0:T(8,128)(2,1)S(1)}, u32[]{:S(2)}, u32[]{:S(2)}) collective-permute-start(bf16[144,512]{1,0:T(8,128)(2,1)S(1)} %collective-permute-done.1.refs_0_), channel_id=1, source_target_pairs={{0,224},{32,0},{64,32},{96,64},{128,96},{160,128},{192,160},{224,1... | collective-permute-start | bytes 442376 | tf_op jit(solution)/shard_map/ppermute | solution.py:41
  35.2 2.9 %collective-permute-done.2.refs_1_ = bf16[144,512]{1,0:T(8,128)(2,1)S(1)} collective-permute-done((bf16[144,512]{1,0:T(8,128)(2,1)S(1)}, bf16[144,512]{1,0:T(8,128)(2,1)S(1)}, u32[]{:S(2)}, u32[]{:S(2)}) %collective-permute-start.2) | collective-permute-done | bytes 147488 | tf_op jit(solution)/shard_map/ppermute | solution.py:38
  38.1 0.0 collective-permute-start.4
  38.1 0.0 copy-done.22
  38.1 0.0 collective-permute-done.3.refs_2_
  38.1 3.4 %collective-permute-start.5 = (bf16[144,512]{1,0:T(8,128)(2,1)S(1)}, bf16[144,512]{1,0:T(8,128)(2,1)S(1)}, u32[]{:S(2)}, u32[]{:S(2)}) collective-permute-start(bf16[144,512]{1,0:T(8,128)(2,1)S(1)} %collective-permute-done.3.refs_2_), channel_id=1, source_target_pairs={{0,224},{32,0},{64,32},{96,64},{128,96},{160,128},{192,160},{224,1... | collective-permute-start | bytes 442376 | tf_op jit(solution)/shard_map/ppermute | solution.py:41
  41.5 2.9 %collective-permute-done.4.refs_3_ = bf16[144,512]{1,0:T(8,128)(2,1)S(1)} collective-permute-done((bf16[144,512]{1,0:T(8,128)(2,1)S(1)}, bf16[144,512]{1,0:T(8,128)(2,1)S(1)}, u32[]{:S(2)}, u32[]{:S(2)}) %collective-permute-start.4) | collective-permute-done | bytes 147488 | tf_op jit(solution)/shard_map/ppermute | solution.py:38
  44.4 0.0 collective-permute-start.6
  44.5 0.0 collective-permute-done.5.refs_4_
  44.5 3.6 %collective-permute-start.7 = (bf16[144,512]{1,0:T(8,128)(2,1)S(1)}, bf16[144,512]{1,0:T(8,128)(2,1)S(1)}, u32[]{:S(2)}, u32[]{:S(2)}) collective-permute-start(bf16[144,512]{1,0:T(8,128)(2,1)S(1)} %collective-permute-done.5.refs_4_), channel_id=1, source_target_pairs={{0,224},{32,0},{64,32},{96,64},{128,96},{160,128},{192,160},{224,1... | collective-permute-start | bytes 442376 | tf_op jit(solution)/shard_map/ppermute | solution.py:41
  48.1 3.9 %collective-permute-done.6.refs_5_ = bf16[144,512]{1,0:T(8,128)(2,1)S(1)} collective-permute-done((bf16[144,512]{1,0:T(8,128)(2,1)S(1)}, bf16[144,512]{1,0:T(8,128)(2,1)S(1)}, u32[]{:S(2)}, u32[]{:S(2)}) %collective-permute-start.6) | collective-permute-done | bytes 147488 | tf_op jit(solution)/shard_map/ppermute | solution.py:38
  52.0 0.0 collective-permute-start.8
  52.0 0.6 pad_add_fusion.place_ref
  52.6 0.0 copy-start.2
  52.6 0.0 collective-permute-done.7.refs_6_
  52.6 0.0 copy-start.9
  52.6 5.7 %collective-permute-done.8.refs_7_ = bf16[144,512]{1,0:T(8,128)(2,1)S(1)} collective-permute-done((bf16[144,512]{1,0:T(8,128)(2,1)S(1)}, bf16[144,512]{1,0:T(8,128)(2,1)S(1)}, u32[]{:S(2)}, u32[]{:S(2)}) %collective-permute-start.8) | collective-permute-done | bytes 147488 | tf_op jit(solution)/shard_map/ppermute | solution.py:38
  58.3 0.0 copy-done.4
  58.4 0.6 copy-done.10
  59.0 7.2 %project.1 = (f32[144,1536]{1,0:T(8,128)}, bf16[144,1536]{1,0:T(8,128)(2,1)}) custom-call(s32[2]{0:T(128)} %pad_add_fusion.place_ref, bf16[144,512]{1,0:T(8,128)(2,1)} %copy-done.3, bf16[144,512]{1,0:T(8,128)(2,1)} %copy-done.4, bf16[144,512]{1,0:T(8,128)(2,1)} %copy-done.5, bf16[144,512]{1,0:T(8,128)(2,1)} %copy-done.6, bf16[144,512]{1,0:T(8,128)(2,1)} %copy-done.7, ...), custom_call_target="tpu_custom_call" | custom-call | tf_op jit(solution)/shard_map/project/pallas_call | solution.py:243
  66.2 1.2 collective-permute-start.9
  67.4 0.6 fusion.1
  68.0 11.1 %collective-permute-done.9.more_ref = bf16[144,1536]{1,0:T(8,128)(2,1)S(1)} collective-permute-done((bf16[144,1536]{1,0:T(8,128)(2,1)}, bf16[144,1536]{1,0:T(8,128)(2,1)S(1)}, u32[]{:S(2)}, u32[]{:S(2)}) %collective-permute-start.9) | collective-permute-done | bytes 442400 | tf_op jit(solution)/shard_map/ppermute | solution.py:266
  79.0 1.2 copy-done
  80.2 0.7 scan.1
  80.9 0.7 broadcast_in_dim.15
  81.6 6.9 %all-to-all-start = ((f32[32,4,512]{2,1,0:T(4,128)}), f32[32,4,512]{2,1,0:T(4,128)S(1)}, u32[]{:S(2)}, u32[]{:S(2)}) async-start(f32[32,4,512]{2,1,0:T(4,128)} %broadcast_in_dim.15), calls=%async_computation | async-start | bytes 524288 | tf_op jit(solution)/shard_map/all_to_all | solution.py:19
  88.6 0.1 fusion.jump_ref
  88.7 7.6 %all-to-all-done.all_ref = f32[32,4,512]{2,1,0:T(4,128)S(1)} async-done(((f32[32,4,512]{2,1,0:T(4,128)}), f32[32,4,512]{2,1,0:T(4,128)S(1)}, u32[]{:S(2)}, u32[]{:S(2)}) %all-to-all-start) | async-done | bytes 262176 | tf_op jit(solution)/shard_map/all_to_all | solution.py:19
  96.2 0.0 copy-done.2
  96.2 0.4 gate.1.refs_0_
  96.6 1.6 %collective-permute-start.10 = (bf16[128,512]{1,0:T(8,128)(2,1)S(1)}, bf16[128,512]{1,0:T(8,128)(2,1)S(1)}, u32[]{:S(2)}, u32[]{:S(2)}) collective-permute-start(bf16[128,512]{1,0:T(8,128)(2,1)S(1)} %gate.1.refs_0_), channel_id=1, source_target_pairs={{0,32},{32,64},{64,96},{96,128},{128,160},{160,192},{192,224},{224... | collective-permute-start | bytes 393224 | tf_op jit(solution)/shard_map/ppermute | solution.py:38
  98.3 1.8 %collective-permute-start.11 = (bf16[128,512]{1,0:T(8,128)(2,1)S(1)}, bf16[128,512]{1,0:T(8,128)(2,1)S(1)}, u32[]{:S(2)}, u32[]{:S(2)}) collective-permute-start(bf16[128,512]{1,0:T(8,128)(2,1)S(1)} %gate.1.refs_0_), channel_id=1, source_target_pairs={{0,224},{32,0},{64,32},{96,64},{128,96},{160,128},{192,160},{224,1... | collective-permute-start | bytes 393224 | tf_op jit(solution)/shard_map/ppermute | solution.py:41
  100.1 4.0 %collective-permute-done.10.refs_1_ = bf16[128,512]{1,0:T(8,128)(2,1)S(1)} collective-permute-done((bf16[128,512]{1,0:T(8,128)(2,1)S(1)}, bf16[128,512]{1,0:T(8,128)(2,1)S(1)}, u32[]{:S(2)}, u32[]{:S(2)}) %collective-permute-start.10) | collective-permute-done | bytes 131104 | tf_op jit(solution)/shard_map/ppermute | solution.py:38
  104.1 0.0 collective-permute-start.12
  104.1 0.0 collective-permute-done.11.refs_2_
  104.2 3.2 %collective-permute-start.13 = (bf16[128,512]{1,0:T(8,128)(2,1)S(1)}, bf16[128,512]{1,0:T(8,128)(2,1)S(1)}, u32[]{:S(2)}, u32[]{:S(2)}) collective-permute-start(bf16[128,512]{1,0:T(8,128)(2,1)S(1)} %collective-permute-done.11.refs_2_), channel_id=1, source_target_pairs={{0,224},{32,0},{64,32},{96,64},{128,96},{160,128},{192,160},{224,1... | collective-permute-start | bytes 393224 | tf_op jit(solution)/shard_map/ppermute | solution.py:41
  107.4 3.3 %collective-permute-done.12.refs_3_ = bf16[128,512]{1,0:T(8,128)(2,1)S(1)} collective-permute-done((bf16[128,512]{1,0:T(8,128)(2,1)S(1)}, bf16[128,512]{1,0:T(8,128)(2,1)S(1)}, u32[]{:S(2)}, u32[]{:S(2)}) %collective-permute-start.12) | collective-permute-done | bytes 131104 | tf_op jit(solution)/shard_map/ppermute | solution.py:38
  110.7 0.0 collective-permute-start.14
  110.7 0.0 collective-permute-done.13.refs_4_
  110.8 3.2 %collective-permute-start.15 = (bf16[128,512]{1,0:T(8,128)(2,1)S(1)}, bf16[128,512]{1,0:T(8,128)(2,1)S(1)}, u32[]{:S(2)}, u32[]{:S(2)}) collective-permute-start(bf16[128,512]{1,0:T(8,128)(2,1)S(1)} %collective-permute-done.13.refs_4_), channel_id=1, source_target_pairs={{0,224},{32,0},{64,32},{96,64},{128,96},{160,128},{192,160},{224,1... | collective-permute-start | bytes 393224 | tf_op jit(solution)/shard_map/ppermute | solution.py:41
  114.0 2.9 %collective-permute-done.14.refs_5_ = bf16[128,512]{1,0:T(8,128)(2,1)S(1)} collective-permute-done((bf16[128,512]{1,0:T(8,128)(2,1)S(1)}, bf16[128,512]{1,0:T(8,128)(2,1)S(1)}, u32[]{:S(2)}, u32[]{:S(2)}) %collective-permute-start.14) | collective-permute-done | bytes 131104 | tf_op jit(solution)/shard_map/ppermute | solution.py:38
  116.9 0.0 collective-permute-start.16
  116.9 0.6 stack.44.which_ref
  117.5 0.0 collective-permute-done.15.refs_6_
  117.6 5.5 %collective-permute-done.16.refs_7_ = bf16[128,512]{1,0:T(8,128)(2,1)S(1)} collective-permute-done((bf16[128,512]{1,0:T(8,128)(2,1)S(1)}, bf16[128,512]{1,0:T(8,128)(2,1)S(1)}, u32[]{:S(2)}, u32[]{:S(2)}) %collective-permute-start.16) | collective-permute-done | bytes 131104 | tf_op jit(solution)/shard_map/ppermute | solution.py:38
  123.1 0.0 copy-done.1
  123.2 0.6 copy-done.18
  123.8 7.3 %mix.1 = bf16[128,512]{1,0:T(8,128)(2,1)} custom-call(s32[8]{0:T(128)} %stack.44.which_ref, bf16[128,512]{1,0:T(8,128)(2,1)} %copy-done.1, bf16[128,512]{1,0:T(8,128)(2,1)} %copy-done.12, bf16[128,512]{1,0:T(8,128)(2,1)} %copy-done.13, bf16[128,512]{1,0:T(8,128)(2,1)} %copy-done.14, bf16[128,512]{1,0:T(8,128)(2,1)} %copy-done.15, ...), custom_call_target="tpu_custom_call" | custom-call | tf_op jit(solution)/shard_map/mix/pallas_call | solution.py:179
  (54 shorter events, 0.2 us)
Async XLA Ops:
  6.5 51.8 %all-gather.3.cloned.1.call-start = ((), (), s32[]{:S(2)}) async-start(), calls=%async_computation.1 | async-start | bytes 6684672 | tf_op jit(solution)/shard_map/all_gather | solution.py:205
  6.5 3.7 %copy-start.11 = (bf16[128,512]{1,0:T(8,128)(2,1)S(1)}, bf16[128,512]{1,0:T(8,128)(2,1)}, u32[]{:S(2)}) copy-start(bf16[128,512]{1,0:T(8,128)(2,1)} %param.8) | copy-start | bytes 393220
  6.5 9.4 %copy-start.19 = (f32[512,2]{0,1:T(2,128)S(1)}, f32[512,2]{0,1:T(2,128)}, u32[]{:S(2)}) copy-start(f32[512,2]{0,1:T(2,128)} %param.13) | copy-start | bytes 12292
  6.5 9.4 %copy-start.20 = (f32[512,2]{0,1:T(2,128)S(1)}, f32[512,2]{0,1:T(2,128)}, u32[]{:S(2)}) copy-start(f32[512,2]{0,1:T(2,128)} %param.12) | copy-start | bytes 12292
  6.5 31.5 %copy-start.22 = (f32[2,512,2]{1,2,0:T(2,128)S(1)}, f32[2,512,2]{1,2,0:T(2,128)}, u32[]{:S(2)}) copy-start(f32[2,512,2]{1,2,0:T(2,128)} %param.14) | copy-start | bytes 24580
  6.5 46.0 %copy-start.21 = (f32[3,3,512]{2,1,0:T(4,128)S(1)}, f32[3,3,512]{2,1,0:T(4,128)}, u32[]{:S(2)}) copy-start(f32[3,3,512]{2,1,0:T(4,128)} %param.11) | copy-start | bytes 55300
  9.5 108.0 %all-gather.5.cloned.1.call-start = ((), (), s32[]{:S(2)}) async-start(), calls=%async_computation.2 | async-start | bytes 4325376 | tf_op jit(solution)/shard_map/all_gather | solution.py:212
  10.3 4.9 %collective-permute-start = (bf16[2,512]{1,0:T(2,128)(2,1)S(1)}, bf16[2,512]{1,0:T(2,128)(2,1)S(1)}, u32[]{:S(2)}, u32[]{:S(2)}) collective-permute-start(bf16[2,512]{1,0:T(2,128)(2,1)S(1)} %slice.18), channel_id=1, source_target_pairs={{0,1},{1,2},{2,3},{3,4},{4,5},{5,6},{6,7},{7,8},{8,9},{9,10},{10,1... | collective-permute-start | bytes 6152 | tf_op jit(solution)/shard_map/ppermute | solution.py:214
  15.3 0.9 collective-permute-start.1
  16.2 42.1 %copy-start.3 = (bf16[144,512]{1,0:T(8,128)(2,1)}, bf16[144,512]{1,0:T(8,128)(2,1)S(1)}, u32[]{:S(2)}) copy-start(bf16[144,512]{1,0:T(8,128)(2,1)S(1)} %collective-permute-done.1.refs_0_) | copy-start | bytes 442372
  16.2 21.9 %collective-permute-start.2 = (bf16[144,512]{1,0:T(8,128)(2,1)S(1)}, bf16[144,512]{1,0:T(8,128)(2,1)S(1)}, u32[]{:S(2)}, u32[]{:S(2)}) collective-permute-start(bf16[144,512]{1,0:T(8,128)(2,1)S(1)} %collective-permute-done.1.refs_0_), channel_id=1, source_target_pairs={{0,32},{32,64},{64,96},{96,128},{128,160},{160,192},{192,224},{224... | collective-permute-start | bytes 442376 | tf_op jit(solution)/shard_map/ppermute | solution.py:38
  18.3 19.8 %collective-permute-start.3 = (bf16[144,512]{1,0:T(8,128)(2,1)S(1)}, bf16[144,512]{1,0:T(8,128)(2,1)S(1)}, u32[]{:S(2)}, u32[]{:S(2)}) collective-permute-start(bf16[144,512]{1,0:T(8,128)(2,1)S(1)} %collective-permute-done.1.refs_0_), channel_id=1, source_target_pairs={{0,224},{32,0},{64,32},{96,64},{128,96},{160,128},{192,160},{224,1... | collective-permute-start | bytes 442376 | tf_op jit(solution)/shard_map/ppermute | solution.py:41
  38.1 20.3 %copy-start.4 = (bf16[144,512]{1,0:T(8,128)(2,1)}, bf16[144,512]{1,0:T(8,128)(2,1)S(1)}, u32[]{:S(2)}) copy-start(bf16[144,512]{1,0:T(8,128)(2,1)S(1)} %collective-permute-done.2.refs_1_) | copy-start | bytes 442372
  38.1 6.4 %collective-permute-start.4 = (bf16[144,512]{1,0:T(8,128)(2,1)S(1)}, bf16[144,512]{1,0:T(8,128)(2,1)S(1)}, u32[]{:S(2)}, u32[]{:S(2)}) collective-permute-start(bf16[144,512]{1,0:T(8,128)(2,1)S(1)} %collective-permute-done.2.refs_1_), channel_id=1, source_target_pairs={{0,32},{32,64},{64,96},{96,128},{128,160},{160,192},{192,224},{224... | collective-permute-start | bytes 442376 | tf_op jit(solution)/shard_map/ppermute | solution.py:38
  38.1 20.2 %copy-start.5 = (bf16[144,512]{1,0:T(8,128)(2,1)}, bf16[144,512]{1,0:T(8,128)(2,1)S(1)}, u32[]{:S(2)}) copy-start(bf16[144,512]{1,0:T(8,128)(2,1)S(1)} %collective-permute-done.3.refs_2_) | copy-start | bytes 442372
  38.1 6.3 %collective-permute-start.5 = (bf16[144,512]{1,0:T(8,128)(2,1)S(1)}, bf16[144,512]{1,0:T(8,128)(2,1)S(1)}, u32[]{:S(2)}, u32[]{:S(2)}) collective-permute-start(bf16[144,512]{1,0:T(8,128)(2,1)S(1)} %collective-permute-done.3.refs_2_), channel_id=1, source_target_pairs={{0,224},{32,0},{64,32},{96,64},{128,96},{160,128},{192,160},{224,1... | collective-permute-start | bytes 442376 | tf_op jit(solution)/shard_map/ppermute | solution.py:41
  44.4 13.9 %copy-start.6 = (bf16[144,512]{1,0:T(8,128)(2,1)}, bf16[144,512]{1,0:T(8,128)(2,1)S(1)}, u32[]{:S(2)}) copy-start(bf16[144,512]{1,0:T(8,128)(2,1)S(1)} %collective-permute-done.4.refs_3_) | copy-start | bytes 442372
  44.4 7.5 %collective-permute-start.6 = (bf16[144,512]{1,0:T(8,128)(2,1)S(1)}, bf16[144,512]{1,0:T(8,128)(2,1)S(1)}, u32[]{:S(2)}, u32[]{:S(2)}) collective-permute-start(bf16[144,512]{1,0:T(8,128)(2,1)S(1)} %collective-permute-done.4.refs_3_), channel_id=1, source_target_pairs={{0,32},{32,64},{64,96},{96,128},{128,160},{160,192},{192,224},{224... | collective-permute-start | bytes 442376 | tf_op jit(solution)/shard_map/ppermute | solution.py:38
  44.5 13.9 %copy-start.7 = (bf16[144,512]{1,0:T(8,128)(2,1)}, bf16[144,512]{1,0:T(8,128)(2,1)S(1)}, u32[]{:S(2)}) copy-start(bf16[144,512]{1,0:T(8,128)(2,1)S(1)} %collective-permute-done.5.refs_4_) | copy-start | bytes 442372
  44.5 8.1 %collective-permute-start.7 = (bf16[144,512]{1,0:T(8,128)(2,1)S(1)}, bf16[144,512]{1,0:T(8,128)(2,1)S(1)}, u32[]{:S(2)}, u32[]{:S(2)}) collective-permute-start(bf16[144,512]{1,0:T(8,128)(2,1)S(1)} %collective-permute-done.5.refs_4_), channel_id=1, source_target_pairs={{0,224},{32,0},{64,32},{96,64},{128,96},{160,128},{192,160},{224,1... | collective-permute-start | bytes 442376 | tf_op jit(solution)/shard_map/ppermute | solution.py:41
  52.0 6.4 %copy-start.8 = (bf16[144,512]{1,0:T(8,128)(2,1)}, bf16[144,512]{1,0:T(8,128)(2,1)S(1)}, u32[]{:S(2)}) copy-start(bf16[144,512]{1,0:T(8,128)(2,1)S(1)} %collective-permute-done.6.refs_5_) | copy-start | bytes 442372
  52.0 6.4 %collective-permute-start.8 = (bf16[144,512]{1,0:T(8,128)(2,1)S(1)}, bf16[144,512]{1,0:T(8,128)(2,1)S(1)}, u32[]{:S(2)}, u32[]{:S(2)}) collective-permute-start(bf16[144,512]{1,0:T(8,128)(2,1)S(1)} %collective-permute-done.6.refs_5_), channel_id=1, source_target_pairs={{0,32},{32,64},{64,96},{96,128},{128,160},{160,192},{192,224},{224... | collective-permute-start | bytes 442376 | tf_op jit(solution)/shard_map/ppermute | solution.py:38
  52.6 43.7 %copy-start.2 = (f32[512]{0:T(512)S(1)}, f32[512]{0:T(512)}, u32[]{:S(2)}) copy-start(f32[512]{0:T(512)} %param.15) | copy-start | bytes 6148
  52.6 5.8 %copy-start.9 = (bf16[144,512]{1,0:T(8,128)(2,1)}, bf16[144,512]{1,0:T(8,128)(2,1)S(1)}, u32[]{:S(2)}) copy-start(bf16[144,512]{1,0:T(8,128)(2,1)S(1)} %collective-permute-done.7.refs_6_) | copy-start | bytes 442372
  58.3 0.7 copy-start.10
  66.2 12.8 %collective-permute-start.9 = (bf16[144,1536]{1,0:T(8,128)(2,1)}, bf16[144,1536]{1,0:T(8,128)(2,1)S(1)}, u32[]{:S(2)}, u32[]{:S(2)}) collective-permute-start(bf16[144,1536]{1,0:T(8,128)(2,1)} %get-tuple-element.12), channel_id=1, source_target_pairs={{0,24},{1,25},{2,26},{3,27},{4,28},{5,29},{6,30},{7,31},{8,16},{9,... | collective-permute-start | bytes 1327112 | tf_op jit(solution)/shard_map/ppermute | solution.py:266
  79.0 1.2 copy-start
  81.6 14.6 %all-to-all-start = ((f32[32,4,512]{2,1,0:T(4,128)}), f32[32,4,512]{2,1,0:T(4,128)S(1)}, u32[]{:S(2)}, u32[]{:S(2)}) async-start(f32[32,4,512]{2,1,0:T(4,128)} %broadcast_in_dim.15), calls=%async_computation | async-start | bytes 524288 | tf_op jit(solution)/shard_map/all_to_all | solution.py:19
  96.6 26.5 %copy-start.1 = (bf16[128,512]{1,0:T(8,128)(2,1)}, bf16[128,512]{1,0:T(8,128)(2,1)S(1)}, u32[]{:S(2)}) copy-start(bf16[128,512]{1,0:T(8,128)(2,1)S(1)} %gate.1.refs_0_) | copy-start | bytes 393220
  96.6 7.5 %collective-permute-start.10 = (bf16[128,512]{1,0:T(8,128)(2,1)S(1)}, bf16[128,512]{1,0:T(8,128)(2,1)S(1)}, u32[]{:S(2)}, u32[]{:S(2)}) collective-permute-start(bf16[128,512]{1,0:T(8,128)(2,1)S(1)} %gate.1.refs_0_), channel_id=1, source_target_pairs={{0,32},{32,64},{64,96},{96,128},{128,160},{160,192},{192,224},{224... | collective-permute-start | bytes 393224 | tf_op jit(solution)/shard_map/ppermute | solution.py:38
  98.3 5.9 %collective-permute-start.11 = (bf16[128,512]{1,0:T(8,128)(2,1)S(1)}, bf16[128,512]{1,0:T(8,128)(2,1)S(1)}, u32[]{:S(2)}, u32[]{:S(2)}) collective-permute-start(bf16[128,512]{1,0:T(8,128)(2,1)S(1)} %gate.1.refs_0_), channel_id=1, source_target_pairs={{0,224},{32,0},{64,32},{96,64},{128,96},{160,128},{192,160},{224,1... | collective-permute-start | bytes 393224 | tf_op jit(solution)/shard_map/ppermute | solution.py:41
  104.1 19.0 %copy-start.12 = (bf16[128,512]{1,0:T(8,128)(2,1)}, bf16[128,512]{1,0:T(8,128)(2,1)S(1)}, u32[]{:S(2)}) copy-start(bf16[128,512]{1,0:T(8,128)(2,1)S(1)} %collective-permute-done.10.refs_1_) | copy-start | bytes 393220
  104.1 6.6 %collective-permute-start.12 = (bf16[128,512]{1,0:T(8,128)(2,1)S(1)}, bf16[128,512]{1,0:T(8,128)(2,1)S(1)}, u32[]{:S(2)}, u32[]{:S(2)}) collective-permute-start(bf16[128,512]{1,0:T(8,128)(2,1)S(1)} %collective-permute-done.10.refs_1_), channel_id=1, source_target_pairs={{0,32},{32,64},{64,96},{96,128},{128,160},{160,192},{192,224},{224... | collective-permute-start | bytes 393224 | tf_op jit(solution)/shard_map/ppermute | solution.py:38
  104.2 19.0 %copy-start.13 = (bf16[128,512]{1,0:T(8,128)(2,1)}, bf16[128,512]{1,0:T(8,128)(2,1)S(1)}, u32[]{:S(2)}) copy-start(bf16[128,512]{1,0:T(8,128)(2,1)S(1)} %collective-permute-done.11.refs_2_) | copy-start | bytes 393220
  104.2 6.6 %collective-permute-start.13 = (bf16[128,512]{1,0:T(8,128)(2,1)S(1)}, bf16[128,512]{1,0:T(8,128)(2,1)S(1)}, u32[]{:S(2)}, u32[]{:S(2)}) collective-permute-start(bf16[128,512]{1,0:T(8,128)(2,1)S(1)} %collective-permute-done.11.refs_2_), channel_id=1, source_target_pairs={{0,224},{32,0},{64,32},{96,64},{128,96},{160,128},{192,160},{224,1... | collective-permute-start | bytes 393224 | tf_op jit(solution)/shard_map/ppermute | solution.py:41
  110.7 12.4 %copy-start.14 = (bf16[128,512]{1,0:T(8,128)(2,1)}, bf16[128,512]{1,0:T(8,128)(2,1)S(1)}, u32[]{:S(2)}) copy-start(bf16[128,512]{1,0:T(8,128)(2,1)S(1)} %collective-permute-done.12.refs_3_) | copy-start | bytes 393220
  110.7 6.2 %collective-permute-start.14 = (bf16[128,512]{1,0:T(8,128)(2,1)S(1)}, bf16[128,512]{1,0:T(8,128)(2,1)S(1)}, u32[]{:S(2)}, u32[]{:S(2)}) collective-permute-start(bf16[128,512]{1,0:T(8,128)(2,1)S(1)} %collective-permute-done.12.refs_3_), channel_id=1, source_target_pairs={{0,32},{32,64},{64,96},{96,128},{128,160},{160,192},{192,224},{224... | collective-permute-start | bytes 393224 | tf_op jit(solution)/shard_map/ppermute | solution.py:38
  110.7 12.4 %copy-start.15 = (bf16[128,512]{1,0:T(8,128)(2,1)}, bf16[128,512]{1,0:T(8,128)(2,1)S(1)}, u32[]{:S(2)}) copy-start(bf16[128,512]{1,0:T(8,128)(2,1)S(1)} %collective-permute-done.13.refs_4_) | copy-start | bytes 393220
  110.8 6.8 %collective-permute-start.15 = (bf16[128,512]{1,0:T(8,128)(2,1)S(1)}, bf16[128,512]{1,0:T(8,128)(2,1)S(1)}, u32[]{:S(2)}, u32[]{:S(2)}) collective-permute-start(bf16[128,512]{1,0:T(8,128)(2,1)S(1)} %collective-permute-done.13.refs_4_), channel_id=1, source_target_pairs={{0,224},{32,0},{64,32},{96,64},{128,96},{160,128},{192,160},{224,1... | collective-permute-start | bytes 393224 | tf_op jit(solution)/shard_map/ppermute | solution.py:41
  116.9 6.2 %copy-start.16 = (bf16[128,512]{1,0:T(8,128)(2,1)}, bf16[128,512]{1,0:T(8,128)(2,1)S(1)}, u32[]{:S(2)}) copy-start(bf16[128,512]{1,0:T(8,128)(2,1)S(1)} %collective-permute-done.14.refs_5_) | copy-start | bytes 393220
  116.9 6.2 %collective-permute-start.16 = (bf16[128,512]{1,0:T(8,128)(2,1)S(1)}, bf16[128,512]{1,0:T(8,128)(2,1)S(1)}, u32[]{:S(2)}, u32[]{:S(2)}) collective-permute-start(bf16[128,512]{1,0:T(8,128)(2,1)S(1)} %collective-permute-done.14.refs_5_), channel_id=1, source_target_pairs={{0,32},{32,64},{64,96},{96,128},{128,160},{160,192},{192,224},{224... | collective-permute-start | bytes 393224 | tf_op jit(solution)/shard_map/ppermute | solution.py:38
  117.6 5.6 %copy-start.17 = (bf16[128,512]{1,0:T(8,128)(2,1)}, bf16[128,512]{1,0:T(8,128)(2,1)S(1)}, u32[]{:S(2)}) copy-start(bf16[128,512]{1,0:T(8,128)(2,1)S(1)} %collective-permute-done.15.refs_6_) | copy-start | bytes 393220
  123.1 0.6 copy-start.18
Sparse Core Ops, SparseCore 0:
  9.6 47.6 all-gather.2
  59.9 51.8 all-gather.4

commit v4 on v3

v4 whole, which is shorter than its diff:
```python
import functools

import jax
import jax.numpy as jnp
from jax import lax
from jax.experimental import pallas as pl
from jax.experimental.pallas import tpu as pltpu
from jax.sharding import PartitionSpec as P

HALO = 16
LANES = 128
SUB = 8
VMEM = 24 * 1024 * 1024


def spread(x, axis):
    count = lax.axis_size(axis)
    return lax.all_to_all(
        jnp.broadcast_to(x[None], (count,) + x.shape), axis, 0, 0, tiled=True
    )


def ring_hops(count):
    hops = [0]
    for hop in range(1, count // 2 + 1):
        hops += [-hop, hop] if 2 * hop < count else [-hop]
    return hops


def ring(x, axis):
    count = lax.axis_size(axis)
    up = [(c, (c + 1) % count) for c in range(count)]
    down = [(c, (c - 1) % count) for c in range(count)]
    arrived = [x]
    below = above = x
    for hop in range(1, count // 2 + 1):
        below = lax.ppermute(below, axis, up)
        arrived.append(below)
        if 2 * hop < count:
            above = lax.ppermute(above, axis, down)
            arrived.append(above)
    return arrived


def powers(exponent, rate, turn):
    mag = jnp.exp(-exponent[:, None, None] * rate[None])
    phase = exponent[:, None, None] * turn[None]
    return mag * jnp.cos(phase), mag * jnp.sin(phase)


def fetch(w_ref, w, sems, starts, sizes):
    copies = []
    for j, (start, size) in enumerate(zip(starts, sizes)):
        at = sum(sizes[:j])
        copies.append(
            pltpu.make_async_copy(w_ref.at[:, pl.ds(start, size)], w.at[:, pl.ds(at, size)], sems.at[j])
        )
        copies[-1].start()
    return copies


def product(lhs_ref, w, copies, chans, keep_ref, send_ref):
    sides, rows, depth = lhs_ref.shape
    both = lhs_ref[...].reshape(sides * rows, depth)
    for j, copy in enumerate(copies):
        copy.wait()
        cols = slice(j * chans, (j + 1) * chans)
        part = jnp.dot(both, w[:, cols], preferred_element_type=jnp.float32)
        keep_ref[:, cols] = part[:rows]
        send_ref[:, cols] = part[rows:].astype(send_ref.dtype)


def mixin_project_kernel(count, place_ref, *refs):
    x_refs, (w_ref, keep_ref, send_ref, lhs_ref, w, sems) = refs[:count], refs[count:]
    chans = x_refs[0].shape[1]
    copies = fetch(w_ref, w, sems, (chans, 2 * chans), (chans, chans))
    half, here = place_ref[0], place_ref[1]
    for x_ref, hop in zip(x_refs, ring_hops(count)):
        origin = lax.rem(here + hop + count, count)
        side = jnp.where(lax.rem(origin, 2) == half, 0, 1)
        at = pl.multiple_of(lax.div(origin, 2) * chans, chans)
        lhs_ref[side, :, pl.ds(at, chans)] = x_ref[...]
    product(lhs_ref, w, copies, chans, keep_ref, send_ref)


def query_project_kernel(lhs_ref, w_ref, keep_ref, send_ref, w, sems):
    chans = keep_ref.shape[1]
    copies = fetch(w_ref, w, sems, (0,), (chans,))
    product(lhs_ref, w, copies, chans, keep_ref, send_ref)


def short_conv(rows, branch, total, taps_ref):
    now = total[:rows]
    past = total[rows : rows + 8]
    one = jnp.concatenate([past[1:2], now[:-1]], axis=0)
    two = jnp.concatenate([past[0:2], now[:-2]], axis=0)
    tap = [taps_ref[3 * j + branch : 3 * j + branch + 1, :] for j in range(3)]
    return tap[0] * now + tap[1] * one + tap[2] * two


def scan_kernel(
    rows, chans, keep_ref, more_ref, taps_ref, step_ref, join_ref, mixin_ref, begin_ref, final_ref
):
    length = rows // SUB

    def filtered(branch):
        cols = slice((branch - 1) * chans, branch * chans)
        total = keep_ref[:, cols] + more_ref[:, cols].astype(jnp.float32)
        return short_conv(rows, branch, total, taps_ref)

    mixin = filtered(1) * filtered(2)
    for q in range(chans // LANES):
        mixin_ref[q] = mixin[:, q * LANES : (q + 1) * LANES]
    for q in range(chans // LANES):
        cols = slice(q * LANES, (q + 1) * LANES)
        wide = lambda row: jnp.broadcast_to(row, (SUB, LANES))
        ar = [wide(step_ref[n : n + 1, cols]) for n in range(2)]
        ai = [wide(step_ref[2 + n : 3 + n, cols]) for n in range(2)]
        re = [jnp.zeros((SUB, LANES), jnp.float32)] * 2
        im = [jnp.zeros((SUB, LANES), jnp.float32)] * 2
        for i in range(length):
            u = mixin_ref[q, pl.ds(i, SUB, stride=length), :]
            for n in range(2):
                re[n], im[n] = ar[n] * re[n] - ai[n] * im[n] + u, ar[n] * im[n] + ai[n] * re[n]
        for n in range(2):
            jr = join_ref[n : n + 1, cols]
            ji = join_ref[2 + n : 3 + n, cols]
            er = jnp.zeros((1, LANES), jnp.float32)
            ei = jnp.zeros((1, LANES), jnp.float32)
            for b in range(SUB):
                begin_ref[n, b : b + 1, cols] = er
                begin_ref[2 + n, b : b + 1, cols] = ei
                er, ei = (
                    jr * er - ji * ei + re[n][b : b + 1],
                    jr * ei + ji * er + im[n][b : b + 1],
                )
            final_ref[n : n + 1, cols] = er
            final_ref[2 + n : 3 + n, cols] = ei


def gate_kernel(
    rows, chans, all_ref, jump_ref, begin_ref, reach_ref, step_ref, residue_ref, bias_ref, mixin_ref, keep_ref, more_ref, taps_ref, out_ref, long
):
    query = short_conv(rows, 0, keep_ref[...] + more_ref[...].astype(jnp.float32), taps_ref)
    length = rows // SUB
    entry = []
    for n in range(2):
        fr, fi = all_ref[:, n, :], all_ref[:, 2 + n, :]
        cr, ci = jump_ref[n], jump_ref[2 + n]
        gr = jnp.sum(cr * fr - ci * fi, axis=0, keepdims=True)
        gi = jnp.sum(cr * fi + ci * fr, axis=0, keepdims=True)
        rr, ri = reach_ref[n], reach_ref[2 + n]
        entry.append((begin_ref[n] + rr * gr - ri * gi, begin_ref[2 + n] + rr * gi + ri * gr))
    for q in range(chans // LANES):
        cols = slice(q * LANES, (q + 1) * LANES)
        wide = lambda row: jnp.broadcast_to(row, (SUB, LANES))
        ar = [wide(step_ref[n : n + 1, cols]) for n in range(2)]
        ai = [wide(step_ref[2 + n : 3 + n, cols]) for n in range(2)]
        pr = [wide(residue_ref[n : n + 1, cols]) for n in range(2)]
        pi = [wide(residue_ref[2 + n : 3 + n, cols]) for n in range(2)]
        direct = wide(bias_ref[:, cols])
        re = [entry[n][0][:, cols] for n in range(2)]
        im = [entry[n][1][:, cols] for n in range(2)]
        for i in range(length):
            u = mixin_ref[q, pl.ds(i, SUB, stride=length), :]
            y = direct * u
            for n in range(2):
                re[n], im[n] = ar[n] * re[n] - ai[n] * im[n] + u, ar[n] * im[n] + ai[n] * re[n]
                y = y + (pr[n] * re[n] - pi[n] * im[n])
            long[q, pl.ds(i, SUB, stride=length), :] = y
        out_ref[:, cols] = (query[:, cols] * long[q]).astype(out_ref.dtype)


def mix_kernel(count, which_ref, *refs):
    x_refs, (w_ref, base_ref, out_ref, w, sems) = refs[:count], refs[count:]
    chans = x_refs[0].shape[1]
    copies = []
    for j in range(count):
        at = pl.multiple_of(which_ref[j] * chans, chans)
        copies.append(pltpu.make_async_copy(w_ref.at[pl.ds(at, chans)], w.at[j], sems.at[j]))
        copies[-1].start()
    total = base_ref[...]
    for j in range(count):
        copies[j].wait()
        total = total + jnp.dot(x_refs[j][...], w[j], preferred_element_type=jnp.float32)
    out_ref[...] = total.astype(out_ref.dtype)


IN_VMEM = pl.BlockSpec(memory_space=pltpu.VMEM)
IN_SMEM = pl.BlockSpec(memory_space=pltpu.SMEM)
IN_HBM = pl.BlockSpec(memory_space=pltpu.HBM)
in_hbm = functools.partial(pltpu.with_memory_space_constraint, memory_space=pltpu.HBM)


def mix(blocks, which, weight, base, dtype):
    rows, chans = blocks[0].shape
    cols = weight.shape[1]
    count = len(blocks)
    return pl.pallas_call(
        functools.partial(mix_kernel, count),
        in_specs=[IN_SMEM] + [IN_VMEM] * count + [IN_HBM, IN_VMEM],
        out_shape=jax.ShapeDtypeStruct((rows, cols), dtype),
        scratch_shapes=[
            pltpu.VMEM((count, chans, cols), weight.dtype),
            pltpu.SemaphoreType.DMA((count,)),
        ],
        compiler_params=pltpu.CompilerParams(vmem_limit_bytes=VMEM),
        cost_estimate=pl.CostEstimate(
            flops=2 * count * rows * chans * cols,
            bytes_accessed=2 * count * chans * cols,
            transcendentals=0,
        ),
        name="mix",
    )(which, *blocks, in_hbm(weight), base)


def body(inputs, in_weight, out_weight, short_filter, decay, angle, residue, bias):
    rows, chans = inputs.shape
    place, blocks = lax.axis_index("seq"), lax.axis_size("seq")
    count = lax.axis_size("ch")
    col_start = lax.axis_index("ch") * chans
    near = [(s % 8) // 4 for s in range(blocks)]
    mirror = [s + 6 - 4 * ((s % 8) // 2) for s in range(blocks)]
    cut = lax.dynamic_slice(in_weight, (0, 0, col_start), (in_weight.shape[0], 3, chans))
    own_weight = jnp.concatenate([cut[:, g] for g in range(3)], axis=1)
    weight = lax.all_gather(
        own_weight,
        "seq",
        axis=0,
        tiled=True,
        axis_index_groups=[[s for s in range(blocks) if near[s] == h] for h in range(2)],
    )
    second = lax.all_gather(out_weight, "seq", axis=0, tiled=True)

    rim = lax.ppermute(inputs[-2:], "seq", [(i, i + 1) for i in range(blocks - 1)])
    tokens = jnp.concatenate([inputs, rim, jnp.zeros((HALO - 2, chans), inputs.dtype)], axis=0)
    swaps = []
    for c in range(count):
        for s in range(blocks):
            to = (c, s) if c % 2 == near[s] else (c ^ 1, mirror[s])
            swaps.append((c * blocks + s, to[0] * blocks + to[1]))
    features = ring(lax.ppermute(tokens, ("ch", "seq"), swaps), "ch")
    here = lax.axis_index("ch")

    rate, turn = decay.T, angle.T
    length = rows // SUB
    pack = lambda pair: jnp.concatenate(pair, axis=1)
    step = pack(powers(jnp.ones((1,), jnp.float32), rate, turn))[0]
    join = pack(powers(jnp.full((1,), length, jnp.float32), rate, turn))[0]
    reach = pack(powers((jnp.arange(SUB) * length).astype(jnp.float32), rate, turn))
    reach = reach.transpose(1, 0, 2)
    gap = place - 1 - jnp.arange(blocks)
    jump = pack(powers((jnp.maximum(gap, 0) * rows).astype(jnp.float32), rate, turn))
    jump = jnp.where((gap >= 0)[:, None, None], jump, 0.0).transpose(1, 0, 2)
    poles = jnp.concatenate([residue[0].T, residue[1].T], axis=0)

    f32, b16 = jnp.float32, jnp.bfloat16
    padded, depth = rows + HALO, chans * count // 2
    params = pltpu.CompilerParams(vmem_limit_bytes=VMEM)
    shape = jax.ShapeDtypeStruct
    half = lax.rem(place, 8) // 4
    keep, send, lhs = pl.pallas_call(
        functools.partial(mixin_project_kernel, count),
        in_specs=[IN_SMEM] + [IN_VMEM] * count + [IN_HBM],
        out_shape=[
            shape((padded, 2 * chans), f32),
            shape((padded, 2 * chans), b16),
            shape((2, padded, depth), b16),
        ],
        scratch_shapes=[pltpu.VMEM((depth, 2 * chans), b16), pltpu.SemaphoreType.DMA((2,))],
        compiler_params=params,
        cost_estimate=pl.CostEstimate(
            flops=8 * padded * depth * chans, bytes_accessed=4 * depth * chans, transcendentals=0
        ),
        name="project_mixin",
    )(jnp.stack([half, here]).astype(jnp.int32), *features, in_hbm(weight))
    pairs = [(s, mirror[s]) for s in range(blocks)]
    more = lax.ppermute(send, "seq", pairs)
    query_keep, query_send = pl.pallas_call(
        query_project_kernel,
        in_specs=[IN_VMEM, IN_HBM],
        out_shape=[shape((padded, chans), f32), shape((padded, chans), b16)],
        scratch_shapes=[pltpu.VMEM((depth, chans), b16), pltpu.SemaphoreType.DMA((1,))],
        compiler_params=params,
        cost_estimate=pl.CostEstimate(
            flops=4 * padded * depth * chans, bytes_accessed=2 * depth * chans, transcendentals=0
        ),
        name="project_query",
    )(lhs, in_hbm(weight))
    taps = short_filter.reshape(9, chans)
    mixin, begin, final = pl.pallas_call(
        functools.partial(scan_kernel, rows, chans),
        out_shape=[
            shape((chans // LANES, rows, LANES), f32),
            shape((4, SUB, chans), f32),
            shape((4, chans), f32),
        ],
        compiler_params=params,
        name="scan",
    )(keep, more, taps, step, join)
    query_more = lax.ppermute(query_send, "seq", pairs)

    states = spread(final, "seq")
    gated = pl.pallas_call(
        functools.partial(gate_kernel, rows, chans),
        out_shape=shape((rows, chans), b16),
        scratch_shapes=[pltpu.VMEM((chans // LANES, rows, LANES), f32)],
        compiler_params=params,
        name="gate",
    )(states, jump, begin, reach, step, poles, bias[None, :], mixin, query_keep, query_more, taps)

    which = jnp.stack([lax.rem(here + hop + count, count) for hop in ring_hops(count)])
    which = which.astype(jnp.int32)
    parts = ring(gated, "ch")
    first = mix(parts[:-1], which[:-1], second, jnp.zeros((rows, chans), f32), f32)
    return mix(parts[-1:], which[-1:], second, first, b16)


def solution(mesh):
    placed = (
        P("seq", "ch"),
        P("seq", None, None),
        P("seq", "ch"),
        P(None, None, "ch"),
        P("ch", None),
        P("ch", None),
        P(None, "ch", None),
        P("ch"),
    )
    return jax.shard_map(
        body, mesh=mesh, in_specs=placed, out_specs=P("seq", "ch"), check_vma=False
    )
```

time: 138 us -> 126 us (0.913); the launches traced: 138 us -> 124 us
  waiting for transfers between devices: 53.5 us -> 44.5 us
  Pallas kernels: 15.6 us -> 11.9 us
  other arithmetic: 2.47 us -> 5.02 us
  starting transfers between devices: 46.5 us -> 44.5 us
  local copies, waits for them, and re-layouts: 6.08 us -> 4.17 us
    ppermute x6, starting transfers between devices: 32.1 us -> 19.3 us  [ring(): above = lax.ppermute(above, axis, down)]
    ppermute x8, waiting for transfers between devices: 31.3 us -> 21.2 us  [ring(): below = lax.ppermute(below, axis, up)]
    ppermute x8, starting transfers between devices: 3.64 us -> 11.3 us  [ring(): below = lax.ppermute(below, axis, up)]
    all_to_all x1, waiting for transfers between devices: 7.58 us -> 0.01 us  [spread(): lax.all_to_all(jnp.broadcast_to(x[None], (count,) + x.shape), axis, 0, 0,...]
    all_gather x1, waiting for transfers between devices: 0.01 us -> 4.31 us  [body(): lax.all_gather(own_weight, 'seq', axis=0, tiled=True, axis_index_groups=[...]
    all_gather x1, waiting for transfers between devices: 0.01 us -> 3.89 us  [body(): second = lax.all_gather(out_weight, 'seq', axis=0, tiled=True)]
    pallas_call x4 -> x6, Pallas kernels: 15.6 us -> 11.9 us  [the longest x2 4.78 us: mix(): pl.pallas_call(functools.partial(mix_kernel, count), in_specs=[IN_SMEM] +...]
    unnamed x46 -> x2, local copies, waits for them, and re-layouts: 2.48 us -> 0.01 us
  transfers between devices with their start and end apart: 20 -> 21, of which waited for: 11 -> 12; matrix products, arithmetic and copies ran while one was open for 2% -> 6% of each run, Pallas kernels for 6% -> 8%
where the time goes in v4:
time: 126 us; the launch traced here: 124 us
  starting transfers between devices  44.5 us (35%)
  waiting for transfers between devices  44.5 us (35%)
  between operations  13.6 us (11%)
  Pallas kernels  11.9 us (9%)
  other arithmetic  5.02 us (4%)
  local copies, waits for them, and re-layouts  4.17 us (3%)
    ppermute x8, waiting for transfers between devices, ring(): below = lax.ppermute(below, axis, up)  21.2 us
    ppermute x6, starting transfers between devices, ring(): above = lax.ppermute(above, axis, down)  19.3 us
    ppermute x8, starting transfers between devices, ring(): below = lax.ppermute(below, axis, up)  11.3 us
    all_to_all x1, starting transfers between devices, spread(): lax.all_to_all(jnp.broadcast_to(x[None], (count,) + x.shape), axis, 0, 0,...  8.1 us
    ppermute x1, waiting for transfers between devices, body(): more = lax.ppermute(send, 'seq', pairs)  7.52 us
    ppermute x1, waiting for transfers between devices, body(): query_more = lax.ppermute(query_send, 'seq', pairs)  5.17 us
    pallas_call x2, Pallas kernels, mix(): pl.pallas_call(functools.partial(mix_kernel, count), in_specs=[IN_SMEM] +...  4.78 us
    all_gather x1, waiting for transfers between devices, body(): lax.all_gather(own_weight, 'seq', axis=0, tiled=True, axis_index_groups=[...  4.31 us
  transfers between devices with their start and end apart: 21, of which 12 were waited for; matrix products, arithmetic and copies ran while one was open for 6% of the time, Pallas kernels for 8%

profile of v4, /device:TPU:2, one launch (start us, length us, event | category | flops | bytes accessed | tf_op | source)
XLA Modules:
  0.0 123.7 jit_solution(136493851692906094)
XLA Ops:
  6.5 1.1 dynamic-slice_bitcast_fusion.2
  7.6 0.8 pad_maximum_fusion
  8.4 0.0 all-gather.3.cloned.1.call-update
  8.4 0.0 all-gather.5.cloned.1.call-start
  8.5 0.7 all-gather.5.cloned.1.call-update
  9.2 0.7 slice.18
  9.9 1.9 %collective-permute-start = (bf16[2,512]{1,0:T(2,128)(2,1)S(1)}, bf16[2,512]{1,0:T(2,128)(2,1)S(1)}, u32[]{:S(2)}, u32[]{:S(2)}) collective-permute-start(bf16[2,512]{1,0:T(2,128)(2,1)S(1)} %slice.18), channel_id=1, source_target_pairs={{0,1},{1,2},{2,3},{3,4},{4,5},{5,6},{6,7},{7,8},{8,9},{9,10},{10,1... | collective-permute-start | bytes 6152 | tf_op jit(solution)/shard_map/ppermute | solution.py:235
  11.8 1.3 %fusion.1 = (f32[32,2,512]{2,0,1:T(8,128)S(1)}, f32[32,2,512]{2,0,1:T(8,128)S(1)}) fusion(f32[2,512]{1,0:T(2,128)} %bitcast.52, f32[32]{0:T(128)S(1)} %multiply_convert_fusion.1, f32[2,512]{1,0:T(2,128)} %bitcast.54, f32[32]{0:T(128)S(1)} %fusion.7), kind=kLoop, calls=%fused_computation.6 | loop fusion | flops 131072 | bytes 270592 | tf_op jit(solution)/shard_map/mul | solution.py:48
  13.1 0.1 pad.15.clone
  13.2 1.6 %collective-permute-done = bf16[2,512]{1,0:T(2,128)(2,1)S(1)} collective-permute-done((bf16[2,512]{1,0:T(2,128)(2,1)S(1)}, bf16[2,512]{1,0:T(2,128)(2,1)S(1)}, u32[]{:S(2)}, u32[]{:S(2)}) %collective-permute-start) | collective-permute-done | bytes 2080 | tf_op jit(solution)/shard_map/ppermute | solution.py:235
  14.8 1.0 maximum_maximum_fusion
  15.8 0.7 collective-permute-start.1
  16.5 0.0 collective-permute-done.1.refs_0_
  16.5 9.8 %collective-permute-start.2 = (bf16[144,512]{1,0:T(8,128)(2,1)S(1)}, bf16[144,512]{1,0:T(8,128)(2,1)S(1)}, u32[]{:S(2)}, u32[]{:S(2)}) collective-permute-start(bf16[144,512]{1,0:T(8,128)(2,1)S(1)} %collective-permute-done.1.refs_0_), channel_id=1, source_target_pairs={{0,32},{32,64},{64,96},{96,128},{128,160},{160,192},{192,224},{224... | collective-permute-start | bytes 442376 | tf_op jit(solution)/shard_map/ppermute | solution.py:37
  26.2 0.9 fusion.3
  27.1 4.0 %collective-permute-start.3 = (bf16[144,512]{1,0:T(8,128)(2,1)S(1)}, bf16[144,512]{1,0:T(8,128)(2,1)S(1)}, u32[]{:S(2)}, u32[]{:S(2)}) collective-permute-start(bf16[144,512]{1,0:T(8,128)(2,1)S(1)} %collective-permute-done.1.refs_0_), channel_id=1, source_target_pairs={{0,224},{32,0},{64,32},{96,64},{128,96},{160,128},{192,160},{224,1... | collective-permute-start | bytes 442376 | tf_op jit(solution)/shard_map/ppermute | solution.py:40
  31.2 2.2 %collective-permute-done.2.refs_1_ = bf16[144,512]{1,0:T(8,128)(2,1)S(1)} collective-permute-done((bf16[144,512]{1,0:T(8,128)(2,1)S(1)}, bf16[144,512]{1,0:T(8,128)(2,1)S(1)}, u32[]{:S(2)}, u32[]{:S(2)}) %collective-permute-start.2) | collective-permute-done | bytes 147488 | tf_op jit(solution)/shard_map/ppermute | solution.py:37
  33.3 0.0 collective-permute-start.4
  33.3 0.8 multiply_bitcast_fusion.1
  34.2 0.0 collective-permute-done.3.refs_2_
  34.2 3.3 %collective-permute-start.5 = (bf16[144,512]{1,0:T(8,128)(2,1)S(1)}, bf16[144,512]{1,0:T(8,128)(2,1)S(1)}, u32[]{:S(2)}, u32[]{:S(2)}) collective-permute-start(bf16[144,512]{1,0:T(8,128)(2,1)S(1)} %collective-permute-done.3.refs_2_), channel_id=1, source_target_pairs={{0,224},{32,0},{64,32},{96,64},{128,96},{160,128},{192,160},{224,1... | collective-permute-start | bytes 442376 | tf_op jit(solution)/shard_map/ppermute | solution.py:40
  37.5 2.2 %collective-permute-done.4.refs_3_ = bf16[144,512]{1,0:T(8,128)(2,1)S(1)} collective-permute-done((bf16[144,512]{1,0:T(8,128)(2,1)S(1)}, bf16[144,512]{1,0:T(8,128)(2,1)S(1)}, u32[]{:S(2)}, u32[]{:S(2)}) %collective-permute-start.4) | collective-permute-done | bytes 147488 | tf_op jit(solution)/shard_map/ppermute | solution.py:37
  39.7 0.0 collective-permute-start.6
  39.7 0.7 slice_bitcast_fusion.1
  40.4 0.0 collective-permute-done.5.refs_4_
  40.4 3.4 %collective-permute-start.7 = (bf16[144,512]{1,0:T(8,128)(2,1)S(1)}, bf16[144,512]{1,0:T(8,128)(2,1)S(1)}, u32[]{:S(2)}, u32[]{:S(2)}) collective-permute-start(bf16[144,512]{1,0:T(8,128)(2,1)S(1)} %collective-permute-done.5.refs_4_), channel_id=1, source_target_pairs={{0,224},{32,0},{64,32},{96,64},{128,96},{160,128},{192,160},{224,1... | collective-permute-start | bytes 442376 | tf_op jit(solution)/shard_map/ppermute | solution.py:40
  43.9 2.4 %collective-permute-done.6.refs_5_ = bf16[144,512]{1,0:T(8,128)(2,1)S(1)} collective-permute-done((bf16[144,512]{1,0:T(8,128)(2,1)S(1)}, bf16[144,512]{1,0:T(8,128)(2,1)S(1)}, u32[]{:S(2)}, u32[]{:S(2)}) %collective-permute-start.6) | collective-permute-done | bytes 147488 | tf_op jit(solution)/shard_map/ppermute | solution.py:37
  46.3 0.0 collective-permute-start.8
  46.3 0.1 pad_add_fusion.place_ref
  46.3 0.8 reshape.42.taps_ref
  47.1 0.0 collective-permute-done.7.refs_6_
  47.1 5.5 %collective-permute-done.8.refs_7_ = bf16[144,512]{1,0:T(8,128)(2,1)S(1)} collective-permute-done((bf16[144,512]{1,0:T(8,128)(2,1)S(1)}, bf16[144,512]{1,0:T(8,128)(2,1)S(1)}, u32[]{:S(2)}, u32[]{:S(2)}) %collective-permute-start.8) | collective-permute-done | bytes 147488 | tf_op jit(solution)/shard_map/ppermute | solution.py:37
  52.6 4.3 %all-gather.3.cloned.1.call-done.refs_8_.w_ref = bf16[2048,1536]{1,0:T(8,128)(2,1)} async-done(((bf16[128,1536]{1,0:T(8,128)(2,1)}), bf16[2048,1536]{1,0:T(8,128)(2,1)}) %all-gather.3.cloned.1.call-update) | async-done | bytes 6291472 | tf_op jit(solution)/shard_map/all_gather | solution.py:226
  56.9 3.7 %project_mixin.1 = (f32[144,1024]{1,0:T(8,128)S(1)}, bf16[144,1024]{1,0:T(8,128)(2,1)S(1)}, bf16[2,144,2048]{2,1,0:T(8,128)(2,1)S(1)}) custom-call(s32[2]{0:T(128)S(1)} %pad_add_fusion.place_ref, bf16[144,512]{1,0:T(8,128)(2,1)S(1)} %collective-permute-done.1.refs_0_, bf16[144,512]{1,0:T(8,128)(2,1)S(1)} %collective-permute-done.2.refs_1_, ...), custom_call_target="tpu_custom_call" | custom-call | flops 1207959552 | bytes 4194304 | tf_op jit(solution)/shard_map/project_mixin/pallas_call | solution.py:262
  60.6 1.6 %collective-permute-start.9 = (bf16[144,1024]{1,0:T(8,128)(2,1)S(1)}, bf16[144,1024]{1,0:T(8,128)(2,1)S(1)}, u32[]{:S(2)}, u32[]{:S(2)}) collective-permute-start(bf16[144,1024]{1,0:T(8,128)(2,1)S(1)} %get-tuple-element.14), channel_id=1, source_target_pairs={{0,6},{1,7},{2,4},{3,5},{4,2},{5,3},{6,0},{7,1},{8,14},{9,15},{10,... | collective-permute-start | bytes 884744 | tf_op jit(solution)/shard_map/ppermute | solution.py:278
  62.2 0.1 fusion.jump_ref
  62.3 7.5 %collective-permute-done.9.more_ref = bf16[144,1024]{1,0:T(8,128)(2,1)S(1)} collective-permute-done((bf16[144,1024]{1,0:T(8,128)(2,1)S(1)}, bf16[144,1024]{1,0:T(8,128)(2,1)S(1)}, u32[]{:S(2)}, u32[]{:S(2)}) %collective-permute-start.9) | collective-permute-done | bytes 294944 | tf_op jit(solution)/shard_map/ppermute | solution.py:278
  69.9 0.5 scan.1
  70.4 0.8 broadcast_in_dim.17
  71.2 8.1 %all-to-all-start = ((f32[32,4,512]{2,1,0:T(4,128)}), f32[32,4,512]{2,1,0:T(4,128)S(1)}, u32[]{:S(2)}, u32[]{:S(2)}) async-start(f32[32,4,512]{2,1,0:T(4,128)} %broadcast_in_dim.17), calls=%async_computation | async-start | bytes 524288 | tf_op jit(solution)/shard_map/all_to_all | solution.py:18
  79.3 0.0 copy-start
  79.3 2.4 %project_query.1 = (f32[144,512]{1,0:T(8,128)S(1)}, bf16[144,512]{1,0:T(8,128)(2,1)S(1)}) custom-call(bf16[2,144,2048]{2,1,0:T(8,128)(2,1)S(1)} %get-tuple-element.18.lhs_ref, bf16[2048,1536]{1,0:T(8,128)(2,1)} %all-gather.3.cloned.1.call-done.refs_8_.w_ref), custom_call_target="tpu_custom_call" | custom-call | flops 603979776 | bytes 2097152 | tf_op jit(solution)/shard_map/project_query/pallas_call | solution.py:279
  81.7 1.6 %collective-permute-start.10 = (bf16[144,512]{1,0:T(8,128)(2,1)S(1)}, bf16[144,512]{1,0:T(8,128)(2,1)S(1)}, u32[]{:S(2)}, u32[]{:S(2)}) collective-permute-start(bf16[144,512]{1,0:T(8,128)(2,1)S(1)} %get-tuple-element.20), channel_id=1, source_target_pairs={{0,6},{1,7},{2,4},{3,5},{4,2},{5,3},{6,0},{7,1},{8,14},{9,15},{10,... | collective-permute-start | bytes 442376 | tf_op jit(solution)/shard_map/ppermute | solution.py:301
  83.3 5.2 %collective-permute-done.10.more_ref = bf16[144,512]{1,0:T(8,128)(2,1)S(1)} collective-permute-done((bf16[144,512]{1,0:T(8,128)(2,1)S(1)}, bf16[144,512]{1,0:T(8,128)(2,1)S(1)}, u32[]{:S(2)}, u32[]{:S(2)}) %collective-permute-start.10) | collective-permute-done | bytes 147488 | tf_op jit(solution)/shard_map/ppermute | solution.py:301
  88.4 0.0 all-to-all-done.all_ref
  88.4 0.5 gate.1.refs_0_
  88.9 1.6 %collective-permute-start.11 = (bf16[128,512]{1,0:T(8,128)(2,1)S(1)}, bf16[128,512]{1,0:T(8,128)(2,1)S(1)}, u32[]{:S(2)}, u32[]{:S(2)}) collective-permute-start(bf16[128,512]{1,0:T(8,128)(2,1)S(1)} %gate.1.refs_0_), channel_id=1, source_target_pairs={{0,32},{32,64},{64,96},{96,128},{128,160},{160,192},{192,224},{224... | collective-permute-start | bytes 393224 | tf_op jit(solution)/shard_map/ppermute | solution.py:37
  90.5 2.0 %collective-permute-start.15 = (bf16[128,512]{1,0:T(8,128)(2,1)S(1)}, bf16[128,512]{1,0:T(8,128)(2,1)S(1)}, u32[]{:S(2)}, u32[]{:S(2)}) collective-permute-start(bf16[128,512]{1,0:T(8,128)(2,1)S(1)} %gate.1.refs_0_), channel_id=1, source_target_pairs={{0,224},{32,0},{64,32},{96,64},{128,96},{160,128},{192,160},{224,1... | collective-permute-start | bytes 393224 | tf_op jit(solution)/shard_map/ppermute | solution.py:40
  92.5 3.1 %collective-permute-done.11.refs_1_ = bf16[128,512]{1,0:T(8,128)(2,1)S(1)} collective-permute-done((bf16[128,512]{1,0:T(8,128)(2,1)S(1)}, bf16[128,512]{1,0:T(8,128)(2,1)S(1)}, u32[]{:S(2)}, u32[]{:S(2)}) %collective-permute-start.11) | collective-permute-done | bytes 131104 | tf_op jit(solution)/shard_map/ppermute | solution.py:37
  95.7 0.0 collective-permute-start.12
  95.7 0.0 collective-permute-done.15.refs_2_
  95.7 3.2 %collective-permute-start.16 = (bf16[128,512]{1,0:T(8,128)(2,1)S(1)}, bf16[128,512]{1,0:T(8,128)(2,1)S(1)}, u32[]{:S(2)}, u32[]{:S(2)}) collective-permute-start(bf16[128,512]{1,0:T(8,128)(2,1)S(1)} %collective-permute-done.15.refs_2_), channel_id=1, source_target_pairs={{0,224},{32,0},{64,32},{96,64},{128,96},{160,128},{192,160},{224,1... | collective-permute-start | bytes 393224 | tf_op jit(solution)/shard_map/ppermute | solution.py:40
  98.9 2.9 %collective-permute-done.12.refs_3_ = bf16[128,512]{1,0:T(8,128)(2,1)S(1)} collective-permute-done((bf16[128,512]{1,0:T(8,128)(2,1)S(1)}, bf16[128,512]{1,0:T(8,128)(2,1)S(1)}, u32[]{:S(2)}, u32[]{:S(2)}) %collective-permute-start.12) | collective-permute-done | bytes 131104 | tf_op jit(solution)/shard_map/ppermute | solution.py:37
  101.9 0.0 collective-permute-start.13
  101.9 0.0 collective-permute-done.16.refs_4_
  101.9 3.2 %collective-permute-start.17 = (bf16[128,512]{1,0:T(8,128)(2,1)S(1)}, bf16[128,512]{1,0:T(8,128)(2,1)S(1)}, u32[]{:S(2)}, u32[]{:S(2)}) collective-permute-start(bf16[128,512]{1,0:T(8,128)(2,1)S(1)} %collective-permute-done.16.refs_4_), channel_id=1, source_target_pairs={{0,224},{32,0},{64,32},{96,64},{128,96},{160,128},{192,160},{224,1... | collective-permute-start | bytes 393224 | tf_op jit(solution)/shard_map/ppermute | solution.py:40
  105.1 2.9 %collective-permute-done.13.refs_5_ = bf16[128,512]{1,0:T(8,128)(2,1)S(1)} collective-permute-done((bf16[128,512]{1,0:T(8,128)(2,1)S(1)}, bf16[128,512]{1,0:T(8,128)(2,1)S(1)}, u32[]{:S(2)}, u32[]{:S(2)}) %collective-permute-start.13) | collective-permute-done | bytes 131104 | tf_op jit(solution)/shard_map/ppermute | solution.py:37
  108.0 0.0 collective-permute-start.14
  108.0 0.1 stack.47.which_ref
  108.1 3.9 %all-gather.5.cloned.1.call-done.refs_7_.refs_1_ = bf16[4096,512]{1,0:T(8,128)(2,1)} async-done(((bf16[128,512]{1,0:T(8,128)(2,1)}), bf16[4096,512]{1,0:T(8,128)(2,1)}) %all-gather.5.cloned.1.call-update) | async-done | bytes 4194320 | tf_op jit(solution)/shard_map/all_gather | solution.py:233
  112.0 0.0 collective-permute-done.17.refs_6_
  112.0 2.8 %mix.2.refs_2_ = f32[128,512]{1,0:T(8,128)S(1)} custom-call(s32[7]{0:T(128)S(1)} %stack.47.which_ref, bf16[128,512]{1,0:T(8,128)(2,1)S(1)} %gate.1.refs_0_, bf16[128,512]{1,0:T(8,128)(2,1)S(1)} %collective-permute-done.11.refs_1_, bf16[128,512]{1,0:T(8,128)(2,1)S(1)} %collective-permute-done.15.refs_2_, ...), custom_call_target="tpu_custom_call" | custom-call | flops 469762048 | bytes 3670016 | tf_op jit(solution)/shard_map/mix/pallas_call | solution.py:199
  114.9 0.0 collective-permute-done.14.refs_0_
  114.9 1.9 %mix.3 = bf16[128,512]{1,0:T(8,128)(2,1)} custom-call(s32[1]{0:T(128)} %bitcast.which_ref, bf16[128,512]{1,0:T(8,128)(2,1)S(1)} %collective-permute-done.14.refs_0_, bf16[4096,512]{1,0:T(8,128)(2,1)} %all-gather.5.cloned.1.call-done.refs_7_.refs_1_, f32[128,512]{1,0:T(8,128)S(1)} %mix.2.refs_2_), custom_call_target="tpu_custom_call" | custom-call | flops 67108864 | bytes 524288 | tf_op jit(solution)/shard_map/mix/pallas_call | solution.py:199
  (13 shorter events, 0.1 us)
Async XLA Ops:
  6.5 50.4 %all-gather.3.cloned.1.call-start = ((), (), s32[]{:S(2)}) async-start(), calls=%async_computation.1 | async-start | bytes 6684672 | tf_op jit(solution)/shard_map/all_gather | solution.py:226
  8.4 103.6 %all-gather.5.cloned.1.call-start = ((), (), s32[]{:S(2)}) async-start(), calls=%async_computation.2 | async-start | bytes 4325376 | tf_op jit(solution)/shard_map/all_gather | solution.py:233
  9.9 4.9 %collective-permute-start = (bf16[2,512]{1,0:T(2,128)(2,1)S(1)}, bf16[2,512]{1,0:T(2,128)(2,1)S(1)}, u32[]{:S(2)}, u32[]{:S(2)}) collective-permute-start(bf16[2,512]{1,0:T(2,128)(2,1)S(1)} %slice.18), channel_id=1, source_target_pairs={{0,1},{1,2},{2,3},{3,4},{4,5},{5,6},{6,7},{7,8},{8,9},{9,10},{10,1... | collective-permute-start | bytes 6152 | tf_op jit(solution)/shard_map/ppermute | solution.py:235
  15.8 0.7 collective-permute-start.1
  16.5 16.9 %collective-permute-start.2 = (bf16[144,512]{1,0:T(8,128)(2,1)S(1)}, bf16[144,512]{1,0:T(8,128)(2,1)S(1)}, u32[]{:S(2)}, u32[]{:S(2)}) collective-permute-start(bf16[144,512]{1,0:T(8,128)(2,1)S(1)} %collective-permute-done.1.refs_0_), channel_id=1, source_target_pairs={{0,32},{32,64},{64,96},{96,128},{128,160},{160,192},{192,224},{224... | collective-permute-start | bytes 442376 | tf_op jit(solution)/shard_map/ppermute | solution.py:37
  27.1 7.0 %collective-permute-start.3 = (bf16[144,512]{1,0:T(8,128)(2,1)S(1)}, bf16[144,512]{1,0:T(8,128)(2,1)S(1)}, u32[]{:S(2)}, u32[]{:S(2)}) collective-permute-start(bf16[144,512]{1,0:T(8,128)(2,1)S(1)} %collective-permute-done.1.refs_0_), channel_id=1, source_target_pairs={{0,224},{32,0},{64,32},{96,64},{128,96},{160,128},{192,160},{224,1... | collective-permute-start | bytes 442376 | tf_op jit(solution)/shard_map/ppermute | solution.py:40
  33.3 6.4 %collective-permute-start.4 = (bf16[144,512]{1,0:T(8,128)(2,1)S(1)}, bf16[144,512]{1,0:T(8,128)(2,1)S(1)}, u32[]{:S(2)}, u32[]{:S(2)}) collective-permute-start(bf16[144,512]{1,0:T(8,128)(2,1)S(1)} %collective-permute-done.2.refs_1_), channel_id=1, source_target_pairs={{0,32},{32,64},{64,96},{96,128},{128,160},{160,192},{192,224},{224... | collective-permute-start | bytes 442376 | tf_op jit(solution)/shard_map/ppermute | solution.py:37
  34.2 6.2 %collective-permute-start.5 = (bf16[144,512]{1,0:T(8,128)(2,1)S(1)}, bf16[144,512]{1,0:T(8,128)(2,1)S(1)}, u32[]{:S(2)}, u32[]{:S(2)}) collective-permute-start(bf16[144,512]{1,0:T(8,128)(2,1)S(1)} %collective-permute-done.3.refs_2_), channel_id=1, source_target_pairs={{0,224},{32,0},{64,32},{96,64},{128,96},{160,128},{192,160},{224,1... | collective-permute-start | bytes 442376 | tf_op jit(solution)/shard_map/ppermute | solution.py:40
  39.7 6.6 %collective-permute-start.6 = (bf16[144,512]{1,0:T(8,128)(2,1)S(1)}, bf16[144,512]{1,0:T(8,128)(2,1)S(1)}, u32[]{:S(2)}, u32[]{:S(2)}) collective-permute-start(bf16[144,512]{1,0:T(8,128)(2,1)S(1)} %collective-permute-done.4.refs_3_), channel_id=1, source_target_pairs={{0,32},{32,64},{64,96},{96,128},{128,160},{160,192},{192,224},{224... | collective-permute-start | bytes 442376 | tf_op jit(solution)/shard_map/ppermute | solution.py:37
  40.4 6.7 %collective-permute-start.7 = (bf16[144,512]{1,0:T(8,128)(2,1)S(1)}, bf16[144,512]{1,0:T(8,128)(2,1)S(1)}, u32[]{:S(2)}, u32[]{:S(2)}) collective-permute-start(bf16[144,512]{1,0:T(8,128)(2,1)S(1)} %collective-permute-done.5.refs_4_), channel_id=1, source_target_pairs={{0,224},{32,0},{64,32},{96,64},{128,96},{160,128},{192,160},{224,1... | collective-permute-start | bytes 442376 | tf_op jit(solution)/shard_map/ppermute | solution.py:40
  46.3 6.4 %collective-permute-start.8 = (bf16[144,512]{1,0:T(8,128)(2,1)S(1)}, bf16[144,512]{1,0:T(8,128)(2,1)S(1)}, u32[]{:S(2)}, u32[]{:S(2)}) collective-permute-start(bf16[144,512]{1,0:T(8,128)(2,1)S(1)} %collective-permute-done.6.refs_5_), channel_id=1, source_target_pairs={{0,32},{32,64},{64,96},{96,128},{128,160},{160,192},{192,224},{224... | collective-permute-start | bytes 442376 | tf_op jit(solution)/shard_map/ppermute | solution.py:37
  60.6 9.2 %collective-permute-start.9 = (bf16[144,1024]{1,0:T(8,128)(2,1)S(1)}, bf16[144,1024]{1,0:T(8,128)(2,1)S(1)}, u32[]{:S(2)}, u32[]{:S(2)}) collective-permute-start(bf16[144,1024]{1,0:T(8,128)(2,1)S(1)} %get-tuple-element.14), channel_id=1, source_target_pairs={{0,6},{1,7},{2,4},{3,5},{4,2},{5,3},{6,0},{7,1},{8,14},{9,15},{10,... | collective-permute-start | bytes 884744 | tf_op jit(solution)/shard_map/ppermute | solution.py:278
  71.2 17.3 %all-to-all-start = ((f32[32,4,512]{2,1,0:T(4,128)}), f32[32,4,512]{2,1,0:T(4,128)S(1)}, u32[]{:S(2)}, u32[]{:S(2)}) async-start(f32[32,4,512]{2,1,0:T(4,128)} %broadcast_in_dim.17), calls=%async_computation | async-start | bytes 524288 | tf_op jit(solution)/shard_map/all_to_all | solution.py:18
  79.3 9.1 %copy-start = (f32[512]{0:T(512)S(1)}, f32[512]{0:T(512)}, u32[]{:S(2)}) copy-start(f32[512]{0:T(512)} %param.15) | copy-start | bytes 6148
  81.7 6.7 %collective-permute-start.10 = (bf16[144,512]{1,0:T(8,128)(2,1)S(1)}, bf16[144,512]{1,0:T(8,128)(2,1)S(1)}, u32[]{:S(2)}, u32[]{:S(2)}) collective-permute-start(bf16[144,512]{1,0:T(8,128)(2,1)S(1)} %get-tuple-element.20), channel_id=1, source_target_pairs={{0,6},{1,7},{2,4},{3,5},{4,2},{5,3},{6,0},{7,1},{8,14},{9,15},{10,... | collective-permute-start | bytes 442376 | tf_op jit(solution)/shard_map/ppermute | solution.py:301
  88.9 6.7 %collective-permute-start.11 = (bf16[128,512]{1,0:T(8,128)(2,1)S(1)}, bf16[128,512]{1,0:T(8,128)(2,1)S(1)}, u32[]{:S(2)}, u32[]{:S(2)}) collective-permute-start(bf16[128,512]{1,0:T(8,128)(2,1)S(1)} %gate.1.refs_0_), channel_id=1, source_target_pairs={{0,32},{32,64},{64,96},{96,128},{128,160},{160,192},{192,224},{224... | collective-permute-start | bytes 393224 | tf_op jit(solution)/shard_map/ppermute | solution.py:37
  90.5 5.2 %collective-permute-start.15 = (bf16[128,512]{1,0:T(8,128)(2,1)S(1)}, bf16[128,512]{1,0:T(8,128)(2,1)S(1)}, u32[]{:S(2)}, u32[]{:S(2)}) collective-permute-start(bf16[128,512]{1,0:T(8,128)(2,1)S(1)} %gate.1.refs_0_), channel_id=1, source_target_pairs={{0,224},{32,0},{64,32},{96,64},{128,96},{160,128},{192,160},{224,1... | collective-permute-start | bytes 393224 | tf_op jit(solution)/shard_map/ppermute | solution.py:40
  95.7 6.2 %collective-permute-start.12 = (bf16[128,512]{1,0:T(8,128)(2,1)S(1)}, bf16[128,512]{1,0:T(8,128)(2,1)S(1)}, u32[]{:S(2)}, u32[]{:S(2)}) collective-permute-start(bf16[128,512]{1,0:T(8,128)(2,1)S(1)} %collective-permute-done.11.refs_1_), channel_id=1, source_target_pairs={{0,32},{32,64},{64,96},{96,128},{128,160},{160,192},{192,224},{224... | collective-permute-start | bytes 393224 | tf_op jit(solution)/shard_map/ppermute | solution.py:37
  95.7 6.2 %collective-permute-start.16 = (bf16[128,512]{1,0:T(8,128)(2,1)S(1)}, bf16[128,512]{1,0:T(8,128)(2,1)S(1)}, u32[]{:S(2)}, u32[]{:S(2)}) collective-permute-start(bf16[128,512]{1,0:T(8,128)(2,1)S(1)} %collective-permute-done.15.refs_2_), channel_id=1, source_target_pairs={{0,224},{32,0},{64,32},{96,64},{128,96},{160,128},{192,160},{224,1... | collective-permute-start | bytes 393224 | tf_op jit(solution)/shard_map/ppermute | solution.py:40
  101.9 6.2 %collective-permute-start.13 = (bf16[128,512]{1,0:T(8,128)(2,1)S(1)}, bf16[128,512]{1,0:T(8,128)(2,1)S(1)}, u32[]{:S(2)}, u32[]{:S(2)}) collective-permute-start(bf16[128,512]{1,0:T(8,128)(2,1)S(1)} %collective-permute-done.12.refs_3_), channel_id=1, source_target_pairs={{0,32},{32,64},{64,96},{96,128},{128,160},{160,192},{192,224},{224... | collective-permute-start | bytes 393224 | tf_op jit(solution)/shard_map/ppermute | solution.py:37
  101.9 10.1 %collective-permute-start.17 = (bf16[128,512]{1,0:T(8,128)(2,1)S(1)}, bf16[128,512]{1,0:T(8,128)(2,1)S(1)}, u32[]{:S(2)}, u32[]{:S(2)}) collective-permute-start(bf16[128,512]{1,0:T(8,128)(2,1)S(1)} %collective-permute-done.16.refs_4_), channel_id=1, source_target_pairs={{0,224},{32,0},{64,32},{96,64},{128,96},{160,128},{192,160},{224,1... | collective-permute-start | bytes 393224 | tf_op jit(solution)/shard_map/ppermute | solution.py:40
  108.0 6.8 %collective-permute-start.14 = (bf16[128,512]{1,0:T(8,128)(2,1)S(1)}, bf16[128,512]{1,0:T(8,128)(2,1)S(1)}, u32[]{:S(2)}, u32[]{:S(2)}) collective-permute-start(bf16[128,512]{1,0:T(8,128)(2,1)S(1)} %collective-permute-done.13.refs_5_), channel_id=1, source_target_pairs={{0,32},{32,64},{64,96},{96,128},{128,160},{160,192},{192,224},{224... | collective-permute-start | bytes 393224 | tf_op jit(solution)/shard_map/ppermute | solution.py:37
Sparse Core Ops, SparseCore 0:
  9.2 47.6 all-gather.2
  59.5 52.4 all-gather.4

commit v5 on v4

--- a/solution.py
+++ b/solution.py
@@ -99,8 +99,20 @@
 
 
 def scan_kernel(
-    rows, chans, keep_ref, more_ref, taps_ref, step_ref, join_ref, mixin_ref, begin_ref, final_ref
+    rows,
+    chans,
+    keep_ref,
+    more_ref,
+    query_ref,
+    taps_ref,
+    step_ref,
+    join_ref,
+    mixin_ref,
+    begin_ref,
+    final_ref,
+    send_ref,
 ):
+    send_ref[...] = query_ref[...]
     length = rows // SUB
 
     def filtered(branch):
@@ -172,17 +184,38 @@
 
 
 def mix_kernel(count, which_ref, *refs):
-    x_refs, (w_ref, base_ref, out_ref, w, sems) = refs[:count], refs[count:]
+    x_refs, (w_ref, out_ref, rest_ref, w, sems) = refs[: count - 1], refs[count - 1 :]
     chans = x_refs[0].shape[1]
+    part = chans // 2
     copies = []
     for j in range(count):
-        at = pl.multiple_of(which_ref[j] * chans, chans)
-        copies.append(pltpu.make_async_copy(w_ref.at[pl.ds(at, chans)], w.at[j], sems.at[j]))
-        copies[-1].start()
-    total = base_ref[...]
+        block = which_ref[j]
+        other = jnp.where(lax.rem(block, 2) == which_ref[count], 0, 1)
+        col = pl.multiple_of(other * chans, chans)
+        pair = []
+        for e in range(2):
+            row = pl.multiple_of(lax.div(block, 2) * chans + jnp.where(other == e, 0, part), part)
+            dst = rest_ref if j == count - 1 else w.at[j]
+            pair.append(
+                pltpu.make_async_copy(
+                    w_ref.at[pl.ds(row, part), pl.ds(col, out_ref.shape[1])],
+                    dst.at[pl.ds(e * part, part)],
+                    sems.at[j, e],
+                )
+            )
+            pair[-1].start()
+        copies.append(pair)
+    total = jnp.zeros(out_ref.shape, jnp.float32)
     for j in range(count):
-        copies[j].wait()
-        total = total + jnp.dot(x_refs[j][...], w[j], preferred_element_type=jnp.float32)
+        for copy in copies[j]:
+            copy.wait()
+        if j < count - 1:
+            total = total + jnp.dot(x_refs[j][...], w[j], preferred_element_type=jnp.float32)
+    out_ref[...] = total
+
+
+def last_mix_kernel(x_ref, w_ref, base_ref, out_ref):
+    total = base_ref[...] + jnp.dot(x_ref[...], w_ref[...], preferred_element_type=jnp.float32)
     out_ref[...] = total.astype(out_ref.dtype)
 
 
@@ -192,17 +225,19 @@
 in_hbm = functools.partial(pltpu.with_memory_space_constraint, memory_space=pltpu.HBM)
 
 
-def mix(blocks, which, weight, base, dtype):
+def mix(blocks, which, weight, cols):
     rows, chans = blocks[0].shape
-    cols = weight.shape[1]
-    count = len(blocks)
+    count = len(blocks) + 1
     return pl.pallas_call(
         functools.partial(mix_kernel, count),
-        in_specs=[IN_SMEM] + [IN_VMEM] * count + [IN_HBM, IN_VMEM],
-        out_shape=jax.ShapeDtypeStruct((rows, cols), dtype),
+        in_specs=[IN_SMEM] + [IN_VMEM] * (count - 1) + [IN_HBM],
+        out_shape=[
+            jax.ShapeDtypeStruct((rows, cols), jnp.float32),
+            jax.ShapeDtypeStruct((chans, cols), weight.dtype),
+        ],
         scratch_shapes=[
-            pltpu.VMEM((count, chans, cols), weight.dtype),
-            pltpu.SemaphoreType.DMA((count,)),
+            pltpu.VMEM((count - 1, chans, cols), weight.dtype),
+            pltpu.SemaphoreType.DMA((count, 2)),
         ],
         compiler_params=pltpu.CompilerParams(vmem_limit_bytes=VMEM),
         cost_estimate=pl.CostEstimate(
@@ -211,7 +246,7 @@
             transcendentals=0,
         ),
         name="mix",
-    )(which, *blocks, in_hbm(weight), base)
+    )(which, *blocks, in_hbm(weight))
 
 
 def body(inputs, in_weight, out_weight, short_filter, decay, angle, residue, bias):
@@ -223,14 +258,12 @@
     mirror = [s + 6 - 4 * ((s % 8) // 2) for s in range(blocks)]
     cut = lax.dynamic_slice(in_weight, (0, 0, col_start), (in_weight.shape[0], 3, chans))
     own_weight = jnp.concatenate([cut[:, g] for g in range(3)], axis=1)
-    weight = lax.all_gather(
-        own_weight,
-        "seq",
-        axis=0,
-        tiled=True,
-        axis_index_groups=[[s for s in range(blocks) if near[s] == h] for h in range(2)],
-    )
-    second = lax.all_gather(out_weight, "seq", axis=0, tiled=True)
+    pairs = [(s, mirror[s]) for s in range(blocks)]
+    halves = [[s for s in range(blocks) if near[s] == h] for h in range(2)]
+    gather = lambda x: lax.all_gather(x, "seq", axis=0, tiled=True, axis_index_groups=halves)
+    weight = gather(own_weight)
+    both = jnp.concatenate([out_weight, lax.ppermute(out_weight, "seq", pairs)], axis=1)
+    second = gather(both)
 
     rim = lax.ppermute(inputs[-2:], "seq", [(i, i + 1) for i in range(blocks - 1)])
     tokens = jnp.concatenate([inputs, rim, jnp.zeros((HALO - 2, chans), inputs.dtype)], axis=0)
@@ -274,7 +307,6 @@
         ),
         name="project_mixin",
     )(jnp.stack([half, here]).astype(jnp.int32), *features, in_hbm(weight))
-    pairs = [(s, mirror[s]) for s in range(blocks)]
     more = lax.ppermute(send, "seq", pairs)
     query_keep, query_send = pl.pallas_call(
         query_project_kernel,
@@ -288,16 +320,17 @@
         name="project_query",
     )(lhs, in_hbm(weight))
     taps = short_filter.reshape(9, chans)
-    mixin, begin, final = pl.pallas_call(
+    mixin, begin, final, query_send = pl.pallas_call(
         functools.partial(scan_kernel, rows, chans),
         out_shape=[
             shape((chans // LANES, rows, LANES), f32),
             shape((4, SUB, chans), f32),
             shape((4, chans), f32),
+            shape((padded, chans), b16),
         ],
         compiler_params=params,
         name="scan",
-    )(keep, more, taps, step, join)
+    )(keep, more, query_send, taps, step, join)
     query_more = lax.ppermute(query_send, "seq", pairs)
 
     states = spread(final, "seq")
@@ -309,11 +342,15 @@
         name="gate",
     )(states, jump, begin, reach, step, poles, bias[None, :], mixin, query_keep, query_more, taps)
 
-    which = jnp.stack([lax.rem(here + hop + count, count) for hop in ring_hops(count)])
-    which = which.astype(jnp.int32)
+    which = jnp.stack([lax.rem(here + hop + count, count) for hop in ring_hops(count)] + [half])
     parts = ring(gated, "ch")
-    first = mix(parts[:-1], which[:-1], second, jnp.zeros((rows, chans), f32), f32)
-    return mix(parts[-1:], which[-1:], second, first, b16)
+    first, rest = mix(parts[:-1], which.astype(jnp.int32), second, out_weight.shape[1])
+    return pl.pallas_call(
+        last_mix_kernel,
+        out_shape=shape(first.shape, b16),
+        compiler_params=params,
+        name="last_mix",
+    )(parts[-1], rest, first)
 
 
 def solution(mesh):

time: 126 us -> 127 us (level); the launches traced: 124 us -> 126 us
  other arithmetic: 5.02 us -> 7.38 us
  waiting for transfers between devices: 44.5 us -> 46 us
  local copies, waits for them, and re-layouts: 4.17 us -> 2.74 us
    all_gather x2, waiting for transfers between devices: 8.19 us -> 0.01 us  [body(): lax.all_gather(x, 'seq', axis=0, tiled=True, axis_index_groups=halves)]
    ppermute x8, waiting for transfers between devices: 21.2 us -> 26.9 us  [ring(): below = lax.ppermute(below, axis, up)]
    ppermute x1, waiting for transfers between devices: 7.52 us -> 3.45 us  [body(): more = lax.ppermute(send, 'seq', pairs)]
    ppermute x0 -> x1, waiting for transfers between devices: none -> 3.96 us  [body(): lax.ppermute(out_weight, 'seq', pairs)]
    ppermute x8, starting transfers between devices: 11.3 us -> 7.53 us  [ring(): below = lax.ppermute(below, axis, up)]
    all_to_all x1, starting transfers between devices: 8.1 us -> 11.2 us  [spread(): lax.all_to_all(jnp.broadcast_to(x[None], (count,) + x.shape), axis, 0, 0,...]
    pallas_call x2 -> x1, Pallas kernels: 4.78 us -> 2.94 us  [mix(): pl.pallas_call(functools.partial(mix_kernel, count), in_specs=[IN_SMEM] +...]
    all_to_all x1, waiting for transfers between devices: 0.01 us -> 1.82 us  [spread(): lax.all_to_all(jnp.broadcast_to(x[None], (count,) + x.shape), axis, 0, 0,...]
  transfers between devices with their start and end apart: 21 -> 22, of which waited for: 12 -> 14; matrix products, arithmetic and copies ran while one was open for 6% -> 7% of each run, Pallas kernels for 8% -> 8%
where the time goes in v5:
time: 127 us; the launch traced here: 126 us
  waiting for transfers between devices  46 us (36%)
  starting transfers between devices  45.3 us (36%)
  between operations  13.7 us (11%)
  Pallas kernels  11 us (9%)
  other arithmetic  7.38 us (6%)
  local copies, waits for them, and re-layouts  2.74 us (2%)
    ppermute x8, waiting for transfers between devices, ring(): below = lax.ppermute(below, axis, up)  26.9 us
    ppermute x6, starting transfers between devices, ring(): above = lax.ppermute(above, axis, down)  20.8 us
    all_to_all x1, starting transfers between devices, spread(): lax.all_to_all(jnp.broadcast_to(x[None], (count,) + x.shape), axis, 0, 0,...  11.2 us
    ppermute x8, starting transfers between devices, ring(): below = lax.ppermute(below, axis, up)  7.53 us
    ppermute x1, waiting for transfers between devices, body(): query_more = lax.ppermute(query_send, 'seq', pairs)  6.77 us
    ppermute x1, waiting for transfers between devices, body(): lax.ppermute(out_weight, 'seq', pairs)  3.96 us
    pallas_call x1, Pallas kernels, body(): pl.pallas_call(functools.partial(mixin_project_kernel, count), in_specs=[...  3.71 us
    ppermute x1, waiting for transfers between devices, body(): more = lax.ppermute(send, 'seq', pairs)  3.45 us
  transfers between devices with their start and end apart: 22, of which 14 were waited for; matrix products, arithmetic and copies ran while one was open for 7% of the time, Pallas kernels for 8%

profile of v5, /device:TPU:2, one launch (start us, length us, event | category | flops | bytes accessed | tf_op | source)
XLA Modules:
  0.0 126.1 jit_solution(12045048804005662085)
XLA Ops:
  6.5 1.1 dynamic-slice_bitcast_fusion.2
  7.6 0.8 pad_maximum_fusion
  8.4 0.0 all-gather.3.cloned.1.call-update
  8.4 0.0 all-gather.5.cloned.1.call-start
  8.5 1.6 %collective-permute-start.18 = (bf16[128,512]{1,0:T(8,128)(2,1)}, bf16[128,512]{1,0:T(8,128)(2,1)S(1)}, u32[]{:S(2)}, u32[]{:S(2)}) collective-permute-start(bf16[128,512]{1,0:T(8,128)(2,1)} %param.10), channel_id=1, source_target_pairs={{0,6},{1,7},{2,4},{3,5},{4,2},{5,3},{6,0},{7,1},{8,14},{9,15},{10,... | collective-permute-start | bytes 393224 | tf_op jit(solution)/shard_map/ppermute | solution.py:265
  10.0 4.0 %collective-permute-done.18 = bf16[128,512]{1,0:T(8,128)(2,1)S(1)} collective-permute-done((bf16[128,512]{1,0:T(8,128)(2,1)}, bf16[128,512]{1,0:T(8,128)(2,1)S(1)}, u32[]{:S(2)}, u32[]{:S(2)}) %collective-permute-start.18) | collective-permute-done | bytes 131104 | tf_op jit(solution)/shard_map/ppermute | solution.py:265
  14.0 1.6 %pad_maximum_fusion.1 = bf16[128,1024]{1,0:T(8,128)(2,1)} fusion(bf16[128,512]{1,0:T(8,128)(2,1)S(1)} %collective-permute-done.18, bf16[128,512]{1,0:T(8,128)(2,1)} %param.10), kind=kLoop, calls=%fused_computation.3 | loop fusion | flops 524288 | bytes 524288 | tf_op jit(solution)/shard_map/concatenate | solution.py:265
  15.6 0.0 all-gather.5.cloned.1.call-update
  15.7 0.7 slice.18
  16.4 1.9 %collective-permute-start = (bf16[2,512]{1,0:T(2,128)(2,1)S(1)}, bf16[2,512]{1,0:T(2,128)(2,1)S(1)}, u32[]{:S(2)}, u32[]{:S(2)}) collective-permute-start(bf16[2,512]{1,0:T(2,128)(2,1)S(1)} %slice.18), channel_id=1, source_target_pairs={{0,1},{1,2},{2,3},{3,4},{4,5},{5,6},{6,7},{7,8},{8,9},{9,10},{10,1... | collective-permute-start | bytes 6152 | tf_op jit(solution)/shard_map/ppermute | solution.py:268
  18.3 0.1 pad.17.clone
  18.4 2.9 %collective-permute-done = bf16[2,512]{1,0:T(2,128)(2,1)S(1)} collective-permute-done((bf16[2,512]{1,0:T(2,128)(2,1)S(1)}, bf16[2,512]{1,0:T(2,128)(2,1)S(1)}, u32[]{:S(2)}, u32[]{:S(2)}) %collective-permute-start) | collective-permute-done | bytes 2080 | tf_op jit(solution)/shard_map/ppermute | solution.py:268
  21.3 1.0 maximum_maximum_fusion
  22.2 0.7 collective-permute-start.1
  22.9 1.9 %fusion.1 = (f32[32,2,512]{2,0,1:T(8,128)S(1)}, f32[32,2,512]{2,0,1:T(8,128)}) fusion(f32[2,512]{1,0:T(2,128)} %bitcast.52, f32[32]{0:T(128)S(1)} %multiply_convert_fusion.1, f32[2,512]{1,0:T(2,128)} %bitcast.54, f32[32]{0:T(128)S(1)} %fusion.7), kind=kLoop, calls=%fused_computation.7 | loop fusion | flops 131072 | bytes 270592 | tf_op jit(solution)/shard_map/mul | solution.py:48
  24.9 0.0 collective-permute-done.1.refs_0_
  24.9 7.3 %collective-permute-start.2 = (bf16[144,512]{1,0:T(8,128)(2,1)S(1)}, bf16[144,512]{1,0:T(8,128)(2,1)S(1)}, u32[]{:S(2)}, u32[]{:S(2)}) collective-permute-start(bf16[144,512]{1,0:T(8,128)(2,1)S(1)} %collective-permute-done.1.refs_0_), channel_id=1, source_target_pairs={{0,32},{32,64},{64,96},{96,128},{128,160},{160,192},{192,224},{224... | collective-permute-start | bytes 442376 | tf_op jit(solution)/shard_map/ppermute | solution.py:37
  32.1 4.2 %collective-permute-start.3 = (bf16[144,512]{1,0:T(8,128)(2,1)S(1)}, bf16[144,512]{1,0:T(8,128)(2,1)S(1)}, u32[]{:S(2)}, u32[]{:S(2)}) collective-permute-start(bf16[144,512]{1,0:T(8,128)(2,1)S(1)} %collective-permute-done.1.refs_0_), channel_id=1, source_target_pairs={{0,224},{32,0},{64,32},{96,64},{128,96},{160,128},{192,160},{224,1... | collective-permute-start | bytes 442376 | tf_op jit(solution)/shard_map/ppermute | solution.py:40
  36.3 3.0 %collective-permute-done.2.refs_1_ = bf16[144,512]{1,0:T(8,128)(2,1)S(1)} collective-permute-done((bf16[144,512]{1,0:T(8,128)(2,1)S(1)}, bf16[144,512]{1,0:T(8,128)(2,1)S(1)}, u32[]{:S(2)}, u32[]{:S(2)}) %collective-permute-start.2) | collective-permute-done | bytes 147488 | tf_op jit(solution)/shard_map/ppermute | solution.py:37
  39.3 0.0 collective-permute-start.4
  39.4 0.8 fusion.3
  40.2 0.0 collective-permute-done.3.refs_2_
  40.2 3.2 %collective-permute-start.5 = (bf16[144,512]{1,0:T(8,128)(2,1)S(1)}, bf16[144,512]{1,0:T(8,128)(2,1)S(1)}, u32[]{:S(2)}, u32[]{:S(2)}) collective-permute-start(bf16[144,512]{1,0:T(8,128)(2,1)S(1)} %collective-permute-done.3.refs_2_), channel_id=1, source_target_pairs={{0,224},{32,0},{64,32},{96,64},{128,96},{160,128},{192,160},{224,1... | collective-permute-start | bytes 442376 | tf_op jit(solution)/shard_map/ppermute | solution.py:40
  43.4 2.3 %collective-permute-done.4.refs_3_ = bf16[144,512]{1,0:T(8,128)(2,1)S(1)} collective-permute-done((bf16[144,512]{1,0:T(8,128)(2,1)S(1)}, bf16[144,512]{1,0:T(8,128)(2,1)S(1)}, u32[]{:S(2)}, u32[]{:S(2)}) %collective-permute-start.4) | collective-permute-done | bytes 147488 | tf_op jit(solution)/shard_map/ppermute | solution.py:37
  45.7 0.0 collective-permute-start.6
  45.7 0.1 multiply_bitcast_fusion.1
  45.9 0.2 collective-permute-done.5.refs_4_
  46.1 3.7 %collective-permute-start.7 = (bf16[144,512]{1,0:T(8,128)(2,1)S(1)}, bf16[144,512]{1,0:T(8,128)(2,1)S(1)}, u32[]{:S(2)}, u32[]{:S(2)}) collective-permute-start(bf16[144,512]{1,0:T(8,128)(2,1)S(1)} %collective-permute-done.5.refs_4_), channel_id=1, source_target_pairs={{0,224},{32,0},{64,32},{96,64},{128,96},{160,128},{192,160},{224,1... | collective-permute-start | bytes 442376 | tf_op jit(solution)/shard_map/ppermute | solution.py:40
  49.7 3.0 %collective-permute-done.6.refs_5_ = bf16[144,512]{1,0:T(8,128)(2,1)S(1)} collective-permute-done((bf16[144,512]{1,0:T(8,128)(2,1)S(1)}, bf16[144,512]{1,0:T(8,128)(2,1)S(1)}, u32[]{:S(2)}, u32[]{:S(2)}) %collective-permute-start.6) | collective-permute-done | bytes 147488 | tf_op jit(solution)/shard_map/ppermute | solution.py:37
  52.8 0.0 collective-permute-start.8
  52.8 0.1 pad_add_fusion.place_ref
  52.9 0.0 collective-permute-done.7.refs_6_
  52.9 6.2 %collective-permute-done.8.refs_7_ = bf16[144,512]{1,0:T(8,128)(2,1)S(1)} collective-permute-done((bf16[144,512]{1,0:T(8,128)(2,1)S(1)}, bf16[144,512]{1,0:T(8,128)(2,1)S(1)}, u32[]{:S(2)}, u32[]{:S(2)}) %collective-permute-start.8) | collective-permute-done | bytes 147488 | tf_op jit(solution)/shard_map/ppermute | solution.py:37
  59.1 3.7 %project_mixin.1 = (f32[144,1024]{1,0:T(8,128)S(1)}, bf16[144,1024]{1,0:T(8,128)(2,1)S(1)}, bf16[2,144,2048]{2,1,0:T(8,128)(2,1)S(1)}) custom-call(s32[2]{0:T(128)S(1)} %pad_add_fusion.place_ref, bf16[144,512]{1,0:T(8,128)(2,1)S(1)} %collective-permute-done.1.refs_0_, bf16[144,512]{1,0:T(8,128)(2,1)S(1)} %collective-permute-done.2.refs_1_, ...), custom_call_target="tpu_custom_call" | custom-call | flops 1207959552 | bytes 4194304 | tf_op jit(solution)/shard_map/project_mixin/pallas_call | solution.py:295
  62.8 0.1 collective-permute-start.9
  63.0 1.0 fusion.jump_ref
  64.0 0.0 copy-start.5
  64.0 0.0 copy-start
  64.0 2.4 %project_query.1 = (f32[144,512]{1,0:T(8,128)S(1)}, bf16[144,512]{1,0:T(8,128)(2,1)S(1)}) custom-call(bf16[2,144,2048]{2,1,0:T(8,128)(2,1)S(1)} %get-tuple-element.18.lhs_ref, bf16[2048,1536]{1,0:T(8,128)(2,1)} %all-gather.3.cloned.1.call-done.refs_8_.w_ref), custom_call_target="tpu_custom_call" | custom-call | flops 603979776 | bytes 2097152 | tf_op jit(solution)/shard_map/project_query/pallas_call | solution.py:311
  66.4 3.5 %collective-permute-done.9.more_ref = bf16[144,1024]{1,0:T(8,128)(2,1)S(1)} collective-permute-done((bf16[144,1024]{1,0:T(8,128)(2,1)S(1)}, bf16[144,1024]{1,0:T(8,128)(2,1)S(1)}, u32[]{:S(2)}, u32[]{:S(2)}) %collective-permute-start.9) | collective-permute-done | bytes 294944 | tf_op jit(solution)/shard_map/ppermute | solution.py:310
  69.9 0.5 scan.1
  70.4 0.7 broadcast_in_dim.15
  71.2 11.2 %all-to-all-start = ((f32[32,4,512]{2,1,0:T(4,128)}), f32[32,4,512]{2,1,0:T(4,128)S(1)}, u32[]{:S(2)}, u32[]{:S(2)}) async-start(f32[32,4,512]{2,1,0:T(4,128)} %broadcast_in_dim.15), calls=%async_computation | async-start | bytes 524288 | tf_op jit(solution)/shard_map/all_to_all | solution.py:18
  82.4 1.6 %collective-permute-start.10 = (bf16[144,512]{1,0:T(8,128)(2,1)S(1)}, bf16[144,512]{1,0:T(8,128)(2,1)S(1)}, u32[]{:S(2)}, u32[]{:S(2)}) collective-permute-start(bf16[144,512]{1,0:T(8,128)(2,1)S(1)} %get-tuple-element.24), channel_id=1, source_target_pairs={{0,6},{1,7},{2,4},{3,5},{4,2},{5,3},{6,0},{7,1},{8,14},{9,15},{10,... | collective-permute-start | bytes 442376 | tf_op jit(solution)/shard_map/ppermute | solution.py:334
  83.9 6.8 %collective-permute-done.10.more_ref = bf16[144,512]{1,0:T(8,128)(2,1)S(1)} collective-permute-done((bf16[144,512]{1,0:T(8,128)(2,1)S(1)}, bf16[144,512]{1,0:T(8,128)(2,1)S(1)}, u32[]{:S(2)}, u32[]{:S(2)}) %collective-permute-start.10) | collective-permute-done | bytes 147488 | tf_op jit(solution)/shard_map/ppermute | solution.py:334
  90.7 1.8 %all-to-all-done.all_ref = f32[32,4,512]{2,1,0:T(4,128)S(1)} async-done(((f32[32,4,512]{2,1,0:T(4,128)}), f32[32,4,512]{2,1,0:T(4,128)S(1)}, u32[]{:S(2)}, u32[]{:S(2)}) %all-to-all-start) | async-done | bytes 262176 | tf_op jit(solution)/shard_map/all_to_all | solution.py:18
  92.5 0.5 gate.1.refs_0_
  93.1 0.3 collective-permute-start.11
  93.3 3.2 %collective-permute-start.15 = (bf16[128,512]{1,0:T(8,128)(2,1)S(1)}, bf16[128,512]{1,0:T(8,128)(2,1)S(1)}, u32[]{:S(2)}, u32[]{:S(2)}) collective-permute-start(bf16[128,512]{1,0:T(8,128)(2,1)S(1)} %gate.1.refs_0_), channel_id=1, source_target_pairs={{0,224},{32,0},{64,32},{96,64},{128,96},{160,128},{192,160},{224,1... | collective-permute-start | bytes 393224 | tf_op jit(solution)/shard_map/ppermute | solution.py:40
  96.6 2.9 %collective-permute-done.11.refs_1_ = bf16[128,512]{1,0:T(8,128)(2,1)S(1)} collective-permute-done((bf16[128,512]{1,0:T(8,128)(2,1)S(1)}, bf16[128,512]{1,0:T(8,128)(2,1)S(1)}, u32[]{:S(2)}, u32[]{:S(2)}) %collective-permute-start.11) | collective-permute-done | bytes 131104 | tf_op jit(solution)/shard_map/ppermute | solution.py:37
  99.5 0.0 collective-permute-start.12
  99.5 0.0 collective-permute-done.15.refs_2_
  99.5 3.2 %collective-permute-start.16 = (bf16[128,512]{1,0:T(8,128)(2,1)S(1)}, bf16[128,512]{1,0:T(8,128)(2,1)S(1)}, u32[]{:S(2)}, u32[]{:S(2)}) collective-permute-start(bf16[128,512]{1,0:T(8,128)(2,1)S(1)} %collective-permute-done.15.refs_2_), channel_id=1, source_target_pairs={{0,224},{32,0},{64,32},{96,64},{128,96},{160,128},{192,160},{224,1... | collective-permute-start | bytes 393224 | tf_op jit(solution)/shard_map/ppermute | solution.py:40
  102.7 2.9 %collective-permute-done.12.refs_3_ = bf16[128,512]{1,0:T(8,128)(2,1)S(1)} collective-permute-done((bf16[128,512]{1,0:T(8,128)(2,1)S(1)}, bf16[128,512]{1,0:T(8,128)(2,1)S(1)}, u32[]{:S(2)}, u32[]{:S(2)}) %collective-permute-start.12) | collective-permute-done | bytes 131104 | tf_op jit(solution)/shard_map/ppermute | solution.py:37
  105.7 0.0 collective-permute-start.13
  105.7 0.0 collective-permute-done.16.refs_4_
  105.7 3.2 %collective-permute-start.17 = (bf16[128,512]{1,0:T(8,128)(2,1)S(1)}, bf16[128,512]{1,0:T(8,128)(2,1)S(1)}, u32[]{:S(2)}, u32[]{:S(2)}) collective-permute-start(bf16[128,512]{1,0:T(8,128)(2,1)S(1)} %collective-permute-done.16.refs_4_), channel_id=1, source_target_pairs={{0,224},{32,0},{64,32},{96,64},{128,96},{160,128},{192,160},{224,1... | collective-permute-start | bytes 393224 | tf_op jit(solution)/shard_map/ppermute | solution.py:40
  108.9 3.3 %collective-permute-done.13.refs_5_ = bf16[128,512]{1,0:T(8,128)(2,1)S(1)} collective-permute-done((bf16[128,512]{1,0:T(8,128)(2,1)S(1)}, bf16[128,512]{1,0:T(8,128)(2,1)S(1)}, u32[]{:S(2)}, u32[]{:S(2)}) %collective-permute-start.13) | collective-permute-done | bytes 131104 | tf_op jit(solution)/shard_map/ppermute | solution.py:37
  112.2 0.0 collective-permute-start.14
  112.2 0.1 stack.48.which_ref
  112.3 0.0 collective-permute-done.17.refs_6_
  112.3 2.9 %mix.1 = (f32[128,512]{1,0:T(8,128)S(1)}, bf16[512,512]{1,0:T(8,128)(2,1)S(1)}) custom-call(s32[9]{0:T(128)S(1)} %stack.48.which_ref, bf16[128,512]{1,0:T(8,128)(2,1)S(1)} %gate.1.refs_0_, bf16[128,512]{1,0:T(8,128)(2,1)S(1)} %collective-permute-done.11.refs_1_, bf16[128,512]{1,0:T(8,128)(2,1)S(1)} %collective-permute-done.15.refs_2_, ...), custom_call_target="tpu_custom_call" | custom-call | flops 536870912 | bytes 4194304 | tf_op jit(solution)/shard_map/mix/pallas_call | solution.py:231
  115.2 3.1 %collective-permute-done.14.x_ref = bf16[128,512]{1,0:T(8,128)(2,1)S(1)} collective-permute-done((bf16[128,512]{1,0:T(8,128)(2,1)S(1)}, bf16[128,512]{1,0:T(8,128)(2,1)S(1)}, u32[]{:S(2)}, u32[]{:S(2)}) %collective-permute-start.14) | collective-permute-done | bytes 131104 | tf_op jit(solution)/shard_map/ppermute | solution.py:37
  118.4 0.9 last_mix.1
  (25 shorter events, 0.1 us)
Async XLA Ops:
  6.5 32.8 %copy-start.3 = (f32[512,2]{0,1:T(2,128)S(1)}, f32[512,2]{0,1:T(2,128)}, u32[]{:S(2)}) copy-start(f32[512,2]{0,1:T(2,128)} %param.12) | copy-start | bytes 12292
  6.5 32.8 %copy-start.2 = (f32[512,2]{0,1:T(2,128)S(1)}, f32[512,2]{0,1:T(2,128)}, u32[]{:S(2)}) copy-start(f32[512,2]{0,1:T(2,128)} %param.13) | copy-start | bytes 12292
  6.5 52.6 %all-gather.3.cloned.1.call-start = ((), (), s32[]{:S(2)}) async-start(), calls=%async_computation.1 | async-start | bytes 6684672 | tf_op jit(solution)/shard_map/all_gather | solution.py:263
  8.4 103.8 %all-gather.5.cloned.1.call-start = ((), (), s32[]{:S(2)}) async-start(), calls=%async_computation.2 | async-start | bytes 4456448 | tf_op jit(solution)/shard_map/all_gather | solution.py:263
  8.5 5.5 %collective-permute-start.18 = (bf16[128,512]{1,0:T(8,128)(2,1)}, bf16[128,512]{1,0:T(8,128)(2,1)S(1)}, u32[]{:S(2)}, u32[]{:S(2)}) collective-permute-start(bf16[128,512]{1,0:T(8,128)(2,1)} %param.10), channel_id=1, source_target_pairs={{0,6},{1,7},{2,4},{3,5},{4,2},{5,3},{6,0},{7,1},{8,14},{9,15},{10,... | collective-permute-start | bytes 393224 | tf_op jit(solution)/shard_map/ppermute | solution.py:265
  16.4 4.9 %collective-permute-start = (bf16[2,512]{1,0:T(2,128)(2,1)S(1)}, bf16[2,512]{1,0:T(2,128)(2,1)S(1)}, u32[]{:S(2)}, u32[]{:S(2)}) collective-permute-start(bf16[2,512]{1,0:T(2,128)(2,1)S(1)} %slice.18), channel_id=1, source_target_pairs={{0,1},{1,2},{2,3},{3,4},{4,5},{5,6},{6,7},{7,8},{8,9},{9,10},{10,1... | collective-permute-start | bytes 6152 | tf_op jit(solution)/shard_map/ppermute | solution.py:268
  22.2 2.6 %collective-permute-start.1 = (bf16[144,512]{1,0:T(8,128)(2,1)S(1)}, bf16[144,512]{1,0:T(8,128)(2,1)S(1)}, u32[]{:S(2)}, u32[]{:S(2)}) collective-permute-start(bf16[144,512]{1,0:T(8,128)(2,1)S(1)} %maximum_maximum_fusion), channel_id=1, source_target_pairs={{0,0},{1,1},{2,2},{3,3},{4,34},{5,35},{6,32},{7,33},{8,8},{9,9},{1... | collective-permute-start | bytes 442376 | tf_op jit(solution)/shard_map/ppermute | solution.py:275
  24.9 14.5 %collective-permute-start.2 = (bf16[144,512]{1,0:T(8,128)(2,1)S(1)}, bf16[144,512]{1,0:T(8,128)(2,1)S(1)}, u32[]{:S(2)}, u32[]{:S(2)}) collective-permute-start(bf16[144,512]{1,0:T(8,128)(2,1)S(1)} %collective-permute-done.1.refs_0_), channel_id=1, source_target_pairs={{0,32},{32,64},{64,96},{96,128},{128,160},{160,192},{192,224},{224... | collective-permute-start | bytes 442376 | tf_op jit(solution)/shard_map/ppermute | solution.py:37
  32.1 8.1 %collective-permute-start.3 = (bf16[144,512]{1,0:T(8,128)(2,1)S(1)}, bf16[144,512]{1,0:T(8,128)(2,1)S(1)}, u32[]{:S(2)}, u32[]{:S(2)}) collective-permute-start(bf16[144,512]{1,0:T(8,128)(2,1)S(1)} %collective-permute-done.1.refs_0_), channel_id=1, source_target_pairs={{0,224},{32,0},{64,32},{96,64},{128,96},{160,128},{192,160},{224,1... | collective-permute-start | bytes 442376 | tf_op jit(solution)/shard_map/ppermute | solution.py:40
  39.3 6.4 %collective-permute-start.4 = (bf16[144,512]{1,0:T(8,128)(2,1)S(1)}, bf16[144,512]{1,0:T(8,128)(2,1)S(1)}, u32[]{:S(2)}, u32[]{:S(2)}) collective-permute-start(bf16[144,512]{1,0:T(8,128)(2,1)S(1)} %collective-permute-done.2.refs_1_), channel_id=1, source_target_pairs={{0,32},{32,64},{64,96},{96,128},{128,160},{160,192},{192,224},{224... | collective-permute-start | bytes 442376 | tf_op jit(solution)/shard_map/ppermute | solution.py:37
  40.2 5.9 %collective-permute-start.5 = (bf16[144,512]{1,0:T(8,128)(2,1)S(1)}, bf16[144,512]{1,0:T(8,128)(2,1)S(1)}, u32[]{:S(2)}, u32[]{:S(2)}) collective-permute-start(bf16[144,512]{1,0:T(8,128)(2,1)S(1)} %collective-permute-done.3.refs_2_), channel_id=1, source_target_pairs={{0,224},{32,0},{64,32},{96,64},{128,96},{160,128},{192,160},{224,1... | collective-permute-start | bytes 442376 | tf_op jit(solution)/shard_map/ppermute | solution.py:40
  45.7 7.1 %collective-permute-start.6 = (bf16[144,512]{1,0:T(8,128)(2,1)S(1)}, bf16[144,512]{1,0:T(8,128)(2,1)S(1)}, u32[]{:S(2)}, u32[]{:S(2)}) collective-permute-start(bf16[144,512]{1,0:T(8,128)(2,1)S(1)} %collective-permute-done.4.refs_3_), channel_id=1, source_target_pairs={{0,32},{32,64},{64,96},{96,128},{128,160},{160,192},{192,224},{224... | collective-permute-start | bytes 442376 | tf_op jit(solution)/shard_map/ppermute | solution.py:37
  46.1 6.8 %collective-permute-start.7 = (bf16[144,512]{1,0:T(8,128)(2,1)S(1)}, bf16[144,512]{1,0:T(8,128)(2,1)S(1)}, u32[]{:S(2)}, u32[]{:S(2)}) collective-permute-start(bf16[144,512]{1,0:T(8,128)(2,1)S(1)} %collective-permute-done.5.refs_4_), channel_id=1, source_target_pairs={{0,224},{32,0},{64,32},{96,64},{128,96},{160,128},{192,160},{224,1... | collective-permute-start | bytes 442376 | tf_op jit(solution)/shard_map/ppermute | solution.py:40
  52.8 6.4 %collective-permute-start.8 = (bf16[144,512]{1,0:T(8,128)(2,1)S(1)}, bf16[144,512]{1,0:T(8,128)(2,1)S(1)}, u32[]{:S(2)}, u32[]{:S(2)}) collective-permute-start(bf16[144,512]{1,0:T(8,128)(2,1)S(1)} %collective-permute-done.6.refs_5_), channel_id=1, source_target_pairs={{0,32},{32,64},{64,96},{96,128},{128,160},{160,192},{192,224},{224... | collective-permute-start | bytes 442376 | tf_op jit(solution)/shard_map/ppermute | solution.py:37
  52.9 10.1 %copy-start.4 = (f32[3,3,512]{2,1,0:T(4,128)S(1)}, f32[3,3,512]{2,1,0:T(4,128)}, u32[]{:S(2)}) copy-start(f32[3,3,512]{2,1,0:T(4,128)} %param.11) | copy-start | bytes 55300
  62.8 7.0 %collective-permute-start.9 = (bf16[144,1024]{1,0:T(8,128)(2,1)S(1)}, bf16[144,1024]{1,0:T(8,128)(2,1)S(1)}, u32[]{:S(2)}, u32[]{:S(2)}) collective-permute-start(bf16[144,1024]{1,0:T(8,128)(2,1)S(1)} %get-tuple-element.17), channel_id=1, source_target_pairs={{0,6},{1,7},{2,4},{3,5},{4,2},{5,3},{6,0},{7,1},{8,14},{9,15},{10,... | collective-permute-start | bytes 884744 | tf_op jit(solution)/shard_map/ppermute | solution.py:310
  64.0 18.4 %copy-start.5 = (f32[2,512,2]{1,2,0:T(2,128)S(1)}, f32[2,512,2]{1,2,0:T(2,128)}, u32[]{:S(2)}) copy-start(f32[2,512,2]{1,2,0:T(2,128)} %param.14) | copy-start | bytes 24580
  64.0 19.9 %copy-start.1 = (f32[8,2,512]{2,0,1:T(8,128)S(1)}, f32[8,2,512]{2,0,1:T(8,128)}, u32[]{:S(2)}) copy-start(f32[8,2,512]{2,0,1:T(8,128)} %get-tuple-element.31) | copy-start | bytes 98308
  64.0 28.5 %copy-start = (f32[512]{0:T(512)S(1)}, f32[512]{0:T(512)}, u32[]{:S(2)}) copy-start(f32[512]{0:T(512)} %param.15) | copy-start | bytes 6148
  71.2 21.4 %all-to-all-start = ((f32[32,4,512]{2,1,0:T(4,128)}), f32[32,4,512]{2,1,0:T(4,128)S(1)}, u32[]{:S(2)}, u32[]{:S(2)}) async-start(f32[32,4,512]{2,1,0:T(4,128)} %broadcast_in_dim.15), calls=%async_computation | async-start | bytes 524288 | tf_op jit(solution)/shard_map/all_to_all | solution.py:18
  82.4 8.3 %collective-permute-start.10 = (bf16[144,512]{1,0:T(8,128)(2,1)S(1)}, bf16[144,512]{1,0:T(8,128)(2,1)S(1)}, u32[]{:S(2)}, u32[]{:S(2)}) collective-permute-start(bf16[144,512]{1,0:T(8,128)(2,1)S(1)} %get-tuple-element.24), channel_id=1, source_target_pairs={{0,6},{1,7},{2,4},{3,5},{4,2},{5,3},{6,0},{7,1},{8,14},{9,15},{10,... | collective-permute-start | bytes 442376 | tf_op jit(solution)/shard_map/ppermute | solution.py:334
  93.1 6.4 %collective-permute-start.11 = (bf16[128,512]{1,0:T(8,128)(2,1)S(1)}, bf16[128,512]{1,0:T(8,128)(2,1)S(1)}, u32[]{:S(2)}, u32[]{:S(2)}) collective-permute-start(bf16[128,512]{1,0:T(8,128)(2,1)S(1)} %gate.1.refs_0_), channel_id=1, source_target_pairs={{0,32},{32,64},{64,96},{96,128},{128,160},{160,192},{192,224},{224... | collective-permute-start | bytes 393224 | tf_op jit(solution)/shard_map/ppermute | solution.py:37
  93.3 6.2 %collective-permute-start.15 = (bf16[128,512]{1,0:T(8,128)(2,1)S(1)}, bf16[128,512]{1,0:T(8,128)(2,1)S(1)}, u32[]{:S(2)}, u32[]{:S(2)}) collective-permute-start(bf16[128,512]{1,0:T(8,128)(2,1)S(1)} %gate.1.refs_0_), channel_id=1, source_target_pairs={{0,224},{32,0},{64,32},{96,64},{128,96},{160,128},{192,160},{224,1... | collective-permute-start | bytes 393224 | tf_op jit(solution)/shard_map/ppermute | solution.py:40
  99.5 6.2 %collective-permute-start.12 = (bf16[128,512]{1,0:T(8,128)(2,1)S(1)}, bf16[128,512]{1,0:T(8,128)(2,1)S(1)}, u32[]{:S(2)}, u32[]{:S(2)}) collective-permute-start(bf16[128,512]{1,0:T(8,128)(2,1)S(1)} %collective-permute-done.11.refs_1_), channel_id=1, source_target_pairs={{0,32},{32,64},{64,96},{96,128},{128,160},{160,192},{192,224},{224... | collective-permute-start | bytes 393224 | tf_op jit(solution)/shard_map/ppermute | solution.py:37
  99.5 6.2 %collective-permute-start.16 = (bf16[128,512]{1,0:T(8,128)(2,1)S(1)}, bf16[128,512]{1,0:T(8,128)(2,1)S(1)}, u32[]{:S(2)}, u32[]{:S(2)}) collective-permute-start(bf16[128,512]{1,0:T(8,128)(2,1)S(1)} %collective-permute-done.15.refs_2_), channel_id=1, source_target_pairs={{0,224},{32,0},{64,32},{96,64},{128,96},{160,128},{192,160},{224,1... | collective-permute-start | bytes 393224 | tf_op jit(solution)/shard_map/ppermute | solution.py:40
  105.7 6.5 %collective-permute-start.13 = (bf16[128,512]{1,0:T(8,128)(2,1)S(1)}, bf16[128,512]{1,0:T(8,128)(2,1)S(1)}, u32[]{:S(2)}, u32[]{:S(2)}) collective-permute-start(bf16[128,512]{1,0:T(8,128)(2,1)S(1)} %collective-permute-done.12.refs_3_), channel_id=1, source_target_pairs={{0,32},{32,64},{64,96},{96,128},{128,160},{160,192},{192,224},{224... | collective-permute-start | bytes 393224 | tf_op jit(solution)/shard_map/ppermute | solution.py:37
  105.7 6.6 %collective-permute-start.17 = (bf16[128,512]{1,0:T(8,128)(2,1)S(1)}, bf16[128,512]{1,0:T(8,128)(2,1)S(1)}, u32[]{:S(2)}, u32[]{:S(2)}) collective-permute-start(bf16[128,512]{1,0:T(8,128)(2,1)S(1)} %collective-permute-done.16.refs_4_), channel_id=1, source_target_pairs={{0,224},{32,0},{64,32},{96,64},{128,96},{160,128},{192,160},{224,1... | collective-permute-start | bytes 393224 | tf_op jit(solution)/shard_map/ppermute | solution.py:40
  112.2 6.2 %collective-permute-start.14 = (bf16[128,512]{1,0:T(8,128)(2,1)S(1)}, bf16[128,512]{1,0:T(8,128)(2,1)S(1)}, u32[]{:S(2)}, u32[]{:S(2)}) collective-permute-start(bf16[128,512]{1,0:T(8,128)(2,1)S(1)} %collective-permute-done.13.refs_5_), channel_id=1, source_target_pairs={{0,32},{32,64},{64,96},{96,128},{128,160},{160,192},{192,224},{224... | collective-permute-start | bytes 393224 | tf_op jit(solution)/shard_map/ppermute | solution.py:37
Sparse Core Ops, SparseCore 0:
  9.2 47.6 all-gather.2
  58.8 43.2 all-gather.4

commit v6 on v5

--- a/solution.py
+++ b/solution.py
@@ -11,13 +11,6 @@
 LANES = 128
 SUB = 8
 VMEM = 24 * 1024 * 1024
-
-
-def spread(x, axis):
-    count = lax.axis_size(axis)
-    return lax.all_to_all(
-        jnp.broadcast_to(x[None], (count,) + x.shape), axis, 0, 0, tiled=True
-    )
 
 
 def ring_hops(count):
@@ -48,45 +41,45 @@
     return mag * jnp.cos(phase), mag * jnp.sin(phase)
 
 
-def fetch(w_ref, w, sems, starts, sizes):
+def product(lhs_ref, w, cols, keep_ref, send_ref, out):
+    sides, rows, depth = lhs_ref.shape
+    part = jnp.dot(
+        lhs_ref[...].reshape(sides * rows, depth), w[:, cols], preferred_element_type=jnp.float32
+    )
+    keep_ref[:, out] = part[:rows]
+    send_ref[:, out] = part[rows:].astype(send_ref.dtype)
+
+
+def mixin_project_kernel(count, place_ref, *refs):
+    x_refs, (w_ref, keep_ref, send_ref, lhs_ref, rest_ref, w, sems) = refs[:count], refs[count:]
+    chans = x_refs[0].shape[1]
     copies = []
-    for j, (start, size) in enumerate(zip(starts, sizes)):
-        at = sum(sizes[:j])
-        copies.append(
-            pltpu.make_async_copy(w_ref.at[:, pl.ds(start, size)], w.at[:, pl.ds(at, size)], sems.at[j])
-        )
+    for j, branch in enumerate((1, 2, 0)):
+        cols = slice(j * chans, (j + 1) * chans)
+        dst = w.at[:, cols] if branch else rest_ref
+        src = w_ref.at[:, pl.ds(branch * chans, chans)]
+        copies.append(pltpu.make_async_copy(src, dst, sems.at[j]))
         copies[-1].start()
-    return copies
-
-
-def product(lhs_ref, w, copies, chans, keep_ref, send_ref):
-    sides, rows, depth = lhs_ref.shape
-    both = lhs_ref[...].reshape(sides * rows, depth)
-    for j, copy in enumerate(copies):
-        copy.wait()
-        cols = slice(j * chans, (j + 1) * chans)
-        part = jnp.dot(both, w[:, cols], preferred_element_type=jnp.float32)
-        keep_ref[:, cols] = part[:rows]
-        send_ref[:, cols] = part[rows:].astype(send_ref.dtype)
-
-
-def mixin_project_kernel(count, place_ref, *refs):
-    x_refs, (w_ref, keep_ref, send_ref, lhs_ref, w, sems) = refs[:count], refs[count:]
-    chans = x_refs[0].shape[1]
-    copies = fetch(w_ref, w, sems, (chans, 2 * chans), (chans, chans))
     half, here = place_ref[0], place_ref[1]
     for x_ref, hop in zip(x_refs, ring_hops(count)):
         origin = lax.rem(here + hop + count, count)
         side = jnp.where(lax.rem(origin, 2) == half, 0, 1)
         at = pl.multiple_of(lax.div(origin, 2) * chans, chans)
         lhs_ref[side, :, pl.ds(at, chans)] = x_ref[...]
-    product(lhs_ref, w, copies, chans, keep_ref, send_ref)
-
-
-def query_project_kernel(lhs_ref, w_ref, keep_ref, send_ref, w, sems):
-    chans = keep_ref.shape[1]
-    copies = fetch(w_ref, w, sems, (0,), (chans,))
-    product(lhs_ref, w, copies, chans, keep_ref, send_ref)
+    for j in range(2):
+        cols = slice(j * chans, (j + 1) * chans)
+        copies[j].wait()
+        product(lhs_ref, w, cols, keep_ref, send_ref, cols)
+    copies[2].wait()
+
+
+def query_project_kernel(lhs_ref, w_ref, keep_ref, send_ref):
+    cols = slice(0, w_ref.shape[1])
+    product(lhs_ref, w_ref, cols, keep_ref, send_ref, cols)
+
+
+def after_kernel(x_ref, done_ref, also_ref, out_ref):
+    out_ref[...] = x_ref[...]
 
 
 def short_conv(rows, branch, total, taps_ref):
@@ -103,16 +96,18 @@
     chans,
     keep_ref,
     more_ref,
-    query_ref,
+    query_keep_ref,
+    query_more_ref,
     taps_ref,
     step_ref,
     join_ref,
     mixin_ref,
+    query_ref,
     begin_ref,
     final_ref,
-    send_ref,
 ):
-    send_ref[...] = query_ref[...]
+    query = query_keep_ref[...] + query_more_ref[...].astype(jnp.float32)
+    query_ref[...] = short_conv(rows, 0, query, taps_ref)
     length = rows // SUB
 
     def filtered(branch):
@@ -146,14 +141,14 @@
                     jr * er - ji * ei + re[n][b : b + 1],
                     jr * ei + ji * er + im[n][b : b + 1],
                 )
-            final_ref[n : n + 1, cols] = er
-            final_ref[2 + n : 3 + n, cols] = ei
+            for copy in range(final_ref.shape[0]):
+                final_ref[copy, n : n + 1, cols] = er
+                final_ref[copy, 2 + n : 3 + n, cols] = ei
 
 
 def gate_kernel(
-    rows, chans, all_ref, jump_ref, begin_ref, reach_ref, step_ref, residue_ref, bias_ref, mixin_ref, keep_ref, more_ref, taps_ref, out_ref, long
+    rows, chans, all_ref, jump_ref, begin_ref, reach_ref, step_ref, residue_ref, bias_ref, mixin_ref, query_ref, out_ref, long
 ):
-    query = short_conv(rows, 0, keep_ref[...] + more_ref[...].astype(jnp.float32), taps_ref)
     length = rows // SUB
     entry = []
     for n in range(2):
@@ -180,7 +175,7 @@
                 re[n], im[n] = ar[n] * re[n] - ai[n] * im[n] + u, ar[n] * im[n] + ai[n] * re[n]
                 y = y + (pr[n] * re[n] - pi[n] * im[n])
             long[q, pl.ds(i, SUB, stride=length), :] = y
-        out_ref[:, cols] = (query[:, cols] * long[q]).astype(out_ref.dtype)
+        out_ref[:, cols] = (query_ref[:, cols] * long[q]).astype(out_ref.dtype)
 
 
 def mix_kernel(count, which_ref, *refs):
@@ -262,9 +257,6 @@
     halves = [[s for s in range(blocks) if near[s] == h] for h in range(2)]
     gather = lambda x: lax.all_gather(x, "seq", axis=0, tiled=True, axis_index_groups=halves)
     weight = gather(own_weight)
-    both = jnp.concatenate([out_weight, lax.ppermute(out_weight, "seq", pairs)], axis=1)
-    second = gather(both)
-
     rim = lax.ppermute(inputs[-2:], "seq", [(i, i + 1) for i in range(blocks - 1)])
     tokens = jnp.concatenate([inputs, rim, jnp.zeros((HALO - 2, chans), inputs.dtype)], axis=0)
     swaps = []
@@ -292,55 +284,61 @@
     params = pltpu.CompilerParams(vmem_limit_bytes=VMEM)
     shape = jax.ShapeDtypeStruct
     half = lax.rem(place, 8) // 4
-    keep, send, lhs = pl.pallas_call(
+    held = pl.pallas_call(
+        after_kernel,
+        in_specs=[IN_VMEM] * 3,
+        out_shape=shape(out_weight.shape, b16),
+        compiler_params=params,
+        name="after",
+    )(out_weight, features[-2], features[-1])
+    second = gather(jnp.concatenate([out_weight, lax.ppermute(held, "seq", pairs)], axis=1))
+    cost = lambda width: pl.CostEstimate(
+        flops=4 * padded * depth * width, bytes_accessed=2 * depth * width, transcendentals=0
+    )
+    keep, send, lhs, query_weight = pl.pallas_call(
         functools.partial(mixin_project_kernel, count),
         in_specs=[IN_SMEM] + [IN_VMEM] * count + [IN_HBM],
         out_shape=[
             shape((padded, 2 * chans), f32),
             shape((padded, 2 * chans), b16),
             shape((2, padded, depth), b16),
+            shape((depth, chans), b16),
         ],
-        scratch_shapes=[pltpu.VMEM((depth, 2 * chans), b16), pltpu.SemaphoreType.DMA((2,))],
-        compiler_params=params,
-        cost_estimate=pl.CostEstimate(
-            flops=8 * padded * depth * chans, bytes_accessed=4 * depth * chans, transcendentals=0
-        ),
+        scratch_shapes=[pltpu.VMEM((depth, 2 * chans), b16), pltpu.SemaphoreType.DMA((3,))],
+        compiler_params=params,
+        cost_estimate=cost(2 * chans),
         name="project_mixin",
     )(jnp.stack([half, here]).astype(jnp.int32), *features, in_hbm(weight))
     more = lax.ppermute(send, "seq", pairs)
     query_keep, query_send = pl.pallas_call(
         query_project_kernel,
-        in_specs=[IN_VMEM, IN_HBM],
         out_shape=[shape((padded, chans), f32), shape((padded, chans), b16)],
-        scratch_shapes=[pltpu.VMEM((depth, chans), b16), pltpu.SemaphoreType.DMA((1,))],
-        compiler_params=params,
-        cost_estimate=pl.CostEstimate(
-            flops=4 * padded * depth * chans, bytes_accessed=2 * depth * chans, transcendentals=0
-        ),
+        compiler_params=params,
+        cost_estimate=cost(chans),
         name="project_query",
-    )(lhs, in_hbm(weight))
+    )(lhs, query_weight)
+    query_more = lax.ppermute(query_send, "seq", pairs)
     taps = short_filter.reshape(9, chans)
-    mixin, begin, final, query_send = pl.pallas_call(
+    mixin, query, begin, final = pl.pallas_call(
         functools.partial(scan_kernel, rows, chans),
         out_shape=[
             shape((chans // LANES, rows, LANES), f32),
+            shape((rows, chans), f32),
             shape((4, SUB, chans), f32),
-            shape((4, chans), f32),
-            shape((padded, chans), b16),
+            shape((blocks, 4, chans), f32),
         ],
         compiler_params=params,
         name="scan",
-    )(keep, more, query_send, taps, step, join)
-    query_more = lax.ppermute(query_send, "seq", pairs)
-
-    states = spread(final, "seq")
+    )(keep, more, query_keep, query_more, taps, step, join)
+
+    states = lax.all_to_all(final, "seq", 0, 0, tiled=True)
     gated = pl.pallas_call(
         functools.partial(gate_kernel, rows, chans),
         out_shape=shape((rows, chans), b16),
         scratch_shapes=[pltpu.VMEM((chans // LANES, rows, LANES), f32)],
         compiler_params=params,
         name="gate",
-    )(states, jump, begin, reach, step, poles, bias[None, :], mixin, query_keep, query_more, taps)
+    )(states, jump, begin, reach, step, poles, bias[None, :], mixin, query)
 
     which = jnp.stack([lax.rem(here + hop + count, count) for hop in ring_hops(count)] + [half])
     parts = ring(gated, "ch")

time: 127 us -> 131 us (1.031)
  waiting for transfers between devices: 46 us -> 53.4 us
  other arithmetic: 7.38 us -> 3.61 us
    all_to_all x1, waiting for transfers between devices: 1.82 us -> 10.4 us  [body(): states = lax.all_to_all(final, 'seq', 0, 0, tiled=True)]
    ppermute x1, waiting for transfers between devices: 3.45 us -> 0.01 us  [body(): more = lax.ppermute(send, 'seq', pairs)]
    ppermute x8, starting transfers between devices: 7.53 us -> 9.62 us  [ring(): below = lax.ppermute(below, axis, up)]
    ppermute x8, waiting for transfers between devices: 26.9 us -> 28.9 us  [ring(): below = lax.ppermute(below, axis, up)]
    mul x3, other arithmetic: 2.86 us -> 0.9 us  [powers(): return (mag * jnp.cos(phase), mag * jnp.sin(phase))]
    pallas_call x1 -> x2, Pallas kernels: 2.39 us -> 0.8 us  [the longest x1 0.79 us: body(): pl.pallas_call(query_project_kernel, out_shape=[shape((padded, chans), f3...]
    ppermute x1, starting transfers between devices: 1.58 us -> 0.09 us  [body(): lax.ppermute(held, 'seq', pairs)]
  transfers between devices with their start and end apart: 22 -> 22, of which waited for: 14 -> 12; matrix products, arithmetic and copies ran while one was open for 7% -> 3% of each run, Pallas kernels for 8% -> 7%
where the time goes in v6:
time: 131 us; the launch traced here: 130 us
  waiting for transfers between devices  53.4 us (41%)
  starting transfers between devices  46.3 us (35%)
  between operations  13.7 us (10%)
  Pallas kernels  10.3 us (8%)
  other arithmetic  3.61 us (3%)
  local copies, waits for them, and re-layouts  2.93 us (2%)
    ppermute x8, waiting for transfers between devices, ring(): below = lax.ppermute(below, axis, up)  28.9 us
    ppermute x6, starting transfers between devices, ring(): above = lax.ppermute(above, axis, down)  20.2 us
    all_to_all x1, starting transfers between devices, body(): states = lax.all_to_all(final, 'seq', 0, 0, tiled=True)  11.5 us
    all_to_all x1, waiting for transfers between devices, body(): states = lax.all_to_all(final, 'seq', 0, 0, tiled=True)  10.4 us
    ppermute x8, starting transfers between devices, ring(): below = lax.ppermute(below, axis, up)  9.62 us
    ppermute x1, waiting for transfers between devices, body(): query_more = lax.ppermute(query_send, 'seq', pairs)  6.1 us
    ppermute x1, waiting for transfers between devices, body(): lax.ppermute(held, 'seq', pairs)  4.95 us
    pallas_call x1, Pallas kernels, body(): pl.pallas_call(functools.partial(mixin_project_kernel, count), in_specs=[...  3.82 us
  transfers between devices with their start and end apart: 22, of which 12 were waited for; matrix products, arithmetic and copies ran while one was open for 3% of the time, Pallas kernels for 7%

profile of v6, /device:TPU:2, one launch (start us, length us, event | category | flops | bytes accessed | tf_op | source)
XLA Modules:
  0.0 130.2 jit_solution(12659033310811959084)
XLA Ops:
  6.5 1.1 dynamic-slice_bitcast_fusion.2
  7.6 0.8 pad_maximum_fusion
  8.4 0.0 all-gather.3.cloned.1.call-update
  8.4 0.0 all-gather.5.cloned.1.call-start
  8.5 0.7 slice.18
  9.2 1.9 %collective-permute-start = (bf16[2,512]{1,0:T(2,128)(2,1)S(1)}, bf16[2,512]{1,0:T(2,128)(2,1)S(1)}, u32[]{:S(2)}, u32[]{:S(2)}) collective-permute-start(bf16[2,512]{1,0:T(2,128)(2,1)S(1)} %slice.18), channel_id=1, source_target_pairs={{0,1},{1,2},{2,3},{3,4},{4,5},{5,6},{6,7},{7,8},{8,9},{9,10},{10,1... | collective-permute-start | bytes 6152 | tf_op jit(solution)/shard_map/ppermute | solution.py:260
  11.1 0.1 pad.17.clone
  11.2 2.9 %collective-permute-done = bf16[2,512]{1,0:T(2,128)(2,1)S(1)} collective-permute-done((bf16[2,512]{1,0:T(2,128)(2,1)S(1)}, bf16[2,512]{1,0:T(2,128)(2,1)S(1)}, u32[]{:S(2)}, u32[]{:S(2)}) %collective-permute-start) | collective-permute-done | bytes 2080 | tf_op jit(solution)/shard_map/ppermute | solution.py:260
  14.1 1.0 maximum_maximum_fusion
  15.1 0.7 collective-permute-start.1
  15.8 0.0 collective-permute-done.1.refs_0_
  15.8 9.3 %collective-permute-start.2 = (bf16[144,512]{1,0:T(8,128)(2,1)S(1)}, bf16[144,512]{1,0:T(8,128)(2,1)S(1)}, u32[]{:S(2)}, u32[]{:S(2)}) collective-permute-start(bf16[144,512]{1,0:T(8,128)(2,1)S(1)} %collective-permute-done.1.refs_0_), channel_id=1, source_target_pairs={{0,32},{32,64},{64,96},{96,128},{128,160},{160,192},{192,224},{224... | collective-permute-start | bytes 442376 | tf_op jit(solution)/shard_map/ppermute | solution.py:30
  25.1 3.8 %collective-permute-start.3 = (bf16[144,512]{1,0:T(8,128)(2,1)S(1)}, bf16[144,512]{1,0:T(8,128)(2,1)S(1)}, u32[]{:S(2)}, u32[]{:S(2)}) collective-permute-start(bf16[144,512]{1,0:T(8,128)(2,1)S(1)} %collective-permute-done.1.refs_0_), channel_id=1, source_target_pairs={{0,224},{32,0},{64,32},{96,64},{128,96},{160,128},{192,160},{224,1... | collective-permute-start | bytes 442376 | tf_op jit(solution)/shard_map/ppermute | solution.py:33
  28.9 3.1 %collective-permute-done.2.refs_1_ = bf16[144,512]{1,0:T(8,128)(2,1)S(1)} collective-permute-done((bf16[144,512]{1,0:T(8,128)(2,1)S(1)}, bf16[144,512]{1,0:T(8,128)(2,1)S(1)}, u32[]{:S(2)}, u32[]{:S(2)}) %collective-permute-start.2) | collective-permute-done | bytes 147488 | tf_op jit(solution)/shard_map/ppermute | solution.py:30
  32.0 0.0 collective-permute-start.4
  32.0 0.0 collective-permute-done.3.refs_2_
  32.0 3.2 %collective-permute-start.5 = (bf16[144,512]{1,0:T(8,128)(2,1)S(1)}, bf16[144,512]{1,0:T(8,128)(2,1)S(1)}, u32[]{:S(2)}, u32[]{:S(2)}) collective-permute-start(bf16[144,512]{1,0:T(8,128)(2,1)S(1)} %collective-permute-done.3.refs_2_), channel_id=1, source_target_pairs={{0,224},{32,0},{64,32},{96,64},{128,96},{160,128},{192,160},{224,1... | collective-permute-start | bytes 442376 | tf_op jit(solution)/shard_map/ppermute | solution.py:33
  35.2 3.1 %collective-permute-done.4.refs_3_ = bf16[144,512]{1,0:T(8,128)(2,1)S(1)} collective-permute-done((bf16[144,512]{1,0:T(8,128)(2,1)S(1)}, bf16[144,512]{1,0:T(8,128)(2,1)S(1)}, u32[]{:S(2)}, u32[]{:S(2)}) %collective-permute-start.4) | collective-permute-done | bytes 147488 | tf_op jit(solution)/shard_map/ppermute | solution.py:30
  38.4 0.0 collective-permute-start.6
  38.4 0.0 collective-permute-done.5.refs_4_
  38.4 3.5 %collective-permute-start.7 = (bf16[144,512]{1,0:T(8,128)(2,1)S(1)}, bf16[144,512]{1,0:T(8,128)(2,1)S(1)}, u32[]{:S(2)}, u32[]{:S(2)}) collective-permute-start(bf16[144,512]{1,0:T(8,128)(2,1)S(1)} %collective-permute-done.5.refs_4_), channel_id=1, source_target_pairs={{0,224},{32,0},{64,32},{96,64},{128,96},{160,128},{192,160},{224,1... | collective-permute-start | bytes 442376 | tf_op jit(solution)/shard_map/ppermute | solution.py:33
  41.9 4.1 %collective-permute-done.6.refs_5_ = bf16[144,512]{1,0:T(8,128)(2,1)S(1)} collective-permute-done((bf16[144,512]{1,0:T(8,128)(2,1)S(1)}, bf16[144,512]{1,0:T(8,128)(2,1)S(1)}, u32[]{:S(2)}, u32[]{:S(2)}) %collective-permute-start.6) | collective-permute-done | bytes 147488 | tf_op jit(solution)/shard_map/ppermute | solution.py:30
  45.9 0.0 collective-permute-start.8
  45.9 0.0 collective-permute-done.7.refs_6_.done_ref
  45.9 6.3 %collective-permute-done.8.refs_7_.also_ref = bf16[144,512]{1,0:T(8,128)(2,1)S(1)} collective-permute-done((bf16[144,512]{1,0:T(8,128)(2,1)S(1)}, bf16[144,512]{1,0:T(8,128)(2,1)S(1)}, u32[]{:S(2)}, u32[]{:S(2)}) %collective-permute-start.8) | collective-permute-done | bytes 147488 | tf_op jit(solution)/shard_map/ppermute | solution.py:30
  52.3 0.9 copy-done
  53.2 0.1 collective-permute-start.18
  53.3 5.0 %collective-permute-done.18 = bf16[128,512]{1,0:T(8,128)(2,1)S(1)} collective-permute-done((bf16[128,512]{1,0:T(8,128)(2,1)S(1)}, bf16[128,512]{1,0:T(8,128)(2,1)S(1)}, u32[]{:S(2)}, u32[]{:S(2)}) %collective-permute-start.18) | collective-permute-done | bytes 131104 | tf_op jit(solution)/shard_map/ppermute | solution.py:294
  58.3 0.7 pad_maximum_fusion.1
  59.0 0.0 all-gather.5.cloned.1.call-update
  59.1 0.1 pad_add_fusion.place_ref
  59.2 0.1 multiply_bitcast_fusion.1
  59.4 0.2 fusion.3
  59.6 0.6 fusion.1
  60.1 0.0 all-gather.3.cloned.1.call-done.refs_8_
  60.2 3.8 %project_mixin.1 = (f32[144,1024]{1,0:T(8,128)S(1)}, bf16[144,1024]{1,0:T(8,128)(2,1)S(1)}, bf16[2,144,2048]{2,1,0:T(8,128)(2,1)S(1)}, bf16[2048,512]{1,0:T(8,128)(2,1)S(1)}) custom-call(s32[2]{0:T(128)S(1)} %pad_add_fusion.place_ref, bf16[144,512]{1,0:T(8,128)(2,1)S(1)} %collective-permute-done.1.refs_0_, ...), custom_call_target="tpu_custom_call" | custom-call | flops 1207959552 | bytes 4194304 | tf_op jit(solution)/shard_map/project_mixin/pallas_call | solution.py:298
  64.0 0.0 copy-start.4
  64.0 0.0 copy-start.1
  64.0 0.1 collective-permute-start.9
  64.1 0.8 project_query.1
  64.9 2.1 %collective-permute-start.10 = (bf16[144,512]{1,0:T(8,128)(2,1)S(1)}, bf16[144,512]{1,0:T(8,128)(2,1)S(1)}, u32[]{:S(2)}, u32[]{:S(2)}) collective-permute-start(bf16[144,512]{1,0:T(8,128)(2,1)S(1)} %get-tuple-element.22), channel_id=1, source_target_pairs={{0,6},{1,7},{2,4},{3,5},{4,2},{5,3},{6,0},{7,1},{8,14},{9,15},{10,... | collective-permute-start | bytes 442376 | tf_op jit(solution)/shard_map/ppermute | solution.py:320
  67.1 6.1 %collective-permute-done.10.query_more_ref = bf16[144,512]{1,0:T(8,128)(2,1)S(1)} collective-permute-done((bf16[144,512]{1,0:T(8,128)(2,1)S(1)}, bf16[144,512]{1,0:T(8,128)(2,1)S(1)}, u32[]{:S(2)}, u32[]{:S(2)}) %collective-permute-start.10) | collective-permute-done | bytes 147488 | tf_op jit(solution)/shard_map/ppermute | solution.py:320
  73.2 0.0 collective-permute-done.9.more_ref
  73.2 1.5 %scan.1 = (f32[4,128,128]{2,1,0:T(8,128)S(1)}, f32[128,512]{1,0:T(8,128)S(1)}, f32[4,8,512]{2,1,0:T(8,128)S(1)}, f32[32,4,512]{2,1,0:T(4,128)}) custom-call(f32[144,1024]{1,0:T(8,128)S(1)} %get-tuple-element.17.keep_ref, bf16[144,1024]{1,0:T(8,128)(2,1)S(1)} %collective-permute-done.9.more_ref, f32[144,512]{1,0:T(8,128)S(1)} %get-tuple-element.21.query_keep_ref, ...), custom_call_target="tpu_custom_call" | custom-call | tf_op jit(solution)/shard_map/scan/pallas_call | solution.py:322
  74.7 11.5 %all-to-all-start = ((f32[32,4,512]{2,1,0:T(4,128)}), f32[32,4,512]{2,1,0:T(4,128)S(1)}, u32[]{:S(2)}, u32[]{:S(2)}) async-start(f32[32,4,512]{2,1,0:T(4,128)} %get-tuple-element.23), calls=%async_computation | async-start | bytes 524288 | tf_op jit(solution)/shard_map/all_to_all | solution.py:334
  86.2 0.1 fusion.jump_ref
  86.3 10.4 %all-to-all-done.all_ref = f32[32,4,512]{2,1,0:T(4,128)S(1)} async-done(((f32[32,4,512]{2,1,0:T(4,128)}), f32[32,4,512]{2,1,0:T(4,128)S(1)}, u32[]{:S(2)}, u32[]{:S(2)}) %all-to-all-start) | async-done | bytes 262176 | tf_op jit(solution)/shard_map/all_to_all | solution.py:334
  96.7 0.4 gate.1.refs_0_
  97.1 0.3 collective-permute-start.11
  97.4 3.2 %collective-permute-start.15 = (bf16[128,512]{1,0:T(8,128)(2,1)S(1)}, bf16[128,512]{1,0:T(8,128)(2,1)S(1)}, u32[]{:S(2)}, u32[]{:S(2)}) collective-permute-start(bf16[128,512]{1,0:T(8,128)(2,1)S(1)} %gate.1.refs_0_), channel_id=1, source_target_pairs={{0,224},{32,0},{64,32},{96,64},{128,96},{160,128},{192,160},{224,1... | collective-permute-start | bytes 393224 | tf_op jit(solution)/shard_map/ppermute | solution.py:33
  100.6 2.9 %collective-permute-done.11.refs_1_ = bf16[128,512]{1,0:T(8,128)(2,1)S(1)} collective-permute-done((bf16[128,512]{1,0:T(8,128)(2,1)S(1)}, bf16[128,512]{1,0:T(8,128)(2,1)S(1)}, u32[]{:S(2)}, u32[]{:S(2)}) %collective-permute-start.11) | collective-permute-done | bytes 131104 | tf_op jit(solution)/shard_map/ppermute | solution.py:30
  103.6 0.0 collective-permute-start.12
  103.6 0.0 collective-permute-done.15.refs_2_
  103.6 3.2 %collective-permute-start.16 = (bf16[128,512]{1,0:T(8,128)(2,1)S(1)}, bf16[128,512]{1,0:T(8,128)(2,1)S(1)}, u32[]{:S(2)}, u32[]{:S(2)}) collective-permute-start(bf16[128,512]{1,0:T(8,128)(2,1)S(1)} %collective-permute-done.15.refs_2_), channel_id=1, source_target_pairs={{0,224},{32,0},{64,32},{96,64},{128,96},{160,128},{192,160},{224,1... | collective-permute-start | bytes 393224 | tf_op jit(solution)/shard_map/ppermute | solution.py:33
  106.8 2.9 %collective-permute-done.12.refs_3_ = bf16[128,512]{1,0:T(8,128)(2,1)S(1)} collective-permute-done((bf16[128,512]{1,0:T(8,128)(2,1)S(1)}, bf16[128,512]{1,0:T(8,128)(2,1)S(1)}, u32[]{:S(2)}, u32[]{:S(2)}) %collective-permute-start.12) | collective-permute-done | bytes 131104 | tf_op jit(solution)/shard_map/ppermute | solution.py:30
  109.7 0.0 collective-permute-start.13
  109.8 0.0 collective-permute-done.16.refs_4_
  109.8 3.2 %collective-permute-start.17 = (bf16[128,512]{1,0:T(8,128)(2,1)S(1)}, bf16[128,512]{1,0:T(8,128)(2,1)S(1)}, u32[]{:S(2)}, u32[]{:S(2)}) collective-permute-start(bf16[128,512]{1,0:T(8,128)(2,1)S(1)} %collective-permute-done.16.refs_4_), channel_id=1, source_target_pairs={{0,224},{32,0},{64,32},{96,64},{128,96},{160,128},{192,160},{224,1... | collective-permute-start | bytes 393224 | tf_op jit(solution)/shard_map/ppermute | solution.py:33
  113.0 3.3 %collective-permute-done.13.refs_5_ = bf16[128,512]{1,0:T(8,128)(2,1)S(1)} collective-permute-done((bf16[128,512]{1,0:T(8,128)(2,1)S(1)}, bf16[128,512]{1,0:T(8,128)(2,1)S(1)}, u32[]{:S(2)}, u32[]{:S(2)}) %collective-permute-start.13) | collective-permute-done | bytes 131104 | tf_op jit(solution)/shard_map/ppermute | solution.py:30
  116.3 0.0 collective-permute-start.14
  116.3 0.1 stack.48.which_ref
  116.4 2.9 %mix.1 = (f32[128,512]{1,0:T(8,128)S(1)}, bf16[512,512]{1,0:T(8,128)(2,1)S(1)}) custom-call(s32[9]{0:T(128)S(1)} %stack.48.which_ref, bf16[128,512]{1,0:T(8,128)(2,1)S(1)} %gate.1.refs_0_, bf16[128,512]{1,0:T(8,128)(2,1)S(1)} %collective-permute-done.11.refs_1_, bf16[128,512]{1,0:T(8,128)(2,1)S(1)} %collective-permute-done.15.refs_2_, ...), custom_call_target="tpu_custom_call" | custom-call | flops 536870912 | bytes 4194304 | tf_op jit(solution)/shard_map/mix/pallas_call | solution.py:226
  119.3 3.1 %collective-permute-done.14.x_ref = bf16[128,512]{1,0:T(8,128)(2,1)S(1)} collective-permute-done((bf16[128,512]{1,0:T(8,128)(2,1)S(1)}, bf16[128,512]{1,0:T(8,128)(2,1)S(1)}, u32[]{:S(2)}, u32[]{:S(2)}) %collective-permute-start.14) | collective-permute-done | bytes 131104 | tf_op jit(solution)/shard_map/ppermute | solution.py:30
  122.4 0.9 last_mix.1
  (25 shorter events, 0.1 us)
Async XLA Ops:
  6.5 52.6 %copy-start.3 = (f32[512,2]{0,1:T(2,128)S(1)}, f32[512,2]{0,1:T(2,128)}, u32[]{:S(2)}) copy-start(f32[512,2]{0,1:T(2,128)} %param.12) | copy-start | bytes 12292
  6.5 52.6 %copy-start.2 = (f32[512,2]{0,1:T(2,128)S(1)}, f32[512,2]{0,1:T(2,128)}, u32[]{:S(2)}) copy-start(f32[512,2]{0,1:T(2,128)} %param.13) | copy-start | bytes 12292
  6.5 52.8 %copy-start.5 = (f32[2,512,2]{1,2,0:T(2,128)S(1)}, f32[2,512,2]{1,2,0:T(2,128)}, u32[]{:S(2)}) copy-start(f32[2,512,2]{1,2,0:T(2,128)} %param.14) | copy-start | bytes 24580
  6.5 53.6 %all-gather.3.cloned.1.call-start = ((), (), s32[]{:S(2)}) async-start(), calls=%async_computation.1 | async-start | bytes 6684672 | tf_op jit(solution)/shard_map/all_gather | solution.py:258
  8.4 107.9 %all-gather.5.cloned.1.call-start = ((), (), s32[]{:S(2)}) async-start(), calls=%async_computation.2 | async-start | bytes 4456448 | tf_op jit(solution)/shard_map/all_gather | solution.py:258
  9.2 4.9 %collective-permute-start = (bf16[2,512]{1,0:T(2,128)(2,1)S(1)}, bf16[2,512]{1,0:T(2,128)(2,1)S(1)}, u32[]{:S(2)}, u32[]{:S(2)}) collective-permute-start(bf16[2,512]{1,0:T(2,128)(2,1)S(1)} %slice.18), channel_id=1, source_target_pairs={{0,1},{1,2},{2,3},{3,4},{4,5},{5,6},{6,7},{7,8},{8,9},{9,10},{10,1... | collective-permute-start | bytes 6152 | tf_op jit(solution)/shard_map/ppermute | solution.py:260
  15.1 0.7 collective-permute-start.1
  15.8 16.2 %collective-permute-start.2 = (bf16[144,512]{1,0:T(8,128)(2,1)S(1)}, bf16[144,512]{1,0:T(8,128)(2,1)S(1)}, u32[]{:S(2)}, u32[]{:S(2)}) collective-permute-start(bf16[144,512]{1,0:T(8,128)(2,1)S(1)} %collective-permute-done.1.refs_0_), channel_id=1, source_target_pairs={{0,32},{32,64},{64,96},{96,128},{128,160},{160,192},{192,224},{224... | collective-permute-start | bytes 442376 | tf_op jit(solution)/shard_map/ppermute | solution.py:30
  25.1 6.9 %collective-permute-start.3 = (bf16[144,512]{1,0:T(8,128)(2,1)S(1)}, bf16[144,512]{1,0:T(8,128)(2,1)S(1)}, u32[]{:S(2)}, u32[]{:S(2)}) collective-permute-start(bf16[144,512]{1,0:T(8,128)(2,1)S(1)} %collective-permute-done.1.refs_0_), channel_id=1, source_target_pairs={{0,224},{32,0},{64,32},{96,64},{128,96},{160,128},{192,160},{224,1... | collective-permute-start | bytes 442376 | tf_op jit(solution)/shard_map/ppermute | solution.py:33
  32.0 6.4 %collective-permute-start.4 = (bf16[144,512]{1,0:T(8,128)(2,1)S(1)}, bf16[144,512]{1,0:T(8,128)(2,1)S(1)}, u32[]{:S(2)}, u32[]{:S(2)}) collective-permute-start(bf16[144,512]{1,0:T(8,128)(2,1)S(1)} %collective-permute-done.2.refs_1_), channel_id=1, source_target_pairs={{0,32},{32,64},{64,96},{96,128},{128,160},{160,192},{192,224},{224... | collective-permute-start | bytes 442376 | tf_op jit(solution)/shard_map/ppermute | solution.py:30
  32.0 6.4 %collective-permute-start.5 = (bf16[144,512]{1,0:T(8,128)(2,1)S(1)}, bf16[144,512]{1,0:T(8,128)(2,1)S(1)}, u32[]{:S(2)}, u32[]{:S(2)}) collective-permute-start(bf16[144,512]{1,0:T(8,128)(2,1)S(1)} %collective-permute-done.3.refs_2_), channel_id=1, source_target_pairs={{0,224},{32,0},{64,32},{96,64},{128,96},{160,128},{192,160},{224,1... | collective-permute-start | bytes 442376 | tf_op jit(solution)/shard_map/ppermute | solution.py:33
  38.4 7.6 %collective-permute-start.6 = (bf16[144,512]{1,0:T(8,128)(2,1)S(1)}, bf16[144,512]{1,0:T(8,128)(2,1)S(1)}, u32[]{:S(2)}, u32[]{:S(2)}) collective-permute-start(bf16[144,512]{1,0:T(8,128)(2,1)S(1)} %collective-permute-done.4.refs_3_), channel_id=1, source_target_pairs={{0,32},{32,64},{64,96},{96,128},{128,160},{160,192},{192,224},{224... | collective-permute-start | bytes 442376 | tf_op jit(solution)/shard_map/ppermute | solution.py:30
  38.4 7.6 %collective-permute-start.7 = (bf16[144,512]{1,0:T(8,128)(2,1)S(1)}, bf16[144,512]{1,0:T(8,128)(2,1)S(1)}, u32[]{:S(2)}, u32[]{:S(2)}) collective-permute-start(bf16[144,512]{1,0:T(8,128)(2,1)S(1)} %collective-permute-done.5.refs_4_), channel_id=1, source_target_pairs={{0,224},{32,0},{64,32},{96,64},{128,96},{160,128},{192,160},{224,1... | collective-permute-start | bytes 442376 | tf_op jit(solution)/shard_map/ppermute | solution.py:33
  45.9 6.4 %collective-permute-start.8 = (bf16[144,512]{1,0:T(8,128)(2,1)S(1)}, bf16[144,512]{1,0:T(8,128)(2,1)S(1)}, u32[]{:S(2)}, u32[]{:S(2)}) collective-permute-start(bf16[144,512]{1,0:T(8,128)(2,1)S(1)} %collective-permute-done.6.refs_5_), channel_id=1, source_target_pairs={{0,32},{32,64},{64,96},{96,128},{128,160},{160,192},{192,224},{224... | collective-permute-start | bytes 442376 | tf_op jit(solution)/shard_map/ppermute | solution.py:30
  52.3 0.9 copy-start
  53.2 5.1 %collective-permute-start.18 = (bf16[128,512]{1,0:T(8,128)(2,1)S(1)}, bf16[128,512]{1,0:T(8,128)(2,1)S(1)}, u32[]{:S(2)}, u32[]{:S(2)}) collective-permute-start(bf16[128,512]{1,0:T(8,128)(2,1)S(1)} %after.1), channel_id=1, source_target_pairs={{0,6},{1,7},{2,4},{3,5},{4,2},{5,3},{6,0},{7,1},{8,14},{9,15},{10,... | collective-permute-start | bytes 393224 | tf_op jit(solution)/shard_map/ppermute | solution.py:294
  64.0 3.0 %copy-start.4 = (f32[3,3,512]{2,1,0:T(4,128)S(1)}, f32[3,3,512]{2,1,0:T(4,128)}, u32[]{:S(2)}) copy-start(f32[3,3,512]{2,1,0:T(4,128)} %param.11) | copy-start | bytes 55300
  64.0 32.7 %copy-start.1 = (f32[512]{0:T(512)S(1)}, f32[512]{0:T(512)}, u32[]{:S(2)}) copy-start(f32[512]{0:T(512)} %param.15) | copy-start | bytes 6148
  64.0 9.2 %collective-permute-start.9 = (bf16[144,1024]{1,0:T(8,128)(2,1)S(1)}, bf16[144,1024]{1,0:T(8,128)(2,1)S(1)}, u32[]{:S(2)}, u32[]{:S(2)}) collective-permute-start(bf16[144,1024]{1,0:T(8,128)(2,1)S(1)} %get-tuple-element.18), channel_id=1, source_target_pairs={{0,6},{1,7},{2,4},{3,5},{4,2},{5,3},{6,0},{7,1},{8,14},{9,15},{10,... | collective-permute-start | bytes 884744 | tf_op jit(solution)/shard_map/ppermute | solution.py:312
  64.9 8.2 %collective-permute-start.10 = (bf16[144,512]{1,0:T(8,128)(2,1)S(1)}, bf16[144,512]{1,0:T(8,128)(2,1)S(1)}, u32[]{:S(2)}, u32[]{:S(2)}) collective-permute-start(bf16[144,512]{1,0:T(8,128)(2,1)S(1)} %get-tuple-element.22), channel_id=1, source_target_pairs={{0,6},{1,7},{2,4},{3,5},{4,2},{5,3},{6,0},{7,1},{8,14},{9,15},{10,... | collective-permute-start | bytes 442376 | tf_op jit(solution)/shard_map/ppermute | solution.py:320
  74.7 22.1 %all-to-all-start = ((f32[32,4,512]{2,1,0:T(4,128)}), f32[32,4,512]{2,1,0:T(4,128)S(1)}, u32[]{:S(2)}, u32[]{:S(2)}) async-start(f32[32,4,512]{2,1,0:T(4,128)} %get-tuple-element.23), calls=%async_computation | async-start | bytes 524288 | tf_op jit(solution)/shard_map/all_to_all | solution.py:334
  97.1 6.4 %collective-permute-start.11 = (bf16[128,512]{1,0:T(8,128)(2,1)S(1)}, bf16[128,512]{1,0:T(8,128)(2,1)S(1)}, u32[]{:S(2)}, u32[]{:S(2)}) collective-permute-start(bf16[128,512]{1,0:T(8,128)(2,1)S(1)} %gate.1.refs_0_), channel_id=1, source_target_pairs={{0,32},{32,64},{64,96},{96,128},{128,160},{160,192},{192,224},{224... | collective-permute-start | bytes 393224 | tf_op jit(solution)/shard_map/ppermute | solution.py:30
  97.4 6.2 %collective-permute-start.15 = (bf16[128,512]{1,0:T(8,128)(2,1)S(1)}, bf16[128,512]{1,0:T(8,128)(2,1)S(1)}, u32[]{:S(2)}, u32[]{:S(2)}) collective-permute-start(bf16[128,512]{1,0:T(8,128)(2,1)S(1)} %gate.1.refs_0_), channel_id=1, source_target_pairs={{0,224},{32,0},{64,32},{96,64},{128,96},{160,128},{192,160},{224,1... | collective-permute-start | bytes 393224 | tf_op jit(solution)/shard_map/ppermute | solution.py:33
  103.6 6.2 %collective-permute-start.12 = (bf16[128,512]{1,0:T(8,128)(2,1)S(1)}, bf16[128,512]{1,0:T(8,128)(2,1)S(1)}, u32[]{:S(2)}, u32[]{:S(2)}) collective-permute-start(bf16[128,512]{1,0:T(8,128)(2,1)S(1)} %collective-permute-done.11.refs_1_), channel_id=1, source_target_pairs={{0,32},{32,64},{64,96},{96,128},{128,160},{160,192},{192,224},{224... | collective-permute-start | bytes 393224 | tf_op jit(solution)/shard_map/ppermute | solution.py:30
  103.6 6.2 %collective-permute-start.16 = (bf16[128,512]{1,0:T(8,128)(2,1)S(1)}, bf16[128,512]{1,0:T(8,128)(2,1)S(1)}, u32[]{:S(2)}, u32[]{:S(2)}) collective-permute-start(bf16[128,512]{1,0:T(8,128)(2,1)S(1)} %collective-permute-done.15.refs_2_), channel_id=1, source_target_pairs={{0,224},{32,0},{64,32},{96,64},{128,96},{160,128},{192,160},{224,1... | collective-permute-start | bytes 393224 | tf_op jit(solution)/shard_map/ppermute | solution.py:33
  109.7 6.5 %collective-permute-start.13 = (bf16[128,512]{1,0:T(8,128)(2,1)S(1)}, bf16[128,512]{1,0:T(8,128)(2,1)S(1)}, u32[]{:S(2)}, u32[]{:S(2)}) collective-permute-start(bf16[128,512]{1,0:T(8,128)(2,1)S(1)} %collective-permute-done.12.refs_3_), channel_id=1, source_target_pairs={{0,32},{32,64},{64,96},{96,128},{128,160},{160,192},{192,224},{224... | collective-permute-start | bytes 393224 | tf_op jit(solution)/shard_map/ppermute | solution.py:30
  109.8 6.6 %collective-permute-start.17 = (bf16[128,512]{1,0:T(8,128)(2,1)S(1)}, bf16[128,512]{1,0:T(8,128)(2,1)S(1)}, u32[]{:S(2)}, u32[]{:S(2)}) collective-permute-start(bf16[128,512]{1,0:T(8,128)(2,1)S(1)} %collective-permute-done.16.refs_4_), channel_id=1, source_target_pairs={{0,224},{32,0},{64,32},{96,64},{128,96},{160,128},{192,160},{224,1... | collective-permute-start | bytes 393224 | tf_op jit(solution)/shard_map/ppermute | solution.py:33
  116.3 6.2 %collective-permute-start.14 = (bf16[128,512]{1,0:T(8,128)(2,1)S(1)}, bf16[128,512]{1,0:T(8,128)(2,1)S(1)}, u32[]{:S(2)}, u32[]{:S(2)}) collective-permute-start(bf16[128,512]{1,0:T(8,128)(2,1)S(1)} %collective-permute-done.13.refs_5_), channel_id=1, source_target_pairs={{0,32},{32,64},{64,96},{96,128},{128,160},{160,192},{192,224},{224... | collective-permute-start | bytes 393224 | tf_op jit(solution)/shard_map/ppermute | solution.py:30
Sparse Core Ops, SparseCore 0:
  9.2 47.6 all-gather.2
  59.1 45.7 all-gather.4

commit v7 on v6

--- a/solution.py
+++ b/solution.py
@@ -78,8 +78,14 @@
     product(lhs_ref, w_ref, cols, keep_ref, send_ref, cols)
 
 
-def after_kernel(x_ref, done_ref, also_ref, out_ref):
-    out_ref[...] = x_ref[...]
+def beside_kernel(x_ref, y_ref, done_ref, also_ref, out_ref, sems):
+    cols = x_ref.shape[1]
+    left = pltpu.make_async_copy(x_ref, out_ref.at[:, pl.ds(0, cols)], sems.at[0])
+    right = pltpu.make_async_copy(y_ref, out_ref.at[:, pl.ds(cols, cols)], sems.at[1])
+    left.start()
+    right.start()
+    left.wait()
+    right.wait()
 
 
 def short_conv(rows, branch, total, taps_ref):
@@ -105,6 +111,7 @@
     query_ref,
     begin_ref,
     final_ref,
+    last,
 ):
     query = query_keep_ref[...] + query_more_ref[...].astype(jnp.float32)
     query_ref[...] = short_conv(rows, 0, query, taps_ref)
@@ -141,9 +148,10 @@
                     jr * er - ji * ei + re[n][b : b + 1],
                     jr * ei + ji * er + im[n][b : b + 1],
                 )
-            for copy in range(final_ref.shape[0]):
-                final_ref[copy, n : n + 1, cols] = er
-                final_ref[copy, 2 + n : 3 + n, cols] = ei
+            last[n : n + 1, cols] = er
+            last[2 + n : 3 + n, cols] = ei
+    for copy in range(final_ref.shape[0]):
+        final_ref[copy] = last[...]
 
 
 def gate_kernel(
@@ -284,14 +292,16 @@
     params = pltpu.CompilerParams(vmem_limit_bytes=VMEM)
     shape = jax.ShapeDtypeStruct
     half = lax.rem(place, 8) // 4
-    held = pl.pallas_call(
-        after_kernel,
-        in_specs=[IN_VMEM] * 3,
-        out_shape=shape(out_weight.shape, b16),
-        compiler_params=params,
-        name="after",
-    )(out_weight, features[-2], features[-1])
-    second = gather(jnp.concatenate([out_weight, lax.ppermute(held, "seq", pairs)], axis=1))
+    both = pl.pallas_call(
+        beside_kernel,
+        in_specs=[IN_HBM] + [pl.BlockSpec(memory_space=pl.ANY)] * 3,
+        out_specs=IN_HBM,
+        out_shape=shape((out_weight.shape[0], 2 * out_weight.shape[1]), b16),
+        scratch_shapes=[pltpu.SemaphoreType.DMA((2,))],
+        compiler_params=params,
+        name="beside",
+    )(in_hbm(out_weight), lax.ppermute(out_weight, "seq", pairs), features[-2], features[-1])
+    second = gather(both)
     cost = lambda width: pl.CostEstimate(
         flops=4 * padded * depth * width, bytes_accessed=2 * depth * width, transcendentals=0
     )
@@ -327,6 +337,7 @@
             shape((4, SUB, chans), f32),
             shape((blocks, 4, chans), f32),
         ],
+        scratch_shapes=[pltpu.VMEM((4, chans), f32)],
         compiler_params=params,
         name="scan",
     )(keep, more, query_keep, query_more, taps, step, join)

time: 131 us -> 128 us (0.977)
  Pallas kernels: 10.3 us -> 15.3 us
  waiting for transfers between devices: 53.4 us -> 49.6 us
  starting transfers between devices: 46.3 us -> 43.6 us
    ppermute x8, waiting for transfers between devices: 28.9 us -> 23.5 us  [ring(): below = lax.ppermute(below, axis, up)]
    pallas_call x1, Pallas kernels: 0.01 us -> 5.09 us  [body(): pl.pallas_call(beside_kernel, in_specs=[IN_HBM] + [pl.BlockSpec(memory_sp...]
    all_to_all x1, starting transfers between devices: 11.5 us -> 8.8 us  [body(): states = lax.all_to_all(final, 'seq', 0, 0, tiled=True)]
    ppermute x1, waiting for transfers between devices: 6.1 us -> 7.71 us  [body(): query_more = lax.ppermute(query_send, 'seq', pairs)]
  transfers between devices with their start and end apart: 22 -> 22, of which waited for: 12 -> 12; matrix products, arithmetic and copies ran while one was open for 3% -> 2% of each run, Pallas kernels for 7% -> 11%
where the time goes in v7:
time: 128 us; the launch traced here: 127 us
  waiting for transfers between devices  49.6 us (39%)
  starting transfers between devices  43.6 us (34%)
  Pallas kernels  15.3 us (12%)
  between operations  13.7 us (11%)
  other arithmetic  2.91 us (2%)
  local copies, waits for them, and re-layouts  2.01 us (2%)
    ppermute x8, waiting for transfers between devices, ring(): below = lax.ppermute(below, axis, up)  23.5 us
    ppermute x6, starting transfers between devices, ring(): above = lax.ppermute(above, axis, down)  19.6 us
    ppermute x8, starting transfers between devices, ring(): below = lax.ppermute(below, axis, up)  10.5 us
    all_to_all x1, waiting for transfers between devices, body(): states = lax.all_to_all(final, 'seq', 0, 0, tiled=True)  10.2 us
    all_to_all x1, starting transfers between devices, body(): states = lax.all_to_all(final, 'seq', 0, 0, tiled=True)  8.8 us
    ppermute x1, waiting for transfers between devices, body(): query_more = lax.ppermute(query_send, 'seq', pairs)  7.71 us
    ppermute x1, waiting for transfers between devices, body(): lax.ppermute(out_weight, 'seq', pairs)  5.18 us
    pallas_call x1, Pallas kernels, body(): pl.pallas_call(beside_kernel, in_specs=[IN_HBM] + [pl.BlockSpec(memory_sp...  5.09 us
  transfers between devices with their start and end apart: 22, of which 12 were waited for; matrix products, arithmetic and copies ran while one was open for 2% of the time, Pallas kernels for 11%

profile of v7, /device:TPU:2, one launch (start us, length us, event | category | flops | bytes accessed | tf_op | source)
XLA Modules:
  0.0 127.1 jit_solution(5906641854638792272)
XLA Ops:
  6.5 1.1 dynamic-slice_bitcast_fusion.2
  7.6 0.8 pad_maximum_fusion
  8.4 0.0 all-gather.3.cloned.1.call-update
  8.5 0.0 all-gather.5.cloned.1.call-start
  8.5 0.7 slice.18
  9.2 1.9 %collective-permute-start = (bf16[2,512]{1,0:T(2,128)(2,1)S(1)}, bf16[2,512]{1,0:T(2,128)(2,1)S(1)}, u32[]{:S(2)}, u32[]{:S(2)}) collective-permute-start(bf16[2,512]{1,0:T(2,128)(2,1)S(1)} %slice.18), channel_id=1, source_target_pairs={{0,1},{1,2},{2,3},{3,4},{4,5},{5,6},{6,7},{7,8},{8,9},{9,10},{10,1... | collective-permute-start | bytes 6152 | tf_op jit(solution)/shard_map/ppermute | solution.py:268
  11.1 0.1 pad.15.clone
  11.2 2.9 %collective-permute-done = bf16[2,512]{1,0:T(2,128)(2,1)S(1)} collective-permute-done((bf16[2,512]{1,0:T(2,128)(2,1)S(1)}, bf16[2,512]{1,0:T(2,128)(2,1)S(1)}, u32[]{:S(2)}, u32[]{:S(2)}) %collective-permute-start) | collective-permute-done | bytes 2080 | tf_op jit(solution)/shard_map/ppermute | solution.py:268
  14.1 1.0 maximum_maximum_fusion
  15.1 0.7 collective-permute-start.1
  15.8 0.0 collective-permute-done.1.refs_0_
  15.8 9.3 %collective-permute-start.2 = (bf16[144,512]{1,0:T(8,128)(2,1)S(1)}, bf16[144,512]{1,0:T(8,128)(2,1)S(1)}, u32[]{:S(2)}, u32[]{:S(2)}) collective-permute-start(bf16[144,512]{1,0:T(8,128)(2,1)S(1)} %collective-permute-done.1.refs_0_), channel_id=1, source_target_pairs={{0,32},{32,64},{64,96},{96,128},{128,160},{160,192},{192,224},{224... | collective-permute-start | bytes 442376 | tf_op jit(solution)/shard_map/ppermute | solution.py:30
  25.1 3.8 %collective-permute-start.3 = (bf16[144,512]{1,0:T(8,128)(2,1)S(1)}, bf16[144,512]{1,0:T(8,128)(2,1)S(1)}, u32[]{:S(2)}, u32[]{:S(2)}) collective-permute-start(bf16[144,512]{1,0:T(8,128)(2,1)S(1)} %collective-permute-done.1.refs_0_), channel_id=1, source_target_pairs={{0,224},{32,0},{64,32},{96,64},{128,96},{160,128},{192,160},{224,1... | collective-permute-start | bytes 442376 | tf_op jit(solution)/shard_map/ppermute | solution.py:33
  28.9 3.1 %collective-permute-done.2.refs_1_ = bf16[144,512]{1,0:T(8,128)(2,1)S(1)} collective-permute-done((bf16[144,512]{1,0:T(8,128)(2,1)S(1)}, bf16[144,512]{1,0:T(8,128)(2,1)S(1)}, u32[]{:S(2)}, u32[]{:S(2)}) %collective-permute-start.2) | collective-permute-done | bytes 147488 | tf_op jit(solution)/shard_map/ppermute | solution.py:30
  32.0 0.0 collective-permute-start.4
  32.0 0.0 collective-permute-done.3.refs_2_
  32.0 3.2 %collective-permute-start.5 = (bf16[144,512]{1,0:T(8,128)(2,1)S(1)}, bf16[144,512]{1,0:T(8,128)(2,1)S(1)}, u32[]{:S(2)}, u32[]{:S(2)}) collective-permute-start(bf16[144,512]{1,0:T(8,128)(2,1)S(1)} %collective-permute-done.3.refs_2_), channel_id=1, source_target_pairs={{0,224},{32,0},{64,32},{96,64},{128,96},{160,128},{192,160},{224,1... | collective-permute-start | bytes 442376 | tf_op jit(solution)/shard_map/ppermute | solution.py:33
  35.3 3.1 %collective-permute-done.4.refs_3_ = bf16[144,512]{1,0:T(8,128)(2,1)S(1)} collective-permute-done((bf16[144,512]{1,0:T(8,128)(2,1)S(1)}, bf16[144,512]{1,0:T(8,128)(2,1)S(1)}, u32[]{:S(2)}, u32[]{:S(2)}) %collective-permute-start.4) | collective-permute-done | bytes 147488 | tf_op jit(solution)/shard_map/ppermute | solution.py:30
  38.4 0.0 collective-permute-start.6
  38.4 0.0 collective-permute-done.5.refs_4_
  38.4 3.5 %collective-permute-start.7 = (bf16[144,512]{1,0:T(8,128)(2,1)S(1)}, bf16[144,512]{1,0:T(8,128)(2,1)S(1)}, u32[]{:S(2)}, u32[]{:S(2)}) collective-permute-start(bf16[144,512]{1,0:T(8,128)(2,1)S(1)} %collective-permute-done.5.refs_4_), channel_id=1, source_target_pairs={{0,224},{32,0},{64,32},{96,64},{128,96},{160,128},{192,160},{224,1... | collective-permute-start | bytes 442376 | tf_op jit(solution)/shard_map/ppermute | solution.py:33
  41.9 4.1 %collective-permute-done.6.refs_5_ = bf16[144,512]{1,0:T(8,128)(2,1)S(1)} collective-permute-done((bf16[144,512]{1,0:T(8,128)(2,1)S(1)}, bf16[144,512]{1,0:T(8,128)(2,1)S(1)}, u32[]{:S(2)}, u32[]{:S(2)}) %collective-permute-start.6) | collective-permute-done | bytes 147488 | tf_op jit(solution)/shard_map/ppermute | solution.py:30
  46.0 0.0 collective-permute-start.8
  46.0 0.0 collective-permute-start.18
  46.0 5.2 %collective-permute-done.18.y_ref = bf16[128,512]{1,0:T(8,128)(2,1)S(1)} collective-permute-done((bf16[128,512]{1,0:T(8,128)(2,1)}, bf16[128,512]{1,0:T(8,128)(2,1)S(1)}, u32[]{:S(2)}, u32[]{:S(2)}) %collective-permute-start.18) | collective-permute-done | bytes 131104 | tf_op jit(solution)/shard_map/ppermute | solution.py:303
  51.1 0.0 collective-permute-done.7.refs_6_.done_ref
  51.1 1.2 collective-permute-done.8.refs_7_.also_ref
  52.3 5.1 %beside.1 = bf16[128,1024]{1,0:T(8,128)(2,1)} custom-call(bf16[128,512]{1,0:T(8,128)(2,1)} %x_ref.1, bf16[128,512]{1,0:T(8,128)(2,1)S(1)} %collective-permute-done.18.y_ref, bf16[144,512]{1,0:T(8,128)(2,1)S(1)} %collective-permute-done.7.refs_6_.done_ref, bf16[144,512]{1,0:T(8,128)(2,1)S(1)} %collective-permute-done.8.refs_7_.also_ref), custom_call_target="tpu_custom_call" | custom-call | tf_op jit(solution)/shard_map/beside/pallas_call | solution.py:295
  57.4 0.0 all-gather.5.cloned.1.call-update
  57.5 0.1 pad_add_fusion.place_ref
  57.6 0.1 multiply_bitcast_fusion.1
  57.8 0.2 fusion.3
  58.0 0.6 fusion.1
  58.5 0.0 all-gather.3.cloned.1.call-done.refs_8_
  58.6 3.8 %project_mixin.1 = (f32[144,1024]{1,0:T(8,128)S(1)}, bf16[144,1024]{1,0:T(8,128)(2,1)S(1)}, bf16[2,144,2048]{2,1,0:T(8,128)(2,1)S(1)}, bf16[2048,512]{1,0:T(8,128)(2,1)S(1)}) custom-call(s32[2]{0:T(128)S(1)} %pad_add_fusion.place_ref, bf16[144,512]{1,0:T(8,128)(2,1)S(1)} %collective-permute-done.1.refs_0_, ...), custom_call_target="tpu_custom_call" | custom-call | flops 1207959552 | bytes 4194304 | tf_op jit(solution)/shard_map/project_mixin/pallas_call | solution.py:308
  62.4 0.0 copy-start.3
  62.4 0.0 copy-start
  62.4 0.1 collective-permute-start.9
  62.5 0.8 project_query.1
  63.3 2.1 %collective-permute-start.10 = (bf16[144,512]{1,0:T(8,128)(2,1)S(1)}, bf16[144,512]{1,0:T(8,128)(2,1)S(1)}, u32[]{:S(2)}, u32[]{:S(2)}) collective-permute-start(bf16[144,512]{1,0:T(8,128)(2,1)S(1)} %get-tuple-element.22), channel_id=1, source_target_pairs={{0,6},{1,7},{2,4},{3,5},{4,2},{5,3},{6,0},{7,1},{8,14},{9,15},{10,... | collective-permute-start | bytes 442376 | tf_op jit(solution)/shard_map/ppermute | solution.py:330
  65.5 7.7 %collective-permute-done.10.query_more_ref = bf16[144,512]{1,0:T(8,128)(2,1)S(1)} collective-permute-done((bf16[144,512]{1,0:T(8,128)(2,1)S(1)}, bf16[144,512]{1,0:T(8,128)(2,1)S(1)}, u32[]{:S(2)}, u32[]{:S(2)}) %collective-permute-start.10) | collective-permute-done | bytes 147488 | tf_op jit(solution)/shard_map/ppermute | solution.py:330
  73.2 0.0 collective-permute-done.9.more_ref
  73.2 1.4 %scan.1 = (f32[4,128,128]{2,1,0:T(8,128)S(1)}, f32[128,512]{1,0:T(8,128)S(1)}, f32[4,8,512]{2,1,0:T(8,128)S(1)}, f32[32,4,512]{2,1,0:T(4,128)}) custom-call(f32[144,1024]{1,0:T(8,128)S(1)} %get-tuple-element.17.keep_ref, bf16[144,1024]{1,0:T(8,128)(2,1)S(1)} %collective-permute-done.9.more_ref, f32[144,512]{1,0:T(8,128)S(1)} %get-tuple-element.21.query_keep_ref, ...), custom_call_target="tpu_custom_call" | custom-call | tf_op jit(solution)/shard_map/scan/pallas_call | solution.py:332
  74.6 8.8 %all-to-all-start = ((f32[32,4,512]{2,1,0:T(4,128)}), f32[32,4,512]{2,1,0:T(4,128)S(1)}, u32[]{:S(2)}, u32[]{:S(2)}) async-start(f32[32,4,512]{2,1,0:T(4,128)} %get-tuple-element.23), calls=%async_computation | async-start | bytes 524288 | tf_op jit(solution)/shard_map/all_to_all | solution.py:345
  83.4 0.1 fusion.jump_ref
  83.5 10.2 %all-to-all-done.all_ref = f32[32,4,512]{2,1,0:T(4,128)S(1)} async-done(((f32[32,4,512]{2,1,0:T(4,128)}), f32[32,4,512]{2,1,0:T(4,128)S(1)}, u32[]{:S(2)}, u32[]{:S(2)}) %all-to-all-start) | async-done | bytes 262176 | tf_op jit(solution)/shard_map/all_to_all | solution.py:345
  93.7 0.4 gate.1.refs_0_
  94.1 1.1 collective-permute-start.11
  95.2 2.6 %collective-permute-start.15 = (bf16[128,512]{1,0:T(8,128)(2,1)S(1)}, bf16[128,512]{1,0:T(8,128)(2,1)S(1)}, u32[]{:S(2)}, u32[]{:S(2)}) collective-permute-start(bf16[128,512]{1,0:T(8,128)(2,1)S(1)} %gate.1.refs_0_), channel_id=1, source_target_pairs={{0,224},{32,0},{64,32},{96,64},{128,96},{160,128},{192,160},{224,1... | collective-permute-start | bytes 393224 | tf_op jit(solution)/shard_map/ppermute | solution.py:33
  97.8 3.0 %collective-permute-done.11.refs_1_ = bf16[128,512]{1,0:T(8,128)(2,1)S(1)} collective-permute-done((bf16[128,512]{1,0:T(8,128)(2,1)S(1)}, bf16[128,512]{1,0:T(8,128)(2,1)S(1)}, u32[]{:S(2)}, u32[]{:S(2)}) %collective-permute-start.11) | collective-permute-done | bytes 131104 | tf_op jit(solution)/shard_map/ppermute | solution.py:30
  100.8 0.0 collective-permute-start.12
  100.8 0.0 collective-permute-done.15.refs_2_
  100.8 3.2 %collective-permute-start.16 = (bf16[128,512]{1,0:T(8,128)(2,1)S(1)}, bf16[128,512]{1,0:T(8,128)(2,1)S(1)}, u32[]{:S(2)}, u32[]{:S(2)}) collective-permute-start(bf16[128,512]{1,0:T(8,128)(2,1)S(1)} %collective-permute-done.15.refs_2_), channel_id=1, source_target_pairs={{0,224},{32,0},{64,32},{96,64},{128,96},{160,128},{192,160},{224,1... | collective-permute-start | bytes 393224 | tf_op jit(solution)/shard_map/ppermute | solution.py:33
  104.1 2.9 %collective-permute-done.12.refs_3_ = bf16[128,512]{1,0:T(8,128)(2,1)S(1)} collective-permute-done((bf16[128,512]{1,0:T(8,128)(2,1)S(1)}, bf16[128,512]{1,0:T(8,128)(2,1)S(1)}, u32[]{:S(2)}, u32[]{:S(2)}) %collective-permute-start.12) | collective-permute-done | bytes 131104 | tf_op jit(solution)/shard_map/ppermute | solution.py:30
  107.0 0.0 collective-permute-start.13
  107.0 0.0 collective-permute-done.16.refs_4_
  107.0 3.2 %collective-permute-start.17 = (bf16[128,512]{1,0:T(8,128)(2,1)S(1)}, bf16[128,512]{1,0:T(8,128)(2,1)S(1)}, u32[]{:S(2)}, u32[]{:S(2)}) collective-permute-start(bf16[128,512]{1,0:T(8,128)(2,1)S(1)} %collective-permute-done.16.refs_4_), channel_id=1, source_target_pairs={{0,224},{32,0},{64,32},{96,64},{128,96},{160,128},{192,160},{224,1... | collective-permute-start | bytes 393224 | tf_op jit(solution)/shard_map/ppermute | solution.py:33
  110.2 2.9 %collective-permute-done.13.refs_5_ = bf16[128,512]{1,0:T(8,128)(2,1)S(1)} collective-permute-done((bf16[128,512]{1,0:T(8,128)(2,1)S(1)}, bf16[128,512]{1,0:T(8,128)(2,1)S(1)}, u32[]{:S(2)}, u32[]{:S(2)}) %collective-permute-start.13) | collective-permute-done | bytes 131104 | tf_op jit(solution)/shard_map/ppermute | solution.py:30
  113.2 0.0 collective-permute-start.14
  113.2 0.1 stack.48.which_ref
  113.3 0.0 collective-permute-done.17.refs_6_
  113.3 2.9 %mix.1 = (f32[128,512]{1,0:T(8,128)S(1)}, bf16[512,512]{1,0:T(8,128)(2,1)S(1)}) custom-call(s32[9]{0:T(128)S(1)} %stack.48.which_ref, bf16[128,512]{1,0:T(8,128)(2,1)S(1)} %gate.1.refs_0_, bf16[128,512]{1,0:T(8,128)(2,1)S(1)} %collective-permute-done.11.refs_1_, bf16[128,512]{1,0:T(8,128)(2,1)S(1)} %collective-permute-done.15.refs_2_, ...), custom_call_target="tpu_custom_call" | custom-call | flops 536870912 | bytes 4194304 | tf_op jit(solution)/shard_map/mix/pallas_call | solution.py:234
  116.2 3.1 %collective-permute-done.14.x_ref = bf16[128,512]{1,0:T(8,128)(2,1)S(1)} collective-permute-done((bf16[128,512]{1,0:T(8,128)(2,1)S(1)}, bf16[128,512]{1,0:T(8,128)(2,1)S(1)}, u32[]{:S(2)}, u32[]{:S(2)}) %collective-permute-start.14) | collective-permute-done | bytes 131104 | tf_op jit(solution)/shard_map/ppermute | solution.py:30
  119.4 0.9 last_mix.1
  (22 shorter events, 0.1 us)
Async XLA Ops:
  6.5 51.0 %copy-start.2 = (f32[512,2]{0,1:T(2,128)S(1)}, f32[512,2]{0,1:T(2,128)}, u32[]{:S(2)}) copy-start(f32[512,2]{0,1:T(2,128)} %param.12) | copy-start | bytes 12292
  6.5 51.0 %copy-start.1 = (f32[512,2]{0,1:T(2,128)S(1)}, f32[512,2]{0,1:T(2,128)}, u32[]{:S(2)}) copy-start(f32[512,2]{0,1:T(2,128)} %param.13) | copy-start | bytes 12292
  6.5 51.2 %copy-start.4 = (f32[2,512,2]{1,2,0:T(2,128)S(1)}, f32[2,512,2]{1,2,0:T(2,128)}, u32[]{:S(2)}) copy-start(f32[2,512,2]{1,2,0:T(2,128)} %param.14) | copy-start | bytes 24580
  6.5 52.0 %all-gather.3.cloned.1.call-start = ((), (), s32[]{:S(2)}) async-start(), calls=%async_computation.1 | async-start | bytes 6684672 | tf_op jit(solution)/shard_map/all_gather | solution.py:266
  8.5 104.8 %all-gather.5.cloned.1.call-start = ((), (), s32[]{:S(2)}) async-start(), calls=%async_computation.2 | async-start | bytes 4456448 | tf_op jit(solution)/shard_map/all_gather | solution.py:266
  9.2 4.9 %collective-permute-start = (bf16[2,512]{1,0:T(2,128)(2,1)S(1)}, bf16[2,512]{1,0:T(2,128)(2,1)S(1)}, u32[]{:S(2)}, u32[]{:S(2)}) collective-permute-start(bf16[2,512]{1,0:T(2,128)(2,1)S(1)} %slice.18), channel_id=1, source_target_pairs={{0,1},{1,2},{2,3},{3,4},{4,5},{5,6},{6,7},{7,8},{8,9},{9,10},{10,1... | collective-permute-start | bytes 6152 | tf_op jit(solution)/shard_map/ppermute | solution.py:268
  15.1 0.7 collective-permute-start.1
  15.8 16.2 %collective-permute-start.2 = (bf16[144,512]{1,0:T(8,128)(2,1)S(1)}, bf16[144,512]{1,0:T(8,128)(2,1)S(1)}, u32[]{:S(2)}, u32[]{:S(2)}) collective-permute-start(bf16[144,512]{1,0:T(8,128)(2,1)S(1)} %collective-permute-done.1.refs_0_), channel_id=1, source_target_pairs={{0,32},{32,64},{64,96},{96,128},{128,160},{160,192},{192,224},{224... | collective-permute-start | bytes 442376 | tf_op jit(solution)/shard_map/ppermute | solution.py:30
  25.1 6.9 %collective-permute-start.3 = (bf16[144,512]{1,0:T(8,128)(2,1)S(1)}, bf16[144,512]{1,0:T(8,128)(2,1)S(1)}, u32[]{:S(2)}, u32[]{:S(2)}) collective-permute-start(bf16[144,512]{1,0:T(8,128)(2,1)S(1)} %collective-permute-done.1.refs_0_), channel_id=1, source_target_pairs={{0,224},{32,0},{64,32},{96,64},{128,96},{160,128},{192,160},{224,1... | collective-permute-start | bytes 442376 | tf_op jit(solution)/shard_map/ppermute | solution.py:33
  32.0 6.4 %collective-permute-start.4 = (bf16[144,512]{1,0:T(8,128)(2,1)S(1)}, bf16[144,512]{1,0:T(8,128)(2,1)S(1)}, u32[]{:S(2)}, u32[]{:S(2)}) collective-permute-start(bf16[144,512]{1,0:T(8,128)(2,1)S(1)} %collective-permute-done.2.refs_1_), channel_id=1, source_target_pairs={{0,32},{32,64},{64,96},{96,128},{128,160},{160,192},{192,224},{224... | collective-permute-start | bytes 442376 | tf_op jit(solution)/shard_map/ppermute | solution.py:30
  32.0 6.4 %collective-permute-start.5 = (bf16[144,512]{1,0:T(8,128)(2,1)S(1)}, bf16[144,512]{1,0:T(8,128)(2,1)S(1)}, u32[]{:S(2)}, u32[]{:S(2)}) collective-permute-start(bf16[144,512]{1,0:T(8,128)(2,1)S(1)} %collective-permute-done.3.refs_2_), channel_id=1, source_target_pairs={{0,224},{32,0},{64,32},{96,64},{128,96},{160,128},{192,160},{224,1... | collective-permute-start | bytes 442376 | tf_op jit(solution)/shard_map/ppermute | solution.py:33
  38.4 7.6 %collective-permute-start.6 = (bf16[144,512]{1,0:T(8,128)(2,1)S(1)}, bf16[144,512]{1,0:T(8,128)(2,1)S(1)}, u32[]{:S(2)}, u32[]{:S(2)}) collective-permute-start(bf16[144,512]{1,0:T(8,128)(2,1)S(1)} %collective-permute-done.4.refs_3_), channel_id=1, source_target_pairs={{0,32},{32,64},{64,96},{96,128},{128,160},{160,192},{192,224},{224... | collective-permute-start | bytes 442376 | tf_op jit(solution)/shard_map/ppermute | solution.py:30
  38.4 12.8 %collective-permute-start.7 = (bf16[144,512]{1,0:T(8,128)(2,1)S(1)}, bf16[144,512]{1,0:T(8,128)(2,1)S(1)}, u32[]{:S(2)}, u32[]{:S(2)}) collective-permute-start(bf16[144,512]{1,0:T(8,128)(2,1)S(1)} %collective-permute-done.5.refs_4_), channel_id=1, source_target_pairs={{0,224},{32,0},{64,32},{96,64},{128,96},{160,128},{192,160},{224,1... | collective-permute-start | bytes 442376 | tf_op jit(solution)/shard_map/ppermute | solution.py:33
  46.0 6.4 %collective-permute-start.8 = (bf16[144,512]{1,0:T(8,128)(2,1)S(1)}, bf16[144,512]{1,0:T(8,128)(2,1)S(1)}, u32[]{:S(2)}, u32[]{:S(2)}) collective-permute-start(bf16[144,512]{1,0:T(8,128)(2,1)S(1)} %collective-permute-done.6.refs_5_), channel_id=1, source_target_pairs={{0,32},{32,64},{64,96},{96,128},{128,160},{160,192},{192,224},{224... | collective-permute-start | bytes 442376 | tf_op jit(solution)/shard_map/ppermute | solution.py:30
  46.0 5.2 %collective-permute-start.18 = (bf16[128,512]{1,0:T(8,128)(2,1)}, bf16[128,512]{1,0:T(8,128)(2,1)S(1)}, u32[]{:S(2)}, u32[]{:S(2)}) collective-permute-start(bf16[128,512]{1,0:T(8,128)(2,1)} %x_ref.1), channel_id=1, source_target_pairs={{0,6},{1,7},{2,4},{3,5},{4,2},{5,3},{6,0},{7,1},{8,14},{9,15},{10,... | collective-permute-start | bytes 393224 | tf_op jit(solution)/shard_map/ppermute | solution.py:303
  62.4 3.0 %copy-start.3 = (f32[3,3,512]{2,1,0:T(4,128)S(1)}, f32[3,3,512]{2,1,0:T(4,128)}, u32[]{:S(2)}) copy-start(f32[3,3,512]{2,1,0:T(4,128)} %param.11) | copy-start | bytes 55300
  62.4 31.3 %copy-start = (f32[512]{0:T(512)S(1)}, f32[512]{0:T(512)}, u32[]{:S(2)}) copy-start(f32[512]{0:T(512)} %param.15) | copy-start | bytes 6148
  62.4 10.8 %collective-permute-start.9 = (bf16[144,1024]{1,0:T(8,128)(2,1)S(1)}, bf16[144,1024]{1,0:T(8,128)(2,1)S(1)}, u32[]{:S(2)}, u32[]{:S(2)}) collective-permute-start(bf16[144,1024]{1,0:T(8,128)(2,1)S(1)} %get-tuple-element.18), channel_id=1, source_target_pairs={{0,6},{1,7},{2,4},{3,5},{4,2},{5,3},{6,0},{7,1},{8,14},{9,15},{10,... | collective-permute-start | bytes 884744 | tf_op jit(solution)/shard_map/ppermute | solution.py:322
  63.3 9.8 %collective-permute-start.10 = (bf16[144,512]{1,0:T(8,128)(2,1)S(1)}, bf16[144,512]{1,0:T(8,128)(2,1)S(1)}, u32[]{:S(2)}, u32[]{:S(2)}) collective-permute-start(bf16[144,512]{1,0:T(8,128)(2,1)S(1)} %get-tuple-element.22), channel_id=1, source_target_pairs={{0,6},{1,7},{2,4},{3,5},{4,2},{5,3},{6,0},{7,1},{8,14},{9,15},{10,... | collective-permute-start | bytes 442376 | tf_op jit(solution)/shard_map/ppermute | solution.py:330
  74.6 19.1 %all-to-all-start = ((f32[32,4,512]{2,1,0:T(4,128)}), f32[32,4,512]{2,1,0:T(4,128)S(1)}, u32[]{:S(2)}, u32[]{:S(2)}) async-start(f32[32,4,512]{2,1,0:T(4,128)} %get-tuple-element.23), calls=%async_computation | async-start | bytes 524288 | tf_op jit(solution)/shard_map/all_to_all | solution.py:345
  94.1 6.7 %collective-permute-start.11 = (bf16[128,512]{1,0:T(8,128)(2,1)S(1)}, bf16[128,512]{1,0:T(8,128)(2,1)S(1)}, u32[]{:S(2)}, u32[]{:S(2)}) collective-permute-start(bf16[128,512]{1,0:T(8,128)(2,1)S(1)} %gate.1.refs_0_), channel_id=1, source_target_pairs={{0,32},{32,64},{64,96},{96,128},{128,160},{160,192},{192,224},{224... | collective-permute-start | bytes 393224 | tf_op jit(solution)/shard_map/ppermute | solution.py:30
  95.2 5.6 %collective-permute-start.15 = (bf16[128,512]{1,0:T(8,128)(2,1)S(1)}, bf16[128,512]{1,0:T(8,128)(2,1)S(1)}, u32[]{:S(2)}, u32[]{:S(2)}) collective-permute-start(bf16[128,512]{1,0:T(8,128)(2,1)S(1)} %gate.1.refs_0_), channel_id=1, source_target_pairs={{0,224},{32,0},{64,32},{96,64},{128,96},{160,128},{192,160},{224,1... | collective-permute-start | bytes 393224 | tf_op jit(solution)/shard_map/ppermute | solution.py:33
  100.8 6.2 %collective-permute-start.12 = (bf16[128,512]{1,0:T(8,128)(2,1)S(1)}, bf16[128,512]{1,0:T(8,128)(2,1)S(1)}, u32[]{:S(2)}, u32[]{:S(2)}) collective-permute-start(bf16[128,512]{1,0:T(8,128)(2,1)S(1)} %collective-permute-done.11.refs_1_), channel_id=1, source_target_pairs={{0,32},{32,64},{64,96},{96,128},{128,160},{160,192},{192,224},{224... | collective-permute-start | bytes 393224 | tf_op jit(solution)/shard_map/ppermute | solution.py:30
  100.8 6.2 %collective-permute-start.16 = (bf16[128,512]{1,0:T(8,128)(2,1)S(1)}, bf16[128,512]{1,0:T(8,128)(2,1)S(1)}, u32[]{:S(2)}, u32[]{:S(2)}) collective-permute-start(bf16[128,512]{1,0:T(8,128)(2,1)S(1)} %collective-permute-done.15.refs_2_), channel_id=1, source_target_pairs={{0,224},{32,0},{64,32},{96,64},{128,96},{160,128},{192,160},{224,1... | collective-permute-start | bytes 393224 | tf_op jit(solution)/shard_map/ppermute | solution.py:33
  107.0 6.2 %collective-permute-start.13 = (bf16[128,512]{1,0:T(8,128)(2,1)S(1)}, bf16[128,512]{1,0:T(8,128)(2,1)S(1)}, u32[]{:S(2)}, u32[]{:S(2)}) collective-permute-start(bf16[128,512]{1,0:T(8,128)(2,1)S(1)} %collective-permute-done.12.refs_3_), channel_id=1, source_target_pairs={{0,32},{32,64},{64,96},{96,128},{128,160},{160,192},{192,224},{224... | collective-permute-start | bytes 393224 | tf_op jit(solution)/shard_map/ppermute | solution.py:30
  107.0 6.3 %collective-permute-start.17 = (bf16[128,512]{1,0:T(8,128)(2,1)S(1)}, bf16[128,512]{1,0:T(8,128)(2,1)S(1)}, u32[]{:S(2)}, u32[]{:S(2)}) collective-permute-start(bf16[128,512]{1,0:T(8,128)(2,1)S(1)} %collective-permute-done.16.refs_4_), channel_id=1, source_target_pairs={{0,224},{32,0},{64,32},{96,64},{128,96},{160,128},{192,160},{224,1... | collective-permute-start | bytes 393224 | tf_op jit(solution)/shard_map/ppermute | solution.py:33
  113.2 6.2 %collective-permute-start.14 = (bf16[128,512]{1,0:T(8,128)(2,1)S(1)}, bf16[128,512]{1,0:T(8,128)(2,1)S(1)}, u32[]{:S(2)}, u32[]{:S(2)}) collective-permute-start(bf16[128,512]{1,0:T(8,128)(2,1)S(1)} %collective-permute-done.13.refs_5_), channel_id=1, source_target_pairs={{0,32},{32,64},{64,96},{96,128},{128,160},{160,192},{192,224},{224... | collective-permute-start | bytes 393224 | tf_op jit(solution)/shard_map/ppermute | solution.py:30
Sparse Core Ops, SparseCore 0:
  9.2 47.6 all-gather.2
  58.8 43.9 all-gather.4

commit v8 on v5

--- a/solution.py
+++ b/solution.py
@@ -87,6 +87,14 @@
     chans = keep_ref.shape[1]
     copies = fetch(w_ref, w, sems, (0,), (chans,))
     product(lhs_ref, w, copies, chans, keep_ref, send_ref)
+
+
+def beside_kernel(x_ref, y_ref, done_ref, also_ref, out_ref, sem):
+    cols = x_ref.shape[1]
+    copy = pltpu.make_async_copy(x_ref, out_ref.at[:, pl.ds(0, cols)], sem)
+    copy.start()
+    out_ref[:, cols:] = y_ref[...]
+    copy.wait()
 
 
 def short_conv(rows, branch, total, taps_ref):
@@ -262,9 +270,6 @@
     halves = [[s for s in range(blocks) if near[s] == h] for h in range(2)]
     gather = lambda x: lax.all_gather(x, "seq", axis=0, tiled=True, axis_index_groups=halves)
     weight = gather(own_weight)
-    both = jnp.concatenate([out_weight, lax.ppermute(out_weight, "seq", pairs)], axis=1)
-    second = gather(both)
-
     rim = lax.ppermute(inputs[-2:], "seq", [(i, i + 1) for i in range(blocks - 1)])
     tokens = jnp.concatenate([inputs, rim, jnp.zeros((HALO - 2, chans), inputs.dtype)], axis=0)
     swaps = []
@@ -292,6 +297,16 @@
     params = pltpu.CompilerParams(vmem_limit_bytes=VMEM)
     shape = jax.ShapeDtypeStruct
     half = lax.rem(place, 8) // 4
+    anywhere = pl.BlockSpec(memory_space=pl.ANY)
+    both = pl.pallas_call(
+        beside_kernel,
+        in_specs=[IN_HBM, IN_VMEM, anywhere, anywhere],
+        out_shape=shape((out_weight.shape[0], 2 * out_weight.shape[1]), b16),
+        scratch_shapes=[pltpu.SemaphoreType.DMA(())],
+        compiler_params=params,
+        name="beside",
+    )(in_hbm(out_weight), lax.ppermute(out_weight, "seq", pairs), features[-2], features[-1])
+    second = gather(both)
     keep, send, lhs = pl.pallas_call(
         functools.partial(mixin_project_kernel, count),
         in_specs=[IN_SMEM] + [IN_VMEM] * count + [IN_HBM],

time: 127 us -> 124 us (0.976)
  other arithmetic: 7.38 us -> 5.05 us
  Pallas kernels: 11 us -> 12.6 us
  starting transfers between devices: 45.3 us -> 43.8 us
    ppermute x8, starting transfers between devices: 7.53 us -> 11.2 us  [ring(): below = lax.ppermute(below, axis, up)]
    all_to_all x1, starting transfers between devices: 11.2 us -> 8.04 us  [spread(): lax.all_to_all(jnp.broadcast_to(x[None], (count,) + x.shape), axis, 0, 0,...]
    ppermute x8, waiting for transfers between devices: 26.9 us -> 24 us  [ring(): below = lax.ppermute(below, axis, up)]
    ppermute x6, starting transfers between devices: 20.8 us -> 18.8 us  [ring(): above = lax.ppermute(above, axis, down)]
    concatenate x1 -> x0, other arithmetic: 1.62 us -> none  [body(): jnp.concatenate([out_weight, lax.ppermute(out_weight, 'seq', pairs)], axi...]
    pallas_call x0 -> x1, Pallas kernels: none -> 1.62 us  [body(): pl.pallas_call(beside_kernel, in_specs=[IN_HBM, IN_VMEM, anywhere, anywhe...]
    ppermute x1, starting transfers between devices: 1.58 us -> 0.01 us  [body(): lax.ppermute(out_weight, 'seq', pairs)]
    ppermute x1, starting transfers between devices: 0.09 us -> 1.61 us  [body(): more = lax.ppermute(send, 'seq', pairs)]
  transfers between devices with their start and end apart: 22 -> 22, of which waited for: 14 -> 14; matrix products, arithmetic and copies ran while one was open for 7% -> 5% of each run, Pallas kernels for 8% -> 9%
where the time goes in v8:
time: 124 us
  waiting for transfers between devices  45.8 us (37%)
  starting transfers between devices  43.8 us (35%)
  between operations  13.6 us (11%)
  Pallas kernels  12.6 us (10%)
  other arithmetic  5.05 us (4%)
  local copies, waits for them, and re-layouts  2.74 us (2%)
    ppermute x8, waiting for transfers between devices, ring(): below = lax.ppermute(below, axis, up)  24 us
    ppermute x6, starting transfers between devices, ring(): above = lax.ppermute(above, axis, down)  18.8 us
    ppermute x8, starting transfers between devices, ring(): below = lax.ppermute(below, axis, up)  11.2 us
    all_to_all x1, starting transfers between devices, spread(): lax.all_to_all(jnp.broadcast_to(x[None], (count,) + x.shape), axis, 0, 0,...  8.04 us
    ppermute x1, waiting for transfers between devices, body(): query_more = lax.ppermute(query_send, 'seq', pairs)  6.77 us
    ppermute x1, waiting for transfers between devices, body(): lax.ppermute(out_weight, 'seq', pairs)  5.18 us
    ppermute x1, waiting for transfers between devices, body(): more = lax.ppermute(send, 'seq', pairs)  4.17 us
    pallas_call x1, Pallas kernels, body(): pl.pallas_call(functools.partial(mixin_project_kernel, count), in_specs=[...  3.7 us
  transfers between devices with their start and end apart: 22, of which 14 were waited for; matrix products, arithmetic and copies ran while one was open for 5% of the time, Pallas kernels for 9%

profile of v8, /device:TPU:2, one launch (start us, length us, event | category | flops | bytes accessed | tf_op | source)
XLA Modules:
  0.0 123.7 jit_solution(9383911514251291258)
XLA Ops:
  6.5 1.1 dynamic-slice_bitcast_fusion.2
  7.6 0.8 pad_maximum_fusion
  8.4 0.0 all-gather.3.cloned.1.call-update
  8.4 0.0 all-gather.5.cloned.1.call-start
  8.5 0.7 slice.18
  9.2 1.9 %collective-permute-start = (bf16[2,512]{1,0:T(2,128)(2,1)S(1)}, bf16[2,512]{1,0:T(2,128)(2,1)S(1)}, u32[]{:S(2)}, u32[]{:S(2)}) collective-permute-start(bf16[2,512]{1,0:T(2,128)(2,1)S(1)} %slice.18), channel_id=1, source_target_pairs={{0,1},{1,2},{2,3},{3,4},{4,5},{5,6},{6,7},{7,8},{8,9},{9,10},{10,1... | collective-permute-start | bytes 6152 | tf_op jit(solution)/shard_map/ppermute | solution.py:273
  11.1 0.1 pad.15.clone
  11.2 2.9 %collective-permute-done = bf16[2,512]{1,0:T(2,128)(2,1)S(1)} collective-permute-done((bf16[2,512]{1,0:T(2,128)(2,1)S(1)}, bf16[2,512]{1,0:T(2,128)(2,1)S(1)}, u32[]{:S(2)}, u32[]{:S(2)}) %collective-permute-start) | collective-permute-done | bytes 2080 | tf_op jit(solution)/shard_map/ppermute | solution.py:273
  14.1 1.0 maximum_maximum_fusion
  15.1 0.7 collective-permute-start.1
  15.7 0.0 collective-permute-done.1.refs_0_
  15.8 9.3 %collective-permute-start.2 = (bf16[144,512]{1,0:T(8,128)(2,1)S(1)}, bf16[144,512]{1,0:T(8,128)(2,1)S(1)}, u32[]{:S(2)}, u32[]{:S(2)}) collective-permute-start(bf16[144,512]{1,0:T(8,128)(2,1)S(1)} %collective-permute-done.1.refs_0_), channel_id=1, source_target_pairs={{0,32},{32,64},{64,96},{96,128},{128,160},{160,192},{192,224},{224... | collective-permute-start | bytes 442376 | tf_op jit(solution)/shard_map/ppermute | solution.py:37
  25.1 3.8 %collective-permute-start.3 = (bf16[144,512]{1,0:T(8,128)(2,1)S(1)}, bf16[144,512]{1,0:T(8,128)(2,1)S(1)}, u32[]{:S(2)}, u32[]{:S(2)}) collective-permute-start(bf16[144,512]{1,0:T(8,128)(2,1)S(1)} %collective-permute-done.1.refs_0_), channel_id=1, source_target_pairs={{0,224},{32,0},{64,32},{96,64},{128,96},{160,128},{192,160},{224,1... | collective-permute-start | bytes 442376 | tf_op jit(solution)/shard_map/ppermute | solution.py:40
  28.9 3.1 %collective-permute-done.2.refs_1_ = bf16[144,512]{1,0:T(8,128)(2,1)S(1)} collective-permute-done((bf16[144,512]{1,0:T(8,128)(2,1)S(1)}, bf16[144,512]{1,0:T(8,128)(2,1)S(1)}, u32[]{:S(2)}, u32[]{:S(2)}) %collective-permute-start.2) | collective-permute-done | bytes 147488 | tf_op jit(solution)/shard_map/ppermute | solution.py:37
  32.0 0.0 collective-permute-start.4
  32.0 0.0 collective-permute-done.3.refs_2_
  32.0 3.2 %collective-permute-start.5 = (bf16[144,512]{1,0:T(8,128)(2,1)S(1)}, bf16[144,512]{1,0:T(8,128)(2,1)S(1)}, u32[]{:S(2)}, u32[]{:S(2)}) collective-permute-start(bf16[144,512]{1,0:T(8,128)(2,1)S(1)} %collective-permute-done.3.refs_2_), channel_id=1, source_target_pairs={{0,224},{32,0},{64,32},{96,64},{128,96},{160,128},{192,160},{224,1... | collective-permute-start | bytes 442376 | tf_op jit(solution)/shard_map/ppermute | solution.py:40
  35.2 3.1 %collective-permute-done.4.refs_3_ = bf16[144,512]{1,0:T(8,128)(2,1)S(1)} collective-permute-done((bf16[144,512]{1,0:T(8,128)(2,1)S(1)}, bf16[144,512]{1,0:T(8,128)(2,1)S(1)}, u32[]{:S(2)}, u32[]{:S(2)}) %collective-permute-start.4) | collective-permute-done | bytes 147488 | tf_op jit(solution)/shard_map/ppermute | solution.py:37
  38.3 0.0 collective-permute-start.6
  38.3 0.0 collective-permute-done.5.refs_4_
  38.3 3.5 %collective-permute-start.7 = (bf16[144,512]{1,0:T(8,128)(2,1)S(1)}, bf16[144,512]{1,0:T(8,128)(2,1)S(1)}, u32[]{:S(2)}, u32[]{:S(2)}) collective-permute-start(bf16[144,512]{1,0:T(8,128)(2,1)S(1)} %collective-permute-done.5.refs_4_), channel_id=1, source_target_pairs={{0,224},{32,0},{64,32},{96,64},{128,96},{160,128},{192,160},{224,1... | collective-permute-start | bytes 442376 | tf_op jit(solution)/shard_map/ppermute | solution.py:40
  41.9 4.1 %collective-permute-done.6.refs_5_ = bf16[144,512]{1,0:T(8,128)(2,1)S(1)} collective-permute-done((bf16[144,512]{1,0:T(8,128)(2,1)S(1)}, bf16[144,512]{1,0:T(8,128)(2,1)S(1)}, u32[]{:S(2)}, u32[]{:S(2)}) %collective-permute-start.6) | collective-permute-done | bytes 147488 | tf_op jit(solution)/shard_map/ppermute | solution.py:37
  45.9 0.0 collective-permute-start.8
  45.9 0.0 collective-permute-start.18
  45.9 5.2 %collective-permute-done.18.y_ref = bf16[128,512]{1,0:T(8,128)(2,1)S(1)} collective-permute-done((bf16[128,512]{1,0:T(8,128)(2,1)}, bf16[128,512]{1,0:T(8,128)(2,1)S(1)}, u32[]{:S(2)}, u32[]{:S(2)}) %collective-permute-start.18) | collective-permute-done | bytes 131104 | tf_op jit(solution)/shard_map/ppermute | solution.py:308
  51.1 0.0 collective-permute-done.7.refs_6_.done_ref
  51.1 1.2 collective-permute-done.8.refs_7_.also_ref
  52.3 1.6 %beside.1 = bf16[128,1024]{1,0:T(8,128)(2,1)} custom-call(bf16[128,512]{1,0:T(8,128)(2,1)} %x_ref.1, bf16[128,512]{1,0:T(8,128)(2,1)S(1)} %collective-permute-done.18.y_ref, bf16[144,512]{1,0:T(8,128)(2,1)S(1)} %collective-permute-done.7.refs_6_.done_ref, bf16[144,512]{1,0:T(8,128)(2,1)S(1)} %collective-permute-done.8.refs_7_.also_ref), custom_call_target="tpu_custom_call" | custom-call | tf_op jit(solution)/shard_map/beside/pallas_call | solution.py:301
  53.9 0.0 all-gather.5.cloned.1.call-update
  54.0 0.1 pad_add_fusion.place_ref
  54.1 0.1 multiply_bitcast_fusion.1
  54.3 0.8 fusion.3
  55.1 1.2 fusion.1
  56.3 0.6 all-gather.3.cloned.1.call-done.refs_8_.w_ref
  56.9 3.7 %project_mixin.1 = (f32[144,1024]{1,0:T(8,128)S(1)}, bf16[144,1024]{1,0:T(8,128)(2,1)S(1)}, bf16[2,144,2048]{2,1,0:T(8,128)(2,1)S(1)}) custom-call(s32[2]{0:T(128)S(1)} %pad_add_fusion.place_ref, bf16[144,512]{1,0:T(8,128)(2,1)S(1)} %collective-permute-done.1.refs_0_, bf16[144,512]{1,0:T(8,128)(2,1)S(1)} %collective-permute-done.2.refs_1_, ...), custom_call_target="tpu_custom_call" | custom-call | flops 1207959552 | bytes 4194304 | tf_op jit(solution)/shard_map/project_mixin/pallas_call | solution.py:310
  60.6 1.6 %collective-permute-start.9 = (bf16[144,1024]{1,0:T(8,128)(2,1)S(1)}, bf16[144,1024]{1,0:T(8,128)(2,1)S(1)}, u32[]{:S(2)}, u32[]{:S(2)}) collective-permute-start(bf16[144,1024]{1,0:T(8,128)(2,1)S(1)} %get-tuple-element.17), channel_id=1, source_target_pairs={{0,6},{1,7},{2,4},{3,5},{4,2},{5,3},{6,0},{7,1},{8,14},{9,15},{10,... | collective-permute-start | bytes 884744 | tf_op jit(solution)/shard_map/ppermute | solution.py:325
  62.3 1.0 fusion.jump_ref
  63.3 0.0 copy-start.5
  63.3 0.0 copy-start
  63.3 2.4 %project_query.1 = (f32[144,512]{1,0:T(8,128)S(1)}, bf16[144,512]{1,0:T(8,128)(2,1)S(1)}) custom-call(bf16[2,144,2048]{2,1,0:T(8,128)(2,1)S(1)} %get-tuple-element.18.lhs_ref, bf16[2048,1536]{1,0:T(8,128)(2,1)} %all-gather.3.cloned.1.call-done.refs_8_.w_ref), custom_call_target="tpu_custom_call" | custom-call | flops 603979776 | bytes 2097152 | tf_op jit(solution)/shard_map/project_query/pallas_call | solution.py:326
  65.7 4.2 %collective-permute-done.9.more_ref = bf16[144,1024]{1,0:T(8,128)(2,1)S(1)} collective-permute-done((bf16[144,1024]{1,0:T(8,128)(2,1)S(1)}, bf16[144,1024]{1,0:T(8,128)(2,1)S(1)}, u32[]{:S(2)}, u32[]{:S(2)}) %collective-permute-start.9) | collective-permute-done | bytes 294944 | tf_op jit(solution)/shard_map/ppermute | solution.py:325
  69.9 0.5 scan.1
  70.4 0.7 broadcast_in_dim.15
  71.2 8.0 %all-to-all-start = ((f32[32,4,512]{2,1,0:T(4,128)}), f32[32,4,512]{2,1,0:T(4,128)S(1)}, u32[]{:S(2)}, u32[]{:S(2)}) async-start(f32[32,4,512]{2,1,0:T(4,128)} %broadcast_in_dim.15), calls=%async_computation | async-start | bytes 524288 | tf_op jit(solution)/shard_map/all_to_all | solution.py:18
  79.2 1.6 %collective-permute-start.10 = (bf16[144,512]{1,0:T(8,128)(2,1)S(1)}, bf16[144,512]{1,0:T(8,128)(2,1)S(1)}, u32[]{:S(2)}, u32[]{:S(2)}) collective-permute-start(bf16[144,512]{1,0:T(8,128)(2,1)S(1)} %get-tuple-element.24), channel_id=1, source_target_pairs={{0,6},{1,7},{2,4},{3,5},{4,2},{5,3},{6,0},{7,1},{8,14},{9,15},{10,... | collective-permute-start | bytes 442376 | tf_op jit(solution)/shard_map/ppermute | solution.py:349
  80.8 6.8 %collective-permute-done.10.more_ref = bf16[144,512]{1,0:T(8,128)(2,1)S(1)} collective-permute-done((bf16[144,512]{1,0:T(8,128)(2,1)S(1)}, bf16[144,512]{1,0:T(8,128)(2,1)S(1)}, u32[]{:S(2)}, u32[]{:S(2)}) %collective-permute-start.10) | collective-permute-done | bytes 147488 | tf_op jit(solution)/shard_map/ppermute | solution.py:349
  87.6 2.2 %all-to-all-done.all_ref = f32[32,4,512]{2,1,0:T(4,128)S(1)} async-done(((f32[32,4,512]{2,1,0:T(4,128)}), f32[32,4,512]{2,1,0:T(4,128)S(1)}, u32[]{:S(2)}, u32[]{:S(2)}) %all-to-all-start) | async-done | bytes 262176 | tf_op jit(solution)/shard_map/all_to_all | solution.py:18
  89.7 0.5 gate.1.refs_0_
  90.3 1.8 %collective-permute-start.11 = (bf16[128,512]{1,0:T(8,128)(2,1)S(1)}, bf16[128,512]{1,0:T(8,128)(2,1)S(1)}, u32[]{:S(2)}, u32[]{:S(2)}) collective-permute-start(bf16[128,512]{1,0:T(8,128)(2,1)S(1)} %gate.1.refs_0_), channel_id=1, source_target_pairs={{0,32},{32,64},{64,96},{96,128},{128,160},{160,192},{192,224},{224... | collective-permute-start | bytes 393224 | tf_op jit(solution)/shard_map/ppermute | solution.py:37
  92.1 1.9 %collective-permute-start.15 = (bf16[128,512]{1,0:T(8,128)(2,1)S(1)}, bf16[128,512]{1,0:T(8,128)(2,1)S(1)}, u32[]{:S(2)}, u32[]{:S(2)}) collective-permute-start(bf16[128,512]{1,0:T(8,128)(2,1)S(1)} %gate.1.refs_0_), channel_id=1, source_target_pairs={{0,224},{32,0},{64,32},{96,64},{128,96},{160,128},{192,160},{224,1... | collective-permute-start | bytes 393224 | tf_op jit(solution)/shard_map/ppermute | solution.py:40
  93.9 3.5 %collective-permute-done.11.refs_1_ = bf16[128,512]{1,0:T(8,128)(2,1)S(1)} collective-permute-done((bf16[128,512]{1,0:T(8,128)(2,1)S(1)}, bf16[128,512]{1,0:T(8,128)(2,1)S(1)}, u32[]{:S(2)}, u32[]{:S(2)}) %collective-permute-start.11) | collective-permute-done | bytes 131104 | tf_op jit(solution)/shard_map/ppermute | solution.py:37
  97.4 0.0 collective-permute-start.12
  97.4 0.0 collective-permute-done.15.refs_2_
  97.4 3.2 %collective-permute-start.16 = (bf16[128,512]{1,0:T(8,128)(2,1)S(1)}, bf16[128,512]{1,0:T(8,128)(2,1)S(1)}, u32[]{:S(2)}, u32[]{:S(2)}) collective-permute-start(bf16[128,512]{1,0:T(8,128)(2,1)S(1)} %collective-permute-done.15.refs_2_), channel_id=1, source_target_pairs={{0,224},{32,0},{64,32},{96,64},{128,96},{160,128},{192,160},{224,1... | collective-permute-start | bytes 393224 | tf_op jit(solution)/shard_map/ppermute | solution.py:40
  100.6 2.9 %collective-permute-done.12.refs_3_ = bf16[128,512]{1,0:T(8,128)(2,1)S(1)} collective-permute-done((bf16[128,512]{1,0:T(8,128)(2,1)S(1)}, bf16[128,512]{1,0:T(8,128)(2,1)S(1)}, u32[]{:S(2)}, u32[]{:S(2)}) %collective-permute-start.12) | collective-permute-done | bytes 131104 | tf_op jit(solution)/shard_map/ppermute | solution.py:37
  103.6 0.0 collective-permute-start.13
  103.6 0.0 collective-permute-done.16.refs_4_
  103.6 3.2 %collective-permute-start.17 = (bf16[128,512]{1,0:T(8,128)(2,1)S(1)}, bf16[128,512]{1,0:T(8,128)(2,1)S(1)}, u32[]{:S(2)}, u32[]{:S(2)}) collective-permute-start(bf16[128,512]{1,0:T(8,128)(2,1)S(1)} %collective-permute-done.16.refs_4_), channel_id=1, source_target_pairs={{0,224},{32,0},{64,32},{96,64},{128,96},{160,128},{192,160},{224,1... | collective-permute-start | bytes 393224 | tf_op jit(solution)/shard_map/ppermute | solution.py:40
  106.8 2.9 %collective-permute-done.13.refs_5_ = bf16[128,512]{1,0:T(8,128)(2,1)S(1)} collective-permute-done((bf16[128,512]{1,0:T(8,128)(2,1)S(1)}, bf16[128,512]{1,0:T(8,128)(2,1)S(1)}, u32[]{:S(2)}, u32[]{:S(2)}) %collective-permute-start.13) | collective-permute-done | bytes 131104 | tf_op jit(solution)/shard_map/ppermute | solution.py:37
  109.8 0.0 collective-permute-start.14
  109.8 0.1 stack.48.which_ref
  109.9 2.9 %mix.1 = (f32[128,512]{1,0:T(8,128)S(1)}, bf16[512,512]{1,0:T(8,128)(2,1)S(1)}) custom-call(s32[9]{0:T(128)S(1)} %stack.48.which_ref, bf16[128,512]{1,0:T(8,128)(2,1)S(1)} %gate.1.refs_0_, bf16[128,512]{1,0:T(8,128)(2,1)S(1)} %collective-permute-done.11.refs_1_, bf16[128,512]{1,0:T(8,128)(2,1)S(1)} %collective-permute-done.15.refs_2_, ...), custom_call_target="tpu_custom_call" | custom-call | flops 536870912 | bytes 4194304 | tf_op jit(solution)/shard_map/mix/pallas_call | solution.py:239
  112.8 3.1 %collective-permute-done.14.x_ref = bf16[128,512]{1,0:T(8,128)(2,1)S(1)} collective-permute-done((bf16[128,512]{1,0:T(8,128)(2,1)S(1)}, bf16[128,512]{1,0:T(8,128)(2,1)S(1)}, u32[]{:S(2)}, u32[]{:S(2)}) %collective-permute-start.14) | collective-permute-done | bytes 131104 | tf_op jit(solution)/shard_map/ppermute | solution.py:37
  115.9 0.9 last_mix.1
  (25 shorter events, 0.1 us)
Async XLA Ops:
  6.5 47.5 %copy-start.3 = (f32[512,2]{0,1:T(2,128)S(1)}, f32[512,2]{0,1:T(2,128)}, u32[]{:S(2)}) copy-start(f32[512,2]{0,1:T(2,128)} %param.12) | copy-start | bytes 12292
  6.5 47.5 %copy-start.2 = (f32[512,2]{0,1:T(2,128)S(1)}, f32[512,2]{0,1:T(2,128)}, u32[]{:S(2)}) copy-start(f32[512,2]{0,1:T(2,128)} %param.13) | copy-start | bytes 12292
  6.5 50.4 %all-gather.3.cloned.1.call-start = ((), (), s32[]{:S(2)}) async-start(), calls=%async_computation.1 | async-start | bytes 6684672 | tf_op jit(solution)/shard_map/all_gather | solution.py:271
  8.4 101.4 %all-gather.5.cloned.1.call-start = ((), (), s32[]{:S(2)}) async-start(), calls=%async_computation.2 | async-start | bytes 4456448 | tf_op jit(solution)/shard_map/all_gather | solution.py:271
  9.2 4.9 %collective-permute-start = (bf16[2,512]{1,0:T(2,128)(2,1)S(1)}, bf16[2,512]{1,0:T(2,128)(2,1)S(1)}, u32[]{:S(2)}, u32[]{:S(2)}) collective-permute-start(bf16[2,512]{1,0:T(2,128)(2,1)S(1)} %slice.18), channel_id=1, source_target_pairs={{0,1},{1,2},{2,3},{3,4},{4,5},{5,6},{6,7},{7,8},{8,9},{9,10},{10,1... | collective-permute-start | bytes 6152 | tf_op jit(solution)/shard_map/ppermute | solution.py:273
  15.1 0.7 collective-permute-start.1
  15.8 16.2 %collective-permute-start.2 = (bf16[144,512]{1,0:T(8,128)(2,1)S(1)}, bf16[144,512]{1,0:T(8,128)(2,1)S(1)}, u32[]{:S(2)}, u32[]{:S(2)}) collective-permute-start(bf16[144,512]{1,0:T(8,128)(2,1)S(1)} %collective-permute-done.1.refs_0_), channel_id=1, source_target_pairs={{0,32},{32,64},{64,96},{96,128},{128,160},{160,192},{192,224},{224... | collective-permute-start | bytes 442376 | tf_op jit(solution)/shard_map/ppermute | solution.py:37
  25.1 6.9 %collective-permute-start.3 = (bf16[144,512]{1,0:T(8,128)(2,1)S(1)}, bf16[144,512]{1,0:T(8,128)(2,1)S(1)}, u32[]{:S(2)}, u32[]{:S(2)}) collective-permute-start(bf16[144,512]{1,0:T(8,128)(2,1)S(1)} %collective-permute-done.1.refs_0_), channel_id=1, source_target_pairs={{0,224},{32,0},{64,32},{96,64},{128,96},{160,128},{192,160},{224,1... | collective-permute-start | bytes 442376 | tf_op jit(solution)/shard_map/ppermute | solution.py:40
  32.0 6.4 %collective-permute-start.4 = (bf16[144,512]{1,0:T(8,128)(2,1)S(1)}, bf16[144,512]{1,0:T(8,128)(2,1)S(1)}, u32[]{:S(2)}, u32[]{:S(2)}) collective-permute-start(bf16[144,512]{1,0:T(8,128)(2,1)S(1)} %collective-permute-done.2.refs_1_), channel_id=1, source_target_pairs={{0,32},{32,64},{64,96},{96,128},{128,160},{160,192},{192,224},{224... | collective-permute-start | bytes 442376 | tf_op jit(solution)/shard_map/ppermute | solution.py:37
  32.0 6.4 %collective-permute-start.5 = (bf16[144,512]{1,0:T(8,128)(2,1)S(1)}, bf16[144,512]{1,0:T(8,128)(2,1)S(1)}, u32[]{:S(2)}, u32[]{:S(2)}) collective-permute-start(bf16[144,512]{1,0:T(8,128)(2,1)S(1)} %collective-permute-done.3.refs_2_), channel_id=1, source_target_pairs={{0,224},{32,0},{64,32},{96,64},{128,96},{160,128},{192,160},{224,1... | collective-permute-start | bytes 442376 | tf_op jit(solution)/shard_map/ppermute | solution.py:40
  38.3 7.6 %collective-permute-start.6 = (bf16[144,512]{1,0:T(8,128)(2,1)S(1)}, bf16[144,512]{1,0:T(8,128)(2,1)S(1)}, u32[]{:S(2)}, u32[]{:S(2)}) collective-permute-start(bf16[144,512]{1,0:T(8,128)(2,1)S(1)} %collective-permute-done.4.refs_3_), channel_id=1, source_target_pairs={{0,32},{32,64},{64,96},{96,128},{128,160},{160,192},{192,224},{224... | collective-permute-start | bytes 442376 | tf_op jit(solution)/shard_map/ppermute | solution.py:37
  38.3 12.8 %collective-permute-start.7 = (bf16[144,512]{1,0:T(8,128)(2,1)S(1)}, bf16[144,512]{1,0:T(8,128)(2,1)S(1)}, u32[]{:S(2)}, u32[]{:S(2)}) collective-permute-start(bf16[144,512]{1,0:T(8,128)(2,1)S(1)} %collective-permute-done.5.refs_4_), channel_id=1, source_target_pairs={{0,224},{32,0},{64,32},{96,64},{128,96},{160,128},{192,160},{224,1... | collective-permute-start | bytes 442376 | tf_op jit(solution)/shard_map/ppermute | solution.py:40
  45.9 6.4 %collective-permute-start.8 = (bf16[144,512]{1,0:T(8,128)(2,1)S(1)}, bf16[144,512]{1,0:T(8,128)(2,1)S(1)}, u32[]{:S(2)}, u32[]{:S(2)}) collective-permute-start(bf16[144,512]{1,0:T(8,128)(2,1)S(1)} %collective-permute-done.6.refs_5_), channel_id=1, source_target_pairs={{0,32},{32,64},{64,96},{96,128},{128,160},{160,192},{192,224},{224... | collective-permute-start | bytes 442376 | tf_op jit(solution)/shard_map/ppermute | solution.py:37
  45.9 5.2 %collective-permute-start.18 = (bf16[128,512]{1,0:T(8,128)(2,1)}, bf16[128,512]{1,0:T(8,128)(2,1)S(1)}, u32[]{:S(2)}, u32[]{:S(2)}) collective-permute-start(bf16[128,512]{1,0:T(8,128)(2,1)} %x_ref.1), channel_id=1, source_target_pairs={{0,6},{1,7},{2,4},{3,5},{4,2},{5,3},{6,0},{7,1},{8,14},{9,15},{10,... | collective-permute-start | bytes 393224 | tf_op jit(solution)/shard_map/ppermute | solution.py:308
  56.3 6.0 %copy-start.4 = (f32[3,3,512]{2,1,0:T(4,128)S(1)}, f32[3,3,512]{2,1,0:T(4,128)}, u32[]{:S(2)}) copy-start(f32[3,3,512]{2,1,0:T(4,128)} %param.11) | copy-start | bytes 55300
  60.6 9.2 %collective-permute-start.9 = (bf16[144,1024]{1,0:T(8,128)(2,1)S(1)}, bf16[144,1024]{1,0:T(8,128)(2,1)S(1)}, u32[]{:S(2)}, u32[]{:S(2)}) collective-permute-start(bf16[144,1024]{1,0:T(8,128)(2,1)S(1)} %get-tuple-element.17), channel_id=1, source_target_pairs={{0,6},{1,7},{2,4},{3,5},{4,2},{5,3},{6,0},{7,1},{8,14},{9,15},{10,... | collective-permute-start | bytes 884744 | tf_op jit(solution)/shard_map/ppermute | solution.py:325
  63.3 15.9 %copy-start.5 = (f32[2,512,2]{1,2,0:T(2,128)S(1)}, f32[2,512,2]{1,2,0:T(2,128)}, u32[]{:S(2)}) copy-start(f32[2,512,2]{1,2,0:T(2,128)} %param.14) | copy-start | bytes 24580
  63.3 17.5 %copy-start.1 = (f32[8,2,512]{2,0,1:T(8,128)S(1)}, f32[8,2,512]{2,0,1:T(8,128)}, u32[]{:S(2)}) copy-start(f32[8,2,512]{2,0,1:T(8,128)} %get-tuple-element.31) | copy-start | bytes 98308
  63.3 26.5 %copy-start = (f32[512]{0:T(512)S(1)}, f32[512]{0:T(512)}, u32[]{:S(2)}) copy-start(f32[512]{0:T(512)} %param.15) | copy-start | bytes 6148
  71.2 18.6 %all-to-all-start = ((f32[32,4,512]{2,1,0:T(4,128)}), f32[32,4,512]{2,1,0:T(4,128)S(1)}, u32[]{:S(2)}, u32[]{:S(2)}) async-start(f32[32,4,512]{2,1,0:T(4,128)} %broadcast_in_dim.15), calls=%async_computation | async-start | bytes 524288 | tf_op jit(solution)/shard_map/all_to_all | solution.py:18
  79.2 8.3 %collective-permute-start.10 = (bf16[144,512]{1,0:T(8,128)(2,1)S(1)}, bf16[144,512]{1,0:T(8,128)(2,1)S(1)}, u32[]{:S(2)}, u32[]{:S(2)}) collective-permute-start(bf16[144,512]{1,0:T(8,128)(2,1)S(1)} %get-tuple-element.24), channel_id=1, source_target_pairs={{0,6},{1,7},{2,4},{3,5},{4,2},{5,3},{6,0},{7,1},{8,14},{9,15},{10,... | collective-permute-start | bytes 442376 | tf_op jit(solution)/shard_map/ppermute | solution.py:349
  90.3 7.1 %collective-permute-start.11 = (bf16[128,512]{1,0:T(8,128)(2,1)S(1)}, bf16[128,512]{1,0:T(8,128)(2,1)S(1)}, u32[]{:S(2)}, u32[]{:S(2)}) collective-permute-start(bf16[128,512]{1,0:T(8,128)(2,1)S(1)} %gate.1.refs_0_), channel_id=1, source_target_pairs={{0,32},{32,64},{64,96},{96,128},{128,160},{160,192},{192,224},{224... | collective-permute-start | bytes 393224 | tf_op jit(solution)/shard_map/ppermute | solution.py:37
  92.1 5.3 %collective-permute-start.15 = (bf16[128,512]{1,0:T(8,128)(2,1)S(1)}, bf16[128,512]{1,0:T(8,128)(2,1)S(1)}, u32[]{:S(2)}, u32[]{:S(2)}) collective-permute-start(bf16[128,512]{1,0:T(8,128)(2,1)S(1)} %gate.1.refs_0_), channel_id=1, source_target_pairs={{0,224},{32,0},{64,32},{96,64},{128,96},{160,128},{192,160},{224,1... | collective-permute-start | bytes 393224 | tf_op jit(solution)/shard_map/ppermute | solution.py:40
  97.4 6.2 %collective-permute-start.12 = (bf16[128,512]{1,0:T(8,128)(2,1)S(1)}, bf16[128,512]{1,0:T(8,128)(2,1)S(1)}, u32[]{:S(2)}, u32[]{:S(2)}) collective-permute-start(bf16[128,512]{1,0:T(8,128)(2,1)S(1)} %collective-permute-done.11.refs_1_), channel_id=1, source_target_pairs={{0,32},{32,64},{64,96},{96,128},{128,160},{160,192},{192,224},{224... | collective-permute-start | bytes 393224 | tf_op jit(solution)/shard_map/ppermute | solution.py:37
  97.4 6.2 %collective-permute-start.16 = (bf16[128,512]{1,0:T(8,128)(2,1)S(1)}, bf16[128,512]{1,0:T(8,128)(2,1)S(1)}, u32[]{:S(2)}, u32[]{:S(2)}) collective-permute-start(bf16[128,512]{1,0:T(8,128)(2,1)S(1)} %collective-permute-done.15.refs_2_), channel_id=1, source_target_pairs={{0,224},{32,0},{64,32},{96,64},{128,96},{160,128},{192,160},{224,1... | collective-permute-start | bytes 393224 | tf_op jit(solution)/shard_map/ppermute | solution.py:40
  103.6 6.2 %collective-permute-start.13 = (bf16[128,512]{1,0:T(8,128)(2,1)S(1)}, bf16[128,512]{1,0:T(8,128)(2,1)S(1)}, u32[]{:S(2)}, u32[]{:S(2)}) collective-permute-start(bf16[128,512]{1,0:T(8,128)(2,1)S(1)} %collective-permute-done.12.refs_3_), channel_id=1, source_target_pairs={{0,32},{32,64},{64,96},{96,128},{128,160},{160,192},{192,224},{224... | collective-permute-start | bytes 393224 | tf_op jit(solution)/shard_map/ppermute | solution.py:37
  103.6 6.3 %collective-permute-start.17 = (bf16[128,512]{1,0:T(8,128)(2,1)S(1)}, bf16[128,512]{1,0:T(8,128)(2,1)S(1)}, u32[]{:S(2)}, u32[]{:S(2)}) collective-permute-start(bf16[128,512]{1,0:T(8,128)(2,1)S(1)} %collective-permute-done.16.refs_4_), channel_id=1, source_target_pairs={{0,224},{32,0},{64,32},{96,64},{128,96},{160,128},{192,160},{224,1... | collective-permute-start | bytes 393224 | tf_op jit(solution)/shard_map/ppermute | solution.py:40
  109.8 6.2 %collective-permute-start.14 = (bf16[128,512]{1,0:T(8,128)(2,1)S(1)}, bf16[128,512]{1,0:T(8,128)(2,1)S(1)}, u32[]{:S(2)}, u32[]{:S(2)}) collective-permute-start(bf16[128,512]{1,0:T(8,128)(2,1)S(1)} %collective-permute-done.13.refs_5_), channel_id=1, source_target_pairs={{0,32},{32,64},{64,96},{96,128},{128,160},{160,192},{192,224},{224... | collective-permute-start | bytes 393224 | tf_op jit(solution)/shard_map/ppermute | solution.py:37
Sparse Core Ops, SparseCore 0:
  9.2 47.6 all-gather.2
  58.8 43.1 all-gather.4

commit v9 on v8

--- a/solution.py
+++ b/solution.py
@@ -89,7 +89,7 @@
     product(lhs_ref, w, copies, chans, keep_ref, send_ref)
 
 
-def beside_kernel(x_ref, y_ref, done_ref, also_ref, out_ref, sem):
+def beside_kernel(x_ref, y_ref, out_ref, sem):
     cols = x_ref.shape[1]
     copy = pltpu.make_async_copy(x_ref, out_ref.at[:, pl.ds(0, cols)], sem)
     copy.start()
@@ -270,16 +270,21 @@
     halves = [[s for s in range(blocks) if near[s] == h] for h in range(2)]
     gather = lambda x: lax.all_gather(x, "seq", axis=0, tiled=True, axis_index_groups=halves)
     weight = gather(own_weight)
+    f32, b16 = jnp.float32, jnp.bfloat16
+    padded, depth = rows + HALO, chans * count // 2
+    params = pltpu.CompilerParams(vmem_limit_bytes=VMEM)
+    shape = jax.ShapeDtypeStruct
+    half = lax.rem(place, 8) // 4
     rim = lax.ppermute(inputs[-2:], "seq", [(i, i + 1) for i in range(blocks - 1)])
+    mirrored = lax.ppermute(out_weight, "seq", pairs)
+    rim, mirrored = lax.optimization_barrier((rim, mirrored))
     tokens = jnp.concatenate([inputs, rim, jnp.zeros((HALO - 2, chans), inputs.dtype)], axis=0)
     swaps = []
     for c in range(count):
         for s in range(blocks):
             to = (c, s) if c % 2 == near[s] else (c ^ 1, mirror[s])
             swaps.append((c * blocks + s, to[0] * blocks + to[1]))
-    features = ring(lax.ppermute(tokens, ("ch", "seq"), swaps), "ch")
-    here = lax.axis_index("ch")
-
+    swapped = lax.ppermute(tokens, ("ch", "seq"), swaps)
     rate, turn = decay.T, angle.T
     length = rows // SUB
     pack = lambda pair: jnp.concatenate(pair, axis=1)
@@ -291,22 +296,20 @@
     jump = pack(powers((jnp.maximum(gap, 0) * rows).astype(jnp.float32), rate, turn))
     jump = jnp.where((gap >= 0)[:, None, None], jump, 0.0).transpose(1, 0, 2)
     poles = jnp.concatenate([residue[0].T, residue[1].T], axis=0)
-
-    f32, b16 = jnp.float32, jnp.bfloat16
-    padded, depth = rows + HALO, chans * count // 2
-    params = pltpu.CompilerParams(vmem_limit_bytes=VMEM)
-    shape = jax.ShapeDtypeStruct
-    half = lax.rem(place, 8) // 4
-    anywhere = pl.BlockSpec(memory_space=pl.ANY)
     both = pl.pallas_call(
         beside_kernel,
-        in_specs=[IN_HBM, IN_VMEM, anywhere, anywhere],
+        in_specs=[IN_HBM, IN_VMEM],
         out_shape=shape((out_weight.shape[0], 2 * out_weight.shape[1]), b16),
         scratch_shapes=[pltpu.SemaphoreType.DMA(())],
         compiler_params=params,
         name="beside",
-    )(in_hbm(out_weight), lax.ppermute(out_weight, "seq", pairs), features[-2], features[-1])
+    )(in_hbm(out_weight), mirrored)
+    tied = lax.optimization_barrier((swapped, both, step, join, reach, jump, poles))
+    swapped, both, step, join, reach, jump, poles = tied
     second = gather(both)
+    features = ring(swapped, "ch")
+    here = lax.axis_index("ch")
+
     keep, send, lhs = pl.pallas_call(
         functools.partial(mixin_project_kernel, count),
         in_specs=[IN_SMEM] + [IN_VMEM] * count + [IN_HBM],

time: 124 us -> 125 us (level)
  waiting for transfers between devices: 45.8 us -> 44.1 us
    ppermute x2, waiting for transfers between devices: 5.18 us -> 0.01 us  [the longest x1 0.01 us: body(): mirrored = lax.ppermute(out_weight, 'seq', pairs)]
    ppermute x8, waiting for transfers between devices: 24 us -> 28.2 us  [ring(): below = lax.ppermute(below, axis, up)]
    ppermute x1, waiting for transfers between devices: 2.89 us -> 0.01 us  [body(): lax.ppermute(inputs[-2:], 'seq', [(i, i + 1) for i in range(blocks - 1)])]
    ppermute x2, starting transfers between devices: 0.67 us -> 2.25 us  [the longest x1 1.58 us: body(): mirrored = lax.ppermute(out_weight, 'seq', pairs)]
  transfers between devices with their start and end apart: 22 -> 22, of which waited for: 14 -> 12; matrix products, arithmetic and copies ran while one was open for 5% -> 5% of each run, Pallas kernels for 9% -> 10%
where the time goes in v9:
time: 125 us; the launch traced here: 124 us
  starting transfers between devices  44.9 us (36%)
  waiting for transfers between devices  44.1 us (35%)
  between operations  13.6 us (11%)
  Pallas kernels  13.3 us (11%)
  other arithmetic  5.03 us (4%)
  local copies, waits for them, and re-layouts  3.4 us (3%)
    ppermute x8, waiting for transfers between devices, ring(): below = lax.ppermute(below, axis, up)  28.2 us
    ppermute x6, starting transfers between devices, ring(): above = lax.ppermute(above, axis, down)  18.6 us
    ppermute x8, starting transfers between devices, ring(): below = lax.ppermute(below, axis, up)  10.8 us
    all_to_all x1, starting transfers between devices, spread(): lax.all_to_all(jnp.broadcast_to(x[None], (count,) + x.shape), axis, 0, 0,...  8.04 us
    ppermute x1, waiting for transfers between devices, body(): query_more = lax.ppermute(query_send, 'seq', pairs)  6.84 us
    ppermute x1, waiting for transfers between devices, body(): more = lax.ppermute(send, 'seq', pairs)  5.42 us
    pallas_call x1, Pallas kernels, body(): pl.pallas_call(functools.partial(mixin_project_kernel, count), in_specs=[...  4.43 us
    mul x3, other arithmetic, powers(): return (mag * jnp.cos(phase), mag * jnp.sin(phase))  3.01 us
  transfers between devices with their start and end apart: 22, of which 12 were waited for; matrix products, arithmetic and copies ran while one was open for 5% of the time, Pallas kernels for 10%

profile of v9, /device:TPU:2, one launch (start us, length us, event | category | flops | bytes accessed | tf_op | source)
XLA Modules:
  0.0 124.3 jit_solution(12800483405211552884)
XLA Ops:
  6.5 1.1 dynamic-slice_bitcast_fusion.2
  7.6 0.8 pad_maximum_fusion
  8.4 0.0 all-gather.3.cloned.1.call-update
  8.4 0.0 all-gather.5.cloned.1.call-start
  8.5 1.6 %collective-permute-start.1 = (bf16[128,512]{1,0:T(8,128)(2,1)}, bf16[128,512]{1,0:T(8,128)(2,1)S(1)}, u32[]{:S(2)}, u32[]{:S(2)}) collective-permute-start(bf16[128,512]{1,0:T(8,128)(2,1)} %x_ref.1), channel_id=1, source_target_pairs={{0,6},{1,7},{2,4},{3,5},{4,2},{5,3},{6,0},{7,1},{8,14},{9,15},{10,... | collective-permute-start | bytes 393224 | tf_op jit(solution)/shard_map/ppermute | solution.py:279
  10.1 0.7 slice.18
  10.8 1.9 %collective-permute-start = (bf16[2,512]{1,0:T(2,128)(2,1)S(1)}, bf16[2,512]{1,0:T(2,128)(2,1)S(1)}, u32[]{:S(2)}, u32[]{:S(2)}) collective-permute-start(bf16[2,512]{1,0:T(2,128)(2,1)S(1)} %slice.18), channel_id=1, source_target_pairs={{0,1},{1,2},{2,3},{3,4},{4,5},{5,6},{6,7},{7,8},{8,9},{9,10},{10,1... | collective-permute-start | bytes 6152 | tf_op jit(solution)/shard_map/ppermute | solution.py:278
  12.7 0.8 multiply_bitcast_fusion.1
  13.6 0.9 fusion.3
  14.5 1.3 %fusion.1 = (f32[32,2,512]{2,0,1:T(8,128)S(1)}, f32[32,2,512]{2,0,1:T(8,128)S(1)}) fusion(f32[2,512]{1,0:T(2,128)} %bitcast.53, f32[32]{0:T(128)S(1)} %multiply_convert_fusion, f32[2,512]{1,0:T(2,128)} %bitcast.55, f32[32]{0:T(128)S(1)} %fusion.7), kind=kLoop, calls=%fused_computation.6 | loop fusion | flops 131072 | bytes 270592 | tf_op jit(solution)/shard_map/mul | solution.py:48
  15.8 0.1 fusion.jump_ref
  15.9 0.7 slice_bitcast_fusion.1
  16.6 0.1 pad.15.clone
  16.7 0.0 collective-permute-done
  16.7 0.0 collective-permute-done.1.y_ref
  16.7 1.0 maximum_maximum_fusion
  17.7 0.7 collective-permute-start.2
  18.4 1.6 %beside.1 = bf16[128,1024]{1,0:T(8,128)(2,1)} custom-call(bf16[128,512]{1,0:T(8,128)(2,1)} %x_ref.1, bf16[128,512]{1,0:T(8,128)(2,1)S(1)} %collective-permute-done.1.y_ref), custom_call_target="tpu_custom_call" | custom-call | tf_op jit(solution)/shard_map/beside/pallas_call | solution.py:299
  20.0 0.0 collective-permute-done.2.refs_0_
  20.0 0.0 all-gather.5.cloned.1.call-update
  20.0 8.8 %collective-permute-start.3 = (bf16[144,512]{1,0:T(8,128)(2,1)S(1)}, bf16[144,512]{1,0:T(8,128)(2,1)S(1)}, u32[]{:S(2)}, u32[]{:S(2)}) collective-permute-start(bf16[144,512]{1,0:T(8,128)(2,1)S(1)} %collective-permute-done.2.refs_0_), channel_id=1, source_target_pairs={{0,32},{32,64},{64,96},{96,128},{128,160},{160,192},{192,224},{224... | collective-permute-start | bytes 442376 | tf_op jit(solution)/shard_map/ppermute | solution.py:37
  28.9 4.0 %collective-permute-start.4 = (bf16[144,512]{1,0:T(8,128)(2,1)S(1)}, bf16[144,512]{1,0:T(8,128)(2,1)S(1)}, u32[]{:S(2)}, u32[]{:S(2)}) collective-permute-start(bf16[144,512]{1,0:T(8,128)(2,1)S(1)} %collective-permute-done.2.refs_0_), channel_id=1, source_target_pairs={{0,224},{32,0},{64,32},{96,64},{128,96},{160,128},{192,160},{224,1... | collective-permute-start | bytes 442376 | tf_op jit(solution)/shard_map/ppermute | solution.py:40
  32.9 3.7 %collective-permute-done.3.refs_1_ = bf16[144,512]{1,0:T(8,128)(2,1)S(1)} collective-permute-done((bf16[144,512]{1,0:T(8,128)(2,1)S(1)}, bf16[144,512]{1,0:T(8,128)(2,1)S(1)}, u32[]{:S(2)}, u32[]{:S(2)}) %collective-permute-start.3) | collective-permute-done | bytes 147488 | tf_op jit(solution)/shard_map/ppermute | solution.py:37
  36.6 0.0 collective-permute-start.5
  36.6 0.0 collective-permute-done.4.refs_2_
  36.6 3.2 %collective-permute-start.6 = (bf16[144,512]{1,0:T(8,128)(2,1)S(1)}, bf16[144,512]{1,0:T(8,128)(2,1)S(1)}, u32[]{:S(2)}, u32[]{:S(2)}) collective-permute-start(bf16[144,512]{1,0:T(8,128)(2,1)S(1)} %collective-permute-done.4.refs_2_), channel_id=1, source_target_pairs={{0,224},{32,0},{64,32},{96,64},{128,96},{160,128},{192,160},{224,1... | collective-permute-start | bytes 442376 | tf_op jit(solution)/shard_map/ppermute | solution.py:40
  39.8 3.1 %collective-permute-done.5.refs_3_ = bf16[144,512]{1,0:T(8,128)(2,1)S(1)} collective-permute-done((bf16[144,512]{1,0:T(8,128)(2,1)S(1)}, bf16[144,512]{1,0:T(8,128)(2,1)S(1)}, u32[]{:S(2)}, u32[]{:S(2)}) %collective-permute-start.5) | collective-permute-done | bytes 147488 | tf_op jit(solution)/shard_map/ppermute | solution.py:37
  43.0 0.0 collective-permute-start.7
  43.0 0.0 collective-permute-done.6.refs_4_
  43.0 3.2 %collective-permute-start.8 = (bf16[144,512]{1,0:T(8,128)(2,1)S(1)}, bf16[144,512]{1,0:T(8,128)(2,1)S(1)}, u32[]{:S(2)}, u32[]{:S(2)}) collective-permute-start(bf16[144,512]{1,0:T(8,128)(2,1)S(1)} %collective-permute-done.6.refs_4_), channel_id=1, source_target_pairs={{0,224},{32,0},{64,32},{96,64},{128,96},{160,128},{192,160},{224,1... | collective-permute-start | bytes 442376 | tf_op jit(solution)/shard_map/ppermute | solution.py:40
  46.2 3.1 %collective-permute-done.7.refs_5_ = bf16[144,512]{1,0:T(8,128)(2,1)S(1)} collective-permute-done((bf16[144,512]{1,0:T(8,128)(2,1)S(1)}, bf16[144,512]{1,0:T(8,128)(2,1)S(1)}, u32[]{:S(2)}, u32[]{:S(2)}) %collective-permute-start.7) | collective-permute-done | bytes 147488 | tf_op jit(solution)/shard_map/ppermute | solution.py:37
  49.3 0.0 collective-permute-start.9
  49.3 0.1 pad_add_fusion.place_ref
  49.4 0.0 collective-permute-done.8.refs_6_
  49.4 6.3 %collective-permute-done.9.refs_7_ = bf16[144,512]{1,0:T(8,128)(2,1)S(1)} collective-permute-done((bf16[144,512]{1,0:T(8,128)(2,1)S(1)}, bf16[144,512]{1,0:T(8,128)(2,1)S(1)}, u32[]{:S(2)}, u32[]{:S(2)}) %collective-permute-start.9) | collective-permute-done | bytes 147488 | tf_op jit(solution)/shard_map/ppermute | solution.py:37
  55.7 1.2 %all-gather.3.cloned.1.call-done.refs_8_.w_ref = bf16[2048,1536]{1,0:T(8,128)(2,1)} async-done(((bf16[128,1536]{1,0:T(8,128)(2,1)}), bf16[2048,1536]{1,0:T(8,128)(2,1)}) %all-gather.3.cloned.1.call-update) | async-done | bytes 6291472 | tf_op jit(solution)/shard_map/all_gather | solution.py:271
  56.9 4.4 %project_mixin.1 = (f32[144,1024]{1,0:T(8,128)S(1)}, bf16[144,1024]{1,0:T(8,128)(2,1)}, bf16[2,144,2048]{2,1,0:T(8,128)(2,1)S(1)}) custom-call(s32[2]{0:T(128)S(1)} %pad_add_fusion.place_ref, bf16[144,512]{1,0:T(8,128)(2,1)S(1)} %collective-permute-done.2.refs_0_, bf16[144,512]{1,0:T(8,128)(2,1)S(1)} %collective-permute-done.3.refs_1_, ...), custom_call_target="tpu_custom_call" | custom-call | flops 1207959552 | bytes 4194304 | tf_op jit(solution)/shard_map/project_mixin/pallas_call | solution.py:313
  61.4 1.6 %collective-permute-start.10 = (bf16[144,1024]{1,0:T(8,128)(2,1)}, bf16[144,1024]{1,0:T(8,128)(2,1)S(1)}, u32[]{:S(2)}, u32[]{:S(2)}) collective-permute-start(bf16[144,1024]{1,0:T(8,128)(2,1)} %get-tuple-element.29), channel_id=1, source_target_pairs={{0,6},{1,7},{2,4},{3,5},{4,2},{5,3},{6,0},{7,1},{8,14},{9,15},{10,... | collective-permute-start | bytes 884744 | tf_op jit(solution)/shard_map/ppermute | solution.py:328
  63.0 0.0 copy-start
  63.0 2.4 %project_query.1 = (f32[144,512]{1,0:T(8,128)S(1)}, bf16[144,512]{1,0:T(8,128)(2,1)S(1)}) custom-call(bf16[2,144,2048]{2,1,0:T(8,128)(2,1)S(1)} %get-tuple-element.30.lhs_ref, bf16[2048,1536]{1,0:T(8,128)(2,1)} %all-gather.3.cloned.1.call-done.refs_8_.w_ref), custom_call_target="tpu_custom_call" | custom-call | flops 603979776 | bytes 2097152 | tf_op jit(solution)/shard_map/project_query/pallas_call | solution.py:329
  65.4 5.4 %collective-permute-done.10.more_ref = bf16[144,1024]{1,0:T(8,128)(2,1)S(1)} collective-permute-done((bf16[144,1024]{1,0:T(8,128)(2,1)}, bf16[144,1024]{1,0:T(8,128)(2,1)S(1)}, u32[]{:S(2)}, u32[]{:S(2)}) %collective-permute-start.10) | collective-permute-done | bytes 294944 | tf_op jit(solution)/shard_map/ppermute | solution.py:328
  70.8 0.5 scan.1
  71.3 0.7 broadcast_in_dim.17
  72.1 8.0 %all-to-all-start = ((f32[32,4,512]{2,1,0:T(4,128)}), f32[32,4,512]{2,1,0:T(4,128)S(1)}, u32[]{:S(2)}, u32[]{:S(2)}) async-start(f32[32,4,512]{2,1,0:T(4,128)} %broadcast_in_dim.17), calls=%async_computation | async-start | bytes 524288 | tf_op jit(solution)/shard_map/all_to_all | solution.py:18
  80.1 1.6 %collective-permute-start.11 = (bf16[144,512]{1,0:T(8,128)(2,1)S(1)}, bf16[144,512]{1,0:T(8,128)(2,1)S(1)}, u32[]{:S(2)}, u32[]{:S(2)}) collective-permute-start(bf16[144,512]{1,0:T(8,128)(2,1)S(1)} %get-tuple-element.41), channel_id=1, source_target_pairs={{0,6},{1,7},{2,4},{3,5},{4,2},{5,3},{6,0},{7,1},{8,14},{9,15},{10,... | collective-permute-start | bytes 442376 | tf_op jit(solution)/shard_map/ppermute | solution.py:352
  81.7 6.8 %collective-permute-done.11.more_ref = bf16[144,512]{1,0:T(8,128)(2,1)S(1)} collective-permute-done((bf16[144,512]{1,0:T(8,128)(2,1)S(1)}, bf16[144,512]{1,0:T(8,128)(2,1)S(1)}, u32[]{:S(2)}, u32[]{:S(2)}) %collective-permute-start.11) | collective-permute-done | bytes 147488 | tf_op jit(solution)/shard_map/ppermute | solution.py:352
  88.5 2.4 %all-to-all-done.all_ref = f32[32,4,512]{2,1,0:T(4,128)S(1)} async-done(((f32[32,4,512]{2,1,0:T(4,128)}), f32[32,4,512]{2,1,0:T(4,128)S(1)}, u32[]{:S(2)}, u32[]{:S(2)}) %all-to-all-start) | async-done | bytes 262176 | tf_op jit(solution)/shard_map/all_to_all | solution.py:18
  90.9 0.5 gate.1.refs_0_
  91.5 1.8 %collective-permute-start.12 = (bf16[128,512]{1,0:T(8,128)(2,1)S(1)}, bf16[128,512]{1,0:T(8,128)(2,1)S(1)}, u32[]{:S(2)}, u32[]{:S(2)}) collective-permute-start(bf16[128,512]{1,0:T(8,128)(2,1)S(1)} %gate.1.refs_0_), channel_id=1, source_target_pairs={{0,32},{32,64},{64,96},{96,128},{128,160},{160,192},{192,224},{224... | collective-permute-start | bytes 393224 | tf_op jit(solution)/shard_map/ppermute | solution.py:37
  93.3 1.8 %collective-permute-start.16 = (bf16[128,512]{1,0:T(8,128)(2,1)S(1)}, bf16[128,512]{1,0:T(8,128)(2,1)S(1)}, u32[]{:S(2)}, u32[]{:S(2)}) collective-permute-start(bf16[128,512]{1,0:T(8,128)(2,1)S(1)} %gate.1.refs_0_), channel_id=1, source_target_pairs={{0,224},{32,0},{64,32},{96,64},{128,96},{160,128},{192,160},{224,1... | collective-permute-start | bytes 393224 | tf_op jit(solution)/shard_map/ppermute | solution.py:40
  95.1 2.9 %collective-permute-done.12.refs_1_ = bf16[128,512]{1,0:T(8,128)(2,1)S(1)} collective-permute-done((bf16[128,512]{1,0:T(8,128)(2,1)S(1)}, bf16[128,512]{1,0:T(8,128)(2,1)S(1)}, u32[]{:S(2)}, u32[]{:S(2)}) %collective-permute-start.12) | collective-permute-done | bytes 131104 | tf_op jit(solution)/shard_map/ppermute | solution.py:37
  98.1 0.2 collective-permute-start.13
  98.2 0.0 collective-permute-done.16.refs_2_
  98.2 3.1 %collective-permute-start.17 = (bf16[128,512]{1,0:T(8,128)(2,1)S(1)}, bf16[128,512]{1,0:T(8,128)(2,1)S(1)}, u32[]{:S(2)}, u32[]{:S(2)}) collective-permute-start(bf16[128,512]{1,0:T(8,128)(2,1)S(1)} %collective-permute-done.16.refs_2_), channel_id=1, source_target_pairs={{0,224},{32,0},{64,32},{96,64},{128,96},{160,128},{192,160},{224,1... | collective-permute-start | bytes 393224 | tf_op jit(solution)/shard_map/ppermute | solution.py:40
  101.3 2.9 %collective-permute-done.13.refs_3_ = bf16[128,512]{1,0:T(8,128)(2,1)S(1)} collective-permute-done((bf16[128,512]{1,0:T(8,128)(2,1)S(1)}, bf16[128,512]{1,0:T(8,128)(2,1)S(1)}, u32[]{:S(2)}, u32[]{:S(2)}) %collective-permute-start.13) | collective-permute-done | bytes 131104 | tf_op jit(solution)/shard_map/ppermute | solution.py:37
  104.2 0.0 collective-permute-start.14
  104.2 3.2 %collective-permute-start.18 = (bf16[128,512]{1,0:T(8,128)(2,1)S(1)}, bf16[128,512]{1,0:T(8,128)(2,1)S(1)}, u32[]{:S(2)}, u32[]{:S(2)}) collective-permute-start(bf16[128,512]{1,0:T(8,128)(2,1)S(1)} %collective-permute-done.17.refs_4_), channel_id=1, source_target_pairs={{0,224},{32,0},{64,32},{96,64},{128,96},{160,128},{192,160},{224,1... | collective-permute-start | bytes 393224 | tf_op jit(solution)/shard_map/ppermute | solution.py:40
  107.5 2.9 %collective-permute-done.14.refs_5_ = bf16[128,512]{1,0:T(8,128)(2,1)S(1)} collective-permute-done((bf16[128,512]{1,0:T(8,128)(2,1)S(1)}, bf16[128,512]{1,0:T(8,128)(2,1)S(1)}, u32[]{:S(2)}, u32[]{:S(2)}) %collective-permute-start.14) | collective-permute-done | bytes 131104 | tf_op jit(solution)/shard_map/ppermute | solution.py:37
  110.4 0.0 collective-permute-start.15
  110.4 0.1 stack.48.which_ref
  110.5 0.0 collective-permute-done.18.refs_6_
  110.5 2.9 %mix.1 = (f32[128,512]{1,0:T(8,128)S(1)}, bf16[512,512]{1,0:T(8,128)(2,1)S(1)}) custom-call(s32[9]{0:T(128)S(1)} %stack.48.which_ref, bf16[128,512]{1,0:T(8,128)(2,1)S(1)} %gate.1.refs_0_, bf16[128,512]{1,0:T(8,128)(2,1)S(1)} %collective-permute-done.12.refs_1_, bf16[128,512]{1,0:T(8,128)(2,1)S(1)} %collective-permute-done.16.refs_2_, ...), custom_call_target="tpu_custom_call" | custom-call | flops 536870912 | bytes 4194304 | tf_op jit(solution)/shard_map/mix/pallas_call | solution.py:239
  113.5 3.1 %collective-permute-done.15.x_ref = bf16[128,512]{1,0:T(8,128)(2,1)S(1)} collective-permute-done((bf16[128,512]{1,0:T(8,128)(2,1)S(1)}, bf16[128,512]{1,0:T(8,128)(2,1)S(1)}, u32[]{:S(2)}, u32[]{:S(2)}) %collective-permute-start.15) | collective-permute-done | bytes 131104 | tf_op jit(solution)/shard_map/ppermute | solution.py:37
  116.6 0.9 last_mix.1
  (16 shorter events, 0.1 us)
Async XLA Ops:
  6.5 50.4 %all-gather.3.cloned.1.call-start = ((), (), s32[]{:S(2)}) async-start(), calls=%async_computation.1 | async-start | bytes 6684672 | tf_op jit(solution)/shard_map/all_gather | solution.py:271
  8.4 102.1 %all-gather.5.cloned.1.call-start = ((), (), s32[]{:S(2)}) async-start(), calls=%async_computation.2 | async-start | bytes 4456448 | tf_op jit(solution)/shard_map/all_gather | solution.py:271
  8.5 8.2 %collective-permute-start.1 = (bf16[128,512]{1,0:T(8,128)(2,1)}, bf16[128,512]{1,0:T(8,128)(2,1)S(1)}, u32[]{:S(2)}, u32[]{:S(2)}) collective-permute-start(bf16[128,512]{1,0:T(8,128)(2,1)} %x_ref.1), channel_id=1, source_target_pairs={{0,6},{1,7},{2,4},{3,5},{4,2},{5,3},{6,0},{7,1},{8,14},{9,15},{10,... | collective-permute-start | bytes 393224 | tf_op jit(solution)/shard_map/ppermute | solution.py:279
  10.8 5.9 %collective-permute-start = (bf16[2,512]{1,0:T(2,128)(2,1)S(1)}, bf16[2,512]{1,0:T(2,128)(2,1)S(1)}, u32[]{:S(2)}, u32[]{:S(2)}) collective-permute-start(bf16[2,512]{1,0:T(2,128)(2,1)S(1)} %slice.18), channel_id=1, source_target_pairs={{0,1},{1,2},{2,3},{3,4},{4,5},{5,6},{6,7},{7,8},{8,9},{9,10},{10,1... | collective-permute-start | bytes 6152 | tf_op jit(solution)/shard_map/ppermute | solution.py:278
  17.7 2.3 %collective-permute-start.2 = (bf16[144,512]{1,0:T(8,128)(2,1)S(1)}, bf16[144,512]{1,0:T(8,128)(2,1)S(1)}, u32[]{:S(2)}, u32[]{:S(2)}) collective-permute-start(bf16[144,512]{1,0:T(8,128)(2,1)S(1)} %maximum_maximum_fusion), channel_id=1, source_target_pairs={{0,0},{1,1},{2,2},{3,3},{4,34},{5,35},{6,32},{7,33},{8,8},{9,9},{1... | collective-permute-start | bytes 442376 | tf_op jit(solution)/shard_map/ppermute | solution.py:287
  20.0 16.6 %collective-permute-start.3 = (bf16[144,512]{1,0:T(8,128)(2,1)S(1)}, bf16[144,512]{1,0:T(8,128)(2,1)S(1)}, u32[]{:S(2)}, u32[]{:S(2)}) collective-permute-start(bf16[144,512]{1,0:T(8,128)(2,1)S(1)} %collective-permute-done.2.refs_0_), channel_id=1, source_target_pairs={{0,32},{32,64},{64,96},{96,128},{128,160},{160,192},{192,224},{224... | collective-permute-start | bytes 442376 | tf_op jit(solution)/shard_map/ppermute | solution.py:37
  28.9 7.7 %collective-permute-start.4 = (bf16[144,512]{1,0:T(8,128)(2,1)S(1)}, bf16[144,512]{1,0:T(8,128)(2,1)S(1)}, u32[]{:S(2)}, u32[]{:S(2)}) collective-permute-start(bf16[144,512]{1,0:T(8,128)(2,1)S(1)} %collective-permute-done.2.refs_0_), channel_id=1, source_target_pairs={{0,224},{32,0},{64,32},{96,64},{128,96},{160,128},{192,160},{224,1... | collective-permute-start | bytes 442376 | tf_op jit(solution)/shard_map/ppermute | solution.py:40
  36.6 6.4 %collective-permute-start.5 = (bf16[144,512]{1,0:T(8,128)(2,1)S(1)}, bf16[144,512]{1,0:T(8,128)(2,1)S(1)}, u32[]{:S(2)}, u32[]{:S(2)}) collective-permute-start(bf16[144,512]{1,0:T(8,128)(2,1)S(1)} %collective-permute-done.3.refs_1_), channel_id=1, source_target_pairs={{0,32},{32,64},{64,96},{96,128},{128,160},{160,192},{192,224},{224... | collective-permute-start | bytes 442376 | tf_op jit(solution)/shard_map/ppermute | solution.py:37
  36.6 6.4 %collective-permute-start.6 = (bf16[144,512]{1,0:T(8,128)(2,1)S(1)}, bf16[144,512]{1,0:T(8,128)(2,1)S(1)}, u32[]{:S(2)}, u32[]{:S(2)}) collective-permute-start(bf16[144,512]{1,0:T(8,128)(2,1)S(1)} %collective-permute-done.4.refs_2_), channel_id=1, source_target_pairs={{0,224},{32,0},{64,32},{96,64},{128,96},{160,128},{192,160},{224,1... | collective-permute-start | bytes 442376 | tf_op jit(solution)/shard_map/ppermute | solution.py:40
  43.0 6.4 %collective-permute-start.7 = (bf16[144,512]{1,0:T(8,128)(2,1)S(1)}, bf16[144,512]{1,0:T(8,128)(2,1)S(1)}, u32[]{:S(2)}, u32[]{:S(2)}) collective-permute-start(bf16[144,512]{1,0:T(8,128)(2,1)S(1)} %collective-permute-done.5.refs_3_), channel_id=1, source_target_pairs={{0,32},{32,64},{64,96},{96,128},{128,160},{160,192},{192,224},{224... | collective-permute-start | bytes 442376 | tf_op jit(solution)/shard_map/ppermute | solution.py:37
  43.0 6.4 %collective-permute-start.8 = (bf16[144,512]{1,0:T(8,128)(2,1)S(1)}, bf16[144,512]{1,0:T(8,128)(2,1)S(1)}, u32[]{:S(2)}, u32[]{:S(2)}) collective-permute-start(bf16[144,512]{1,0:T(8,128)(2,1)S(1)} %collective-permute-done.6.refs_4_), channel_id=1, source_target_pairs={{0,224},{32,0},{64,32},{96,64},{128,96},{160,128},{192,160},{224,1... | collective-permute-start | bytes 442376 | tf_op jit(solution)/shard_map/ppermute | solution.py:40
  49.3 6.4 %collective-permute-start.9 = (bf16[144,512]{1,0:T(8,128)(2,1)S(1)}, bf16[144,512]{1,0:T(8,128)(2,1)S(1)}, u32[]{:S(2)}, u32[]{:S(2)}) collective-permute-start(bf16[144,512]{1,0:T(8,128)(2,1)S(1)} %collective-permute-done.7.refs_5_), channel_id=1, source_target_pairs={{0,32},{32,64},{64,96},{96,128},{128,160},{160,192},{192,224},{224... | collective-permute-start | bytes 442376 | tf_op jit(solution)/shard_map/ppermute | solution.py:37
  49.4 13.6 %copy-start.1 = (f32[3,3,512]{2,1,0:T(4,128)S(1)}, f32[3,3,512]{2,1,0:T(4,128)}, u32[]{:S(2)}) copy-start(f32[3,3,512]{2,1,0:T(4,128)} %param.11) | copy-start | bytes 55300
  61.4 9.4 %collective-permute-start.10 = (bf16[144,1024]{1,0:T(8,128)(2,1)}, bf16[144,1024]{1,0:T(8,128)(2,1)S(1)}, u32[]{:S(2)}, u32[]{:S(2)}) collective-permute-start(bf16[144,1024]{1,0:T(8,128)(2,1)} %get-tuple-element.29), channel_id=1, source_target_pairs={{0,6},{1,7},{2,4},{3,5},{4,2},{5,3},{6,0},{7,1},{8,14},{9,15},{10,... | collective-permute-start | bytes 884744 | tf_op jit(solution)/shard_map/ppermute | solution.py:328
  63.0 28.0 %copy-start = (f32[512]{0:T(512)S(1)}, f32[512]{0:T(512)}, u32[]{:S(2)}) copy-start(f32[512]{0:T(512)} %param.15) | copy-start | bytes 6148
  72.1 18.8 %all-to-all-start = ((f32[32,4,512]{2,1,0:T(4,128)}), f32[32,4,512]{2,1,0:T(4,128)S(1)}, u32[]{:S(2)}, u32[]{:S(2)}) async-start(f32[32,4,512]{2,1,0:T(4,128)} %broadcast_in_dim.17), calls=%async_computation | async-start | bytes 524288 | tf_op jit(solution)/shard_map/all_to_all | solution.py:18
  80.1 8.4 %collective-permute-start.11 = (bf16[144,512]{1,0:T(8,128)(2,1)S(1)}, bf16[144,512]{1,0:T(8,128)(2,1)S(1)}, u32[]{:S(2)}, u32[]{:S(2)}) collective-permute-start(bf16[144,512]{1,0:T(8,128)(2,1)S(1)} %get-tuple-element.41), channel_id=1, source_target_pairs={{0,6},{1,7},{2,4},{3,5},{4,2},{5,3},{6,0},{7,1},{8,14},{9,15},{10,... | collective-permute-start | bytes 442376 | tf_op jit(solution)/shard_map/ppermute | solution.py:352
  91.5 6.6 %collective-permute-start.12 = (bf16[128,512]{1,0:T(8,128)(2,1)S(1)}, bf16[128,512]{1,0:T(8,128)(2,1)S(1)}, u32[]{:S(2)}, u32[]{:S(2)}) collective-permute-start(bf16[128,512]{1,0:T(8,128)(2,1)S(1)} %gate.1.refs_0_), channel_id=1, source_target_pairs={{0,32},{32,64},{64,96},{96,128},{128,160},{160,192},{192,224},{224... | collective-permute-start | bytes 393224 | tf_op jit(solution)/shard_map/ppermute | solution.py:37
  93.3 5.0 %collective-permute-start.16 = (bf16[128,512]{1,0:T(8,128)(2,1)S(1)}, bf16[128,512]{1,0:T(8,128)(2,1)S(1)}, u32[]{:S(2)}, u32[]{:S(2)}) collective-permute-start(bf16[128,512]{1,0:T(8,128)(2,1)S(1)} %gate.1.refs_0_), channel_id=1, source_target_pairs={{0,224},{32,0},{64,32},{96,64},{128,96},{160,128},{192,160},{224,1... | collective-permute-start | bytes 393224 | tf_op jit(solution)/shard_map/ppermute | solution.py:40
  98.1 6.2 %collective-permute-start.13 = (bf16[128,512]{1,0:T(8,128)(2,1)S(1)}, bf16[128,512]{1,0:T(8,128)(2,1)S(1)}, u32[]{:S(2)}, u32[]{:S(2)}) collective-permute-start(bf16[128,512]{1,0:T(8,128)(2,1)S(1)} %collective-permute-done.12.refs_1_), channel_id=1, source_target_pairs={{0,32},{32,64},{64,96},{96,128},{128,160},{160,192},{192,224},{224... | collective-permute-start | bytes 393224 | tf_op jit(solution)/shard_map/ppermute | solution.py:37
  98.2 6.0 %collective-permute-start.17 = (bf16[128,512]{1,0:T(8,128)(2,1)S(1)}, bf16[128,512]{1,0:T(8,128)(2,1)S(1)}, u32[]{:S(2)}, u32[]{:S(2)}) collective-permute-start(bf16[128,512]{1,0:T(8,128)(2,1)S(1)} %collective-permute-done.16.refs_2_), channel_id=1, source_target_pairs={{0,224},{32,0},{64,32},{96,64},{128,96},{160,128},{192,160},{224,1... | collective-permute-start | bytes 393224 | tf_op jit(solution)/shard_map/ppermute | solution.py:40
  104.2 6.2 %collective-permute-start.14 = (bf16[128,512]{1,0:T(8,128)(2,1)S(1)}, bf16[128,512]{1,0:T(8,128)(2,1)S(1)}, u32[]{:S(2)}, u32[]{:S(2)}) collective-permute-start(bf16[128,512]{1,0:T(8,128)(2,1)S(1)} %collective-permute-done.13.refs_3_), channel_id=1, source_target_pairs={{0,32},{32,64},{64,96},{96,128},{128,160},{160,192},{192,224},{224... | collective-permute-start | bytes 393224 | tf_op jit(solution)/shard_map/ppermute | solution.py:37
  104.2 6.3 %collective-permute-start.18 = (bf16[128,512]{1,0:T(8,128)(2,1)S(1)}, bf16[128,512]{1,0:T(8,128)(2,1)S(1)}, u32[]{:S(2)}, u32[]{:S(2)}) collective-permute-start(bf16[128,512]{1,0:T(8,128)(2,1)S(1)} %collective-permute-done.17.refs_4_), channel_id=1, source_target_pairs={{0,224},{32,0},{64,32},{96,64},{128,96},{160,128},{192,160},{224,1... | collective-permute-start | bytes 393224 | tf_op jit(solution)/shard_map/ppermute | solution.py:40
  110.4 6.2 %collective-permute-start.15 = (bf16[128,512]{1,0:T(8,128)(2,1)S(1)}, bf16[128,512]{1,0:T(8,128)(2,1)S(1)}, u32[]{:S(2)}, u32[]{:S(2)}) collective-permute-start(bf16[128,512]{1,0:T(8,128)(2,1)S(1)} %collective-permute-done.14.refs_5_), channel_id=1, source_target_pairs={{0,32},{32,64},{64,96},{96,128},{128,160},{160,192},{192,224},{224... | collective-permute-start | bytes 393224 | tf_op jit(solution)/shard_map/ppermute | solution.py:37
Sparse Core Ops, SparseCore 0:
  9.2 47.6 all-gather.2
  58.8 42.3 all-gather.4

commit v10 on v9

--- a/solution.py
+++ b/solution.py
@@ -27,18 +27,20 @@
     return hops
 
 
-def ring(x, axis):
-    count = lax.axis_size(axis)
-    up = [(c, (c + 1) % count) for c in range(count)]
-    down = [(c, (c - 1) % count) for c in range(count)]
+def ring(x):
+    count, blocks = lax.axis_size("ch"), lax.axis_size("seq")
+    onward = []
+    for c in range(count):
+        for s in range(blocks):
+            to = (c + 1) % count if s % 2 == 0 else (c - 1) % count
+            onward.append((c * blocks + s, to * blocks + s))
+    hand = lambda block: lax.ppermute(block, "seq", [(s, s ^ 1) for s in range(blocks)])
+    pair = jnp.stack([x, hand(x)])
     arrived = [x]
-    below = above = x
-    for hop in range(1, count // 2 + 1):
-        below = lax.ppermute(below, axis, up)
-        arrived.append(below)
-        if 2 * hop < count:
-            above = lax.ppermute(above, axis, down)
-            arrived.append(above)
+    for hop in range(1, count // 2):
+        pair = lax.ppermute(pair, ("ch", "seq"), onward)
+        arrived += [pair[0], hand(pair[1])]
+    arrived.append(lax.ppermute(pair[0], ("ch", "seq"), onward))
     return arrived
 
 
@@ -74,9 +76,9 @@
     x_refs, (w_ref, keep_ref, send_ref, lhs_ref, w, sems) = refs[:count], refs[count:]
     chans = x_refs[0].shape[1]
     copies = fetch(w_ref, w, sems, (chans, 2 * chans), (chans, chans))
-    half, here = place_ref[0], place_ref[1]
+    half, here, sign = place_ref[0], place_ref[1], place_ref[2]
     for x_ref, hop in zip(x_refs, ring_hops(count)):
-        origin = lax.rem(here + hop + count, count)
+        origin = lax.rem(here + sign * hop + count, count)
         side = jnp.where(lax.rem(origin, 2) == half, 0, 1)
         at = pl.multiple_of(lax.div(origin, 2) * chans, chans)
         lhs_ref[side, :, pl.ds(at, chans)] = x_ref[...]
@@ -307,8 +309,9 @@
     tied = lax.optimization_barrier((swapped, both, step, join, reach, jump, poles))
     swapped, both, step, join, reach, jump, poles = tied
     second = gather(both)
-    features = ring(swapped, "ch")
+    features = ring(swapped)
     here = lax.axis_index("ch")
+    sign = 1 - 2 * lax.rem(place, 2)
 
     keep, send, lhs = pl.pallas_call(
         functools.partial(mixin_project_kernel, count),
@@ -324,7 +327,7 @@
             flops=8 * padded * depth * chans, bytes_accessed=4 * depth * chans, transcendentals=0
         ),
         name="project_mixin",
-    )(jnp.stack([half, here]).astype(jnp.int32), *features, in_hbm(weight))
+    )(jnp.stack([half, here, sign]).astype(jnp.int32), *features, in_hbm(weight))
     more = lax.ppermute(send, "seq", pairs)
     query_keep, query_send = pl.pallas_call(
         query_project_kernel,
@@ -360,8 +363,8 @@
         name="gate",
     )(states, jump, begin, reach, step, poles, bias[None, :], mixin, query_keep, query_more, taps)
 
-    which = jnp.stack([lax.rem(here + hop + count, count) for hop in ring_hops(count)] + [half])
-    parts = ring(gated, "ch")
+    which = jnp.stack([lax.rem(here + sign * hop + count, count) for hop in ring_hops(count)] + [half])
+    parts = ring(gated)
     first, rest = mix(parts[:-1], which.astype(jnp.int32), second, out_weight.shape[1])
     return pl.pallas_call(
         last_mix_kernel,

time: 125 us -> 133 us (1.064)
  waiting for transfers between devices: 44.1 us -> 70.3 us
  starting transfers between devices: 44.9 us -> 26.4 us
    ppermute x14 -> x16, waiting for transfers between devices: 28.2 us -> 57 us  [the longest x6 45.5 us: ring(): pair = lax.ppermute(pair, ('ch', 'seq'), onward)]
    ppermute x14 -> x16, starting transfers between devices: 29.5 us -> 11.7 us  [the longest x6 8.65 us: ring(): pair = lax.ppermute(pair, ('ch', 'seq'), onward)]
    ppermute x1, starting transfers between devices: 1.61 us -> 0.09 us  [body(): more = lax.ppermute(send, 'seq', pairs)]
  transfers between devices with their start and end apart: 22 -> 24, of which waited for: 12 -> 14; matrix products, arithmetic and copies ran while one was open for 5% -> 5% of each run, Pallas kernels for 10% -> 9%
where the time goes in v10:
time: 133 us; the launch traced here: 132 us
  waiting for transfers between devices  70.3 us (53%)
  starting transfers between devices  26.4 us (20%)
  between operations  13.8 us (10%)
  Pallas kernels  13.3 us (10%)
  other arithmetic  5.06 us (4%)
  local copies, waits for them, and re-layouts  3.52 us (3%)
    ppermute x6, waiting for transfers between devices, ring(): pair = lax.ppermute(pair, ('ch', 'seq'), onward)  45.5 us
    all_to_all x1, starting transfers between devices, spread(): lax.all_to_all(jnp.broadcast_to(x[None], (count,) + x.shape), axis, 0, 0,...  8.87 us
    ppermute x6, starting transfers between devices, ring(): pair = lax.ppermute(pair, ('ch', 'seq'), onward)  8.65 us
    ppermute x2, waiting for transfers between devices, ring(): arrived.append(lax.ppermute(pair[0], ('ch', 'seq'), onward))  8.11 us
    ppermute x1, waiting for transfers between devices, body(): query_more = lax.ppermute(query_send, 'seq', pairs)  6.82 us
    ppermute x1, waiting for transfers between devices, body(): more = lax.ppermute(send, 'seq', pairs)  4.49 us
    pallas_call x1, Pallas kernels, body(): pl.pallas_call(functools.partial(mixin_project_kernel, count), in_specs=[...  4.42 us
    ppermute x8, waiting for transfers between devices, ring(): lax.ppermute(block, 'seq', [(s, s ^ 1) for s in range(blocks)])  3.46 us
  transfers between devices with their start and end apart: 24, of which 14 were waited for; matrix products, arithmetic and copies ran while one was open for 5% of the time, Pallas kernels for 9%

profile of v10, /device:TPU:2, one launch (start us, length us, event | category | flops | bytes accessed | tf_op | source)
XLA Modules:
  0.0 132.3 jit_solution(3135267758099749536)
XLA Ops:
  6.5 1.1 dynamic-slice_bitcast_fusion.2
  7.6 0.8 pad_maximum_fusion
  8.4 0.0 all-gather.3.cloned.1.call-update
  8.4 0.0 all-gather.5.cloned.1.call-start
  8.4 1.6 %collective-permute-start.1 = (bf16[128,512]{1,0:T(8,128)(2,1)}, bf16[128,512]{1,0:T(8,128)(2,1)S(1)}, u32[]{:S(2)}, u32[]{:S(2)}) collective-permute-start(bf16[128,512]{1,0:T(8,128)(2,1)} %x_ref.1), channel_id=1, source_target_pairs={{0,6},{1,7},{2,4},{3,5},{4,2},{5,3},{6,0},{7,1},{8,14},{9,15},{10,... | collective-permute-start | bytes 393224 | tf_op jit(solution)/shard_map/ppermute | solution.py:281
  10.0 0.7 slice.56
  10.7 1.9 %collective-permute-start = (bf16[2,512]{1,0:T(2,128)(2,1)S(1)}, bf16[2,512]{1,0:T(2,128)(2,1)S(1)}, u32[]{:S(2)}, u32[]{:S(2)}) collective-permute-start(bf16[2,512]{1,0:T(2,128)(2,1)S(1)} %slice.56), channel_id=1, source_target_pairs={{0,1},{1,2},{2,3},{3,4},{4,5},{5,6},{6,7},{7,8},{8,9},{9,10},{10,1... | collective-permute-start | bytes 6152 | tf_op jit(solution)/shard_map/ppermute | solution.py:280
  12.7 0.8 multiply_bitcast_fusion.1
  13.6 0.9 fusion.3
  14.5 1.3 fusion.1
  15.7 0.1 fusion.jump_ref
  15.8 0.7 slice_bitcast_fusion.13
  16.6 0.1 pad.19.clone
  16.6 0.0 collective-permute-done
  16.6 1.0 maximum_maximum_fusion
  17.6 0.7 collective-permute-start.2
  18.3 1.6 %beside.1 = bf16[128,1024]{1,0:T(8,128)(2,1)} custom-call(bf16[128,512]{1,0:T(8,128)(2,1)} %x_ref.1, bf16[128,512]{1,0:T(8,128)(2,1)S(1)} %collective-permute-done.1.y_ref), custom_call_target="tpu_custom_call" | custom-call | tf_op jit(solution)/shard_map/beside/pallas_call | solution.py:301
  20.0 0.0 collective-permute-done.2.refs_0_
  20.0 0.0 all-gather.5.cloned.1.call-update
  20.0 0.7 collective-permute-start.3
  20.7 1.0 collective-permute-done.3
  21.8 8.6 %collective-permute-start.4 = (bf16[2,144,512]{2,1,0:T(8,128)(2,1)S(1)}, bf16[2,144,512]{2,1,0:T(8,128)(2,1)S(1)}, u32[]{:S(2)}, u32[]{:S(2)}) collective-permute-start(bf16[2,144,512]{2,1,0:T(8,128)(2,1)S(1)} %pad_maximum_fusion.1), channel_id=1, source_target_pairs={{0,32},{1,225},{2,34},{3,227},{4,36},{5,229},{6,38},{7,231},{8,40}... | collective-permute-start | bytes 884744 | tf_op jit(solution)/shard_map/ppermute | solution.py:41
  30.3 8.6 %collective-permute-done.4 = bf16[2,144,512]{2,1,0:T(8,128)(2,1)S(1)} collective-permute-done((bf16[2,144,512]{2,1,0:T(8,128)(2,1)S(1)}, bf16[2,144,512]{2,1,0:T(8,128)(2,1)S(1)}, u32[]{:S(2)}, u32[]{:S(2)}) %collective-permute-start.4) | collective-permute-done | bytes 294944 | tf_op jit(solution)/shard_map/ppermute | solution.py:41
  39.0 7.9 %collective-permute-done.6 = bf16[2,144,512]{2,1,0:T(8,128)(2,1)S(1)} collective-permute-done((bf16[2,144,512]{2,1,0:T(8,128)(2,1)S(1)}, bf16[2,144,512]{2,1,0:T(8,128)(2,1)S(1)}, u32[]{:S(2)}, u32[]{:S(2)}) %collective-permute-start.6) | collective-permute-done | bytes 294944 | tf_op jit(solution)/shard_map/ppermute | solution.py:41
  46.9 0.0 collective-permute-start.8
  46.9 0.9 collective-permute-start.5
  47.8 0.1 collective-permute-start.7
  47.9 6.9 %collective-permute-done.8 = bf16[2,144,512]{2,1,0:T(8,128)(2,1)S(1)} collective-permute-done((bf16[2,144,512]{2,1,0:T(8,128)(2,1)S(1)}, bf16[2,144,512]{2,1,0:T(8,128)(2,1)S(1)}, u32[]{:S(2)}, u32[]{:S(2)}) %collective-permute-start.8) | collective-permute-done | bytes 294944 | tf_op jit(solution)/shard_map/ppermute | solution.py:41
  54.9 0.1 collective-permute-start.10
  55.0 0.1 collective-permute-start.9
  55.1 0.1 pad_add_fusion.place_ref
  55.2 0.0 collective-permute-done.5.refs_2_
  55.2 6.1 %collective-permute-done.10.refs_7_ = bf16[144,512]{1,0:T(8,128)(2,1)S(1)} collective-permute-done((bf16[144,512]{1,0:T(8,128)(2,1)S(1)}, bf16[144,512]{1,0:T(8,128)(2,1)S(1)}, u32[]{:S(2)}, u32[]{:S(2)}) %collective-permute-start.10) | collective-permute-done | bytes 147488 | tf_op jit(solution)/shard_map/ppermute | solution.py:43
  61.3 0.0 collective-permute-done.9.refs_6_
  61.3 4.4 %project_mixin.1 = (f32[144,1024]{1,0:T(8,128)S(1)}, bf16[144,1024]{1,0:T(8,128)(2,1)}, bf16[2,144,2048]{2,1,0:T(8,128)(2,1)S(1)}) custom-call(s32[3]{0:T(128)S(1)} %pad_add_fusion.place_ref, bf16[144,512]{1,0:T(8,128)(2,1)S(1)} %collective-permute-done.2.refs_0_, bf16[144,512]{1,0:T(8,128)(2,1)S(1)} %get-tuple-element.53.refs_1_, ...), custom_call_target="tpu_custom_call" | custom-call | flops 1207959552 | bytes 4194304 | tf_op jit(solution)/shard_map/project_mixin/pallas_call | solution.py:316
  65.7 0.1 collective-permute-start.11
  65.9 0.0 copy-start
  65.9 2.4 %project_query.1 = (f32[144,512]{1,0:T(8,128)S(1)}, bf16[144,512]{1,0:T(8,128)(2,1)S(1)}) custom-call(bf16[2,144,2048]{2,1,0:T(8,128)(2,1)S(1)} %get-tuple-element.30.lhs_ref, bf16[2048,1536]{1,0:T(8,128)(2,1)} %all-gather.3.cloned.1.call-done.refs_8_.w_ref), custom_call_target="tpu_custom_call" | custom-call | flops 603979776 | bytes 2097152 | tf_op jit(solution)/shard_map/project_query/pallas_call | solution.py:332
  68.3 4.5 %collective-permute-done.11.more_ref = bf16[144,1024]{1,0:T(8,128)(2,1)S(1)} collective-permute-done((bf16[144,1024]{1,0:T(8,128)(2,1)}, bf16[144,1024]{1,0:T(8,128)(2,1)S(1)}, u32[]{:S(2)}, u32[]{:S(2)}) %collective-permute-start.11) | collective-permute-done | bytes 294944 | tf_op jit(solution)/shard_map/ppermute | solution.py:331
  72.8 0.5 scan.1
  73.3 0.7 broadcast_in_dim.17
  74.1 8.9 %all-to-all-start = ((f32[32,4,512]{2,1,0:T(4,128)}), f32[32,4,512]{2,1,0:T(4,128)S(1)}, u32[]{:S(2)}, u32[]{:S(2)}) async-start(f32[32,4,512]{2,1,0:T(4,128)} %broadcast_in_dim.17), calls=%async_computation | async-start | bytes 524288 | tf_op jit(solution)/shard_map/all_to_all | solution.py:18
  82.9 1.6 %collective-permute-start.12 = (bf16[144,512]{1,0:T(8,128)(2,1)S(1)}, bf16[144,512]{1,0:T(8,128)(2,1)S(1)}, u32[]{:S(2)}, u32[]{:S(2)}) collective-permute-start(bf16[144,512]{1,0:T(8,128)(2,1)S(1)} %get-tuple-element.41), channel_id=1, source_target_pairs={{0,6},{1,7},{2,4},{3,5},{4,2},{5,3},{6,0},{7,1},{8,14},{9,15},{10,... | collective-permute-start | bytes 442376 | tf_op jit(solution)/shard_map/ppermute | solution.py:355
  84.5 6.8 %collective-permute-done.12.more_ref = bf16[144,512]{1,0:T(8,128)(2,1)S(1)} collective-permute-done((bf16[144,512]{1,0:T(8,128)(2,1)S(1)}, bf16[144,512]{1,0:T(8,128)(2,1)S(1)}, u32[]{:S(2)}, u32[]{:S(2)}) %collective-permute-start.12) | collective-permute-done | bytes 147488 | tf_op jit(solution)/shard_map/ppermute | solution.py:355
  91.3 1.9 %all-to-all-done.all_ref = f32[32,4,512]{2,1,0:T(4,128)S(1)} async-done(((f32[32,4,512]{2,1,0:T(4,128)}), f32[32,4,512]{2,1,0:T(4,128)S(1)}, u32[]{:S(2)}, u32[]{:S(2)}) %all-to-all-start) | async-done | bytes 262176 | tf_op jit(solution)/shard_map/all_to_all | solution.py:18
  93.2 0.5 gate.1.refs_0_
  93.7 0.3 collective-permute-start.13
  94.0 1.3 %collective-permute-done.13 = bf16[128,512]{1,0:T(8,128)(2,1)S(1)} collective-permute-done((bf16[128,512]{1,0:T(8,128)(2,1)S(1)}, bf16[128,512]{1,0:T(8,128)(2,1)S(1)}, u32[]{:S(2)}, u32[]{:S(2)}) %collective-permute-start.13) | collective-permute-done | bytes 131104 | tf_op jit(solution)/shard_map/ppermute | solution.py:37
  95.4 0.1 collective-permute-start.14
  95.4 7.6 %collective-permute-done.14 = bf16[2,128,512]{2,1,0:T(8,128)(2,1)S(1)} collective-permute-done((bf16[2,128,512]{2,1,0:T(8,128)(2,1)S(1)}, bf16[2,128,512]{2,1,0:T(8,128)(2,1)S(1)}, u32[]{:S(2)}, u32[]{:S(2)}) %collective-permute-start.14) | collective-permute-done | bytes 262176 | tf_op jit(solution)/shard_map/ppermute | solution.py:41
  103.0 0.0 collective-permute-start.15
  103.0 7.6 %collective-permute-done.15 = bf16[2,128,512]{2,1,0:T(8,128)(2,1)S(1)} collective-permute-done((bf16[2,128,512]{2,1,0:T(8,128)(2,1)S(1)}, bf16[2,128,512]{2,1,0:T(8,128)(2,1)S(1)}, u32[]{:S(2)}, u32[]{:S(2)}) %collective-permute-start.15) | collective-permute-done | bytes 262176 | tf_op jit(solution)/shard_map/ppermute | solution.py:41
  110.6 0.0 collective-permute-start.16
  110.6 0.1 collective-permute-start.18
  110.7 0.6 collective-permute-start.19
  111.3 6.9 %collective-permute-done.16 = bf16[2,128,512]{2,1,0:T(8,128)(2,1)S(1)} collective-permute-done((bf16[2,128,512]{2,1,0:T(8,128)(2,1)S(1)}, bf16[2,128,512]{2,1,0:T(8,128)(2,1)S(1)}, u32[]{:S(2)}, u32[]{:S(2)}) %collective-permute-start.16) | collective-permute-done | bytes 262176 | tf_op jit(solution)/shard_map/ppermute | solution.py:41
  118.2 0.1 collective-permute-start.20
  118.3 0.1 collective-permute-start.17
  118.4 0.1 stack.76.which_ref
  118.5 0.0 collective-permute-done.19.refs_4_
  118.5 1.1 collective-permute-done.20.refs_6_
  119.6 2.9 %mix.1 = (f32[128,512]{1,0:T(8,128)S(1)}, bf16[512,512]{1,0:T(8,128)(2,1)S(1)}) custom-call(s32[9]{0:T(128)S(1)} %stack.76.which_ref, bf16[128,512]{1,0:T(8,128)(2,1)S(1)} %gate.1.refs_0_, bf16[128,512]{1,0:T(8,128)(2,1)S(1)} %get-tuple-element.59.refs_1_, bf16[128,512]{1,0:T(8,128)(2,1)S(1)} %collective-permute-done.18.refs_2_, ...), custom_call_target="tpu_custom_call" | custom-call | flops 536870912 | bytes 4194304 | tf_op jit(solution)/shard_map/mix/pallas_call | solution.py:241
  122.6 2.0 %collective-permute-done.17.x_ref = bf16[128,512]{1,0:T(8,128)(2,1)S(1)} collective-permute-done((bf16[128,512]{1,0:T(8,128)(2,1)S(1)}, bf16[128,512]{1,0:T(8,128)(2,1)S(1)}, u32[]{:S(2)}, u32[]{:S(2)}) %collective-permute-start.17) | collective-permute-done | bytes 131104 | tf_op jit(solution)/shard_map/ppermute | solution.py:43
  124.6 0.9 last_mix.1
  (28 shorter events, 0.3 us)
Async XLA Ops:
  6.5 54.8 %all-gather.3.cloned.1.call-start = ((), (), s32[]{:S(2)}) async-start(), calls=%async_computation.1 | async-start | bytes 6684672 | tf_op jit(solution)/shard_map/all_gather | solution.py:273
  8.4 110.1 %all-gather.5.cloned.1.call-start = ((), (), s32[]{:S(2)}) async-start(), calls=%async_computation.2 | async-start | bytes 4456448 | tf_op jit(solution)/shard_map/all_gather | solution.py:273
  8.4 8.2 %collective-permute-start.1 = (bf16[128,512]{1,0:T(8,128)(2,1)}, bf16[128,512]{1,0:T(8,128)(2,1)S(1)}, u32[]{:S(2)}, u32[]{:S(2)}) collective-permute-start(bf16[128,512]{1,0:T(8,128)(2,1)} %x_ref.1), channel_id=1, source_target_pairs={{0,6},{1,7},{2,4},{3,5},{4,2},{5,3},{6,0},{7,1},{8,14},{9,15},{10,... | collective-permute-start | bytes 393224 | tf_op jit(solution)/shard_map/ppermute | solution.py:281
  10.7 5.9 %collective-permute-start = (bf16[2,512]{1,0:T(2,128)(2,1)S(1)}, bf16[2,512]{1,0:T(2,128)(2,1)S(1)}, u32[]{:S(2)}, u32[]{:S(2)}) collective-permute-start(bf16[2,512]{1,0:T(2,128)(2,1)S(1)} %slice.56), channel_id=1, source_target_pairs={{0,1},{1,2},{2,3},{3,4},{4,5},{5,6},{6,7},{7,8},{8,9},{9,10},{10,1... | collective-permute-start | bytes 6152 | tf_op jit(solution)/shard_map/ppermute | solution.py:280
  17.6 2.3 %collective-permute-start.2 = (bf16[144,512]{1,0:T(8,128)(2,1)S(1)}, bf16[144,512]{1,0:T(8,128)(2,1)S(1)}, u32[]{:S(2)}, u32[]{:S(2)}) collective-permute-start(bf16[144,512]{1,0:T(8,128)(2,1)S(1)} %maximum_maximum_fusion), channel_id=1, source_target_pairs={{0,0},{1,1},{2,2},{3,3},{4,34},{5,35},{6,32},{7,33},{8,8},{9,9},{1... | collective-permute-start | bytes 442376 | tf_op jit(solution)/shard_map/ppermute | solution.py:289
  20.0 1.7 %collective-permute-start.3 = (bf16[144,512]{1,0:T(8,128)(2,1)S(1)}, bf16[144,512]{1,0:T(8,128)(2,1)S(1)}, u32[]{:S(2)}, u32[]{:S(2)}) collective-permute-start(bf16[144,512]{1,0:T(8,128)(2,1)S(1)} %collective-permute-done.2.refs_0_), channel_id=1, source_target_pairs={{0,1},{1,0},{2,3},{3,2},{4,5},{5,4},{6,7},{7,6},{8,9},{9,8},{10,11... | collective-permute-start | bytes 442376 | tf_op jit(solution)/shard_map/ppermute | solution.py:37
  21.8 17.2 %collective-permute-start.4 = (bf16[2,144,512]{2,1,0:T(8,128)(2,1)S(1)}, bf16[2,144,512]{2,1,0:T(8,128)(2,1)S(1)}, u32[]{:S(2)}, u32[]{:S(2)}) collective-permute-start(bf16[2,144,512]{2,1,0:T(8,128)(2,1)S(1)} %pad_maximum_fusion.1), channel_id=1, source_target_pairs={{0,32},{1,225},{2,34},{3,227},{4,36},{5,229},{6,38},{7,231},{8,40}... | collective-permute-start | bytes 884744 | tf_op jit(solution)/shard_map/ppermute | solution.py:41
  39.0 7.9 %collective-permute-start.6 = (bf16[2,144,512]{2,1,0:T(8,128)(2,1)S(1)}, bf16[2,144,512]{2,1,0:T(8,128)(2,1)S(1)}, u32[]{:S(2)}, u32[]{:S(2)}) collective-permute-start(bf16[2,144,512]{2,1,0:T(8,128)(2,1)S(1)} %collective-permute-done.4), channel_id=1, source_target_pairs={{0,32},{1,225},{2,34},{3,227},{4,36},{5,229},{6,38},{7,231},{8,40}... | collective-permute-start | bytes 884744 | tf_op jit(solution)/shard_map/ppermute | solution.py:41
  46.9 7.9 %collective-permute-start.8 = (bf16[2,144,512]{2,1,0:T(8,128)(2,1)S(1)}, bf16[2,144,512]{2,1,0:T(8,128)(2,1)S(1)}, u32[]{:S(2)}, u32[]{:S(2)}) collective-permute-start(bf16[2,144,512]{2,1,0:T(8,128)(2,1)S(1)} %collective-permute-done.6), channel_id=1, source_target_pairs={{0,32},{1,225},{2,34},{3,227},{4,36},{5,229},{6,38},{7,231},{8,40}... | collective-permute-start | bytes 884744 | tf_op jit(solution)/shard_map/ppermute | solution.py:41
  46.9 8.2 %collective-permute-start.5 = (bf16[144,512]{1,0:T(8,128)(2,1)S(1)}, bf16[144,512]{1,0:T(8,128)(2,1)S(1)}, u32[]{:S(2)}, u32[]{:S(2)}) collective-permute-start(bf16[144,512]{1,0:T(8,128)(2,1)S(1)} %get-tuple-element.52), channel_id=1, source_target_pairs={{0,1},{1,0},{2,3},{3,2},{4,5},{5,4},{6,7},{7,6},{8,9},{9,8},{10,11... | collective-permute-start | bytes 442376 | tf_op jit(solution)/shard_map/ppermute | solution.py:37
  47.8 7.3 %collective-permute-start.7 = (bf16[144,512]{1,0:T(8,128)(2,1)S(1)}, bf16[144,512]{1,0:T(8,128)(2,1)S(1)}, u32[]{:S(2)}, u32[]{:S(2)}) collective-permute-start(bf16[144,512]{1,0:T(8,128)(2,1)S(1)} %get-tuple-element.50), channel_id=1, source_target_pairs={{0,1},{1,0},{2,3},{3,2},{4,5},{5,4},{6,7},{7,6},{8,9},{9,8},{10,11... | collective-permute-start | bytes 442376 | tf_op jit(solution)/shard_map/ppermute | solution.py:37
  54.9 6.4 %collective-permute-start.10 = (bf16[144,512]{1,0:T(8,128)(2,1)S(1)}, bf16[144,512]{1,0:T(8,128)(2,1)S(1)}, u32[]{:S(2)}, u32[]{:S(2)}) collective-permute-start(bf16[144,512]{1,0:T(8,128)(2,1)S(1)} %get-tuple-element.49.refs_5_), channel_id=1, source_target_pairs={{0,32},{1,225},{2,34},{3,227},{4,36},{5,229},{6,38},{7,231},{8,40}... | collective-permute-start | bytes 442376 | tf_op jit(solution)/shard_map/ppermute | solution.py:43
  55.0 6.3 %collective-permute-start.9 = (bf16[144,512]{1,0:T(8,128)(2,1)S(1)}, bf16[144,512]{1,0:T(8,128)(2,1)S(1)}, u32[]{:S(2)}, u32[]{:S(2)}) collective-permute-start(bf16[144,512]{1,0:T(8,128)(2,1)S(1)} %get-tuple-element.48), channel_id=1, source_target_pairs={{0,1},{1,0},{2,3},{3,2},{4,5},{5,4},{6,7},{7,6},{8,9},{9,8},{10,11... | collective-permute-start | bytes 442376 | tf_op jit(solution)/shard_map/ppermute | solution.py:37
  61.3 4.5 %copy-start.1 = (f32[3,3,512]{2,1,0:T(4,128)S(1)}, f32[3,3,512]{2,1,0:T(4,128)}, u32[]{:S(2)}) copy-start(f32[3,3,512]{2,1,0:T(4,128)} %param.11) | copy-start | bytes 55300
  65.7 7.0 %collective-permute-start.11 = (bf16[144,1024]{1,0:T(8,128)(2,1)}, bf16[144,1024]{1,0:T(8,128)(2,1)S(1)}, u32[]{:S(2)}, u32[]{:S(2)}) collective-permute-start(bf16[144,1024]{1,0:T(8,128)(2,1)} %get-tuple-element.29), channel_id=1, source_target_pairs={{0,6},{1,7},{2,4},{3,5},{4,2},{5,3},{6,0},{7,1},{8,14},{9,15},{10,... | collective-permute-start | bytes 884744 | tf_op jit(solution)/shard_map/ppermute | solution.py:331
  65.9 27.3 %copy-start = (f32[512]{0:T(512)S(1)}, f32[512]{0:T(512)}, u32[]{:S(2)}) copy-start(f32[512]{0:T(512)} %param.15) | copy-start | bytes 6148
  74.1 19.1 %all-to-all-start = ((f32[32,4,512]{2,1,0:T(4,128)}), f32[32,4,512]{2,1,0:T(4,128)S(1)}, u32[]{:S(2)}, u32[]{:S(2)}) async-start(f32[32,4,512]{2,1,0:T(4,128)} %broadcast_in_dim.17), calls=%async_computation | async-start | bytes 524288 | tf_op jit(solution)/shard_map/all_to_all | solution.py:18
  82.9 8.4 %collective-permute-start.12 = (bf16[144,512]{1,0:T(8,128)(2,1)S(1)}, bf16[144,512]{1,0:T(8,128)(2,1)S(1)}, u32[]{:S(2)}, u32[]{:S(2)}) collective-permute-start(bf16[144,512]{1,0:T(8,128)(2,1)S(1)} %get-tuple-element.41), channel_id=1, source_target_pairs={{0,6},{1,7},{2,4},{3,5},{4,2},{5,3},{6,0},{7,1},{8,14},{9,15},{10,... | collective-permute-start | bytes 442376 | tf_op jit(solution)/shard_map/ppermute | solution.py:355
  93.7 1.6 %collective-permute-start.13 = (bf16[128,512]{1,0:T(8,128)(2,1)S(1)}, bf16[128,512]{1,0:T(8,128)(2,1)S(1)}, u32[]{:S(2)}, u32[]{:S(2)}) collective-permute-start(bf16[128,512]{1,0:T(8,128)(2,1)S(1)} %gate.1.refs_0_), channel_id=1, source_target_pairs={{0,1},{1,0},{2,3},{3,2},{4,5},{5,4},{6,7},{7,6},{8,9},{9,8},{10,11... | collective-permute-start | bytes 393224 | tf_op jit(solution)/shard_map/ppermute | solution.py:37
  95.4 7.7 %collective-permute-start.14 = (bf16[2,128,512]{2,1,0:T(8,128)(2,1)S(1)}, bf16[2,128,512]{2,1,0:T(8,128)(2,1)S(1)}, u32[]{:S(2)}, u32[]{:S(2)}) collective-permute-start(bf16[2,128,512]{2,1,0:T(8,128)(2,1)S(1)} %pad_maximum_fusion.2), channel_id=1, source_target_pairs={{0,32},{1,225},{2,34},{3,227},{4,36},{5,229},{6,38},{7,231},{8,40}... | collective-permute-start | bytes 786440 | tf_op jit(solution)/shard_map/ppermute | solution.py:41
  103.0 7.6 %collective-permute-start.15 = (bf16[2,128,512]{2,1,0:T(8,128)(2,1)S(1)}, bf16[2,128,512]{2,1,0:T(8,128)(2,1)S(1)}, u32[]{:S(2)}, u32[]{:S(2)}) collective-permute-start(bf16[2,128,512]{2,1,0:T(8,128)(2,1)S(1)} %collective-permute-done.14), channel_id=1, source_target_pairs={{0,32},{1,225},{2,34},{3,227},{4,36},{5,229},{6,38},{7,231},{8,40}... | collective-permute-start | bytes 786440 | tf_op jit(solution)/shard_map/ppermute | solution.py:41
  110.6 7.6 %collective-permute-start.16 = (bf16[2,128,512]{2,1,0:T(8,128)(2,1)S(1)}, bf16[2,128,512]{2,1,0:T(8,128)(2,1)S(1)}, u32[]{:S(2)}, u32[]{:S(2)}) collective-permute-start(bf16[2,128,512]{2,1,0:T(8,128)(2,1)S(1)} %collective-permute-done.15), channel_id=1, source_target_pairs={{0,32},{1,225},{2,34},{3,227},{4,36},{5,229},{6,38},{7,231},{8,40}... | collective-permute-start | bytes 786440 | tf_op jit(solution)/shard_map/ppermute | solution.py:41
  110.6 7.9 %collective-permute-start.18 = (bf16[128,512]{1,0:T(8,128)(2,1)S(1)}, bf16[128,512]{1,0:T(8,128)(2,1)S(1)}, u32[]{:S(2)}, u32[]{:S(2)}) collective-permute-start(bf16[128,512]{1,0:T(8,128)(2,1)S(1)} %get-tuple-element.58), channel_id=1, source_target_pairs={{0,1},{1,0},{2,3},{3,2},{4,5},{5,4},{6,7},{7,6},{8,9},{9,8},{10,11... | collective-permute-start | bytes 393224 | tf_op jit(solution)/shard_map/ppermute | solution.py:37
  110.7 7.8 %collective-permute-start.19 = (bf16[128,512]{1,0:T(8,128)(2,1)S(1)}, bf16[128,512]{1,0:T(8,128)(2,1)S(1)}, u32[]{:S(2)}, u32[]{:S(2)}) collective-permute-start(bf16[128,512]{1,0:T(8,128)(2,1)S(1)} %get-tuple-element.56), channel_id=1, source_target_pairs={{0,1},{1,0},{2,3},{3,2},{4,5},{5,4},{6,7},{7,6},{8,9},{9,8},{10,11... | collective-permute-start | bytes 393224 | tf_op jit(solution)/shard_map/ppermute | solution.py:37
  118.2 1.4 %collective-permute-start.20 = (bf16[128,512]{1,0:T(8,128)(2,1)S(1)}, bf16[128,512]{1,0:T(8,128)(2,1)S(1)}, u32[]{:S(2)}, u32[]{:S(2)}) collective-permute-start(bf16[128,512]{1,0:T(8,128)(2,1)S(1)} %get-tuple-element.54), channel_id=1, source_target_pairs={{0,1},{1,0},{2,3},{3,2},{4,5},{5,4},{6,7},{7,6},{8,9},{9,8},{10,11... | collective-permute-start | bytes 393224 | tf_op jit(solution)/shard_map/ppermute | solution.py:37
  118.3 6.3 %collective-permute-start.17 = (bf16[128,512]{1,0:T(8,128)(2,1)S(1)}, bf16[128,512]{1,0:T(8,128)(2,1)S(1)}, u32[]{:S(2)}, u32[]{:S(2)}) collective-permute-start(bf16[128,512]{1,0:T(8,128)(2,1)S(1)} %get-tuple-element.55.refs_5_), channel_id=1, source_target_pairs={{0,32},{1,225},{2,34},{3,227},{4,36},{5,229},{6,38},{7,231},{8,40}... | collective-permute-start | bytes 393224 | tf_op jit(solution)/shard_map/ppermute | solution.py:43
Sparse Core Ops, SparseCore 0:
  9.2 47.6 all-gather.2
  58.8 43.3 all-gather.4

commit v11 on v9

--- a/solution.py
+++ b/solution.py
@@ -42,10 +42,30 @@
     return arrived
 
 
-def powers(exponent, rate, turn):
-    mag = jnp.exp(-exponent[:, None, None] * rate[None])
-    phase = exponent[:, None, None] * turn[None]
-    return mag * jnp.cos(phase), mag * jnp.sin(phase)
+def powers_kernel(rows, place_ref, rate_ref, turn_ref, residue_ref, step_ref, join_ref, reach_ref, jump_ref, poles_ref):
+    chans = rate_ref.shape[1]
+    length = rows // SUB
+    blocks = jump_ref.shape[1]
+    gap = place_ref[0] - 1 - lax.broadcasted_iota(jnp.int32, (blocks, chans), 0)
+    far = (jnp.maximum(gap, 0) * rows).astype(jnp.float32)
+    near = (lax.broadcasted_iota(jnp.int32, (SUB, chans), 0) * length).astype(jnp.float32)
+    short = jnp.where(lax.broadcasted_iota(jnp.int32, (SUB, chans), 0) == 0, 1.0, float(length))
+    for n in range(2):
+        rate, turn = rate_ref[n : n + 1, :], turn_ref[n : n + 1, :]
+        mag, phase = jnp.exp(-far * rate), far * turn
+        jump_ref[n] = jnp.where(gap >= 0, mag * jnp.cos(phase), 0.0)
+        jump_ref[2 + n] = jnp.where(gap >= 0, mag * jnp.sin(phase), 0.0)
+        mag, phase = jnp.exp(-near * rate), near * turn
+        reach_ref[n] = mag * jnp.cos(phase)
+        reach_ref[2 + n] = mag * jnp.sin(phase)
+        mag, phase = jnp.exp(-short * rate), short * turn
+        re, im = mag * jnp.cos(phase), mag * jnp.sin(phase)
+        step_ref[n : n + 1, :] = re[0:1]
+        step_ref[2 + n : 3 + n, :] = im[0:1]
+        join_ref[n : n + 1, :] = re[1:2]
+        join_ref[2 + n : 3 + n, :] = im[1:2]
+        poles_ref[n : n + 1, :] = residue_ref[0, n : n + 1, :]
+        poles_ref[2 + n : 3 + n, :] = residue_ref[1, n : n + 1, :]
 
 
 def fetch(w_ref, w, sems, starts, sizes):
@@ -102,7 +122,7 @@
     past = total[rows : rows + 8]
     one = jnp.concatenate([past[1:2], now[:-1]], axis=0)
     two = jnp.concatenate([past[0:2], now[:-2]], axis=0)
-    tap = [taps_ref[3 * j + branch : 3 * j + branch + 1, :] for j in range(3)]
+    tap = [taps_ref[j, branch : branch + 1, :] for j in range(3)]
     return tap[0] * now + tap[1] * one + tap[2] * two
 
 
@@ -285,17 +305,19 @@
             to = (c, s) if c % 2 == near[s] else (c ^ 1, mirror[s])
             swaps.append((c * blocks + s, to[0] * blocks + to[1]))
     swapped = lax.ppermute(tokens, ("ch", "seq"), swaps)
-    rate, turn = decay.T, angle.T
-    length = rows // SUB
-    pack = lambda pair: jnp.concatenate(pair, axis=1)
-    step = pack(powers(jnp.ones((1,), jnp.float32), rate, turn))[0]
-    join = pack(powers(jnp.full((1,), length, jnp.float32), rate, turn))[0]
-    reach = pack(powers((jnp.arange(SUB) * length).astype(jnp.float32), rate, turn))
-    reach = reach.transpose(1, 0, 2)
-    gap = place - 1 - jnp.arange(blocks)
-    jump = pack(powers((jnp.maximum(gap, 0) * rows).astype(jnp.float32), rate, turn))
-    jump = jnp.where((gap >= 0)[:, None, None], jump, 0.0).transpose(1, 0, 2)
-    poles = jnp.concatenate([residue[0].T, residue[1].T], axis=0)
+    step, join, reach, jump, poles = pl.pallas_call(
+        functools.partial(powers_kernel, rows),
+        in_specs=[IN_SMEM] + [IN_VMEM] * 3,
+        out_shape=[
+            shape((4, chans), f32),
+            shape((4, chans), f32),
+            shape((4, SUB, chans), f32),
+            shape((4, blocks, chans), f32),
+            shape((4, chans), f32),
+        ],
+        compiler_params=params,
+        name="powers",
+    )(place.reshape(1).astype(jnp.int32), decay.T, angle.T, residue.transpose(0, 2, 1))
     both = pl.pallas_call(
         beside_kernel,
         in_specs=[IN_HBM, IN_VMEM],
@@ -314,8 +336,8 @@
         functools.partial(mixin_project_kernel, count),
         in_specs=[IN_SMEM] + [IN_VMEM] * count + [IN_HBM],
         out_shape=[
-            shape((padded, 2 * chans), f32),
-            shape((padded, 2 * chans), b16),
+            pltpu.VMEM((padded, 2 * chans), f32),
+            pltpu.VMEM((padded, 2 * chans), b16),
             shape((2, padded, depth), b16),
         ],
         scratch_shapes=[pltpu.VMEM((depth, 2 * chans), b16), pltpu.SemaphoreType.DMA((2,))],
@@ -337,7 +359,7 @@
         ),
         name="project_query",
     )(lhs, in_hbm(weight))
-    taps = short_filter.reshape(9, chans)
+    taps = short_filter
     mixin, begin, final, query_send = pl.pallas_call(
         functools.partial(scan_kernel, rows, chans),
         out_shape=[

time: 125 us -> 124 us (level)
  waiting for transfers between devices: 44.1 us -> 48.9 us
  starting transfers between devices: 44.9 us -> 41.3 us
  other arithmetic: 5.03 us -> 1.86 us
  local copies, waits for them, and re-layouts: 3.4 us -> 4.74 us
    ppermute x8, starting transfers between devices: 10.8 us -> 6.61 us  [ring(): below = lax.ppermute(below, axis, up)]
    mul x3 -> x0, other arithmetic: 3.01 us -> none  [powers(): return (mag * jnp.cos(phase), mag * jnp.sin(phase))]
    ppermute x1, waiting for transfers between devices: 0.01 us -> 2.89 us  [body(): lax.ppermute(inputs[-2:], 'seq', [(i, i + 1) for i in range(blocks - 1)])]
    unnamed x4 -> x10, local copies, waits for them, and re-layouts: 0.01 us -> 2.07 us
    all_gather x2, waiting for transfers between devices: 1.25 us -> 2.96 us  [body(): lax.all_gather(x, 'seq', axis=0, tiled=True, axis_index_groups=halves)]
  transfers between devices with their start and end apart: 22 -> 22, of which waited for: 12 -> 13; matrix products, arithmetic and copies ran while one was open for 5% -> 2% of each run, Pallas kernels for 10% -> 10%
where the time goes in v11:
time: 124 us
  waiting for transfers between devices  48.9 us (39%)
  starting transfers between devices  41.3 us (33%)
  between operations  13.5 us (11%)
  Pallas kernels  13.4 us (11%)
  local copies, waits for them, and re-layouts  4.74 us (4%)
  other arithmetic  1.86 us (2%)
    ppermute x8, waiting for transfers between devices, ring(): below = lax.ppermute(below, axis, up)  28.8 us
    ppermute x6, starting transfers between devices, ring(): above = lax.ppermute(above, axis, down)  19.2 us
    all_to_all x1, starting transfers between devices, spread(): lax.all_to_all(jnp.broadcast_to(x[None], (count,) + x.shape), axis, 0, 0,...  8.04 us
    ppermute x1, waiting for transfers between devices, body(): query_more = lax.ppermute(query_send, 'seq', pairs)  6.83 us
    ppermute x8, starting transfers between devices, ring(): below = lax.ppermute(below, axis, up)  6.61 us
    ppermute x1, waiting for transfers between devices, body(): more = lax.ppermute(send, 'seq', pairs)  5.23 us
    pallas_call x1, Pallas kernels, body(): pl.pallas_call(functools.partial(mixin_project_kernel, count), in_specs=[...  3.7 us
    all_gather x2, waiting for transfers between devices, body(): lax.all_gather(x, 'seq', axis=0, tiled=True, axis_index_groups=halves)  2.96 us
  transfers between devices with their start and end apart: 22, of which 13 were waited for; matrix products, arithmetic and copies ran while one was open for 2% of the time, Pallas kernels for 10%

profile of v11, /device:TPU:2, one launch (start us, length us, event | category | flops | bytes accessed | tf_op | source)
XLA Modules:
  0.0 123.7 jit_solution(8944316551205084165)
XLA Ops:
  6.5 1.1 dynamic-slice_bitcast_fusion.2
  7.6 0.8 pad_maximum_fusion
  8.4 0.0 all-gather.3.cloned.1.call-update
  8.4 0.0 all-gather.5.cloned.1.call-start
  8.5 1.6 %collective-permute-start.1 = (bf16[128,512]{1,0:T(8,128)(2,1)}, bf16[128,512]{1,0:T(8,128)(2,1)S(1)}, u32[]{:S(2)}, u32[]{:S(2)}) collective-permute-start(bf16[128,512]{1,0:T(8,128)(2,1)} %x_ref.1), channel_id=1, source_target_pairs={{0,6},{1,7},{2,4},{3,5},{4,2},{5,3},{6,0},{7,1},{8,14},{9,15},{10,... | collective-permute-start | bytes 393224 | tf_op jit(solution)/shard_map/ppermute | solution.py:299
  10.0 0.7 slice.12
  10.8 1.9 %collective-permute-start = (bf16[2,512]{1,0:T(2,128)(2,1)S(1)}, bf16[2,512]{1,0:T(2,128)(2,1)S(1)}, u32[]{:S(2)}, u32[]{:S(2)}) collective-permute-start(bf16[2,512]{1,0:T(2,128)(2,1)S(1)} %slice.12), channel_id=1, source_target_pairs={{0,1},{1,2},{2,3},{3,4},{4,5},{5,6},{6,7},{7,8},{8,9},{9,10},{10,1... | collective-permute-start | bytes 6152 | tf_op jit(solution)/shard_map/ppermute | solution.py:298
  12.7 0.1 pad.5.clone
  12.8 2.9 %collective-permute-done = bf16[2,512]{1,0:T(2,128)(2,1)S(1)} collective-permute-done((bf16[2,512]{1,0:T(2,128)(2,1)S(1)}, bf16[2,512]{1,0:T(2,128)(2,1)S(1)}, u32[]{:S(2)}, u32[]{:S(2)}) %collective-permute-start) | collective-permute-done | bytes 2080 | tf_op jit(solution)/shard_map/ppermute | solution.py:298
  15.6 0.0 collective-permute-done.1.y_ref
  15.6 1.0 maximum_maximum_fusion
  16.6 0.7 collective-permute-start.2
  17.3 0.0 copy-start.1
  17.3 0.7 copy-done.1
  18.0 0.7 copy-done.2
  18.7 0.7 copy-done.3
  19.4 0.8 powers.1
  20.2 1.6 %beside.1 = bf16[128,1024]{1,0:T(8,128)(2,1)} custom-call(bf16[128,512]{1,0:T(8,128)(2,1)} %x_ref.1, bf16[128,512]{1,0:T(8,128)(2,1)S(1)} %collective-permute-done.1.y_ref), custom_call_target="tpu_custom_call" | custom-call | tf_op jit(solution)/shard_map/beside/pallas_call | solution.py:321
  21.8 0.0 collective-permute-done.2.refs_0_
  21.8 0.0 all-gather.5.cloned.1.call-update
  21.8 4.8 %collective-permute-start.3 = (bf16[144,512]{1,0:T(8,128)(2,1)S(1)}, bf16[144,512]{1,0:T(8,128)(2,1)S(1)}, u32[]{:S(2)}, u32[]{:S(2)}) collective-permute-start(bf16[144,512]{1,0:T(8,128)(2,1)S(1)} %collective-permute-done.2.refs_0_), channel_id=1, source_target_pairs={{0,32},{32,64},{64,96},{96,128},{128,160},{160,192},{192,224},{224... | collective-permute-start | bytes 442376 | tf_op jit(solution)/shard_map/ppermute | solution.py:37
  26.6 4.0 %collective-permute-start.4 = (bf16[144,512]{1,0:T(8,128)(2,1)S(1)}, bf16[144,512]{1,0:T(8,128)(2,1)S(1)}, u32[]{:S(2)}, u32[]{:S(2)}) collective-permute-start(bf16[144,512]{1,0:T(8,128)(2,1)S(1)} %collective-permute-done.2.refs_0_), channel_id=1, source_target_pairs={{0,224},{32,0},{64,32},{96,64},{128,96},{160,128},{192,160},{224,1... | collective-permute-start | bytes 442376 | tf_op jit(solution)/shard_map/ppermute | solution.py:40
  30.6 3.0 %collective-permute-done.3.refs_1_ = bf16[144,512]{1,0:T(8,128)(2,1)S(1)} collective-permute-done((bf16[144,512]{1,0:T(8,128)(2,1)S(1)}, bf16[144,512]{1,0:T(8,128)(2,1)S(1)}, u32[]{:S(2)}, u32[]{:S(2)}) %collective-permute-start.3) | collective-permute-done | bytes 147488 | tf_op jit(solution)/shard_map/ppermute | solution.py:37
  33.7 0.0 collective-permute-start.5
  33.7 0.0 collective-permute-done.4.refs_2_
  33.7 3.3 %collective-permute-start.6 = (bf16[144,512]{1,0:T(8,128)(2,1)S(1)}, bf16[144,512]{1,0:T(8,128)(2,1)S(1)}, u32[]{:S(2)}, u32[]{:S(2)}) collective-permute-start(bf16[144,512]{1,0:T(8,128)(2,1)S(1)} %collective-permute-done.4.refs_2_), channel_id=1, source_target_pairs={{0,224},{32,0},{64,32},{96,64},{128,96},{160,128},{192,160},{224,1... | collective-permute-start | bytes 442376 | tf_op jit(solution)/shard_map/ppermute | solution.py:40
  37.0 3.0 %collective-permute-done.5.refs_3_ = bf16[144,512]{1,0:T(8,128)(2,1)S(1)} collective-permute-done((bf16[144,512]{1,0:T(8,128)(2,1)S(1)}, bf16[144,512]{1,0:T(8,128)(2,1)S(1)}, u32[]{:S(2)}, u32[]{:S(2)}) %collective-permute-start.5) | collective-permute-done | bytes 147488 | tf_op jit(solution)/shard_map/ppermute | solution.py:37
  40.0 0.0 collective-permute-start.7
  40.0 0.0 collective-permute-done.6.refs_4_
  40.0 3.6 %collective-permute-start.8 = (bf16[144,512]{1,0:T(8,128)(2,1)S(1)}, bf16[144,512]{1,0:T(8,128)(2,1)S(1)}, u32[]{:S(2)}, u32[]{:S(2)}) collective-permute-start(bf16[144,512]{1,0:T(8,128)(2,1)S(1)} %collective-permute-done.6.refs_4_), channel_id=1, source_target_pairs={{0,224},{32,0},{64,32},{96,64},{128,96},{160,128},{192,160},{224,1... | collective-permute-start | bytes 442376 | tf_op jit(solution)/shard_map/ppermute | solution.py:40
  43.6 4.0 %collective-permute-done.7.refs_5_ = bf16[144,512]{1,0:T(8,128)(2,1)S(1)} collective-permute-done((bf16[144,512]{1,0:T(8,128)(2,1)S(1)}, bf16[144,512]{1,0:T(8,128)(2,1)S(1)}, u32[]{:S(2)}, u32[]{:S(2)}) %collective-permute-start.7) | collective-permute-done | bytes 147488 | tf_op jit(solution)/shard_map/ppermute | solution.py:37
  47.6 0.0 collective-permute-start.9
  47.6 0.1 pad_add_fusion.place_ref
  47.7 0.0 collective-permute-done.8.refs_6_
  47.7 6.3 %collective-permute-done.9.refs_7_ = bf16[144,512]{1,0:T(8,128)(2,1)S(1)} collective-permute-done((bf16[144,512]{1,0:T(8,128)(2,1)S(1)}, bf16[144,512]{1,0:T(8,128)(2,1)S(1)}, u32[]{:S(2)}, u32[]{:S(2)}) %collective-permute-start.9) | collective-permute-done | bytes 147488 | tf_op jit(solution)/shard_map/ppermute | solution.py:37
  54.0 3.0 %all-gather.3.cloned.1.call-done.refs_8_.w_ref = bf16[2048,1536]{1,0:T(8,128)(2,1)} async-done(((bf16[128,1536]{1,0:T(8,128)(2,1)}), bf16[2048,1536]{1,0:T(8,128)(2,1)}) %all-gather.3.cloned.1.call-update) | async-done | bytes 6291472 | tf_op jit(solution)/shard_map/all_gather | solution.py:291
  56.9 3.7 %project_mixin.1 = (f32[144,1024]{1,0:T(8,128)S(1)}, bf16[144,1024]{1,0:T(8,128)(2,1)S(1)}, bf16[2,144,2048]{2,1,0:T(8,128)(2,1)S(1)}) custom-call(s32[2]{0:T(128)S(1)} %pad_add_fusion.place_ref, bf16[144,512]{1,0:T(8,128)(2,1)S(1)} %collective-permute-done.2.refs_0_, bf16[144,512]{1,0:T(8,128)(2,1)S(1)} %collective-permute-done.3.refs_1_, ...), custom_call_target="tpu_custom_call" | custom-call | flops 1207959552 | bytes 4194304 | tf_op jit(solution)/shard_map/project_mixin/pallas_call | solution.py:335
  60.6 1.6 %collective-permute-start.10 = (bf16[144,1024]{1,0:T(8,128)(2,1)S(1)}, bf16[144,1024]{1,0:T(8,128)(2,1)S(1)}, u32[]{:S(2)}, u32[]{:S(2)}) collective-permute-start(bf16[144,1024]{1,0:T(8,128)(2,1)S(1)} %get-tuple-element.39), channel_id=1, source_target_pairs={{0,6},{1,7},{2,4},{3,5},{4,2},{5,3},{6,0},{7,1},{8,14},{9,15},{10,... | collective-permute-start | bytes 884744 | tf_op jit(solution)/shard_map/ppermute | solution.py:350
  62.2 2.4 %project_query.1 = (f32[144,512]{1,0:T(8,128)S(1)}, bf16[144,512]{1,0:T(8,128)(2,1)S(1)}) custom-call(bf16[2,144,2048]{2,1,0:T(8,128)(2,1)S(1)} %get-tuple-element.40.lhs_ref, bf16[2048,1536]{1,0:T(8,128)(2,1)} %all-gather.3.cloned.1.call-done.refs_8_.w_ref), custom_call_target="tpu_custom_call" | custom-call | flops 603979776 | bytes 2097152 | tf_op jit(solution)/shard_map/project_query/pallas_call | solution.py:351
  64.6 5.2 %collective-permute-done.10.more_ref = bf16[144,1024]{1,0:T(8,128)(2,1)S(1)} collective-permute-done((bf16[144,1024]{1,0:T(8,128)(2,1)S(1)}, bf16[144,1024]{1,0:T(8,128)(2,1)S(1)}, u32[]{:S(2)}, u32[]{:S(2)}) %collective-permute-start.10) | collective-permute-done | bytes 294944 | tf_op jit(solution)/shard_map/ppermute | solution.py:350
  69.9 0.6 scan.1
  70.4 0.7 broadcast_in_dim.13
  71.2 8.0 %all-to-all-start = ((f32[32,4,512]{2,1,0:T(4,128)}), f32[32,4,512]{2,1,0:T(4,128)S(1)}, u32[]{:S(2)}, u32[]{:S(2)}) async-start(f32[32,4,512]{2,1,0:T(4,128)} %broadcast_in_dim.13), calls=%async_computation | async-start | bytes 524288 | tf_op jit(solution)/shard_map/all_to_all | solution.py:18
  79.2 1.6 %collective-permute-start.11 = (bf16[144,512]{1,0:T(8,128)(2,1)S(1)}, bf16[144,512]{1,0:T(8,128)(2,1)S(1)}, u32[]{:S(2)}, u32[]{:S(2)}) collective-permute-start(bf16[144,512]{1,0:T(8,128)(2,1)S(1)} %get-tuple-element.51), channel_id=1, source_target_pairs={{0,6},{1,7},{2,4},{3,5},{4,2},{5,3},{6,0},{7,1},{8,14},{9,15},{10,... | collective-permute-start | bytes 442376 | tf_op jit(solution)/shard_map/ppermute | solution.py:374
  80.8 6.8 %collective-permute-done.11.more_ref = bf16[144,512]{1,0:T(8,128)(2,1)S(1)} collective-permute-done((bf16[144,512]{1,0:T(8,128)(2,1)S(1)}, bf16[144,512]{1,0:T(8,128)(2,1)S(1)}, u32[]{:S(2)}, u32[]{:S(2)}) %collective-permute-start.11) | collective-permute-done | bytes 147488 | tf_op jit(solution)/shard_map/ppermute | solution.py:374
  87.6 2.1 %all-to-all-done.all_ref = f32[32,4,512]{2,1,0:T(4,128)S(1)} async-done(((f32[32,4,512]{2,1,0:T(4,128)}), f32[32,4,512]{2,1,0:T(4,128)S(1)}, u32[]{:S(2)}, u32[]{:S(2)}) %all-to-all-start) | async-done | bytes 262176 | tf_op jit(solution)/shard_map/all_to_all | solution.py:18
  89.7 0.5 gate.1.refs_0_
  90.3 1.8 %collective-permute-start.12 = (bf16[128,512]{1,0:T(8,128)(2,1)S(1)}, bf16[128,512]{1,0:T(8,128)(2,1)S(1)}, u32[]{:S(2)}, u32[]{:S(2)}) collective-permute-start(bf16[128,512]{1,0:T(8,128)(2,1)S(1)} %gate.1.refs_0_), channel_id=1, source_target_pairs={{0,32},{32,64},{64,96},{96,128},{128,160},{160,192},{192,224},{224... | collective-permute-start | bytes 393224 | tf_op jit(solution)/shard_map/ppermute | solution.py:37
  92.1 1.8 %collective-permute-start.16 = (bf16[128,512]{1,0:T(8,128)(2,1)S(1)}, bf16[128,512]{1,0:T(8,128)(2,1)S(1)}, u32[]{:S(2)}, u32[]{:S(2)}) collective-permute-start(bf16[128,512]{1,0:T(8,128)(2,1)S(1)} %gate.1.refs_0_), channel_id=1, source_target_pairs={{0,224},{32,0},{64,32},{96,64},{128,96},{160,128},{192,160},{224,1... | collective-permute-start | bytes 393224 | tf_op jit(solution)/shard_map/ppermute | solution.py:40
  93.9 3.5 %collective-permute-done.12.refs_1_ = bf16[128,512]{1,0:T(8,128)(2,1)S(1)} collective-permute-done((bf16[128,512]{1,0:T(8,128)(2,1)S(1)}, bf16[128,512]{1,0:T(8,128)(2,1)S(1)}, u32[]{:S(2)}, u32[]{:S(2)}) %collective-permute-start.12) | collective-permute-done | bytes 131104 | tf_op jit(solution)/shard_map/ppermute | solution.py:37
  97.4 0.0 collective-permute-start.13
  97.4 0.0 collective-permute-done.16.refs_2_
  97.4 3.2 %collective-permute-start.17 = (bf16[128,512]{1,0:T(8,128)(2,1)S(1)}, bf16[128,512]{1,0:T(8,128)(2,1)S(1)}, u32[]{:S(2)}, u32[]{:S(2)}) collective-permute-start(bf16[128,512]{1,0:T(8,128)(2,1)S(1)} %collective-permute-done.16.refs_2_), channel_id=1, source_target_pairs={{0,224},{32,0},{64,32},{96,64},{128,96},{160,128},{192,160},{224,1... | collective-permute-start | bytes 393224 | tf_op jit(solution)/shard_map/ppermute | solution.py:40
  100.7 2.9 %collective-permute-done.13.refs_3_ = bf16[128,512]{1,0:T(8,128)(2,1)S(1)} collective-permute-done((bf16[128,512]{1,0:T(8,128)(2,1)S(1)}, bf16[128,512]{1,0:T(8,128)(2,1)S(1)}, u32[]{:S(2)}, u32[]{:S(2)}) %collective-permute-start.13) | collective-permute-done | bytes 131104 | tf_op jit(solution)/shard_map/ppermute | solution.py:37
  103.6 0.0 collective-permute-start.14
  103.6 0.0 collective-permute-done.17.refs_4_
  103.6 3.2 %collective-permute-start.18 = (bf16[128,512]{1,0:T(8,128)(2,1)S(1)}, bf16[128,512]{1,0:T(8,128)(2,1)S(1)}, u32[]{:S(2)}, u32[]{:S(2)}) collective-permute-start(bf16[128,512]{1,0:T(8,128)(2,1)S(1)} %collective-permute-done.17.refs_4_), channel_id=1, source_target_pairs={{0,224},{32,0},{64,32},{96,64},{128,96},{160,128},{192,160},{224,1... | collective-permute-start | bytes 393224 | tf_op jit(solution)/shard_map/ppermute | solution.py:40
  106.8 2.9 %collective-permute-done.14.refs_5_ = bf16[128,512]{1,0:T(8,128)(2,1)S(1)} collective-permute-done((bf16[128,512]{1,0:T(8,128)(2,1)S(1)}, bf16[128,512]{1,0:T(8,128)(2,1)S(1)}, u32[]{:S(2)}, u32[]{:S(2)}) %collective-permute-start.14) | collective-permute-done | bytes 131104 | tf_op jit(solution)/shard_map/ppermute | solution.py:37
  109.8 0.0 collective-permute-start.15
  109.8 0.1 stack.48.which_ref
  109.9 0.0 collective-permute-done.18.refs_6_
  109.9 2.9 %mix.1 = (f32[128,512]{1,0:T(8,128)S(1)}, bf16[512,512]{1,0:T(8,128)(2,1)S(1)}) custom-call(s32[9]{0:T(128)S(1)} %stack.48.which_ref, bf16[128,512]{1,0:T(8,128)(2,1)S(1)} %gate.1.refs_0_, bf16[128,512]{1,0:T(8,128)(2,1)S(1)} %collective-permute-done.12.refs_1_, bf16[128,512]{1,0:T(8,128)(2,1)S(1)} %collective-permute-done.16.refs_2_, ...), custom_call_target="tpu_custom_call" | custom-call | flops 536870912 | bytes 4194304 | tf_op jit(solution)/shard_map/mix/pallas_call | solution.py:259
  112.8 3.1 %collective-permute-done.15.x_ref = bf16[128,512]{1,0:T(8,128)(2,1)S(1)} collective-permute-done((bf16[128,512]{1,0:T(8,128)(2,1)S(1)}, bf16[128,512]{1,0:T(8,128)(2,1)S(1)}, u32[]{:S(2)}, u32[]{:S(2)}) %collective-permute-start.15) | collective-permute-done | bytes 131104 | tf_op jit(solution)/shard_map/ppermute | solution.py:37
  116.0 0.9 last_mix.1
  (9 shorter events, 0.0 us)
Async XLA Ops:
  6.5 50.4 %all-gather.3.cloned.1.call-start = ((), (), s32[]{:S(2)}) async-start(), calls=%async_computation.1 | async-start | bytes 6684672 | tf_op jit(solution)/shard_map/all_gather | solution.py:291
  8.4 101.4 %all-gather.5.cloned.1.call-start = ((), (), s32[]{:S(2)}) async-start(), calls=%async_computation.2 | async-start | bytes 4456448 | tf_op jit(solution)/shard_map/all_gather | solution.py:291
  8.5 7.2 %collective-permute-start.1 = (bf16[128,512]{1,0:T(8,128)(2,1)}, bf16[128,512]{1,0:T(8,128)(2,1)S(1)}, u32[]{:S(2)}, u32[]{:S(2)}) collective-permute-start(bf16[128,512]{1,0:T(8,128)(2,1)} %x_ref.1), channel_id=1, source_target_pairs={{0,6},{1,7},{2,4},{3,5},{4,2},{5,3},{6,0},{7,1},{8,14},{9,15},{10,... | collective-permute-start | bytes 393224 | tf_op jit(solution)/shard_map/ppermute | solution.py:299
  10.8 4.9 %collective-permute-start = (bf16[2,512]{1,0:T(2,128)(2,1)S(1)}, bf16[2,512]{1,0:T(2,128)(2,1)S(1)}, u32[]{:S(2)}, u32[]{:S(2)}) collective-permute-start(bf16[2,512]{1,0:T(2,128)(2,1)S(1)} %slice.12), channel_id=1, source_target_pairs={{0,1},{1,2},{2,3},{3,4},{4,5},{5,6},{6,7},{7,8},{8,9},{9,10},{10,1... | collective-permute-start | bytes 6152 | tf_op jit(solution)/shard_map/ppermute | solution.py:298
  16.6 5.1 %collective-permute-start.2 = (bf16[144,512]{1,0:T(8,128)(2,1)S(1)}, bf16[144,512]{1,0:T(8,128)(2,1)S(1)}, u32[]{:S(2)}, u32[]{:S(2)}) collective-permute-start(bf16[144,512]{1,0:T(8,128)(2,1)S(1)} %maximum_maximum_fusion), channel_id=1, source_target_pairs={{0,0},{1,1},{2,2},{3,3},{4,34},{5,35},{6,32},{7,33},{8,8},{9,9},{1... | collective-permute-start | bytes 442376 | tf_op jit(solution)/shard_map/ppermute | solution.py:307
  17.3 0.7 copy-start.1
  18.0 0.7 copy-start.2
  18.7 0.7 copy-start.3
  21.8 11.8 %collective-permute-start.3 = (bf16[144,512]{1,0:T(8,128)(2,1)S(1)}, bf16[144,512]{1,0:T(8,128)(2,1)S(1)}, u32[]{:S(2)}, u32[]{:S(2)}) collective-permute-start(bf16[144,512]{1,0:T(8,128)(2,1)S(1)} %collective-permute-done.2.refs_0_), channel_id=1, source_target_pairs={{0,32},{32,64},{64,96},{96,128},{128,160},{160,192},{192,224},{224... | collective-permute-start | bytes 442376 | tf_op jit(solution)/shard_map/ppermute | solution.py:37
  26.6 7.1 %collective-permute-start.4 = (bf16[144,512]{1,0:T(8,128)(2,1)S(1)}, bf16[144,512]{1,0:T(8,128)(2,1)S(1)}, u32[]{:S(2)}, u32[]{:S(2)}) collective-permute-start(bf16[144,512]{1,0:T(8,128)(2,1)S(1)} %collective-permute-done.2.refs_0_), channel_id=1, source_target_pairs={{0,224},{32,0},{64,32},{96,64},{128,96},{160,128},{192,160},{224,1... | collective-permute-start | bytes 442376 | tf_op jit(solution)/shard_map/ppermute | solution.py:40
  33.7 6.4 %collective-permute-start.5 = (bf16[144,512]{1,0:T(8,128)(2,1)S(1)}, bf16[144,512]{1,0:T(8,128)(2,1)S(1)}, u32[]{:S(2)}, u32[]{:S(2)}) collective-permute-start(bf16[144,512]{1,0:T(8,128)(2,1)S(1)} %collective-permute-done.3.refs_1_), channel_id=1, source_target_pairs={{0,32},{32,64},{64,96},{96,128},{128,160},{160,192},{192,224},{224... | collective-permute-start | bytes 442376 | tf_op jit(solution)/shard_map/ppermute | solution.py:37
  33.7 6.4 %collective-permute-start.6 = (bf16[144,512]{1,0:T(8,128)(2,1)S(1)}, bf16[144,512]{1,0:T(8,128)(2,1)S(1)}, u32[]{:S(2)}, u32[]{:S(2)}) collective-permute-start(bf16[144,512]{1,0:T(8,128)(2,1)S(1)} %collective-permute-done.4.refs_2_), channel_id=1, source_target_pairs={{0,224},{32,0},{64,32},{96,64},{128,96},{160,128},{192,160},{224,1... | collective-permute-start | bytes 442376 | tf_op jit(solution)/shard_map/ppermute | solution.py:40
  40.0 7.6 %collective-permute-start.7 = (bf16[144,512]{1,0:T(8,128)(2,1)S(1)}, bf16[144,512]{1,0:T(8,128)(2,1)S(1)}, u32[]{:S(2)}, u32[]{:S(2)}) collective-permute-start(bf16[144,512]{1,0:T(8,128)(2,1)S(1)} %collective-permute-done.5.refs_3_), channel_id=1, source_target_pairs={{0,32},{32,64},{64,96},{96,128},{128,160},{160,192},{192,224},{224... | collective-permute-start | bytes 442376 | tf_op jit(solution)/shard_map/ppermute | solution.py:37
  40.0 7.7 %collective-permute-start.8 = (bf16[144,512]{1,0:T(8,128)(2,1)S(1)}, bf16[144,512]{1,0:T(8,128)(2,1)S(1)}, u32[]{:S(2)}, u32[]{:S(2)}) collective-permute-start(bf16[144,512]{1,0:T(8,128)(2,1)S(1)} %collective-permute-done.6.refs_4_), channel_id=1, source_target_pairs={{0,224},{32,0},{64,32},{96,64},{128,96},{160,128},{192,160},{224,1... | collective-permute-start | bytes 442376 | tf_op jit(solution)/shard_map/ppermute | solution.py:40
  47.6 6.4 %collective-permute-start.9 = (bf16[144,512]{1,0:T(8,128)(2,1)S(1)}, bf16[144,512]{1,0:T(8,128)(2,1)S(1)}, u32[]{:S(2)}, u32[]{:S(2)}) collective-permute-start(bf16[144,512]{1,0:T(8,128)(2,1)S(1)} %collective-permute-done.7.refs_5_), channel_id=1, source_target_pairs={{0,32},{32,64},{64,96},{96,128},{128,160},{160,192},{192,224},{224... | collective-permute-start | bytes 442376 | tf_op jit(solution)/shard_map/ppermute | solution.py:37
  60.6 9.2 %collective-permute-start.10 = (bf16[144,1024]{1,0:T(8,128)(2,1)S(1)}, bf16[144,1024]{1,0:T(8,128)(2,1)S(1)}, u32[]{:S(2)}, u32[]{:S(2)}) collective-permute-start(bf16[144,1024]{1,0:T(8,128)(2,1)S(1)} %get-tuple-element.39), channel_id=1, source_target_pairs={{0,6},{1,7},{2,4},{3,5},{4,2},{5,3},{6,0},{7,1},{8,14},{9,15},{10,... | collective-permute-start | bytes 884744 | tf_op jit(solution)/shard_map/ppermute | solution.py:350
  62.2 7.6 %copy-start = (f32[3,3,512]{2,1,0:T(4,128)S(1)}, f32[3,3,512]{2,1,0:T(4,128)}, u32[]{:S(2)}) copy-start(f32[3,3,512]{2,1,0:T(4,128)} %taps_ref.3) | copy-start | bytes 55300
  62.2 27.5 %copy-start.4 = (f32[512]{0:T(512)S(1)}, f32[512]{0:T(512)}, u32[]{:S(2)}) copy-start(f32[512]{0:T(512)} %param.15) | copy-start | bytes 6148
  71.2 18.6 %all-to-all-start = ((f32[32,4,512]{2,1,0:T(4,128)}), f32[32,4,512]{2,1,0:T(4,128)S(1)}, u32[]{:S(2)}, u32[]{:S(2)}) async-start(f32[32,4,512]{2,1,0:T(4,128)} %broadcast_in_dim.13), calls=%async_computation | async-start | bytes 524288 | tf_op jit(solution)/shard_map/all_to_all | solution.py:18
  79.2 8.4 %collective-permute-start.11 = (bf16[144,512]{1,0:T(8,128)(2,1)S(1)}, bf16[144,512]{1,0:T(8,128)(2,1)S(1)}, u32[]{:S(2)}, u32[]{:S(2)}) collective-permute-start(bf16[144,512]{1,0:T(8,128)(2,1)S(1)} %get-tuple-element.51), channel_id=1, source_target_pairs={{0,6},{1,7},{2,4},{3,5},{4,2},{5,3},{6,0},{7,1},{8,14},{9,15},{10,... | collective-permute-start | bytes 442376 | tf_op jit(solution)/shard_map/ppermute | solution.py:374
  90.3 7.2 %collective-permute-start.12 = (bf16[128,512]{1,0:T(8,128)(2,1)S(1)}, bf16[128,512]{1,0:T(8,128)(2,1)S(1)}, u32[]{:S(2)}, u32[]{:S(2)}) collective-permute-start(bf16[128,512]{1,0:T(8,128)(2,1)S(1)} %gate.1.refs_0_), channel_id=1, source_target_pairs={{0,32},{32,64},{64,96},{96,128},{128,160},{160,192},{192,224},{224... | collective-permute-start | bytes 393224 | tf_op jit(solution)/shard_map/ppermute | solution.py:37
  92.1 5.4 %collective-permute-start.16 = (bf16[128,512]{1,0:T(8,128)(2,1)S(1)}, bf16[128,512]{1,0:T(8,128)(2,1)S(1)}, u32[]{:S(2)}, u32[]{:S(2)}) collective-permute-start(bf16[128,512]{1,0:T(8,128)(2,1)S(1)} %gate.1.refs_0_), channel_id=1, source_target_pairs={{0,224},{32,0},{64,32},{96,64},{128,96},{160,128},{192,160},{224,1... | collective-permute-start | bytes 393224 | tf_op jit(solution)/shard_map/ppermute | solution.py:40
  97.4 6.2 %collective-permute-start.13 = (bf16[128,512]{1,0:T(8,128)(2,1)S(1)}, bf16[128,512]{1,0:T(8,128)(2,1)S(1)}, u32[]{:S(2)}, u32[]{:S(2)}) collective-permute-start(bf16[128,512]{1,0:T(8,128)(2,1)S(1)} %collective-permute-done.12.refs_1_), channel_id=1, source_target_pairs={{0,32},{32,64},{64,96},{96,128},{128,160},{160,192},{192,224},{224... | collective-permute-start | bytes 393224 | tf_op jit(solution)/shard_map/ppermute | solution.py:37
  97.4 6.2 %collective-permute-start.17 = (bf16[128,512]{1,0:T(8,128)(2,1)S(1)}, bf16[128,512]{1,0:T(8,128)(2,1)S(1)}, u32[]{:S(2)}, u32[]{:S(2)}) collective-permute-start(bf16[128,512]{1,0:T(8,128)(2,1)S(1)} %collective-permute-done.16.refs_2_), channel_id=1, source_target_pairs={{0,224},{32,0},{64,32},{96,64},{128,96},{160,128},{192,160},{224,1... | collective-permute-start | bytes 393224 | tf_op jit(solution)/shard_map/ppermute | solution.py:40
  103.6 6.2 %collective-permute-start.14 = (bf16[128,512]{1,0:T(8,128)(2,1)S(1)}, bf16[128,512]{1,0:T(8,128)(2,1)S(1)}, u32[]{:S(2)}, u32[]{:S(2)}) collective-permute-start(bf16[128,512]{1,0:T(8,128)(2,1)S(1)} %collective-permute-done.13.refs_3_), channel_id=1, source_target_pairs={{0,32},{32,64},{64,96},{96,128},{128,160},{160,192},{192,224},{224... | collective-permute-start | bytes 393224 | tf_op jit(solution)/shard_map/ppermute | solution.py:37
  103.6 6.3 %collective-permute-start.18 = (bf16[128,512]{1,0:T(8,128)(2,1)S(1)}, bf16[128,512]{1,0:T(8,128)(2,1)S(1)}, u32[]{:S(2)}, u32[]{:S(2)}) collective-permute-start(bf16[128,512]{1,0:T(8,128)(2,1)S(1)} %collective-permute-done.17.refs_4_), channel_id=1, source_target_pairs={{0,224},{32,0},{64,32},{96,64},{128,96},{160,128},{192,160},{224,1... | collective-permute-start | bytes 393224 | tf_op jit(solution)/shard_map/ppermute | solution.py:40
  109.8 6.2 %collective-permute-start.15 = (bf16[128,512]{1,0:T(8,128)(2,1)S(1)}, bf16[128,512]{1,0:T(8,128)(2,1)S(1)}, u32[]{:S(2)}, u32[]{:S(2)}) collective-permute-start(bf16[128,512]{1,0:T(8,128)(2,1)S(1)} %collective-permute-done.14.refs_5_), channel_id=1, source_target_pairs={{0,32},{32,64},{64,96},{96,128},{128,160},{160,192},{192,224},{224... | collective-permute-start | bytes 393224 | tf_op jit(solution)/shard_map/ppermute | solution.py:37
Sparse Core Ops, SparseCore 0:
  9.2 47.6 all-gather.2
  58.8 43.0 all-gather.4

commit v12 on v11

--- a/solution.py
+++ b/solution.py
@@ -27,17 +27,25 @@
     return hops
 
 
-def ring(x, axis):
-    count = lax.axis_size(axis)
-    up = [(c, (c + 1) % count) for c in range(count)]
-    down = [(c, (c - 1) % count) for c in range(count)]
+def ring(x):
+    count, blocks = lax.axis_size("ch"), lax.axis_size("seq")
+
+    def onward(turn):
+        pairs = []
+        for c in range(count):
+            for s in range(blocks):
+                to = (c + 1 if s % 2 == turn else c - 1) % count
+                pairs.append((c * blocks + s, to * blocks + s))
+        return pairs
+
+    first, second = onward(0), onward(1)
     arrived = [x]
     below = above = x
     for hop in range(1, count // 2 + 1):
-        below = lax.ppermute(below, axis, up)
+        below = lax.ppermute(below, ("ch", "seq"), first)
         arrived.append(below)
         if 2 * hop < count:
-            above = lax.ppermute(above, axis, down)
+            above = lax.ppermute(above, ("ch", "seq"), second)
             arrived.append(above)
     return arrived
 
@@ -94,9 +102,9 @@
     x_refs, (w_ref, keep_ref, send_ref, lhs_ref, w, sems) = refs[:count], refs[count:]
     chans = x_refs[0].shape[1]
     copies = fetch(w_ref, w, sems, (chans, 2 * chans), (chans, chans))
-    half, here = place_ref[0], place_ref[1]
+    half, here, sign = place_ref[0], place_ref[1], place_ref[2]
     for x_ref, hop in zip(x_refs, ring_hops(count)):
-        origin = lax.rem(here + hop + count, count)
+        origin = lax.rem(here + sign * hop + count, count)
         side = jnp.where(lax.rem(origin, 2) == half, 0, 1)
         at = pl.multiple_of(lax.div(origin, 2) * chans, chans)
         lhs_ref[side, :, pl.ds(at, chans)] = x_ref[...]
@@ -329,8 +337,9 @@
     tied = lax.optimization_barrier((swapped, both, step, join, reach, jump, poles))
     swapped, both, step, join, reach, jump, poles = tied
     second = gather(both)
-    features = ring(swapped, "ch")
+    features = ring(swapped)
     here = lax.axis_index("ch")
+    sign = 1 - 2 * lax.rem(place, 2)
 
     keep, send, lhs = pl.pallas_call(
         functools.partial(mixin_project_kernel, count),
@@ -346,7 +355,7 @@
             flops=8 * padded * depth * chans, bytes_accessed=4 * depth * chans, transcendentals=0
         ),
         name="project_mixin",
-    )(jnp.stack([half, here]).astype(jnp.int32), *features, in_hbm(weight))
+    )(jnp.stack([half, here, sign]).astype(jnp.int32), *features, in_hbm(weight))
     more = lax.ppermute(send, "seq", pairs)
     query_keep, query_send = pl.pallas_call(
         query_project_kernel,
@@ -382,8 +391,8 @@
         name="gate",
     )(states, jump, begin, reach, step, poles, bias[None, :], mixin, query_keep, query_more, taps)
 
-    which = jnp.stack([lax.rem(here + hop + count, count) for hop in ring_hops(count)] + [half])
-    parts = ring(gated, "ch")
+    which = jnp.stack([lax.rem(here + sign * hop + count, count) for hop in ring_hops(count)] + [half])
+    parts = ring(gated)
     first, rest = mix(parts[:-1], which.astype(jnp.int32), second, out_weight.shape[1])
     return pl.pallas_call(
         last_mix_kernel,

time: 124 us -> 125 us (level)
    ppermute x14, waiting for transfers between devices: 28.9 us -> 30.5 us  [the longest x8 29.6 us: ring(): below = lax.ppermute(below, ('ch', 'seq'), first)]
  transfers between devices with their start and end apart: 22 -> 22, of which waited for: 13 -> 15; matrix products, arithmetic and copies ran while one was open for 2% -> 2% of each run, Pallas kernels for 10% -> 10%
where the time goes in v12:
time: 125 us
  waiting for transfers between devices  49.7 us (40%)
  starting transfers between devices  41.6 us (33%)
  between operations  13.5 us (11%)
  Pallas kernels  13.4 us (11%)
  local copies, waits for them, and re-layouts  4.74 us (4%)
  other arithmetic  1.87 us (1%)
    ppermute x8, waiting for transfers between devices, ring(): below = lax.ppermute(below, ('ch', 'seq'), first)  29.6 us
    ppermute x6, starting transfers between devices, ring(): above = lax.ppermute(above, ('ch', 'seq'), second)  18.5 us
    all_to_all x1, starting transfers between devices, spread(): lax.all_to_all(jnp.broadcast_to(x[None], (count,) + x.shape), axis, 0, 0,...  8.04 us
    ppermute x8, starting transfers between devices, ring(): below = lax.ppermute(below, ('ch', 'seq'), first)  7.76 us
    ppermute x1, waiting for transfers between devices, body(): query_more = lax.ppermute(query_send, 'seq', pairs)  6.83 us
    ppermute x1, waiting for transfers between devices, body(): more = lax.ppermute(send, 'seq', pairs)  5.23 us
    pallas_call x1, Pallas kernels, body(): pl.pallas_call(functools.partial(mixin_project_kernel, count), in_specs=[...  3.7 us
    pallas_call x1, Pallas kernels, mix(): pl.pallas_call(functools.partial(mix_kernel, count), in_specs=[IN_SMEM] +...  2.94 us
  transfers between devices with their start and end apart: 22, of which 15 were waited for; matrix products, arithmetic and copies ran while one was open for 2% of the time, Pallas kernels for 10%

profile of v12, /device:TPU:2, one launch (start us, length us, event | category | flops | bytes accessed | tf_op | source)
XLA Modules:
  0.0 124.9 jit_solution(1442205808885965882)
XLA Ops:
  6.5 1.1 dynamic-slice_bitcast_fusion.2
  7.6 0.8 pad_maximum_fusion
  8.4 0.0 all-gather.3.cloned.1.call-update
  8.4 0.0 all-gather.5.cloned.1.call-start
  8.5 1.6 %collective-permute-start.1 = (bf16[128,512]{1,0:T(8,128)(2,1)}, bf16[128,512]{1,0:T(8,128)(2,1)S(1)}, u32[]{:S(2)}, u32[]{:S(2)}) collective-permute-start(bf16[128,512]{1,0:T(8,128)(2,1)} %x_ref.1), channel_id=1, source_target_pairs={{0,6},{1,7},{2,4},{3,5},{4,2},{5,3},{6,0},{7,1},{8,14},{9,15},{10,... | collective-permute-start | bytes 393224 | tf_op jit(solution)/shard_map/ppermute | solution.py:307
  10.0 0.7 slice.12
  10.8 1.9 %collective-permute-start = (bf16[2,512]{1,0:T(2,128)(2,1)S(1)}, bf16[2,512]{1,0:T(2,128)(2,1)S(1)}, u32[]{:S(2)}, u32[]{:S(2)}) collective-permute-start(bf16[2,512]{1,0:T(2,128)(2,1)S(1)} %slice.12), channel_id=1, source_target_pairs={{0,1},{1,2},{2,3},{3,4},{4,5},{5,6},{6,7},{7,8},{8,9},{9,10},{10,1... | collective-permute-start | bytes 6152 | tf_op jit(solution)/shard_map/ppermute | solution.py:306
  12.7 0.1 pad.5.clone
  12.8 2.9 %collective-permute-done = bf16[2,512]{1,0:T(2,128)(2,1)S(1)} collective-permute-done((bf16[2,512]{1,0:T(2,128)(2,1)S(1)}, bf16[2,512]{1,0:T(2,128)(2,1)S(1)}, u32[]{:S(2)}, u32[]{:S(2)}) %collective-permute-start) | collective-permute-done | bytes 2080 | tf_op jit(solution)/shard_map/ppermute | solution.py:306
  15.6 0.0 collective-permute-done.1.y_ref
  15.6 1.0 maximum_maximum_fusion
  16.6 0.7 collective-permute-start.2
  17.3 0.0 copy-start.1
  17.3 0.7 copy-done.1
  18.0 0.7 copy-done.2
  18.7 0.7 copy-done.3
  19.4 0.8 powers.1
  20.2 1.6 %beside.1 = bf16[128,1024]{1,0:T(8,128)(2,1)} custom-call(bf16[128,512]{1,0:T(8,128)(2,1)} %x_ref.1, bf16[128,512]{1,0:T(8,128)(2,1)S(1)} %collective-permute-done.1.y_ref), custom_call_target="tpu_custom_call" | custom-call | tf_op jit(solution)/shard_map/beside/pallas_call | solution.py:329
  21.8 0.0 collective-permute-done.2.refs_0_
  21.8 0.0 all-gather.5.cloned.1.call-update
  21.8 4.8 %collective-permute-start.3 = (bf16[144,512]{1,0:T(8,128)(2,1)S(1)}, bf16[144,512]{1,0:T(8,128)(2,1)S(1)}, u32[]{:S(2)}, u32[]{:S(2)}) collective-permute-start(bf16[144,512]{1,0:T(8,128)(2,1)S(1)} %collective-permute-done.2.refs_0_), channel_id=1, source_target_pairs={{0,32},{1,225},{2,34},{3,227},{4,36},{5,229},{6,38},{7,231},{8,40}... | collective-permute-start | bytes 442376 | tf_op jit(solution)/shard_map/ppermute | solution.py:45
  26.6 4.0 %collective-permute-start.4 = (bf16[144,512]{1,0:T(8,128)(2,1)S(1)}, bf16[144,512]{1,0:T(8,128)(2,1)S(1)}, u32[]{:S(2)}, u32[]{:S(2)}) collective-permute-start(bf16[144,512]{1,0:T(8,128)(2,1)S(1)} %collective-permute-done.2.refs_0_), channel_id=1, source_target_pairs={{0,224},{1,33},{2,226},{3,35},{4,228},{5,37},{6,230},{7,39},{8,232... | collective-permute-start | bytes 442376 | tf_op jit(solution)/shard_map/ppermute | solution.py:48
  30.6 4.4 %collective-permute-done.3.refs_1_ = bf16[144,512]{1,0:T(8,128)(2,1)S(1)} collective-permute-done((bf16[144,512]{1,0:T(8,128)(2,1)S(1)}, bf16[144,512]{1,0:T(8,128)(2,1)S(1)}, u32[]{:S(2)}, u32[]{:S(2)}) %collective-permute-start.3) | collective-permute-done | bytes 147488 | tf_op jit(solution)/shard_map/ppermute | solution.py:45
  35.1 0.0 collective-permute-start.5
  35.1 0.0 collective-permute-done.4.refs_2_
  35.1 3.2 %collective-permute-start.6 = (bf16[144,512]{1,0:T(8,128)(2,1)S(1)}, bf16[144,512]{1,0:T(8,128)(2,1)S(1)}, u32[]{:S(2)}, u32[]{:S(2)}) collective-permute-start(bf16[144,512]{1,0:T(8,128)(2,1)S(1)} %collective-permute-done.4.refs_2_), channel_id=1, source_target_pairs={{0,224},{1,33},{2,226},{3,35},{4,228},{5,37},{6,230},{7,39},{8,232... | collective-permute-start | bytes 442376 | tf_op jit(solution)/shard_map/ppermute | solution.py:48
  38.3 3.8 %collective-permute-done.5.refs_3_ = bf16[144,512]{1,0:T(8,128)(2,1)S(1)} collective-permute-done((bf16[144,512]{1,0:T(8,128)(2,1)S(1)}, bf16[144,512]{1,0:T(8,128)(2,1)S(1)}, u32[]{:S(2)}, u32[]{:S(2)}) %collective-permute-start.5) | collective-permute-done | bytes 147488 | tf_op jit(solution)/shard_map/ppermute | solution.py:45
  42.2 0.0 collective-permute-start.7
  42.2 0.2 collective-permute-done.6.refs_4_
  42.4 3.7 %collective-permute-start.8 = (bf16[144,512]{1,0:T(8,128)(2,1)S(1)}, bf16[144,512]{1,0:T(8,128)(2,1)S(1)}, u32[]{:S(2)}, u32[]{:S(2)}) collective-permute-start(bf16[144,512]{1,0:T(8,128)(2,1)S(1)} %collective-permute-done.6.refs_4_), channel_id=1, source_target_pairs={{0,224},{1,33},{2,226},{3,35},{4,228},{5,37},{6,230},{7,39},{8,232... | collective-permute-start | bytes 442376 | tf_op jit(solution)/shard_map/ppermute | solution.py:48
  46.1 2.4 %collective-permute-done.7.refs_5_ = bf16[144,512]{1,0:T(8,128)(2,1)S(1)} collective-permute-done((bf16[144,512]{1,0:T(8,128)(2,1)S(1)}, bf16[144,512]{1,0:T(8,128)(2,1)S(1)}, u32[]{:S(2)}, u32[]{:S(2)}) %collective-permute-start.7) | collective-permute-done | bytes 147488 | tf_op jit(solution)/shard_map/ppermute | solution.py:45
  48.5 0.0 collective-permute-start.9
  48.5 0.1 pad_add_fusion.place_ref
  48.6 0.7 collective-permute-done.8.refs_6_
  49.3 5.5 %collective-permute-done.9.refs_7_ = bf16[144,512]{1,0:T(8,128)(2,1)S(1)} collective-permute-done((bf16[144,512]{1,0:T(8,128)(2,1)S(1)}, bf16[144,512]{1,0:T(8,128)(2,1)S(1)}, u32[]{:S(2)}, u32[]{:S(2)}) %collective-permute-start.9) | collective-permute-done | bytes 147488 | tf_op jit(solution)/shard_map/ppermute | solution.py:45
  54.9 2.0 %all-gather.3.cloned.1.call-done.refs_8_.w_ref = bf16[2048,1536]{1,0:T(8,128)(2,1)} async-done(((bf16[128,1536]{1,0:T(8,128)(2,1)}), bf16[2048,1536]{1,0:T(8,128)(2,1)}) %all-gather.3.cloned.1.call-update) | async-done | bytes 6291472 | tf_op jit(solution)/shard_map/all_gather | solution.py:299
  56.9 3.7 %project_mixin.1 = (f32[144,1024]{1,0:T(8,128)S(1)}, bf16[144,1024]{1,0:T(8,128)(2,1)S(1)}, bf16[2,144,2048]{2,1,0:T(8,128)(2,1)S(1)}) custom-call(s32[3]{0:T(128)S(1)} %pad_add_fusion.place_ref, bf16[144,512]{1,0:T(8,128)(2,1)S(1)} %collective-permute-done.2.refs_0_, bf16[144,512]{1,0:T(8,128)(2,1)S(1)} %collective-permute-done.3.refs_1_, ...), custom_call_target="tpu_custom_call" | custom-call | flops 1207959552 | bytes 4194304 | tf_op jit(solution)/shard_map/project_mixin/pallas_call | solution.py:344
  60.6 1.6 %collective-permute-start.10 = (bf16[144,1024]{1,0:T(8,128)(2,1)S(1)}, bf16[144,1024]{1,0:T(8,128)(2,1)S(1)}, u32[]{:S(2)}, u32[]{:S(2)}) collective-permute-start(bf16[144,1024]{1,0:T(8,128)(2,1)S(1)} %get-tuple-element.39), channel_id=1, source_target_pairs={{0,6},{1,7},{2,4},{3,5},{4,2},{5,3},{6,0},{7,1},{8,14},{9,15},{10,... | collective-permute-start | bytes 884744 | tf_op jit(solution)/shard_map/ppermute | solution.py:359
  62.2 2.4 %project_query.1 = (f32[144,512]{1,0:T(8,128)S(1)}, bf16[144,512]{1,0:T(8,128)(2,1)S(1)}) custom-call(bf16[2,144,2048]{2,1,0:T(8,128)(2,1)S(1)} %get-tuple-element.40.lhs_ref, bf16[2048,1536]{1,0:T(8,128)(2,1)} %all-gather.3.cloned.1.call-done.refs_8_.w_ref), custom_call_target="tpu_custom_call" | custom-call | flops 603979776 | bytes 2097152 | tf_op jit(solution)/shard_map/project_query/pallas_call | solution.py:360
  64.6 5.2 %collective-permute-done.10.more_ref = bf16[144,1024]{1,0:T(8,128)(2,1)S(1)} collective-permute-done((bf16[144,1024]{1,0:T(8,128)(2,1)S(1)}, bf16[144,1024]{1,0:T(8,128)(2,1)S(1)}, u32[]{:S(2)}, u32[]{:S(2)}) %collective-permute-start.10) | collective-permute-done | bytes 294944 | tf_op jit(solution)/shard_map/ppermute | solution.py:359
  69.9 0.6 scan.1
  70.4 0.7 broadcast_in_dim.13
  71.2 8.0 %all-to-all-start = ((f32[32,4,512]{2,1,0:T(4,128)}), f32[32,4,512]{2,1,0:T(4,128)S(1)}, u32[]{:S(2)}, u32[]{:S(2)}) async-start(f32[32,4,512]{2,1,0:T(4,128)} %broadcast_in_dim.13), calls=%async_computation | async-start | bytes 524288 | tf_op jit(solution)/shard_map/all_to_all | solution.py:18
  79.2 1.6 %collective-permute-start.11 = (bf16[144,512]{1,0:T(8,128)(2,1)S(1)}, bf16[144,512]{1,0:T(8,128)(2,1)S(1)}, u32[]{:S(2)}, u32[]{:S(2)}) collective-permute-start(bf16[144,512]{1,0:T(8,128)(2,1)S(1)} %get-tuple-element.51), channel_id=1, source_target_pairs={{0,6},{1,7},{2,4},{3,5},{4,2},{5,3},{6,0},{7,1},{8,14},{9,15},{10,... | collective-permute-start | bytes 442376 | tf_op jit(solution)/shard_map/ppermute | solution.py:383
  80.8 6.8 %collective-permute-done.11.more_ref = bf16[144,512]{1,0:T(8,128)(2,1)S(1)} collective-permute-done((bf16[144,512]{1,0:T(8,128)(2,1)S(1)}, bf16[144,512]{1,0:T(8,128)(2,1)S(1)}, u32[]{:S(2)}, u32[]{:S(2)}) %collective-permute-start.11) | collective-permute-done | bytes 147488 | tf_op jit(solution)/shard_map/ppermute | solution.py:383
  87.6 2.1 %all-to-all-done.all_ref = f32[32,4,512]{2,1,0:T(4,128)S(1)} async-done(((f32[32,4,512]{2,1,0:T(4,128)}), f32[32,4,512]{2,1,0:T(4,128)S(1)}, u32[]{:S(2)}, u32[]{:S(2)}) %all-to-all-start) | async-done | bytes 262176 | tf_op jit(solution)/shard_map/all_to_all | solution.py:18
  89.7 0.5 gate.1.refs_0_
  90.3 1.8 %collective-permute-start.12 = (bf16[128,512]{1,0:T(8,128)(2,1)S(1)}, bf16[128,512]{1,0:T(8,128)(2,1)S(1)}, u32[]{:S(2)}, u32[]{:S(2)}) collective-permute-start(bf16[128,512]{1,0:T(8,128)(2,1)S(1)} %gate.1.refs_0_), channel_id=1, source_target_pairs={{0,32},{1,225},{2,34},{3,227},{4,36},{5,229},{6,38},{7,231},{8,40}... | collective-permute-start | bytes 393224 | tf_op jit(solution)/shard_map/ppermute | solution.py:45
  92.1 1.9 %collective-permute-start.16 = (bf16[128,512]{1,0:T(8,128)(2,1)S(1)}, bf16[128,512]{1,0:T(8,128)(2,1)S(1)}, u32[]{:S(2)}, u32[]{:S(2)}) collective-permute-start(bf16[128,512]{1,0:T(8,128)(2,1)S(1)} %gate.1.refs_0_), channel_id=1, source_target_pairs={{0,224},{1,33},{2,226},{3,35},{4,228},{5,37},{6,230},{7,39},{8,232... | collective-permute-start | bytes 393224 | tf_op jit(solution)/shard_map/ppermute | solution.py:48
  93.9 2.9 %collective-permute-done.12.refs_1_ = bf16[128,512]{1,0:T(8,128)(2,1)S(1)} collective-permute-done((bf16[128,512]{1,0:T(8,128)(2,1)S(1)}, bf16[128,512]{1,0:T(8,128)(2,1)S(1)}, u32[]{:S(2)}, u32[]{:S(2)}) %collective-permute-start.12) | collective-permute-done | bytes 131104 | tf_op jit(solution)/shard_map/ppermute | solution.py:45
  96.8 1.0 collective-permute-start.13
  97.8 0.0 collective-permute-done.16.refs_2_
  97.8 2.6 %collective-permute-start.17 = (bf16[128,512]{1,0:T(8,128)(2,1)S(1)}, bf16[128,512]{1,0:T(8,128)(2,1)S(1)}, u32[]{:S(2)}, u32[]{:S(2)}) collective-permute-start(bf16[128,512]{1,0:T(8,128)(2,1)S(1)} %collective-permute-done.16.refs_2_), channel_id=1, source_target_pairs={{0,224},{1,33},{2,226},{3,35},{4,228},{5,37},{6,230},{7,39},{8,232... | collective-permute-start | bytes 393224 | tf_op jit(solution)/shard_map/ppermute | solution.py:48
  100.4 3.0 %collective-permute-done.13.refs_3_ = bf16[128,512]{1,0:T(8,128)(2,1)S(1)} collective-permute-done((bf16[128,512]{1,0:T(8,128)(2,1)S(1)}, bf16[128,512]{1,0:T(8,128)(2,1)S(1)}, u32[]{:S(2)}, u32[]{:S(2)}) %collective-permute-start.13) | collective-permute-done | bytes 131104 | tf_op jit(solution)/shard_map/ppermute | solution.py:45
  103.4 0.2 collective-permute-start.14
  103.6 0.0 collective-permute-done.17.refs_4_
  103.6 3.0 %collective-permute-start.18 = (bf16[128,512]{1,0:T(8,128)(2,1)S(1)}, bf16[128,512]{1,0:T(8,128)(2,1)S(1)}, u32[]{:S(2)}, u32[]{:S(2)}) collective-permute-start(bf16[128,512]{1,0:T(8,128)(2,1)S(1)} %collective-permute-done.17.refs_4_), channel_id=1, source_target_pairs={{0,224},{1,33},{2,226},{3,35},{4,228},{5,37},{6,230},{7,39},{8,232... | collective-permute-start | bytes 393224 | tf_op jit(solution)/shard_map/ppermute | solution.py:48
  106.6 4.3 %collective-permute-done.14.refs_5_ = bf16[128,512]{1,0:T(8,128)(2,1)S(1)} collective-permute-done((bf16[128,512]{1,0:T(8,128)(2,1)S(1)}, bf16[128,512]{1,0:T(8,128)(2,1)S(1)}, u32[]{:S(2)}, u32[]{:S(2)}) %collective-permute-start.14) | collective-permute-done | bytes 131104 | tf_op jit(solution)/shard_map/ppermute | solution.py:45
  110.9 0.0 collective-permute-start.15
  111.0 0.1 stack.52.which_ref
  111.0 0.0 collective-permute-done.18.refs_6_
  111.0 2.9 %mix.1 = (f32[128,512]{1,0:T(8,128)S(1)}, bf16[512,512]{1,0:T(8,128)(2,1)S(1)}) custom-call(s32[9]{0:T(128)S(1)} %stack.52.which_ref, bf16[128,512]{1,0:T(8,128)(2,1)S(1)} %gate.1.refs_0_, bf16[128,512]{1,0:T(8,128)(2,1)S(1)} %collective-permute-done.12.refs_1_, bf16[128,512]{1,0:T(8,128)(2,1)S(1)} %collective-permute-done.16.refs_2_, ...), custom_call_target="tpu_custom_call" | custom-call | flops 536870912 | bytes 4194304 | tf_op jit(solution)/shard_map/mix/pallas_call | solution.py:267
  114.0 3.1 %collective-permute-done.15.x_ref = bf16[128,512]{1,0:T(8,128)(2,1)S(1)} collective-permute-done((bf16[128,512]{1,0:T(8,128)(2,1)S(1)}, bf16[128,512]{1,0:T(8,128)(2,1)S(1)}, u32[]{:S(2)}, u32[]{:S(2)}) %collective-permute-start.15) | collective-permute-done | bytes 131104 | tf_op jit(solution)/shard_map/ppermute | solution.py:45
  117.1 0.9 last_mix.1
  (9 shorter events, 0.0 us)
Async XLA Ops:
  6.5 50.4 %all-gather.3.cloned.1.call-start = ((), (), s32[]{:S(2)}) async-start(), calls=%async_computation.1 | async-start | bytes 6684672 | tf_op jit(solution)/shard_map/all_gather | solution.py:299
  8.4 102.6 %all-gather.5.cloned.1.call-start = ((), (), s32[]{:S(2)}) async-start(), calls=%async_computation.2 | async-start | bytes 4456448 | tf_op jit(solution)/shard_map/all_gather | solution.py:299
  8.5 7.2 %collective-permute-start.1 = (bf16[128,512]{1,0:T(8,128)(2,1)}, bf16[128,512]{1,0:T(8,128)(2,1)S(1)}, u32[]{:S(2)}, u32[]{:S(2)}) collective-permute-start(bf16[128,512]{1,0:T(8,128)(2,1)} %x_ref.1), channel_id=1, source_target_pairs={{0,6},{1,7},{2,4},{3,5},{4,2},{5,3},{6,0},{7,1},{8,14},{9,15},{10,... | collective-permute-start | bytes 393224 | tf_op jit(solution)/shard_map/ppermute | solution.py:307
  10.8 4.9 %collective-permute-start = (bf16[2,512]{1,0:T(2,128)(2,1)S(1)}, bf16[2,512]{1,0:T(2,128)(2,1)S(1)}, u32[]{:S(2)}, u32[]{:S(2)}) collective-permute-start(bf16[2,512]{1,0:T(2,128)(2,1)S(1)} %slice.12), channel_id=1, source_target_pairs={{0,1},{1,2},{2,3},{3,4},{4,5},{5,6},{6,7},{7,8},{8,9},{9,10},{10,1... | collective-permute-start | bytes 6152 | tf_op jit(solution)/shard_map/ppermute | solution.py:306
  16.6 5.1 %collective-permute-start.2 = (bf16[144,512]{1,0:T(8,128)(2,1)S(1)}, bf16[144,512]{1,0:T(8,128)(2,1)S(1)}, u32[]{:S(2)}, u32[]{:S(2)}) collective-permute-start(bf16[144,512]{1,0:T(8,128)(2,1)S(1)} %maximum_maximum_fusion), channel_id=1, source_target_pairs={{0,0},{1,1},{2,2},{3,3},{4,34},{5,35},{6,32},{7,33},{8,8},{9,9},{1... | collective-permute-start | bytes 442376 | tf_op jit(solution)/shard_map/ppermute | solution.py:315
  17.3 0.7 copy-start.1
  18.0 0.7 copy-start.2
  18.7 0.7 copy-start.3
  21.8 13.3 %collective-permute-start.3 = (bf16[144,512]{1,0:T(8,128)(2,1)S(1)}, bf16[144,512]{1,0:T(8,128)(2,1)S(1)}, u32[]{:S(2)}, u32[]{:S(2)}) collective-permute-start(bf16[144,512]{1,0:T(8,128)(2,1)S(1)} %collective-permute-done.2.refs_0_), channel_id=1, source_target_pairs={{0,32},{1,225},{2,34},{3,227},{4,36},{5,229},{6,38},{7,231},{8,40}... | collective-permute-start | bytes 442376 | tf_op jit(solution)/shard_map/ppermute | solution.py:45
  26.6 8.5 %collective-permute-start.4 = (bf16[144,512]{1,0:T(8,128)(2,1)S(1)}, bf16[144,512]{1,0:T(8,128)(2,1)S(1)}, u32[]{:S(2)}, u32[]{:S(2)}) collective-permute-start(bf16[144,512]{1,0:T(8,128)(2,1)S(1)} %collective-permute-done.2.refs_0_), channel_id=1, source_target_pairs={{0,224},{1,33},{2,226},{3,35},{4,228},{5,37},{6,230},{7,39},{8,232... | collective-permute-start | bytes 442376 | tf_op jit(solution)/shard_map/ppermute | solution.py:48
  35.1 7.1 %collective-permute-start.5 = (bf16[144,512]{1,0:T(8,128)(2,1)S(1)}, bf16[144,512]{1,0:T(8,128)(2,1)S(1)}, u32[]{:S(2)}, u32[]{:S(2)}) collective-permute-start(bf16[144,512]{1,0:T(8,128)(2,1)S(1)} %collective-permute-done.3.refs_1_), channel_id=1, source_target_pairs={{0,32},{1,225},{2,34},{3,227},{4,36},{5,229},{6,38},{7,231},{8,40}... | collective-permute-start | bytes 442376 | tf_op jit(solution)/shard_map/ppermute | solution.py:45
  35.1 7.3 %collective-permute-start.6 = (bf16[144,512]{1,0:T(8,128)(2,1)S(1)}, bf16[144,512]{1,0:T(8,128)(2,1)S(1)}, u32[]{:S(2)}, u32[]{:S(2)}) collective-permute-start(bf16[144,512]{1,0:T(8,128)(2,1)S(1)} %collective-permute-done.4.refs_2_), channel_id=1, source_target_pairs={{0,224},{1,33},{2,226},{3,35},{4,228},{5,37},{6,230},{7,39},{8,232... | collective-permute-start | bytes 442376 | tf_op jit(solution)/shard_map/ppermute | solution.py:48
  42.2 6.4 %collective-permute-start.7 = (bf16[144,512]{1,0:T(8,128)(2,1)S(1)}, bf16[144,512]{1,0:T(8,128)(2,1)S(1)}, u32[]{:S(2)}, u32[]{:S(2)}) collective-permute-start(bf16[144,512]{1,0:T(8,128)(2,1)S(1)} %collective-permute-done.5.refs_3_), channel_id=1, source_target_pairs={{0,32},{1,225},{2,34},{3,227},{4,36},{5,229},{6,38},{7,231},{8,40}... | collective-permute-start | bytes 442376 | tf_op jit(solution)/shard_map/ppermute | solution.py:45
  42.4 6.9 %collective-permute-start.8 = (bf16[144,512]{1,0:T(8,128)(2,1)S(1)}, bf16[144,512]{1,0:T(8,128)(2,1)S(1)}, u32[]{:S(2)}, u32[]{:S(2)}) collective-permute-start(bf16[144,512]{1,0:T(8,128)(2,1)S(1)} %collective-permute-done.6.refs_4_), channel_id=1, source_target_pairs={{0,224},{1,33},{2,226},{3,35},{4,228},{5,37},{6,230},{7,39},{8,232... | collective-permute-start | bytes 442376 | tf_op jit(solution)/shard_map/ppermute | solution.py:48
  48.5 6.4 %collective-permute-start.9 = (bf16[144,512]{1,0:T(8,128)(2,1)S(1)}, bf16[144,512]{1,0:T(8,128)(2,1)S(1)}, u32[]{:S(2)}, u32[]{:S(2)}) collective-permute-start(bf16[144,512]{1,0:T(8,128)(2,1)S(1)} %collective-permute-done.7.refs_5_), channel_id=1, source_target_pairs={{0,32},{1,225},{2,34},{3,227},{4,36},{5,229},{6,38},{7,231},{8,40}... | collective-permute-start | bytes 442376 | tf_op jit(solution)/shard_map/ppermute | solution.py:45
  60.6 9.2 %collective-permute-start.10 = (bf16[144,1024]{1,0:T(8,128)(2,1)S(1)}, bf16[144,1024]{1,0:T(8,128)(2,1)S(1)}, u32[]{:S(2)}, u32[]{:S(2)}) collective-permute-start(bf16[144,1024]{1,0:T(8,128)(2,1)S(1)} %get-tuple-element.39), channel_id=1, source_target_pairs={{0,6},{1,7},{2,4},{3,5},{4,2},{5,3},{6,0},{7,1},{8,14},{9,15},{10,... | collective-permute-start | bytes 884744 | tf_op jit(solution)/shard_map/ppermute | solution.py:359
  62.2 7.6 %copy-start = (f32[3,3,512]{2,1,0:T(4,128)S(1)}, f32[3,3,512]{2,1,0:T(4,128)}, u32[]{:S(2)}) copy-start(f32[3,3,512]{2,1,0:T(4,128)} %taps_ref.3) | copy-start | bytes 55300
  62.2 27.5 %copy-start.4 = (f32[512]{0:T(512)S(1)}, f32[512]{0:T(512)}, u32[]{:S(2)}) copy-start(f32[512]{0:T(512)} %param.15) | copy-start | bytes 6148
  71.2 18.6 %all-to-all-start = ((f32[32,4,512]{2,1,0:T(4,128)}), f32[32,4,512]{2,1,0:T(4,128)S(1)}, u32[]{:S(2)}, u32[]{:S(2)}) async-start(f32[32,4,512]{2,1,0:T(4,128)} %broadcast_in_dim.13), calls=%async_computation | async-start | bytes 524288 | tf_op jit(solution)/shard_map/all_to_all | solution.py:18
  79.2 8.4 %collective-permute-start.11 = (bf16[144,512]{1,0:T(8,128)(2,1)S(1)}, bf16[144,512]{1,0:T(8,128)(2,1)S(1)}, u32[]{:S(2)}, u32[]{:S(2)}) collective-permute-start(bf16[144,512]{1,0:T(8,128)(2,1)S(1)} %get-tuple-element.51), channel_id=1, source_target_pairs={{0,6},{1,7},{2,4},{3,5},{4,2},{5,3},{6,0},{7,1},{8,14},{9,15},{10,... | collective-permute-start | bytes 442376 | tf_op jit(solution)/shard_map/ppermute | solution.py:383
  90.3 6.5 %collective-permute-start.12 = (bf16[128,512]{1,0:T(8,128)(2,1)S(1)}, bf16[128,512]{1,0:T(8,128)(2,1)S(1)}, u32[]{:S(2)}, u32[]{:S(2)}) collective-permute-start(bf16[128,512]{1,0:T(8,128)(2,1)S(1)} %gate.1.refs_0_), channel_id=1, source_target_pairs={{0,32},{1,225},{2,34},{3,227},{4,36},{5,229},{6,38},{7,231},{8,40}... | collective-permute-start | bytes 393224 | tf_op jit(solution)/shard_map/ppermute | solution.py:45
  92.1 5.7 %collective-permute-start.16 = (bf16[128,512]{1,0:T(8,128)(2,1)S(1)}, bf16[128,512]{1,0:T(8,128)(2,1)S(1)}, u32[]{:S(2)}, u32[]{:S(2)}) collective-permute-start(bf16[128,512]{1,0:T(8,128)(2,1)S(1)} %gate.1.refs_0_), channel_id=1, source_target_pairs={{0,224},{1,33},{2,226},{3,35},{4,228},{5,37},{6,230},{7,39},{8,232... | collective-permute-start | bytes 393224 | tf_op jit(solution)/shard_map/ppermute | solution.py:48
  96.8 6.6 %collective-permute-start.13 = (bf16[128,512]{1,0:T(8,128)(2,1)S(1)}, bf16[128,512]{1,0:T(8,128)(2,1)S(1)}, u32[]{:S(2)}, u32[]{:S(2)}) collective-permute-start(bf16[128,512]{1,0:T(8,128)(2,1)S(1)} %collective-permute-done.12.refs_1_), channel_id=1, source_target_pairs={{0,32},{1,225},{2,34},{3,227},{4,36},{5,229},{6,38},{7,231},{8,40}... | collective-permute-start | bytes 393224 | tf_op jit(solution)/shard_map/ppermute | solution.py:45
  97.8 5.8 %collective-permute-start.17 = (bf16[128,512]{1,0:T(8,128)(2,1)S(1)}, bf16[128,512]{1,0:T(8,128)(2,1)S(1)}, u32[]{:S(2)}, u32[]{:S(2)}) collective-permute-start(bf16[128,512]{1,0:T(8,128)(2,1)S(1)} %collective-permute-done.16.refs_2_), channel_id=1, source_target_pairs={{0,224},{1,33},{2,226},{3,35},{4,228},{5,37},{6,230},{7,39},{8,232... | collective-permute-start | bytes 393224 | tf_op jit(solution)/shard_map/ppermute | solution.py:48
  103.4 7.6 %collective-permute-start.14 = (bf16[128,512]{1,0:T(8,128)(2,1)S(1)}, bf16[128,512]{1,0:T(8,128)(2,1)S(1)}, u32[]{:S(2)}, u32[]{:S(2)}) collective-permute-start(bf16[128,512]{1,0:T(8,128)(2,1)S(1)} %collective-permute-done.13.refs_3_), channel_id=1, source_target_pairs={{0,32},{1,225},{2,34},{3,227},{4,36},{5,229},{6,38},{7,231},{8,40}... | collective-permute-start | bytes 393224 | tf_op jit(solution)/shard_map/ppermute | solution.py:45
  103.6 7.5 %collective-permute-start.18 = (bf16[128,512]{1,0:T(8,128)(2,1)S(1)}, bf16[128,512]{1,0:T(8,128)(2,1)S(1)}, u32[]{:S(2)}, u32[]{:S(2)}) collective-permute-start(bf16[128,512]{1,0:T(8,128)(2,1)S(1)} %collective-permute-done.17.refs_4_), channel_id=1, source_target_pairs={{0,224},{1,33},{2,226},{3,35},{4,228},{5,37},{6,230},{7,39},{8,232... | collective-permute-start | bytes 393224 | tf_op jit(solution)/shard_map/ppermute | solution.py:48
  110.9 6.2 %collective-permute-start.15 = (bf16[128,512]{1,0:T(8,128)(2,1)S(1)}, bf16[128,512]{1,0:T(8,128)(2,1)S(1)}, u32[]{:S(2)}, u32[]{:S(2)}) collective-permute-start(bf16[128,512]{1,0:T(8,128)(2,1)S(1)} %collective-permute-done.14.refs_5_), channel_id=1, source_target_pairs={{0,32},{1,225},{2,34},{3,227},{4,36},{5,229},{6,38},{7,231},{8,40}... | collective-permute-start | bytes 393224 | tf_op jit(solution)/shard_map/ppermute | solution.py:45
Sparse Core Ops, SparseCore 0:
  9.2 47.6 all-gather.2
  58.8 43.0 all-gather.4

commit v13 on v11

--- a/solution.py
+++ b/solution.py
@@ -68,12 +68,12 @@
         poles_ref[2 + n : 3 + n, :] = residue_ref[1, n : n + 1, :]
 
 
-def fetch(w_ref, w, sems, starts, sizes):
+def fetch(w_ref, w, sems, branches):
     copies = []
-    for j, (start, size) in enumerate(zip(starts, sizes)):
-        at = sum(sizes[:j])
+    for j, branch in enumerate(branches):
+        chans = w_ref.shape[2]
         copies.append(
-            pltpu.make_async_copy(w_ref.at[:, pl.ds(start, size)], w.at[:, pl.ds(at, size)], sems.at[j])
+            pltpu.make_async_copy(w_ref.at[branch], w.at[:, pl.ds(j * chans, chans)], sems.at[j])
         )
         copies[-1].start()
     return copies
@@ -93,7 +93,7 @@
 def mixin_project_kernel(count, place_ref, *refs):
     x_refs, (w_ref, keep_ref, send_ref, lhs_ref, w, sems) = refs[:count], refs[count:]
     chans = x_refs[0].shape[1]
-    copies = fetch(w_ref, w, sems, (chans, 2 * chans), (chans, chans))
+    copies = fetch(w_ref, w, sems, (1, 2))
     half, here = place_ref[0], place_ref[1]
     for x_ref, hop in zip(x_refs, ring_hops(count)):
         origin = lax.rem(here + hop + count, count)
@@ -105,8 +105,16 @@
 
 def query_project_kernel(lhs_ref, w_ref, keep_ref, send_ref, w, sems):
     chans = keep_ref.shape[1]
-    copies = fetch(w_ref, w, sems, (0,), (chans,))
+    copies = fetch(w_ref, w, sems, (0,))
     product(lhs_ref, w, copies, chans, keep_ref, send_ref)
+
+
+def cut_kernel(place_ref, w_ref, out_ref, sem):
+    cols = out_ref.shape[2]
+    at = pl.multiple_of(place_ref[0] * cols, cols)
+    copy = pltpu.make_async_copy(w_ref.at[:, :, pl.ds(at, cols)], out_ref, sem)
+    copy.start()
+    copy.wait()
 
 
 def beside_kernel(x_ref, y_ref, out_ref, sem):
@@ -281,15 +289,20 @@
     rows, chans = inputs.shape
     place, blocks = lax.axis_index("seq"), lax.axis_size("seq")
     count = lax.axis_size("ch")
-    col_start = lax.axis_index("ch") * chans
     near = [(s % 8) // 4 for s in range(blocks)]
     mirror = [s + 6 - 4 * ((s % 8) // 2) for s in range(blocks)]
-    cut = lax.dynamic_slice(in_weight, (0, 0, col_start), (in_weight.shape[0], 3, chans))
-    own_weight = jnp.concatenate([cut[:, g] for g in range(3)], axis=1)
+    cut = pl.pallas_call(
+        cut_kernel,
+        in_specs=[IN_SMEM, IN_HBM],
+        out_shape=jax.ShapeDtypeStruct((3, in_weight.shape[0], chans), jnp.bfloat16),
+        scratch_shapes=[pltpu.SemaphoreType.DMA(())],
+        compiler_params=pltpu.CompilerParams(vmem_limit_bytes=VMEM),
+        name="cut",
+    )(lax.axis_index("ch").reshape(1).astype(jnp.int32), in_hbm(in_weight.transpose(1, 0, 2)))
     pairs = [(s, mirror[s]) for s in range(blocks)]
     halves = [[s for s in range(blocks) if near[s] == h] for h in range(2)]
-    gather = lambda x: lax.all_gather(x, "seq", axis=0, tiled=True, axis_index_groups=halves)
-    weight = gather(own_weight)
+    gather = lambda x, axis: lax.all_gather(x, "seq", axis=axis, tiled=True, axis_index_groups=halves)
+    weight = gather(cut, 1)
     f32, b16 = jnp.float32, jnp.bfloat16
     padded, depth = rows + HALO, chans * count // 2
     params = pltpu.CompilerParams(vmem_limit_bytes=VMEM)
@@ -328,7 +341,7 @@
     )(in_hbm(out_weight), mirrored)
     tied = lax.optimization_barrier((swapped, both, step, join, reach, jump, poles))
     swapped, both, step, join, reach, jump, poles = tied
-    second = gather(both)
+    second = gather(both, 0)
     features = ring(swapped, "ch")
     here = lax.axis_index("ch")
 

time: 124 us -> 124 us (level)
  local copies, waits for them, and re-layouts: 4.74 us -> 1.63 us
  starting transfers between devices: 41.3 us -> 43.8 us
  Pallas kernels: 13.4 us -> 15.2 us
    unnamed x10, local copies, waits for them, and re-layouts: 2.07 us -> 0.02 us
    ppermute x8, starting transfers between devices: 6.61 us -> 8.65 us  [ring(): below = lax.ppermute(below, axis, up)]
    pallas_call x0 -> x1, Pallas kernels: none -> 1.8 us  [body(): pl.pallas_call(cut_kernel, in_specs=[IN_SMEM, IN_HBM], out_shape=jax.Shap...]
  transfers between devices with their start and end apart: 22 -> 22, of which waited for: 13 -> 14; matrix products, arithmetic and copies ran while one was open for 2% -> 2% of each run, Pallas kernels for 10% -> 10%
where the time goes in v13:
time: 124 us
  waiting for transfers between devices  48.4 us (39%)
  starting transfers between devices  43.8 us (35%)
  Pallas kernels  15.2 us (12%)
  between operations  13.6 us (11%)
  local copies, waits for them, and re-layouts  1.63 us (1%)
    ppermute x8, waiting for transfers between devices, ring(): below = lax.ppermute(below, axis, up)  29.2 us
    ppermute x6, starting transfers between devices, ring(): above = lax.ppermute(above, axis, down)  19.8 us
    ppermute x8, starting transfers between devices, ring(): below = lax.ppermute(below, axis, up)  8.65 us
    all_to_all x1, starting transfers between devices, spread(): lax.all_to_all(jnp.broadcast_to(x[None], (count,) + x.shape), axis, 0, 0,...  8.04 us
    ppermute x1, waiting for transfers between devices, body(): query_more = lax.ppermute(query_send, 'seq', pairs)  6.84 us
    ppermute x1, waiting for transfers between devices, body(): more = lax.ppermute(send, 'seq', pairs)  5.23 us
    pallas_call x1, Pallas kernels, body(): pl.pallas_call(functools.partial(mixin_project_kernel, count), in_specs=[...  3.7 us
    pallas_call x1, Pallas kernels, mix(): pl.pallas_call(functools.partial(mix_kernel, count), in_specs=[IN_SMEM] +...  2.94 us
  transfers between devices with their start and end apart: 22, of which 14 were waited for; matrix products, arithmetic and copies ran while one was open for 2% of the time, Pallas kernels for 10%

profile of v13, /device:TPU:2, one launch (start us, length us, event | category | flops | bytes accessed | tf_op | source)
XLA Modules:
  0.0 123.7 jit_solution(10798779279699422514)
XLA Ops:
  6.5 0.0 all-gather.3.cloned.1.call-start
  6.5 1.8 %cut.1 = bf16[3,128,512]{2,1,0:T(8,128)(2,1)} custom-call(s32[1]{0:T(128)} %bitcast.1.place_ref, bf16[3,128,4096]{2,1,0:T(8,128)(2,1)} %bitcast.20), custom_call_target="tpu_custom_call" | custom-call | tf_op jit(solution)/shard_map/cut/pallas_call | solution.py:294
  8.4 0.0 all-gather.3.cloned.1.call-update
  8.4 0.0 all-gather.5.cloned.1.call-start
  8.4 1.6 %collective-permute-start.1 = (bf16[128,512]{1,0:T(8,128)(2,1)}, bf16[128,512]{1,0:T(8,128)(2,1)S(1)}, u32[]{:S(2)}, u32[]{:S(2)}) collective-permute-start(bf16[128,512]{1,0:T(8,128)(2,1)} %x_ref.1), channel_id=1, source_target_pairs={{0,6},{1,7},{2,4},{3,5},{4,2},{5,3},{6,0},{7,1},{8,14},{9,15},{10,... | collective-permute-start | bytes 393224 | tf_op jit(solution)/shard_map/ppermute | solution.py:312
  10.0 0.7 slice.3
  10.7 1.9 %collective-permute-start = (bf16[2,512]{1,0:T(2,128)(2,1)S(1)}, bf16[2,512]{1,0:T(2,128)(2,1)S(1)}, u32[]{:S(2)}, u32[]{:S(2)}) collective-permute-start(bf16[2,512]{1,0:T(2,128)(2,1)S(1)} %slice.3), channel_id=1, source_target_pairs={{0,1},{1,2},{2,3},{3,4},{4,5},{5,6},{6,7},{7,8},{8,9},{9,10},{10,1... | collective-permute-start | bytes 6152 | tf_op jit(solution)/shard_map/ppermute | solution.py:311
  12.6 0.1 pad.2.clone
  12.7 2.9 %collective-permute-done = bf16[2,512]{1,0:T(2,128)(2,1)S(1)} collective-permute-done((bf16[2,512]{1,0:T(2,128)(2,1)S(1)}, bf16[2,512]{1,0:T(2,128)(2,1)S(1)}, u32[]{:S(2)}, u32[]{:S(2)}) %collective-permute-start) | collective-permute-done | bytes 2080 | tf_op jit(solution)/shard_map/ppermute | solution.py:311
  15.6 0.0 collective-permute-done.1.y_ref
  15.6 1.0 maximum_maximum_fusion
  16.6 0.7 collective-permute-start.2
  17.3 0.0 copy-done.2
  17.3 0.0 copy-done.3
  17.3 0.0 copy-done.1
  17.3 0.8 powers.1
  18.1 1.6 %beside.1 = bf16[128,1024]{1,0:T(8,128)(2,1)} custom-call(bf16[128,512]{1,0:T(8,128)(2,1)} %x_ref.1, bf16[128,512]{1,0:T(8,128)(2,1)S(1)} %collective-permute-done.1.y_ref), custom_call_target="tpu_custom_call" | custom-call | tf_op jit(solution)/shard_map/beside/pallas_call | solution.py:334
  19.7 0.0 collective-permute-done.2.refs_0_
  19.7 0.0 all-gather.5.cloned.1.call-update
  19.7 6.8 %collective-permute-start.3 = (bf16[144,512]{1,0:T(8,128)(2,1)S(1)}, bf16[144,512]{1,0:T(8,128)(2,1)S(1)}, u32[]{:S(2)}, u32[]{:S(2)}) collective-permute-start(bf16[144,512]{1,0:T(8,128)(2,1)S(1)} %collective-permute-done.2.refs_0_), channel_id=1, source_target_pairs={{0,32},{32,64},{64,96},{96,128},{128,160},{160,192},{192,224},{224... | collective-permute-start | bytes 442376 | tf_op jit(solution)/shard_map/ppermute | solution.py:37
  26.6 4.2 %collective-permute-start.4 = (bf16[144,512]{1,0:T(8,128)(2,1)S(1)}, bf16[144,512]{1,0:T(8,128)(2,1)S(1)}, u32[]{:S(2)}, u32[]{:S(2)}) collective-permute-start(bf16[144,512]{1,0:T(8,128)(2,1)S(1)} %collective-permute-done.2.refs_0_), channel_id=1, source_target_pairs={{0,224},{32,0},{64,32},{96,64},{128,96},{160,128},{192,160},{224,1... | collective-permute-start | bytes 442376 | tf_op jit(solution)/shard_map/ppermute | solution.py:40
  30.8 3.0 %collective-permute-done.3.refs_1_ = bf16[144,512]{1,0:T(8,128)(2,1)S(1)} collective-permute-done((bf16[144,512]{1,0:T(8,128)(2,1)S(1)}, bf16[144,512]{1,0:T(8,128)(2,1)S(1)}, u32[]{:S(2)}, u32[]{:S(2)}) %collective-permute-start.3) | collective-permute-done | bytes 147488 | tf_op jit(solution)/shard_map/ppermute | solution.py:37
  33.8 0.0 collective-permute-start.5
  33.8 0.0 collective-permute-done.4.refs_2_
  33.8 3.6 %collective-permute-start.6 = (bf16[144,512]{1,0:T(8,128)(2,1)S(1)}, bf16[144,512]{1,0:T(8,128)(2,1)S(1)}, u32[]{:S(2)}, u32[]{:S(2)}) collective-permute-start(bf16[144,512]{1,0:T(8,128)(2,1)S(1)} %collective-permute-done.4.refs_2_), channel_id=1, source_target_pairs={{0,224},{32,0},{64,32},{96,64},{128,96},{160,128},{192,160},{224,1... | collective-permute-start | bytes 442376 | tf_op jit(solution)/shard_map/ppermute | solution.py:40
  37.4 4.0 %collective-permute-done.5.refs_3_ = bf16[144,512]{1,0:T(8,128)(2,1)S(1)} collective-permute-done((bf16[144,512]{1,0:T(8,128)(2,1)S(1)}, bf16[144,512]{1,0:T(8,128)(2,1)S(1)}, u32[]{:S(2)}, u32[]{:S(2)}) %collective-permute-start.5) | collective-permute-done | bytes 147488 | tf_op jit(solution)/shard_map/ppermute | solution.py:37
  41.4 0.0 collective-permute-start.7
  41.4 0.1 collective-permute-done.6.refs_4_
  41.5 3.7 %collective-permute-start.8 = (bf16[144,512]{1,0:T(8,128)(2,1)S(1)}, bf16[144,512]{1,0:T(8,128)(2,1)S(1)}, u32[]{:S(2)}, u32[]{:S(2)}) collective-permute-start(bf16[144,512]{1,0:T(8,128)(2,1)S(1)} %collective-permute-done.6.refs_4_), channel_id=1, source_target_pairs={{0,224},{32,0},{64,32},{96,64},{128,96},{160,128},{192,160},{224,1... | collective-permute-start | bytes 442376 | tf_op jit(solution)/shard_map/ppermute | solution.py:40
  45.2 3.4 %collective-permute-done.7.refs_5_ = bf16[144,512]{1,0:T(8,128)(2,1)S(1)} collective-permute-done((bf16[144,512]{1,0:T(8,128)(2,1)S(1)}, bf16[144,512]{1,0:T(8,128)(2,1)S(1)}, u32[]{:S(2)}, u32[]{:S(2)}) %collective-permute-start.7) | collective-permute-done | bytes 147488 | tf_op jit(solution)/shard_map/ppermute | solution.py:37
  48.5 0.0 collective-permute-start.9
  48.5 0.1 pad_add_fusion.place_ref
  48.6 0.0 collective-permute-done.8.refs_6_
  48.6 6.3 %collective-permute-done.9.refs_7_ = bf16[144,512]{1,0:T(8,128)(2,1)S(1)} collective-permute-done((bf16[144,512]{1,0:T(8,128)(2,1)S(1)}, bf16[144,512]{1,0:T(8,128)(2,1)S(1)}, u32[]{:S(2)}, u32[]{:S(2)}) %collective-permute-start.9) | collective-permute-done | bytes 147488 | tf_op jit(solution)/shard_map/ppermute | solution.py:37
  54.9 2.0 %all-gather.3.cloned.1.call-done.refs_8_.w_ref = bf16[3,2048,512]{2,1,0:T(8,128)(2,1)} async-done(((bf16[3,128,512]{2,1,0:T(8,128)(2,1)}), bf16[3,2048,512]{2,1,0:T(8,128)(2,1)}) %all-gather.3.cloned.1.call-update) | async-done | bytes 6291472 | tf_op jit(solution)/shard_map/all_gather | solution.py:304
  56.9 3.7 %project_mixin.1 = (f32[144,1024]{1,0:T(8,128)S(1)}, bf16[144,1024]{1,0:T(8,128)(2,1)S(1)}, bf16[2,144,2048]{2,1,0:T(8,128)(2,1)S(1)}) custom-call(s32[2]{0:T(128)S(1)} %pad_add_fusion.place_ref, bf16[144,512]{1,0:T(8,128)(2,1)S(1)} %collective-permute-done.2.refs_0_, bf16[144,512]{1,0:T(8,128)(2,1)S(1)} %collective-permute-done.3.refs_1_, ...), custom_call_target="tpu_custom_call" | custom-call | flops 1207959552 | bytes 4194304 | tf_op jit(solution)/shard_map/project_mixin/pallas_call | solution.py:348
  60.6 0.0 copy-start
  60.6 1.6 %collective-permute-start.10 = (bf16[144,1024]{1,0:T(8,128)(2,1)S(1)}, bf16[144,1024]{1,0:T(8,128)(2,1)S(1)}, u32[]{:S(2)}, u32[]{:S(2)}) collective-permute-start(bf16[144,1024]{1,0:T(8,128)(2,1)S(1)} %get-tuple-element.39), channel_id=1, source_target_pairs={{0,6},{1,7},{2,4},{3,5},{4,2},{5,3},{6,0},{7,1},{8,14},{9,15},{10,... | collective-permute-start | bytes 884744 | tf_op jit(solution)/shard_map/ppermute | solution.py:363
  62.2 2.4 %project_query.1 = (f32[144,512]{1,0:T(8,128)S(1)}, bf16[144,512]{1,0:T(8,128)(2,1)S(1)}) custom-call(bf16[2,144,2048]{2,1,0:T(8,128)(2,1)S(1)} %get-tuple-element.40.lhs_ref, bf16[3,2048,512]{2,1,0:T(8,128)(2,1)} %all-gather.3.cloned.1.call-done.refs_8_.w_ref), custom_call_target="tpu_custom_call" | custom-call | flops 603979776 | bytes 2097152 | tf_op jit(solution)/shard_map/project_query/pallas_call | solution.py:364
  64.6 5.2 %collective-permute-done.10.more_ref = bf16[144,1024]{1,0:T(8,128)(2,1)S(1)} collective-permute-done((bf16[144,1024]{1,0:T(8,128)(2,1)S(1)}, bf16[144,1024]{1,0:T(8,128)(2,1)S(1)}, u32[]{:S(2)}, u32[]{:S(2)}) %collective-permute-start.10) | collective-permute-done | bytes 294944 | tf_op jit(solution)/shard_map/ppermute | solution.py:363
  69.8 0.6 scan.1
  70.4 0.7 broadcast_in_dim.13
  71.1 8.0 %all-to-all-start = ((f32[32,4,512]{2,1,0:T(4,128)}), f32[32,4,512]{2,1,0:T(4,128)S(1)}, u32[]{:S(2)}, u32[]{:S(2)}) async-start(f32[32,4,512]{2,1,0:T(4,128)} %broadcast_in_dim.13), calls=%async_computation | async-start | bytes 524288 | tf_op jit(solution)/shard_map/all_to_all | solution.py:18
  79.2 1.6 %collective-permute-start.11 = (bf16[144,512]{1,0:T(8,128)(2,1)S(1)}, bf16[144,512]{1,0:T(8,128)(2,1)S(1)}, u32[]{:S(2)}, u32[]{:S(2)}) collective-permute-start(bf16[144,512]{1,0:T(8,128)(2,1)S(1)} %get-tuple-element.51), channel_id=1, source_target_pairs={{0,6},{1,7},{2,4},{3,5},{4,2},{5,3},{6,0},{7,1},{8,14},{9,15},{10,... | collective-permute-start | bytes 442376 | tf_op jit(solution)/shard_map/ppermute | solution.py:387
  80.8 6.8 %collective-permute-done.11.more_ref = bf16[144,512]{1,0:T(8,128)(2,1)S(1)} collective-permute-done((bf16[144,512]{1,0:T(8,128)(2,1)S(1)}, bf16[144,512]{1,0:T(8,128)(2,1)S(1)}, u32[]{:S(2)}, u32[]{:S(2)}) %collective-permute-start.11) | collective-permute-done | bytes 147488 | tf_op jit(solution)/shard_map/ppermute | solution.py:387
  87.6 2.1 %all-to-all-done.all_ref = f32[32,4,512]{2,1,0:T(4,128)S(1)} async-done(((f32[32,4,512]{2,1,0:T(4,128)}), f32[32,4,512]{2,1,0:T(4,128)S(1)}, u32[]{:S(2)}, u32[]{:S(2)}) %all-to-all-start) | async-done | bytes 262176 | tf_op jit(solution)/shard_map/all_to_all | solution.py:18
  89.7 0.5 gate.1.refs_0_
  90.3 1.8 %collective-permute-start.12 = (bf16[128,512]{1,0:T(8,128)(2,1)S(1)}, bf16[128,512]{1,0:T(8,128)(2,1)S(1)}, u32[]{:S(2)}, u32[]{:S(2)}) collective-permute-start(bf16[128,512]{1,0:T(8,128)(2,1)S(1)} %gate.1.refs_0_), channel_id=1, source_target_pairs={{0,32},{32,64},{64,96},{96,128},{128,160},{160,192},{192,224},{224... | collective-permute-start | bytes 393224 | tf_op jit(solution)/shard_map/ppermute | solution.py:37
  92.1 1.8 %collective-permute-start.16 = (bf16[128,512]{1,0:T(8,128)(2,1)S(1)}, bf16[128,512]{1,0:T(8,128)(2,1)S(1)}, u32[]{:S(2)}, u32[]{:S(2)}) collective-permute-start(bf16[128,512]{1,0:T(8,128)(2,1)S(1)} %gate.1.refs_0_), channel_id=1, source_target_pairs={{0,224},{32,0},{64,32},{96,64},{128,96},{160,128},{192,160},{224,1... | collective-permute-start | bytes 393224 | tf_op jit(solution)/shard_map/ppermute | solution.py:40
  93.9 3.5 %collective-permute-done.12.refs_1_ = bf16[128,512]{1,0:T(8,128)(2,1)S(1)} collective-permute-done((bf16[128,512]{1,0:T(8,128)(2,1)S(1)}, bf16[128,512]{1,0:T(8,128)(2,1)S(1)}, u32[]{:S(2)}, u32[]{:S(2)}) %collective-permute-start.12) | collective-permute-done | bytes 131104 | tf_op jit(solution)/shard_map/ppermute | solution.py:37
  97.4 0.0 collective-permute-start.13
  97.4 0.0 collective-permute-done.16.refs_2_
  97.4 3.2 %collective-permute-start.17 = (bf16[128,512]{1,0:T(8,128)(2,1)S(1)}, bf16[128,512]{1,0:T(8,128)(2,1)S(1)}, u32[]{:S(2)}, u32[]{:S(2)}) collective-permute-start(bf16[128,512]{1,0:T(8,128)(2,1)S(1)} %collective-permute-done.16.refs_2_), channel_id=1, source_target_pairs={{0,224},{32,0},{64,32},{96,64},{128,96},{160,128},{192,160},{224,1... | collective-permute-start | bytes 393224 | tf_op jit(solution)/shard_map/ppermute | solution.py:40
  100.7 2.9 %collective-permute-done.13.refs_3_ = bf16[128,512]{1,0:T(8,128)(2,1)S(1)} collective-permute-done((bf16[128,512]{1,0:T(8,128)(2,1)S(1)}, bf16[128,512]{1,0:T(8,128)(2,1)S(1)}, u32[]{:S(2)}, u32[]{:S(2)}) %collective-permute-start.13) | collective-permute-done | bytes 131104 | tf_op jit(solution)/shard_map/ppermute | solution.py:37
  103.6 0.0 collective-permute-start.14
  103.6 0.0 collective-permute-done.17.refs_4_
  103.6 3.2 %collective-permute-start.18 = (bf16[128,512]{1,0:T(8,128)(2,1)S(1)}, bf16[128,512]{1,0:T(8,128)(2,1)S(1)}, u32[]{:S(2)}, u32[]{:S(2)}) collective-permute-start(bf16[128,512]{1,0:T(8,128)(2,1)S(1)} %collective-permute-done.17.refs_4_), channel_id=1, source_target_pairs={{0,224},{32,0},{64,32},{96,64},{128,96},{160,128},{192,160},{224,1... | collective-permute-start | bytes 393224 | tf_op jit(solution)/shard_map/ppermute | solution.py:40
  106.8 2.9 %collective-permute-done.14.refs_5_ = bf16[128,512]{1,0:T(8,128)(2,1)S(1)} collective-permute-done((bf16[128,512]{1,0:T(8,128)(2,1)S(1)}, bf16[128,512]{1,0:T(8,128)(2,1)S(1)}, u32[]{:S(2)}, u32[]{:S(2)}) %collective-permute-start.14) | collective-permute-done | bytes 131104 | tf_op jit(solution)/shard_map/ppermute | solution.py:37
  109.8 0.0 collective-permute-start.15
  109.8 0.1 stack.48.which_ref
  109.9 0.0 collective-permute-done.18.refs_6_
  109.9 2.9 %mix.1 = (f32[128,512]{1,0:T(8,128)S(1)}, bf16[512,512]{1,0:T(8,128)(2,1)S(1)}) custom-call(s32[9]{0:T(128)S(1)} %stack.48.which_ref, bf16[128,512]{1,0:T(8,128)(2,1)S(1)} %gate.1.refs_0_, bf16[128,512]{1,0:T(8,128)(2,1)S(1)} %collective-permute-done.12.refs_1_, bf16[128,512]{1,0:T(8,128)(2,1)S(1)} %collective-permute-done.16.refs_2_, ...), custom_call_target="tpu_custom_call" | custom-call | flops 536870912 | bytes 4194304 | tf_op jit(solution)/shard_map/mix/pallas_call | solution.py:267
  112.8 3.1 %collective-permute-done.15.x_ref = bf16[128,512]{1,0:T(8,128)(2,1)S(1)} collective-permute-done((bf16[128,512]{1,0:T(8,128)(2,1)S(1)}, bf16[128,512]{1,0:T(8,128)(2,1)S(1)}, u32[]{:S(2)}, u32[]{:S(2)}) %collective-permute-start.15) | collective-permute-done | bytes 131104 | tf_op jit(solution)/shard_map/ppermute | solution.py:37
  116.0 0.9 last_mix.1
  (8 shorter events, 0.0 us)
Async XLA Ops:
  6.5 10.7 %copy-start.2 = (f32[512,2]{0,1:T(2,128)S(1)}, f32[512,2]{0,1:T(2,128)}, u32[]{:S(2)}) copy-start(f32[512,2]{0,1:T(2,128)} %param.12) | copy-start | bytes 12292
  6.5 10.8 %copy-start.3 = (f32[512,2]{0,1:T(2,128)S(1)}, f32[512,2]{0,1:T(2,128)}, u32[]{:S(2)}) copy-start(f32[512,2]{0,1:T(2,128)} %param.13) | copy-start | bytes 12292
  6.5 10.8 %copy-start.1 = (f32[2,512,2]{1,2,0:T(2,128)S(1)}, f32[2,512,2]{1,2,0:T(2,128)}, u32[]{:S(2)}) copy-start(f32[2,512,2]{1,2,0:T(2,128)} %param.14) | copy-start | bytes 24580
  6.5 50.3 %all-gather.3.cloned.1.call-start = ((), (), s32[]{:S(2)}) async-start(), calls=%async_computation.1 | async-start | bytes 6684672 | tf_op jit(solution)/shard_map/all_gather | solution.py:304
  8.4 101.5 %all-gather.5.cloned.1.call-start = ((), (), s32[]{:S(2)}) async-start(), calls=%async_computation.2 | async-start | bytes 4456448 | tf_op jit(solution)/shard_map/all_gather | solution.py:304
  8.4 7.2 %collective-permute-start.1 = (bf16[128,512]{1,0:T(8,128)(2,1)}, bf16[128,512]{1,0:T(8,128)(2,1)S(1)}, u32[]{:S(2)}, u32[]{:S(2)}) collective-permute-start(bf16[128,512]{1,0:T(8,128)(2,1)} %x_ref.1), channel_id=1, source_target_pairs={{0,6},{1,7},{2,4},{3,5},{4,2},{5,3},{6,0},{7,1},{8,14},{9,15},{10,... | collective-permute-start | bytes 393224 | tf_op jit(solution)/shard_map/ppermute | solution.py:312
  10.7 4.9 %collective-permute-start = (bf16[2,512]{1,0:T(2,128)(2,1)S(1)}, bf16[2,512]{1,0:T(2,128)(2,1)S(1)}, u32[]{:S(2)}, u32[]{:S(2)}) collective-permute-start(bf16[2,512]{1,0:T(2,128)(2,1)S(1)} %slice.3), channel_id=1, source_target_pairs={{0,1},{1,2},{2,3},{3,4},{4,5},{5,6},{6,7},{7,8},{8,9},{9,10},{10,1... | collective-permute-start | bytes 6152 | tf_op jit(solution)/shard_map/ppermute | solution.py:311
  16.6 3.1 %collective-permute-start.2 = (bf16[144,512]{1,0:T(8,128)(2,1)S(1)}, bf16[144,512]{1,0:T(8,128)(2,1)S(1)}, u32[]{:S(2)}, u32[]{:S(2)}) collective-permute-start(bf16[144,512]{1,0:T(8,128)(2,1)S(1)} %maximum_maximum_fusion), channel_id=1, source_target_pairs={{0,0},{1,1},{2,2},{3,3},{4,34},{5,35},{6,32},{7,33},{8,8},{9,9},{1... | collective-permute-start | bytes 442376 | tf_op jit(solution)/shard_map/ppermute | solution.py:320
  19.7 14.1 %collective-permute-start.3 = (bf16[144,512]{1,0:T(8,128)(2,1)S(1)}, bf16[144,512]{1,0:T(8,128)(2,1)S(1)}, u32[]{:S(2)}, u32[]{:S(2)}) collective-permute-start(bf16[144,512]{1,0:T(8,128)(2,1)S(1)} %collective-permute-done.2.refs_0_), channel_id=1, source_target_pairs={{0,32},{32,64},{64,96},{96,128},{128,160},{160,192},{192,224},{224... | collective-permute-start | bytes 442376 | tf_op jit(solution)/shard_map/ppermute | solution.py:37
  26.6 7.3 %collective-permute-start.4 = (bf16[144,512]{1,0:T(8,128)(2,1)S(1)}, bf16[144,512]{1,0:T(8,128)(2,1)S(1)}, u32[]{:S(2)}, u32[]{:S(2)}) collective-permute-start(bf16[144,512]{1,0:T(8,128)(2,1)S(1)} %collective-permute-done.2.refs_0_), channel_id=1, source_target_pairs={{0,224},{32,0},{64,32},{96,64},{128,96},{160,128},{192,160},{224,1... | collective-permute-start | bytes 442376 | tf_op jit(solution)/shard_map/ppermute | solution.py:40
  33.8 7.6 %collective-permute-start.5 = (bf16[144,512]{1,0:T(8,128)(2,1)S(1)}, bf16[144,512]{1,0:T(8,128)(2,1)S(1)}, u32[]{:S(2)}, u32[]{:S(2)}) collective-permute-start(bf16[144,512]{1,0:T(8,128)(2,1)S(1)} %collective-permute-done.3.refs_1_), channel_id=1, source_target_pairs={{0,32},{32,64},{64,96},{96,128},{128,160},{160,192},{192,224},{224... | collective-permute-start | bytes 442376 | tf_op jit(solution)/shard_map/ppermute | solution.py:37
  33.8 7.7 %collective-permute-start.6 = (bf16[144,512]{1,0:T(8,128)(2,1)S(1)}, bf16[144,512]{1,0:T(8,128)(2,1)S(1)}, u32[]{:S(2)}, u32[]{:S(2)}) collective-permute-start(bf16[144,512]{1,0:T(8,128)(2,1)S(1)} %collective-permute-done.4.refs_2_), channel_id=1, source_target_pairs={{0,224},{32,0},{64,32},{96,64},{128,96},{160,128},{192,160},{224,1... | collective-permute-start | bytes 442376 | tf_op jit(solution)/shard_map/ppermute | solution.py:40
  41.4 7.1 %collective-permute-start.7 = (bf16[144,512]{1,0:T(8,128)(2,1)S(1)}, bf16[144,512]{1,0:T(8,128)(2,1)S(1)}, u32[]{:S(2)}, u32[]{:S(2)}) collective-permute-start(bf16[144,512]{1,0:T(8,128)(2,1)S(1)} %collective-permute-done.5.refs_3_), channel_id=1, source_target_pairs={{0,32},{32,64},{64,96},{96,128},{128,160},{160,192},{192,224},{224... | collective-permute-start | bytes 442376 | tf_op jit(solution)/shard_map/ppermute | solution.py:37
  41.5 7.1 %collective-permute-start.8 = (bf16[144,512]{1,0:T(8,128)(2,1)S(1)}, bf16[144,512]{1,0:T(8,128)(2,1)S(1)}, u32[]{:S(2)}, u32[]{:S(2)}) collective-permute-start(bf16[144,512]{1,0:T(8,128)(2,1)S(1)} %collective-permute-done.6.refs_4_), channel_id=1, source_target_pairs={{0,224},{32,0},{64,32},{96,64},{128,96},{160,128},{192,160},{224,1... | collective-permute-start | bytes 442376 | tf_op jit(solution)/shard_map/ppermute | solution.py:40
  48.5 6.4 %collective-permute-start.9 = (bf16[144,512]{1,0:T(8,128)(2,1)S(1)}, bf16[144,512]{1,0:T(8,128)(2,1)S(1)}, u32[]{:S(2)}, u32[]{:S(2)}) collective-permute-start(bf16[144,512]{1,0:T(8,128)(2,1)S(1)} %collective-permute-done.7.refs_5_), channel_id=1, source_target_pairs={{0,32},{32,64},{64,96},{96,128},{128,160},{160,192},{192,224},{224... | collective-permute-start | bytes 442376 | tf_op jit(solution)/shard_map/ppermute | solution.py:37
  60.6 9.3 %copy-start = (f32[3,3,512]{2,1,0:T(4,128)S(1)}, f32[3,3,512]{2,1,0:T(4,128)}, u32[]{:S(2)}) copy-start(f32[3,3,512]{2,1,0:T(4,128)} %taps_ref.3) | copy-start | bytes 55300
  60.6 9.2 %collective-permute-start.10 = (bf16[144,1024]{1,0:T(8,128)(2,1)S(1)}, bf16[144,1024]{1,0:T(8,128)(2,1)S(1)}, u32[]{:S(2)}, u32[]{:S(2)}) collective-permute-start(bf16[144,1024]{1,0:T(8,128)(2,1)S(1)} %get-tuple-element.39), channel_id=1, source_target_pairs={{0,6},{1,7},{2,4},{3,5},{4,2},{5,3},{6,0},{7,1},{8,14},{9,15},{10,... | collective-permute-start | bytes 884744 | tf_op jit(solution)/shard_map/ppermute | solution.py:363
  62.2 27.5 %copy-start.4 = (f32[512]{0:T(512)S(1)}, f32[512]{0:T(512)}, u32[]{:S(2)}) copy-start(f32[512]{0:T(512)} %param.15) | copy-start | bytes 6148
  71.1 18.6 %all-to-all-start = ((f32[32,4,512]{2,1,0:T(4,128)}), f32[32,4,512]{2,1,0:T(4,128)S(1)}, u32[]{:S(2)}, u32[]{:S(2)}) async-start(f32[32,4,512]{2,1,0:T(4,128)} %broadcast_in_dim.13), calls=%async_computation | async-start | bytes 524288 | tf_op jit(solution)/shard_map/all_to_all | solution.py:18
  79.2 8.4 %collective-permute-start.11 = (bf16[144,512]{1,0:T(8,128)(2,1)S(1)}, bf16[144,512]{1,0:T(8,128)(2,1)S(1)}, u32[]{:S(2)}, u32[]{:S(2)}) collective-permute-start(bf16[144,512]{1,0:T(8,128)(2,1)S(1)} %get-tuple-element.51), channel_id=1, source_target_pairs={{0,6},{1,7},{2,4},{3,5},{4,2},{5,3},{6,0},{7,1},{8,14},{9,15},{10,... | collective-permute-start | bytes 442376 | tf_op jit(solution)/shard_map/ppermute | solution.py:387
  90.3 7.2 %collective-permute-start.12 = (bf16[128,512]{1,0:T(8,128)(2,1)S(1)}, bf16[128,512]{1,0:T(8,128)(2,1)S(1)}, u32[]{:S(2)}, u32[]{:S(2)}) collective-permute-start(bf16[128,512]{1,0:T(8,128)(2,1)S(1)} %gate.1.refs_0_), channel_id=1, source_target_pairs={{0,32},{32,64},{64,96},{96,128},{128,160},{160,192},{192,224},{224... | collective-permute-start | bytes 393224 | tf_op jit(solution)/shard_map/ppermute | solution.py:37
  92.1 5.4 %collective-permute-start.16 = (bf16[128,512]{1,0:T(8,128)(2,1)S(1)}, bf16[128,512]{1,0:T(8,128)(2,1)S(1)}, u32[]{:S(2)}, u32[]{:S(2)}) collective-permute-start(bf16[128,512]{1,0:T(8,128)(2,1)S(1)} %gate.1.refs_0_), channel_id=1, source_target_pairs={{0,224},{32,0},{64,32},{96,64},{128,96},{160,128},{192,160},{224,1... | collective-permute-start | bytes 393224 | tf_op jit(solution)/shard_map/ppermute | solution.py:40
  97.4 6.2 %collective-permute-start.13 = (bf16[128,512]{1,0:T(8,128)(2,1)S(1)}, bf16[128,512]{1,0:T(8,128)(2,1)S(1)}, u32[]{:S(2)}, u32[]{:S(2)}) collective-permute-start(bf16[128,512]{1,0:T(8,128)(2,1)S(1)} %collective-permute-done.12.refs_1_), channel_id=1, source_target_pairs={{0,32},{32,64},{64,96},{96,128},{128,160},{160,192},{192,224},{224... | collective-permute-start | bytes 393224 | tf_op jit(solution)/shard_map/ppermute | solution.py:37
  97.4 6.2 %collective-permute-start.17 = (bf16[128,512]{1,0:T(8,128)(2,1)S(1)}, bf16[128,512]{1,0:T(8,128)(2,1)S(1)}, u32[]{:S(2)}, u32[]{:S(2)}) collective-permute-start(bf16[128,512]{1,0:T(8,128)(2,1)S(1)} %collective-permute-done.16.refs_2_), channel_id=1, source_target_pairs={{0,224},{32,0},{64,32},{96,64},{128,96},{160,128},{192,160},{224,1... | collective-permute-start | bytes 393224 | tf_op jit(solution)/shard_map/ppermute | solution.py:40
  103.6 6.2 %collective-permute-start.14 = (bf16[128,512]{1,0:T(8,128)(2,1)S(1)}, bf16[128,512]{1,0:T(8,128)(2,1)S(1)}, u32[]{:S(2)}, u32[]{:S(2)}) collective-permute-start(bf16[128,512]{1,0:T(8,128)(2,1)S(1)} %collective-permute-done.13.refs_3_), channel_id=1, source_target_pairs={{0,32},{32,64},{64,96},{96,128},{128,160},{160,192},{192,224},{224... | collective-permute-start | bytes 393224 | tf_op jit(solution)/shard_map/ppermute | solution.py:37
  103.6 6.3 %collective-permute-start.18 = (bf16[128,512]{1,0:T(8,128)(2,1)S(1)}, bf16[128,512]{1,0:T(8,128)(2,1)S(1)}, u32[]{:S(2)}, u32[]{:S(2)}) collective-permute-start(bf16[128,512]{1,0:T(8,128)(2,1)S(1)} %collective-permute-done.17.refs_4_), channel_id=1, source_target_pairs={{0,224},{32,0},{64,32},{96,64},{128,96},{160,128},{192,160},{224,1... | collective-permute-start | bytes 393224 | tf_op jit(solution)/shard_map/ppermute | solution.py:40
  109.8 6.2 %collective-permute-start.15 = (bf16[128,512]{1,0:T(8,128)(2,1)S(1)}, bf16[128,512]{1,0:T(8,128)(2,1)S(1)}, u32[]{:S(2)}, u32[]{:S(2)}) collective-permute-start(bf16[128,512]{1,0:T(8,128)(2,1)S(1)} %collective-permute-done.14.refs_5_), channel_id=1, source_target_pairs={{0,32},{32,64},{64,96},{96,128},{128,160},{160,192},{192,224},{224... | collective-permute-start | bytes 393224 | tf_op jit(solution)/shard_map/ppermute | solution.py:37
Sparse Core Ops, SparseCore 0:
  9.2 47.6 all-gather.2
  58.7 43.0 all-gather.4

commit v14 on v13

--- a/solution.py
+++ b/solution.py
@@ -27,7 +27,8 @@
     return hops
 
 
-def ring(x, axis):
+def ring(x, axis, tied=()):
+    tied = list(tied)
     count = lax.axis_size(axis)
     up = [(c, (c + 1) % count) for c in range(count)]
     down = [(c, (c - 1) % count) for c in range(count)]
@@ -39,7 +40,10 @@
         if 2 * hop < count:
             above = lax.ppermute(above, axis, down)
             arrived.append(above)
-    return arrived
+        if hop <= len(tied):
+            below, tied[hop - 1] = lax.optimization_barrier((below, tied[hop - 1]))
+            arrived[2 * hop - 1] = below
+    return arrived, tied
 
 
 def powers_kernel(rows, place_ref, rate_ref, turn_ref, residue_ref, step_ref, join_ref, reach_ref, jump_ref, poles_ref):
@@ -339,10 +343,9 @@
         compiler_params=params,
         name="beside",
     )(in_hbm(out_weight), mirrored)
-    tied = lax.optimization_barrier((swapped, both, step, join, reach, jump, poles))
-    swapped, both, step, join, reach, jump, poles = tied
-    second = gather(both, 0)
-    features = ring(swapped, "ch")
+    features, tied = ring(swapped, "ch", (both, (step, join, reach, jump, poles)))
+    second = gather(tied[0], 0)
+    step, join, reach, jump, poles = tied[1]
     here = lax.axis_index("ch")
 
     keep, send, lhs = pl.pallas_call(
@@ -396,7 +399,7 @@
     )(states, jump, begin, reach, step, poles, bias[None, :], mixin, query_keep, query_more, taps)
 
     which = jnp.stack([lax.rem(here + hop + count, count) for hop in ring_hops(count)] + [half])
-    parts = ring(gated, "ch")
+    parts, _ = ring(gated, "ch")
     first, rest = mix(parts[:-1], which.astype(jnp.int32), second, out_weight.shape[1])
     return pl.pallas_call(
         last_mix_kernel,

time: 124 us -> 124 us (level)
  starting transfers between devices: 43.8 us -> 45.1 us
    ppermute x6, waiting for transfers between devices: 0.08 us -> 8.09 us  [ring(): above = lax.ppermute(above, axis, down)]
    ppermute x8, waiting for transfers between devices: 29.2 us -> 21.9 us  [ring(): below = lax.ppermute(below, axis, up)]
    ppermute x8, starting transfers between devices: 8.65 us -> 11 us  [ring(): below = lax.ppermute(below, axis, up)]
    all_gather x2, waiting for transfers between devices: 2.01 us -> 0.01 us  [body(): lax.all_gather(x, 'seq', axis=axis, tiled=True, axis_index_groups=halves)]
  transfers between devices with their start and end apart: 22 -> 22, of which waited for: 14 -> 13; matrix products, arithmetic and copies ran while one was open for 2% -> 2% of each run, Pallas kernels for 10% -> 10%
where the time goes in v14:
time: 124 us
  waiting for transfers between devices  47.2 us (38%)
  starting transfers between devices  45.1 us (36%)
  Pallas kernels  15.2 us (12%)
  between operations  13.5 us (11%)
  local copies, waits for them, and re-layouts  1.63 us (1%)
    ppermute x8, waiting for transfers between devices, ring(): below = lax.ppermute(below, axis, up)  21.9 us
    ppermute x6, starting transfers between devices, ring(): above = lax.ppermute(above, axis, down)  18.9 us
    ppermute x8, starting transfers between devices, ring(): below = lax.ppermute(below, axis, up)  11 us
    ppermute x6, waiting for transfers between devices, ring(): above = lax.ppermute(above, axis, down)  8.09 us
    all_to_all x1, starting transfers between devices, spread(): lax.all_to_all(jnp.broadcast_to(x[None], (count,) + x.shape), axis, 0, 0,...  8.04 us
    ppermute x1, waiting for transfers between devices, body(): query_more = lax.ppermute(query_send, 'seq', pairs)  6.84 us
    ppermute x1, waiting for transfers between devices, body(): more = lax.ppermute(send, 'seq', pairs)  5.23 us
    pallas_call x1, Pallas kernels, body(): pl.pallas_call(functools.partial(mixin_project_kernel, count), in_specs=[...  3.71 us
  transfers between devices with their start and end apart: 22, of which 13 were waited for; matrix products, arithmetic and copies ran while one was open for 2% of the time, Pallas kernels for 10%

profile of v14, /device:TPU:2, one launch (start us, length us, event | category | flops | bytes accessed | tf_op | source)
XLA Modules:
  0.0 123.7 jit_solution(18281842755584426460)
XLA Ops:
  6.5 0.0 all-gather.3.cloned.1.call-start
  6.5 1.8 %cut.1 = bf16[3,128,512]{2,1,0:T(8,128)(2,1)} custom-call(s32[1]{0:T(128)} %bitcast.1.place_ref, bf16[3,128,4096]{2,1,0:T(8,128)(2,1)} %bitcast.20), custom_call_target="tpu_custom_call" | custom-call | tf_op jit(solution)/shard_map/cut/pallas_call | solution.py:298
  8.4 0.0 all-gather.3.cloned.1.call-update
  8.4 0.0 all-gather.5.cloned.1.call-start
  8.4 1.6 %collective-permute-start.1 = (bf16[128,512]{1,0:T(8,128)(2,1)}, bf16[128,512]{1,0:T(8,128)(2,1)S(1)}, u32[]{:S(2)}, u32[]{:S(2)}) collective-permute-start(bf16[128,512]{1,0:T(8,128)(2,1)} %x_ref.1), channel_id=1, source_target_pairs={{0,6},{1,7},{2,4},{3,5},{4,2},{5,3},{6,0},{7,1},{8,14},{9,15},{10,... | collective-permute-start | bytes 393224 | tf_op jit(solution)/shard_map/ppermute | solution.py:316
  10.0 0.7 slice.3
  10.7 1.9 %collective-permute-start = (bf16[2,512]{1,0:T(2,128)(2,1)S(1)}, bf16[2,512]{1,0:T(2,128)(2,1)S(1)}, u32[]{:S(2)}, u32[]{:S(2)}) collective-permute-start(bf16[2,512]{1,0:T(2,128)(2,1)S(1)} %slice.3), channel_id=1, source_target_pairs={{0,1},{1,2},{2,3},{3,4},{4,5},{5,6},{6,7},{7,8},{8,9},{9,10},{10,1... | collective-permute-start | bytes 6152 | tf_op jit(solution)/shard_map/ppermute | solution.py:315
  12.6 0.1 pad.2.clone
  12.7 2.9 %collective-permute-done = bf16[2,512]{1,0:T(2,128)(2,1)S(1)} collective-permute-done((bf16[2,512]{1,0:T(2,128)(2,1)S(1)}, bf16[2,512]{1,0:T(2,128)(2,1)S(1)}, u32[]{:S(2)}, u32[]{:S(2)}) %collective-permute-start) | collective-permute-done | bytes 2080 | tf_op jit(solution)/shard_map/ppermute | solution.py:315
  15.6 0.0 collective-permute-done.1.y_ref
  15.6 1.0 maximum_maximum_fusion
  16.6 0.7 collective-permute-start.2
  17.3 0.0 collective-permute-done.2.refs_0_
  17.3 9.2 %collective-permute-start.3 = (bf16[144,512]{1,0:T(8,128)(2,1)S(1)}, bf16[144,512]{1,0:T(8,128)(2,1)S(1)}, u32[]{:S(2)}, u32[]{:S(2)}) collective-permute-start(bf16[144,512]{1,0:T(8,128)(2,1)S(1)} %collective-permute-done.2.refs_0_), channel_id=1, source_target_pairs={{0,32},{32,64},{64,96},{96,128},{128,160},{160,192},{192,224},{224... | collective-permute-start | bytes 442376 | tf_op jit(solution)/shard_map/ppermute | solution.py:38
  26.5 1.6 %beside.1 = bf16[128,1024]{1,0:T(8,128)(2,1)} custom-call(bf16[128,512]{1,0:T(8,128)(2,1)} %x_ref.1, bf16[128,512]{1,0:T(8,128)(2,1)S(1)} %collective-permute-done.1.y_ref), custom_call_target="tpu_custom_call" | custom-call | tf_op jit(solution)/shard_map/beside/pallas_call | solution.py:338
  28.1 5.7 %collective-permute-done.3.refs_1_ = bf16[144,512]{1,0:T(8,128)(2,1)S(1)} collective-permute-done((bf16[144,512]{1,0:T(8,128)(2,1)S(1)}, bf16[144,512]{1,0:T(8,128)(2,1)S(1)}, u32[]{:S(2)}, u32[]{:S(2)}) %collective-permute-start.3) | collective-permute-done | bytes 147488 | tf_op jit(solution)/shard_map/ppermute | solution.py:38
  33.8 0.0 all-gather.5.cloned.1.call-update
  33.8 3.2 %collective-permute-start.4 = (bf16[144,512]{1,0:T(8,128)(2,1)S(1)}, bf16[144,512]{1,0:T(8,128)(2,1)S(1)}, u32[]{:S(2)}, u32[]{:S(2)}) collective-permute-start(bf16[144,512]{1,0:T(8,128)(2,1)S(1)} %collective-permute-done.2.refs_0_), channel_id=1, source_target_pairs={{0,224},{32,0},{64,32},{96,64},{128,96},{160,128},{192,160},{224,1... | collective-permute-start | bytes 442376 | tf_op jit(solution)/shard_map/ppermute | solution.py:41
  37.0 0.0 collective-permute-start.5
  37.0 0.0 copy-done.2
  37.0 0.0 copy-done.3
  37.1 0.0 copy-done.1
  37.1 0.8 powers.1
  37.8 2.8 %collective-permute-done.4.refs_2_ = bf16[144,512]{1,0:T(8,128)(2,1)S(1)} collective-permute-done((bf16[144,512]{1,0:T(8,128)(2,1)S(1)}, bf16[144,512]{1,0:T(8,128)(2,1)S(1)}, u32[]{:S(2)}, u32[]{:S(2)}) %collective-permute-start.4) | collective-permute-done | bytes 147488 | tf_op jit(solution)/shard_map/ppermute | solution.py:41
  40.6 3.7 %collective-permute-start.6 = (bf16[144,512]{1,0:T(8,128)(2,1)S(1)}, bf16[144,512]{1,0:T(8,128)(2,1)S(1)}, u32[]{:S(2)}, u32[]{:S(2)}) collective-permute-start(bf16[144,512]{1,0:T(8,128)(2,1)S(1)} %collective-permute-done.4.refs_2_), channel_id=1, source_target_pairs={{0,224},{32,0},{64,32},{96,64},{128,96},{160,128},{192,160},{224,1... | collective-permute-start | bytes 442376 | tf_op jit(solution)/shard_map/ppermute | solution.py:41
  44.3 0.0 collective-permute-done.5.refs_3_
  44.3 0.0 collective-permute-start.7
  44.3 2.7 %collective-permute-done.6.refs_4_ = bf16[144,512]{1,0:T(8,128)(2,1)S(1)} collective-permute-done((bf16[144,512]{1,0:T(8,128)(2,1)S(1)}, bf16[144,512]{1,0:T(8,128)(2,1)S(1)}, u32[]{:S(2)}, u32[]{:S(2)}) %collective-permute-start.6) | collective-permute-done | bytes 147488 | tf_op jit(solution)/shard_map/ppermute | solution.py:41
  47.0 3.7 %collective-permute-start.8 = (bf16[144,512]{1,0:T(8,128)(2,1)S(1)}, bf16[144,512]{1,0:T(8,128)(2,1)S(1)}, u32[]{:S(2)}, u32[]{:S(2)}) collective-permute-start(bf16[144,512]{1,0:T(8,128)(2,1)S(1)} %collective-permute-done.6.refs_4_), channel_id=1, source_target_pairs={{0,224},{32,0},{64,32},{96,64},{128,96},{160,128},{192,160},{224,1... | collective-permute-start | bytes 442376 | tf_op jit(solution)/shard_map/ppermute | solution.py:41
  50.7 0.0 collective-permute-done.7.refs_5_
  50.7 0.0 collective-permute-start.9
  50.7 0.1 pad_add_fusion.place_ref
  50.8 2.6 %collective-permute-done.8.refs_6_ = bf16[144,512]{1,0:T(8,128)(2,1)S(1)} collective-permute-done((bf16[144,512]{1,0:T(8,128)(2,1)S(1)}, bf16[144,512]{1,0:T(8,128)(2,1)S(1)}, u32[]{:S(2)}, u32[]{:S(2)}) %collective-permute-start.8) | collective-permute-done | bytes 147488 | tf_op jit(solution)/shard_map/ppermute | solution.py:41
  53.4 3.7 %collective-permute-done.9.refs_7_ = bf16[144,512]{1,0:T(8,128)(2,1)S(1)} collective-permute-done((bf16[144,512]{1,0:T(8,128)(2,1)S(1)}, bf16[144,512]{1,0:T(8,128)(2,1)S(1)}, u32[]{:S(2)}, u32[]{:S(2)}) %collective-permute-start.9) | collective-permute-done | bytes 147488 | tf_op jit(solution)/shard_map/ppermute | solution.py:38
  57.1 3.7 %project_mixin.1 = (f32[144,1024]{1,0:T(8,128)S(1)}, bf16[144,1024]{1,0:T(8,128)(2,1)S(1)}, bf16[2,144,2048]{2,1,0:T(8,128)(2,1)S(1)}) custom-call(s32[2]{0:T(128)S(1)} %pad_add_fusion.place_ref, bf16[144,512]{1,0:T(8,128)(2,1)S(1)} %collective-permute-done.2.refs_0_, bf16[144,512]{1,0:T(8,128)(2,1)S(1)} %collective-permute-done.3.refs_1_, ...), custom_call_target="tpu_custom_call" | custom-call | flops 1207959552 | bytes 4194304 | tf_op jit(solution)/shard_map/project_mixin/pallas_call | solution.py:351
  60.8 0.0 copy-start
  60.8 1.4 %collective-permute-start.10 = (bf16[144,1024]{1,0:T(8,128)(2,1)S(1)}, bf16[144,1024]{1,0:T(8,128)(2,1)S(1)}, u32[]{:S(2)}, u32[]{:S(2)}) collective-permute-start(bf16[144,1024]{1,0:T(8,128)(2,1)S(1)} %get-tuple-element.41), channel_id=1, source_target_pairs={{0,6},{1,7},{2,4},{3,5},{4,2},{5,3},{6,0},{7,1},{8,14},{9,15},{10,... | collective-permute-start | bytes 884744 | tf_op jit(solution)/shard_map/ppermute | solution.py:366
  62.2 2.4 %project_query.1 = (f32[144,512]{1,0:T(8,128)S(1)}, bf16[144,512]{1,0:T(8,128)(2,1)S(1)}) custom-call(bf16[2,144,2048]{2,1,0:T(8,128)(2,1)S(1)} %get-tuple-element.42.lhs_ref, bf16[3,2048,512]{2,1,0:T(8,128)(2,1)} %all-gather.3.cloned.1.call-done.refs_8_.w_ref), custom_call_target="tpu_custom_call" | custom-call | flops 603979776 | bytes 2097152 | tf_op jit(solution)/shard_map/project_query/pallas_call | solution.py:367
  64.6 5.2 %collective-permute-done.10.more_ref = bf16[144,1024]{1,0:T(8,128)(2,1)S(1)} collective-permute-done((bf16[144,1024]{1,0:T(8,128)(2,1)S(1)}, bf16[144,1024]{1,0:T(8,128)(2,1)S(1)}, u32[]{:S(2)}, u32[]{:S(2)}) %collective-permute-start.10) | collective-permute-done | bytes 294944 | tf_op jit(solution)/shard_map/ppermute | solution.py:366
  69.8 0.0 copy-done
  69.8 0.6 scan.1
  70.4 0.7 broadcast_in_dim.13
  71.1 8.0 %all-to-all-start = ((f32[32,4,512]{2,1,0:T(4,128)}), f32[32,4,512]{2,1,0:T(4,128)S(1)}, u32[]{:S(2)}, u32[]{:S(2)}) async-start(f32[32,4,512]{2,1,0:T(4,128)} %broadcast_in_dim.13), calls=%async_computation | async-start | bytes 524288 | tf_op jit(solution)/shard_map/all_to_all | solution.py:18
  79.2 1.6 %collective-permute-start.11 = (bf16[144,512]{1,0:T(8,128)(2,1)S(1)}, bf16[144,512]{1,0:T(8,128)(2,1)S(1)}, u32[]{:S(2)}, u32[]{:S(2)}) collective-permute-start(bf16[144,512]{1,0:T(8,128)(2,1)S(1)} %get-tuple-element.53), channel_id=1, source_target_pairs={{0,6},{1,7},{2,4},{3,5},{4,2},{5,3},{6,0},{7,1},{8,14},{9,15},{10,... | collective-permute-start | bytes 442376 | tf_op jit(solution)/shard_map/ppermute | solution.py:390
  80.8 6.8 %collective-permute-done.11.more_ref = bf16[144,512]{1,0:T(8,128)(2,1)S(1)} collective-permute-done((bf16[144,512]{1,0:T(8,128)(2,1)S(1)}, bf16[144,512]{1,0:T(8,128)(2,1)S(1)}, u32[]{:S(2)}, u32[]{:S(2)}) %collective-permute-start.11) | collective-permute-done | bytes 147488 | tf_op jit(solution)/shard_map/ppermute | solution.py:390
  87.6 2.1 %all-to-all-done.all_ref = f32[32,4,512]{2,1,0:T(4,128)S(1)} async-done(((f32[32,4,512]{2,1,0:T(4,128)}), f32[32,4,512]{2,1,0:T(4,128)S(1)}, u32[]{:S(2)}, u32[]{:S(2)}) %all-to-all-start) | async-done | bytes 262176 | tf_op jit(solution)/shard_map/all_to_all | solution.py:18
  89.7 0.5 gate.1.refs_0_
  90.2 1.8 %collective-permute-start.12 = (bf16[128,512]{1,0:T(8,128)(2,1)S(1)}, bf16[128,512]{1,0:T(8,128)(2,1)S(1)}, u32[]{:S(2)}, u32[]{:S(2)}) collective-permute-start(bf16[128,512]{1,0:T(8,128)(2,1)S(1)} %gate.1.refs_0_), channel_id=1, source_target_pairs={{0,32},{32,64},{64,96},{96,128},{128,160},{160,192},{192,224},{224... | collective-permute-start | bytes 393224 | tf_op jit(solution)/shard_map/ppermute | solution.py:38
  92.1 1.8 %collective-permute-start.16 = (bf16[128,512]{1,0:T(8,128)(2,1)S(1)}, bf16[128,512]{1,0:T(8,128)(2,1)S(1)}, u32[]{:S(2)}, u32[]{:S(2)}) collective-permute-start(bf16[128,512]{1,0:T(8,128)(2,1)S(1)} %gate.1.refs_0_), channel_id=1, source_target_pairs={{0,224},{32,0},{64,32},{96,64},{128,96},{160,128},{192,160},{224,1... | collective-permute-start | bytes 393224 | tf_op jit(solution)/shard_map/ppermute | solution.py:41
  93.9 3.5 %collective-permute-done.12.refs_1_ = bf16[128,512]{1,0:T(8,128)(2,1)S(1)} collective-permute-done((bf16[128,512]{1,0:T(8,128)(2,1)S(1)}, bf16[128,512]{1,0:T(8,128)(2,1)S(1)}, u32[]{:S(2)}, u32[]{:S(2)}) %collective-permute-start.12) | collective-permute-done | bytes 131104 | tf_op jit(solution)/shard_map/ppermute | solution.py:38
  97.4 0.0 collective-permute-start.13
  97.4 0.0 collective-permute-done.16.refs_2_
  97.4 3.2 %collective-permute-start.17 = (bf16[128,512]{1,0:T(8,128)(2,1)S(1)}, bf16[128,512]{1,0:T(8,128)(2,1)S(1)}, u32[]{:S(2)}, u32[]{:S(2)}) collective-permute-start(bf16[128,512]{1,0:T(8,128)(2,1)S(1)} %collective-permute-done.16.refs_2_), channel_id=1, source_target_pairs={{0,224},{32,0},{64,32},{96,64},{128,96},{160,128},{192,160},{224,1... | collective-permute-start | bytes 393224 | tf_op jit(solution)/shard_map/ppermute | solution.py:41
  100.7 2.9 %collective-permute-done.13.refs_3_ = bf16[128,512]{1,0:T(8,128)(2,1)S(1)} collective-permute-done((bf16[128,512]{1,0:T(8,128)(2,1)S(1)}, bf16[128,512]{1,0:T(8,128)(2,1)S(1)}, u32[]{:S(2)}, u32[]{:S(2)}) %collective-permute-start.13) | collective-permute-done | bytes 131104 | tf_op jit(solution)/shard_map/ppermute | solution.py:38
  103.6 0.0 collective-permute-start.14
  103.6 0.0 collective-permute-done.17.refs_4_
  103.6 3.2 %collective-permute-start.18 = (bf16[128,512]{1,0:T(8,128)(2,1)S(1)}, bf16[128,512]{1,0:T(8,128)(2,1)S(1)}, u32[]{:S(2)}, u32[]{:S(2)}) collective-permute-start(bf16[128,512]{1,0:T(8,128)(2,1)S(1)} %collective-permute-done.17.refs_4_), channel_id=1, source_target_pairs={{0,224},{32,0},{64,32},{96,64},{128,96},{160,128},{192,160},{224,1... | collective-permute-start | bytes 393224 | tf_op jit(solution)/shard_map/ppermute | solution.py:41
  106.8 2.9 %collective-permute-done.14.refs_5_ = bf16[128,512]{1,0:T(8,128)(2,1)S(1)} collective-permute-done((bf16[128,512]{1,0:T(8,128)(2,1)S(1)}, bf16[128,512]{1,0:T(8,128)(2,1)S(1)}, u32[]{:S(2)}, u32[]{:S(2)}) %collective-permute-start.14) | collective-permute-done | bytes 131104 | tf_op jit(solution)/shard_map/ppermute | solution.py:38
  109.8 0.0 collective-permute-start.15
  109.8 0.1 stack.48.which_ref
  109.9 0.0 collective-permute-done.18.refs_6_
  109.9 2.9 %mix.1 = (f32[128,512]{1,0:T(8,128)S(1)}, bf16[512,512]{1,0:T(8,128)(2,1)S(1)}) custom-call(s32[9]{0:T(128)S(1)} %stack.48.which_ref, bf16[128,512]{1,0:T(8,128)(2,1)S(1)} %gate.1.refs_0_, bf16[128,512]{1,0:T(8,128)(2,1)S(1)} %collective-permute-done.12.refs_1_, bf16[128,512]{1,0:T(8,128)(2,1)S(1)} %collective-permute-done.16.refs_2_, ...), custom_call_target="tpu_custom_call" | custom-call | flops 536870912 | bytes 4194304 | tf_op jit(solution)/shard_map/mix/pallas_call | solution.py:271
  112.8 3.1 %collective-permute-done.15.x_ref = bf16[128,512]{1,0:T(8,128)(2,1)S(1)} collective-permute-done((bf16[128,512]{1,0:T(8,128)(2,1)S(1)}, bf16[128,512]{1,0:T(8,128)(2,1)S(1)}, u32[]{:S(2)}, u32[]{:S(2)}) %collective-permute-start.15) | collective-permute-done | bytes 131104 | tf_op jit(solution)/shard_map/ppermute | solution.py:38
  116.0 0.9 last_mix.1
  (8 shorter events, 0.0 us)
Async XLA Ops:
  6.5 30.5 %copy-start.2 = (f32[512,2]{0,1:T(2,128)S(1)}, f32[512,2]{0,1:T(2,128)}, u32[]{:S(2)}) copy-start(f32[512,2]{0,1:T(2,128)} %param.12) | copy-start | bytes 12292
  6.5 30.5 %copy-start.3 = (f32[512,2]{0,1:T(2,128)S(1)}, f32[512,2]{0,1:T(2,128)}, u32[]{:S(2)}) copy-start(f32[512,2]{0,1:T(2,128)} %param.13) | copy-start | bytes 12292
  6.5 30.5 %copy-start.1 = (f32[2,512,2]{1,2,0:T(2,128)S(1)}, f32[2,512,2]{1,2,0:T(2,128)}, u32[]{:S(2)}) copy-start(f32[2,512,2]{1,2,0:T(2,128)} %param.14) | copy-start | bytes 24580
  6.5 50.5 %all-gather.3.cloned.1.call-start = ((), (), s32[]{:S(2)}) async-start(), calls=%async_computation.1 | async-start | bytes 6684672 | tf_op jit(solution)/shard_map/all_gather | solution.py:308
  8.4 101.5 %all-gather.5.cloned.1.call-start = ((), (), s32[]{:S(2)}) async-start(), calls=%async_computation.2 | async-start | bytes 4456448 | tf_op jit(solution)/shard_map/all_gather | solution.py:308
  8.4 7.2 %collective-permute-start.1 = (bf16[128,512]{1,0:T(8,128)(2,1)}, bf16[128,512]{1,0:T(8,128)(2,1)S(1)}, u32[]{:S(2)}, u32[]{:S(2)}) collective-permute-start(bf16[128,512]{1,0:T(8,128)(2,1)} %x_ref.1), channel_id=1, source_target_pairs={{0,6},{1,7},{2,4},{3,5},{4,2},{5,3},{6,0},{7,1},{8,14},{9,15},{10,... | collective-permute-start | bytes 393224 | tf_op jit(solution)/shard_map/ppermute | solution.py:316
  10.7 4.9 %collective-permute-start = (bf16[2,512]{1,0:T(2,128)(2,1)S(1)}, bf16[2,512]{1,0:T(2,128)(2,1)S(1)}, u32[]{:S(2)}, u32[]{:S(2)}) collective-permute-start(bf16[2,512]{1,0:T(2,128)(2,1)S(1)} %slice.3), channel_id=1, source_target_pairs={{0,1},{1,2},{2,3},{3,4},{4,5},{5,6},{6,7},{7,8},{8,9},{9,10},{10,1... | collective-permute-start | bytes 6152 | tf_op jit(solution)/shard_map/ppermute | solution.py:315
  16.6 0.7 collective-permute-start.2
  17.3 16.5 %collective-permute-start.3 = (bf16[144,512]{1,0:T(8,128)(2,1)S(1)}, bf16[144,512]{1,0:T(8,128)(2,1)S(1)}, u32[]{:S(2)}, u32[]{:S(2)}) collective-permute-start(bf16[144,512]{1,0:T(8,128)(2,1)S(1)} %collective-permute-done.2.refs_0_), channel_id=1, source_target_pairs={{0,32},{32,64},{64,96},{96,128},{128,160},{160,192},{192,224},{224... | collective-permute-start | bytes 442376 | tf_op jit(solution)/shard_map/ppermute | solution.py:38
  33.8 6.8 %collective-permute-start.4 = (bf16[144,512]{1,0:T(8,128)(2,1)S(1)}, bf16[144,512]{1,0:T(8,128)(2,1)S(1)}, u32[]{:S(2)}, u32[]{:S(2)}) collective-permute-start(bf16[144,512]{1,0:T(8,128)(2,1)S(1)} %collective-permute-done.2.refs_0_), channel_id=1, source_target_pairs={{0,224},{32,0},{64,32},{96,64},{128,96},{160,128},{192,160},{224,1... | collective-permute-start | bytes 442376 | tf_op jit(solution)/shard_map/ppermute | solution.py:41
  37.0 7.2 %collective-permute-start.5 = (bf16[144,512]{1,0:T(8,128)(2,1)S(1)}, bf16[144,512]{1,0:T(8,128)(2,1)S(1)}, u32[]{:S(2)}, u32[]{:S(2)}) collective-permute-start(bf16[144,512]{1,0:T(8,128)(2,1)S(1)} %collective-permute-done.3.refs_1_), channel_id=1, source_target_pairs={{0,32},{32,64},{64,96},{96,128},{128,160},{160,192},{192,224},{224... | collective-permute-start | bytes 442376 | tf_op jit(solution)/shard_map/ppermute | solution.py:38
  40.6 6.4 %collective-permute-start.6 = (bf16[144,512]{1,0:T(8,128)(2,1)S(1)}, bf16[144,512]{1,0:T(8,128)(2,1)S(1)}, u32[]{:S(2)}, u32[]{:S(2)}) collective-permute-start(bf16[144,512]{1,0:T(8,128)(2,1)S(1)} %collective-permute-done.4.refs_2_), channel_id=1, source_target_pairs={{0,224},{32,0},{64,32},{96,64},{128,96},{160,128},{192,160},{224,1... | collective-permute-start | bytes 442376 | tf_op jit(solution)/shard_map/ppermute | solution.py:41
  44.3 6.4 %collective-permute-start.7 = (bf16[144,512]{1,0:T(8,128)(2,1)S(1)}, bf16[144,512]{1,0:T(8,128)(2,1)S(1)}, u32[]{:S(2)}, u32[]{:S(2)}) collective-permute-start(bf16[144,512]{1,0:T(8,128)(2,1)S(1)} %collective-permute-done.5.refs_3_), channel_id=1, source_target_pairs={{0,32},{32,64},{64,96},{96,128},{128,160},{160,192},{192,224},{224... | collective-permute-start | bytes 442376 | tf_op jit(solution)/shard_map/ppermute | solution.py:38
  47.0 6.4 %collective-permute-start.8 = (bf16[144,512]{1,0:T(8,128)(2,1)S(1)}, bf16[144,512]{1,0:T(8,128)(2,1)S(1)}, u32[]{:S(2)}, u32[]{:S(2)}) collective-permute-start(bf16[144,512]{1,0:T(8,128)(2,1)S(1)} %collective-permute-done.6.refs_4_), channel_id=1, source_target_pairs={{0,224},{32,0},{64,32},{96,64},{128,96},{160,128},{192,160},{224,1... | collective-permute-start | bytes 442376 | tf_op jit(solution)/shard_map/ppermute | solution.py:41
  50.7 6.4 %collective-permute-start.9 = (bf16[144,512]{1,0:T(8,128)(2,1)S(1)}, bf16[144,512]{1,0:T(8,128)(2,1)S(1)}, u32[]{:S(2)}, u32[]{:S(2)}) collective-permute-start(bf16[144,512]{1,0:T(8,128)(2,1)S(1)} %collective-permute-done.7.refs_5_), channel_id=1, source_target_pairs={{0,32},{32,64},{64,96},{96,128},{128,160},{160,192},{192,224},{224... | collective-permute-start | bytes 442376 | tf_op jit(solution)/shard_map/ppermute | solution.py:38
  60.8 9.1 %copy-start = (f32[3,3,512]{2,1,0:T(4,128)S(1)}, f32[3,3,512]{2,1,0:T(4,128)}, u32[]{:S(2)}) copy-start(f32[3,3,512]{2,1,0:T(4,128)} %taps_ref.3) | copy-start | bytes 55300
  60.8 9.1 %collective-permute-start.10 = (bf16[144,1024]{1,0:T(8,128)(2,1)S(1)}, bf16[144,1024]{1,0:T(8,128)(2,1)S(1)}, u32[]{:S(2)}, u32[]{:S(2)}) collective-permute-start(bf16[144,1024]{1,0:T(8,128)(2,1)S(1)} %get-tuple-element.41), channel_id=1, source_target_pairs={{0,6},{1,7},{2,4},{3,5},{4,2},{5,3},{6,0},{7,1},{8,14},{9,15},{10,... | collective-permute-start | bytes 884744 | tf_op jit(solution)/shard_map/ppermute | solution.py:366
  62.2 27.5 %copy-start.4 = (f32[512]{0:T(512)S(1)}, f32[512]{0:T(512)}, u32[]{:S(2)}) copy-start(f32[512]{0:T(512)} %param.15) | copy-start | bytes 6148
  71.1 18.6 %all-to-all-start = ((f32[32,4,512]{2,1,0:T(4,128)}), f32[32,4,512]{2,1,0:T(4,128)S(1)}, u32[]{:S(2)}, u32[]{:S(2)}) async-start(f32[32,4,512]{2,1,0:T(4,128)} %broadcast_in_dim.13), calls=%async_computation | async-start | bytes 524288 | tf_op jit(solution)/shard_map/all_to_all | solution.py:18
  79.2 8.4 %collective-permute-start.11 = (bf16[144,512]{1,0:T(8,128)(2,1)S(1)}, bf16[144,512]{1,0:T(8,128)(2,1)S(1)}, u32[]{:S(2)}, u32[]{:S(2)}) collective-permute-start(bf16[144,512]{1,0:T(8,128)(2,1)S(1)} %get-tuple-element.53), channel_id=1, source_target_pairs={{0,6},{1,7},{2,4},{3,5},{4,2},{5,3},{6,0},{7,1},{8,14},{9,15},{10,... | collective-permute-start | bytes 442376 | tf_op jit(solution)/shard_map/ppermute | solution.py:390
  90.2 7.2 %collective-permute-start.12 = (bf16[128,512]{1,0:T(8,128)(2,1)S(1)}, bf16[128,512]{1,0:T(8,128)(2,1)S(1)}, u32[]{:S(2)}, u32[]{:S(2)}) collective-permute-start(bf16[128,512]{1,0:T(8,128)(2,1)S(1)} %gate.1.refs_0_), channel_id=1, source_target_pairs={{0,32},{32,64},{64,96},{96,128},{128,160},{160,192},{192,224},{224... | collective-permute-start | bytes 393224 | tf_op jit(solution)/shard_map/ppermute | solution.py:38
  92.1 5.4 %collective-permute-start.16 = (bf16[128,512]{1,0:T(8,128)(2,1)S(1)}, bf16[128,512]{1,0:T(8,128)(2,1)S(1)}, u32[]{:S(2)}, u32[]{:S(2)}) collective-permute-start(bf16[128,512]{1,0:T(8,128)(2,1)S(1)} %gate.1.refs_0_), channel_id=1, source_target_pairs={{0,224},{32,0},{64,32},{96,64},{128,96},{160,128},{192,160},{224,1... | collective-permute-start | bytes 393224 | tf_op jit(solution)/shard_map/ppermute | solution.py:41
  97.4 6.2 %collective-permute-start.13 = (bf16[128,512]{1,0:T(8,128)(2,1)S(1)}, bf16[128,512]{1,0:T(8,128)(2,1)S(1)}, u32[]{:S(2)}, u32[]{:S(2)}) collective-permute-start(bf16[128,512]{1,0:T(8,128)(2,1)S(1)} %collective-permute-done.12.refs_1_), channel_id=1, source_target_pairs={{0,32},{32,64},{64,96},{96,128},{128,160},{160,192},{192,224},{224... | collective-permute-start | bytes 393224 | tf_op jit(solution)/shard_map/ppermute | solution.py:38
  97.4 6.2 %collective-permute-start.17 = (bf16[128,512]{1,0:T(8,128)(2,1)S(1)}, bf16[128,512]{1,0:T(8,128)(2,1)S(1)}, u32[]{:S(2)}, u32[]{:S(2)}) collective-permute-start(bf16[128,512]{1,0:T(8,128)(2,1)S(1)} %collective-permute-done.16.refs_2_), channel_id=1, source_target_pairs={{0,224},{32,0},{64,32},{96,64},{128,96},{160,128},{192,160},{224,1... | collective-permute-start | bytes 393224 | tf_op jit(solution)/shard_map/ppermute | solution.py:41
  103.6 6.2 %collective-permute-start.14 = (bf16[128,512]{1,0:T(8,128)(2,1)S(1)}, bf16[128,512]{1,0:T(8,128)(2,1)S(1)}, u32[]{:S(2)}, u32[]{:S(2)}) collective-permute-start(bf16[128,512]{1,0:T(8,128)(2,1)S(1)} %collective-permute-done.13.refs_3_), channel_id=1, source_target_pairs={{0,32},{32,64},{64,96},{96,128},{128,160},{160,192},{192,224},{224... | collective-permute-start | bytes 393224 | tf_op jit(solution)/shard_map/ppermute | solution.py:38
  103.6 6.3 %collective-permute-start.18 = (bf16[128,512]{1,0:T(8,128)(2,1)S(1)}, bf16[128,512]{1,0:T(8,128)(2,1)S(1)}, u32[]{:S(2)}, u32[]{:S(2)}) collective-permute-start(bf16[128,512]{1,0:T(8,128)(2,1)S(1)} %collective-permute-done.17.refs_4_), channel_id=1, source_target_pairs={{0,224},{32,0},{64,32},{96,64},{128,96},{160,128},{192,160},{224,1... | collective-permute-start | bytes 393224 | tf_op jit(solution)/shard_map/ppermute | solution.py:41
  109.8 6.2 %collective-permute-start.15 = (bf16[128,512]{1,0:T(8,128)(2,1)S(1)}, bf16[128,512]{1,0:T(8,128)(2,1)S(1)}, u32[]{:S(2)}, u32[]{:S(2)}) collective-permute-start(bf16[128,512]{1,0:T(8,128)(2,1)S(1)} %collective-permute-done.14.refs_5_), channel_id=1, source_target_pairs={{0,32},{32,64},{64,96},{96,128},{128,160},{160,192},{192,224},{224... | collective-permute-start | bytes 393224 | tf_op jit(solution)/shard_map/ppermute | solution.py:38
Sparse Core Ops, SparseCore 0:
  9.2 47.6 all-gather.2
  58.7 43.0 all-gather.4

commit v15 on v14

--- a/solution.py
+++ b/solution.py
@@ -41,8 +41,8 @@
             above = lax.ppermute(above, axis, down)
             arrived.append(above)
         if hop <= len(tied):
-            below, tied[hop - 1] = lax.optimization_barrier((below, tied[hop - 1]))
-            arrived[2 * hop - 1] = below
+            below, above, tied[hop - 1] = lax.optimization_barrier((below, above, tied[hop - 1]))
+            arrived[2 * hop - 1 :] = [below, above]
     return arrived, tied
 
 

time: 124 us -> 124 us (level)
    ppermute x6, waiting for transfers between devices: 8.09 us -> 0.02 us  [ring(): above = lax.ppermute(above, axis, down)]
    ppermute x8, waiting for transfers between devices: 21.9 us -> 27.3 us  [ring(): below = lax.ppermute(below, axis, up)]
    ppermute x8, starting transfers between devices: 11 us -> 13.3 us  [ring(): below = lax.ppermute(below, axis, up)]
    all_gather x2, waiting for transfers between devices: 0.01 us -> 1.7 us  [body(): lax.all_gather(x, 'seq', axis=axis, tiled=True, axis_index_groups=halves)]
    ppermute x6, starting transfers between devices: 18.9 us -> 17.4 us  [ring(): above = lax.ppermute(above, axis, down)]
where the time goes in v15:
time: 124 us
  starting transfers between devices  46.1 us (37%)
  waiting for transfers between devices  46.1 us (37%)
  Pallas kernels  15.2 us (12%)
  between operations  13.5 us (11%)
  local copies, waits for them, and re-layouts  1.63 us (1%)
    ppermute x8, waiting for transfers between devices, ring(): below = lax.ppermute(below, axis, up)  27.3 us
    ppermute x6, starting transfers between devices, ring(): above = lax.ppermute(above, axis, down)  17.4 us
    ppermute x8, starting transfers between devices, ring(): below = lax.ppermute(below, axis, up)  13.3 us
    all_to_all x1, starting transfers between devices, spread(): lax.all_to_all(jnp.broadcast_to(x[None], (count,) + x.shape), axis, 0, 0,...  8.04 us
    ppermute x1, waiting for transfers between devices, body(): query_more = lax.ppermute(query_send, 'seq', pairs)  6.84 us
    ppermute x1, waiting for transfers between devices, body(): more = lax.ppermute(send, 'seq', pairs)  5.23 us
    pallas_call x1, Pallas kernels, body(): pl.pallas_call(functools.partial(mixin_project_kernel, count), in_specs=[...  3.7 us
    pallas_call x1, Pallas kernels, mix(): pl.pallas_call(functools.partial(mix_kernel, count), in_specs=[IN_SMEM] +...  2.94 us
  transfers between devices with their start and end apart: 22, of which 13 were waited for; matrix products, arithmetic and copies ran while one was open for 2% of the time, Pallas kernels for 10%

profile of v15, /device:TPU:2, one launch (start us, length us, event | category | flops | bytes accessed | tf_op | source)
XLA Modules:
  0.0 123.7 jit_solution(11846310681249011485)
XLA Ops:
  6.5 0.0 all-gather.3.cloned.1.call-start
  6.5 1.8 %cut.1 = bf16[3,128,512]{2,1,0:T(8,128)(2,1)} custom-call(s32[1]{0:T(128)} %bitcast.1.place_ref, bf16[3,128,4096]{2,1,0:T(8,128)(2,1)} %bitcast.20), custom_call_target="tpu_custom_call" | custom-call | tf_op jit(solution)/shard_map/cut/pallas_call | solution.py:298
  8.4 0.0 all-gather.3.cloned.1.call-update
  8.4 0.0 all-gather.5.cloned.1.call-start
  8.4 1.6 %collective-permute-start.1 = (bf16[128,512]{1,0:T(8,128)(2,1)}, bf16[128,512]{1,0:T(8,128)(2,1)S(1)}, u32[]{:S(2)}, u32[]{:S(2)}) collective-permute-start(bf16[128,512]{1,0:T(8,128)(2,1)} %x_ref.1), channel_id=1, source_target_pairs={{0,6},{1,7},{2,4},{3,5},{4,2},{5,3},{6,0},{7,1},{8,14},{9,15},{10,... | collective-permute-start | bytes 393224 | tf_op jit(solution)/shard_map/ppermute | solution.py:316
  10.0 0.7 slice.3
  10.7 1.9 %collective-permute-start = (bf16[2,512]{1,0:T(2,128)(2,1)S(1)}, bf16[2,512]{1,0:T(2,128)(2,1)S(1)}, u32[]{:S(2)}, u32[]{:S(2)}) collective-permute-start(bf16[2,512]{1,0:T(2,128)(2,1)S(1)} %slice.3), channel_id=1, source_target_pairs={{0,1},{1,2},{2,3},{3,4},{4,5},{5,6},{6,7},{7,8},{8,9},{9,10},{10,1... | collective-permute-start | bytes 6152 | tf_op jit(solution)/shard_map/ppermute | solution.py:315
  12.6 0.1 pad.2.clone
  12.7 2.9 %collective-permute-done = bf16[2,512]{1,0:T(2,128)(2,1)S(1)} collective-permute-done((bf16[2,512]{1,0:T(2,128)(2,1)S(1)}, bf16[2,512]{1,0:T(2,128)(2,1)S(1)}, u32[]{:S(2)}, u32[]{:S(2)}) %collective-permute-start) | collective-permute-done | bytes 2080 | tf_op jit(solution)/shard_map/ppermute | solution.py:315
  15.6 0.0 collective-permute-done.1.y_ref
  15.6 1.0 maximum_maximum_fusion
  16.6 0.7 collective-permute-start.2
  17.3 0.0 collective-permute-done.2.refs_0_
  17.3 9.2 %collective-permute-start.3 = (bf16[144,512]{1,0:T(8,128)(2,1)S(1)}, bf16[144,512]{1,0:T(8,128)(2,1)S(1)}, u32[]{:S(2)}, u32[]{:S(2)}) collective-permute-start(bf16[144,512]{1,0:T(8,128)(2,1)S(1)} %collective-permute-done.2.refs_0_), channel_id=1, source_target_pairs={{0,32},{32,64},{64,96},{96,128},{128,160},{160,192},{192,224},{224... | collective-permute-start | bytes 442376 | tf_op jit(solution)/shard_map/ppermute | solution.py:38
  26.5 4.2 %collective-permute-start.4 = (bf16[144,512]{1,0:T(8,128)(2,1)S(1)}, bf16[144,512]{1,0:T(8,128)(2,1)S(1)}, u32[]{:S(2)}, u32[]{:S(2)}) collective-permute-start(bf16[144,512]{1,0:T(8,128)(2,1)S(1)} %collective-permute-done.2.refs_0_), channel_id=1, source_target_pairs={{0,224},{32,0},{64,32},{96,64},{128,96},{160,128},{192,160},{224,1... | collective-permute-start | bytes 442376 | tf_op jit(solution)/shard_map/ppermute | solution.py:41
  30.7 1.6 %beside.1 = bf16[128,1024]{1,0:T(8,128)(2,1)} custom-call(bf16[128,512]{1,0:T(8,128)(2,1)} %x_ref.1, bf16[128,512]{1,0:T(8,128)(2,1)S(1)} %collective-permute-done.1.y_ref), custom_call_target="tpu_custom_call" | custom-call | tf_op jit(solution)/shard_map/beside/pallas_call | solution.py:338
  32.3 1.5 %collective-permute-done.3.refs_1_ = bf16[144,512]{1,0:T(8,128)(2,1)S(1)} collective-permute-done((bf16[144,512]{1,0:T(8,128)(2,1)S(1)}, bf16[144,512]{1,0:T(8,128)(2,1)S(1)}, u32[]{:S(2)}, u32[]{:S(2)}) %collective-permute-start.3) | collective-permute-done | bytes 147488 | tf_op jit(solution)/shard_map/ppermute | solution.py:38
  33.8 0.0 collective-permute-done.4.refs_2_
  33.8 0.0 all-gather.5.cloned.1.call-update
  33.8 1.2 collective-permute-start.5
  35.0 2.4 %collective-permute-start.6 = (bf16[144,512]{1,0:T(8,128)(2,1)S(1)}, bf16[144,512]{1,0:T(8,128)(2,1)S(1)}, u32[]{:S(2)}, u32[]{:S(2)}) collective-permute-start(bf16[144,512]{1,0:T(8,128)(2,1)S(1)} %collective-permute-done.4.refs_2_), channel_id=1, source_target_pairs={{0,224},{32,0},{64,32},{96,64},{128,96},{160,128},{192,160},{224,1... | collective-permute-start | bytes 442376 | tf_op jit(solution)/shard_map/ppermute | solution.py:41
  37.4 0.0 copy-done.2
  37.4 0.0 copy-done.3
  37.4 0.0 copy-done.1
  37.4 0.8 powers.1
  38.2 3.5 %collective-permute-done.5.refs_3_ = bf16[144,512]{1,0:T(8,128)(2,1)S(1)} collective-permute-done((bf16[144,512]{1,0:T(8,128)(2,1)S(1)}, bf16[144,512]{1,0:T(8,128)(2,1)S(1)}, u32[]{:S(2)}, u32[]{:S(2)}) %collective-permute-start.5) | collective-permute-done | bytes 147488 | tf_op jit(solution)/shard_map/ppermute | solution.py:38
  41.7 0.0 collective-permute-done.6.refs_4_
  41.7 1.1 collective-permute-start.7
  42.8 2.5 %collective-permute-start.8 = (bf16[144,512]{1,0:T(8,128)(2,1)S(1)}, bf16[144,512]{1,0:T(8,128)(2,1)S(1)}, u32[]{:S(2)}, u32[]{:S(2)}) collective-permute-start(bf16[144,512]{1,0:T(8,128)(2,1)S(1)} %collective-permute-done.6.refs_4_), channel_id=1, source_target_pairs={{0,224},{32,0},{64,32},{96,64},{128,96},{160,128},{192,160},{224,1... | collective-permute-start | bytes 442376 | tf_op jit(solution)/shard_map/ppermute | solution.py:41
  45.3 3.5 %collective-permute-done.7.refs_5_ = bf16[144,512]{1,0:T(8,128)(2,1)S(1)} collective-permute-done((bf16[144,512]{1,0:T(8,128)(2,1)S(1)}, bf16[144,512]{1,0:T(8,128)(2,1)S(1)}, u32[]{:S(2)}, u32[]{:S(2)}) %collective-permute-start.7) | collective-permute-done | bytes 147488 | tf_op jit(solution)/shard_map/ppermute | solution.py:38
  48.8 0.0 collective-permute-start.9
  48.8 0.1 pad_add_fusion.place_ref
  48.9 0.0 collective-permute-done.8.refs_6_
  48.9 6.3 %collective-permute-done.9.refs_7_ = bf16[144,512]{1,0:T(8,128)(2,1)S(1)} collective-permute-done((bf16[144,512]{1,0:T(8,128)(2,1)S(1)}, bf16[144,512]{1,0:T(8,128)(2,1)S(1)}, u32[]{:S(2)}, u32[]{:S(2)}) %collective-permute-start.9) | collective-permute-done | bytes 147488 | tf_op jit(solution)/shard_map/ppermute | solution.py:38
  55.2 1.7 %all-gather.3.cloned.1.call-done.refs_8_.w_ref = bf16[3,2048,512]{2,1,0:T(8,128)(2,1)} async-done(((bf16[3,128,512]{2,1,0:T(8,128)(2,1)}), bf16[3,2048,512]{2,1,0:T(8,128)(2,1)}) %all-gather.3.cloned.1.call-update) | async-done | bytes 6291472 | tf_op jit(solution)/shard_map/all_gather | solution.py:308
  56.9 3.7 %project_mixin.1 = (f32[144,1024]{1,0:T(8,128)S(1)}, bf16[144,1024]{1,0:T(8,128)(2,1)S(1)}, bf16[2,144,2048]{2,1,0:T(8,128)(2,1)S(1)}) custom-call(s32[2]{0:T(128)S(1)} %pad_add_fusion.place_ref, bf16[144,512]{1,0:T(8,128)(2,1)S(1)} %collective-permute-done.2.refs_0_, bf16[144,512]{1,0:T(8,128)(2,1)S(1)} %collective-permute-done.3.refs_1_, ...), custom_call_target="tpu_custom_call" | custom-call | flops 1207959552 | bytes 4194304 | tf_op jit(solution)/shard_map/project_mixin/pallas_call | solution.py:351
  60.6 0.0 copy-start
  60.6 1.6 %collective-permute-start.10 = (bf16[144,1024]{1,0:T(8,128)(2,1)S(1)}, bf16[144,1024]{1,0:T(8,128)(2,1)S(1)}, u32[]{:S(2)}, u32[]{:S(2)}) collective-permute-start(bf16[144,1024]{1,0:T(8,128)(2,1)S(1)} %get-tuple-element.45), channel_id=1, source_target_pairs={{0,6},{1,7},{2,4},{3,5},{4,2},{5,3},{6,0},{7,1},{8,14},{9,15},{10,... | collective-permute-start | bytes 884744 | tf_op jit(solution)/shard_map/ppermute | solution.py:366
  62.2 2.4 %project_query.1 = (f32[144,512]{1,0:T(8,128)S(1)}, bf16[144,512]{1,0:T(8,128)(2,1)S(1)}) custom-call(bf16[2,144,2048]{2,1,0:T(8,128)(2,1)S(1)} %get-tuple-element.46.lhs_ref, bf16[3,2048,512]{2,1,0:T(8,128)(2,1)} %all-gather.3.cloned.1.call-done.refs_8_.w_ref), custom_call_target="tpu_custom_call" | custom-call | flops 603979776 | bytes 2097152 | tf_op jit(solution)/shard_map/project_query/pallas_call | solution.py:367
  64.6 5.2 %collective-permute-done.10.more_ref = bf16[144,1024]{1,0:T(8,128)(2,1)S(1)} collective-permute-done((bf16[144,1024]{1,0:T(8,128)(2,1)S(1)}, bf16[144,1024]{1,0:T(8,128)(2,1)S(1)}, u32[]{:S(2)}, u32[]{:S(2)}) %collective-permute-start.10) | collective-permute-done | bytes 294944 | tf_op jit(solution)/shard_map/ppermute | solution.py:366
  69.8 0.6 scan.1
  70.4 0.7 broadcast_in_dim.13
  71.1 8.0 %all-to-all-start = ((f32[32,4,512]{2,1,0:T(4,128)}), f32[32,4,512]{2,1,0:T(4,128)S(1)}, u32[]{:S(2)}, u32[]{:S(2)}) async-start(f32[32,4,512]{2,1,0:T(4,128)} %broadcast_in_dim.13), calls=%async_computation | async-start | bytes 524288 | tf_op jit(solution)/shard_map/all_to_all | solution.py:18
  79.2 1.6 %collective-permute-start.11 = (bf16[144,512]{1,0:T(8,128)(2,1)S(1)}, bf16[144,512]{1,0:T(8,128)(2,1)S(1)}, u32[]{:S(2)}, u32[]{:S(2)}) collective-permute-start(bf16[144,512]{1,0:T(8,128)(2,1)S(1)} %get-tuple-element.57), channel_id=1, source_target_pairs={{0,6},{1,7},{2,4},{3,5},{4,2},{5,3},{6,0},{7,1},{8,14},{9,15},{10,... | collective-permute-start | bytes 442376 | tf_op jit(solution)/shard_map/ppermute | solution.py:390
  80.8 6.8 %collective-permute-done.11.more_ref = bf16[144,512]{1,0:T(8,128)(2,1)S(1)} collective-permute-done((bf16[144,512]{1,0:T(8,128)(2,1)S(1)}, bf16[144,512]{1,0:T(8,128)(2,1)S(1)}, u32[]{:S(2)}, u32[]{:S(2)}) %collective-permute-start.11) | collective-permute-done | bytes 147488 | tf_op jit(solution)/shard_map/ppermute | solution.py:390
  87.6 2.1 %all-to-all-done.all_ref = f32[32,4,512]{2,1,0:T(4,128)S(1)} async-done(((f32[32,4,512]{2,1,0:T(4,128)}), f32[32,4,512]{2,1,0:T(4,128)S(1)}, u32[]{:S(2)}, u32[]{:S(2)}) %all-to-all-start) | async-done | bytes 262176 | tf_op jit(solution)/shard_map/all_to_all | solution.py:18
  89.7 0.5 gate.1.refs_0_
  90.3 1.8 %collective-permute-start.12 = (bf16[128,512]{1,0:T(8,128)(2,1)S(1)}, bf16[128,512]{1,0:T(8,128)(2,1)S(1)}, u32[]{:S(2)}, u32[]{:S(2)}) collective-permute-start(bf16[128,512]{1,0:T(8,128)(2,1)S(1)} %gate.1.refs_0_), channel_id=1, source_target_pairs={{0,32},{32,64},{64,96},{96,128},{128,160},{160,192},{192,224},{224... | collective-permute-start | bytes 393224 | tf_op jit(solution)/shard_map/ppermute | solution.py:38
  92.1 1.8 %collective-permute-start.16 = (bf16[128,512]{1,0:T(8,128)(2,1)S(1)}, bf16[128,512]{1,0:T(8,128)(2,1)S(1)}, u32[]{:S(2)}, u32[]{:S(2)}) collective-permute-start(bf16[128,512]{1,0:T(8,128)(2,1)S(1)} %gate.1.refs_0_), channel_id=1, source_target_pairs={{0,224},{32,0},{64,32},{96,64},{128,96},{160,128},{192,160},{224,1... | collective-permute-start | bytes 393224 | tf_op jit(solution)/shard_map/ppermute | solution.py:41
  93.9 3.5 %collective-permute-done.12.refs_1_ = bf16[128,512]{1,0:T(8,128)(2,1)S(1)} collective-permute-done((bf16[128,512]{1,0:T(8,128)(2,1)S(1)}, bf16[128,512]{1,0:T(8,128)(2,1)S(1)}, u32[]{:S(2)}, u32[]{:S(2)}) %collective-permute-start.12) | collective-permute-done | bytes 131104 | tf_op jit(solution)/shard_map/ppermute | solution.py:38
  97.4 0.0 collective-permute-start.13
  97.4 0.0 collective-permute-done.16.refs_2_
  97.4 3.2 %collective-permute-start.17 = (bf16[128,512]{1,0:T(8,128)(2,1)S(1)}, bf16[128,512]{1,0:T(8,128)(2,1)S(1)}, u32[]{:S(2)}, u32[]{:S(2)}) collective-permute-start(bf16[128,512]{1,0:T(8,128)(2,1)S(1)} %collective-permute-done.16.refs_2_), channel_id=1, source_target_pairs={{0,224},{32,0},{64,32},{96,64},{128,96},{160,128},{192,160},{224,1... | collective-permute-start | bytes 393224 | tf_op jit(solution)/shard_map/ppermute | solution.py:41
  100.7 2.9 %collective-permute-done.13.refs_3_ = bf16[128,512]{1,0:T(8,128)(2,1)S(1)} collective-permute-done((bf16[128,512]{1,0:T(8,128)(2,1)S(1)}, bf16[128,512]{1,0:T(8,128)(2,1)S(1)}, u32[]{:S(2)}, u32[]{:S(2)}) %collective-permute-start.13) | collective-permute-done | bytes 131104 | tf_op jit(solution)/shard_map/ppermute | solution.py:38
  103.6 0.0 collective-permute-start.14
  103.6 0.0 collective-permute-done.17.refs_4_
  103.6 3.2 %collective-permute-start.18 = (bf16[128,512]{1,0:T(8,128)(2,1)S(1)}, bf16[128,512]{1,0:T(8,128)(2,1)S(1)}, u32[]{:S(2)}, u32[]{:S(2)}) collective-permute-start(bf16[128,512]{1,0:T(8,128)(2,1)S(1)} %collective-permute-done.17.refs_4_), channel_id=1, source_target_pairs={{0,224},{32,0},{64,32},{96,64},{128,96},{160,128},{192,160},{224,1... | collective-permute-start | bytes 393224 | tf_op jit(solution)/shard_map/ppermute | solution.py:41
  106.8 2.9 %collective-permute-done.14.refs_5_ = bf16[128,512]{1,0:T(8,128)(2,1)S(1)} collective-permute-done((bf16[128,512]{1,0:T(8,128)(2,1)S(1)}, bf16[128,512]{1,0:T(8,128)(2,1)S(1)}, u32[]{:S(2)}, u32[]{:S(2)}) %collective-permute-start.14) | collective-permute-done | bytes 131104 | tf_op jit(solution)/shard_map/ppermute | solution.py:38
  109.8 0.0 collective-permute-start.15
  109.8 0.1 stack.48.which_ref
  109.9 0.0 collective-permute-done.18.refs_6_
  109.9 2.9 %mix.1 = (f32[128,512]{1,0:T(8,128)S(1)}, bf16[512,512]{1,0:T(8,128)(2,1)S(1)}) custom-call(s32[9]{0:T(128)S(1)} %stack.48.which_ref, bf16[128,512]{1,0:T(8,128)(2,1)S(1)} %gate.1.refs_0_, bf16[128,512]{1,0:T(8,128)(2,1)S(1)} %collective-permute-done.12.refs_1_, bf16[128,512]{1,0:T(8,128)(2,1)S(1)} %collective-permute-done.16.refs_2_, ...), custom_call_target="tpu_custom_call" | custom-call | flops 536870912 | bytes 4194304 | tf_op jit(solution)/shard_map/mix/pallas_call | solution.py:271
  112.8 3.1 %collective-permute-done.15.x_ref = bf16[128,512]{1,0:T(8,128)(2,1)S(1)} collective-permute-done((bf16[128,512]{1,0:T(8,128)(2,1)S(1)}, bf16[128,512]{1,0:T(8,128)(2,1)S(1)}, u32[]{:S(2)}, u32[]{:S(2)}) %collective-permute-start.15) | collective-permute-done | bytes 131104 | tf_op jit(solution)/shard_map/ppermute | solution.py:38
  116.0 0.9 last_mix.1
  (8 shorter events, 0.0 us)
Async XLA Ops:
  6.5 30.9 %copy-start.2 = (f32[512,2]{0,1:T(2,128)S(1)}, f32[512,2]{0,1:T(2,128)}, u32[]{:S(2)}) copy-start(f32[512,2]{0,1:T(2,128)} %param.12) | copy-start | bytes 12292
  6.5 30.9 %copy-start.3 = (f32[512,2]{0,1:T(2,128)S(1)}, f32[512,2]{0,1:T(2,128)}, u32[]{:S(2)}) copy-start(f32[512,2]{0,1:T(2,128)} %param.13) | copy-start | bytes 12292
  6.5 30.9 %copy-start.1 = (f32[2,512,2]{1,2,0:T(2,128)S(1)}, f32[2,512,2]{1,2,0:T(2,128)}, u32[]{:S(2)}) copy-start(f32[2,512,2]{1,2,0:T(2,128)} %param.14) | copy-start | bytes 24580
  6.5 50.3 %all-gather.3.cloned.1.call-start = ((), (), s32[]{:S(2)}) async-start(), calls=%async_computation.1 | async-start | bytes 6684672 | tf_op jit(solution)/shard_map/all_gather | solution.py:308
  8.4 101.5 %all-gather.5.cloned.1.call-start = ((), (), s32[]{:S(2)}) async-start(), calls=%async_computation.2 | async-start | bytes 4456448 | tf_op jit(solution)/shard_map/all_gather | solution.py:308
  8.4 7.2 %collective-permute-start.1 = (bf16[128,512]{1,0:T(8,128)(2,1)}, bf16[128,512]{1,0:T(8,128)(2,1)S(1)}, u32[]{:S(2)}, u32[]{:S(2)}) collective-permute-start(bf16[128,512]{1,0:T(8,128)(2,1)} %x_ref.1), channel_id=1, source_target_pairs={{0,6},{1,7},{2,4},{3,5},{4,2},{5,3},{6,0},{7,1},{8,14},{9,15},{10,... | collective-permute-start | bytes 393224 | tf_op jit(solution)/shard_map/ppermute | solution.py:316
  10.7 4.9 %collective-permute-start = (bf16[2,512]{1,0:T(2,128)(2,1)S(1)}, bf16[2,512]{1,0:T(2,128)(2,1)S(1)}, u32[]{:S(2)}, u32[]{:S(2)}) collective-permute-start(bf16[2,512]{1,0:T(2,128)(2,1)S(1)} %slice.3), channel_id=1, source_target_pairs={{0,1},{1,2},{2,3},{3,4},{4,5},{5,6},{6,7},{7,8},{8,9},{9,10},{10,1... | collective-permute-start | bytes 6152 | tf_op jit(solution)/shard_map/ppermute | solution.py:315
  16.6 0.7 collective-permute-start.2
  17.3 16.5 %collective-permute-start.3 = (bf16[144,512]{1,0:T(8,128)(2,1)S(1)}, bf16[144,512]{1,0:T(8,128)(2,1)S(1)}, u32[]{:S(2)}, u32[]{:S(2)}) collective-permute-start(bf16[144,512]{1,0:T(8,128)(2,1)S(1)} %collective-permute-done.2.refs_0_), channel_id=1, source_target_pairs={{0,32},{32,64},{64,96},{96,128},{128,160},{160,192},{192,224},{224... | collective-permute-start | bytes 442376 | tf_op jit(solution)/shard_map/ppermute | solution.py:38
  26.5 7.4 %collective-permute-start.4 = (bf16[144,512]{1,0:T(8,128)(2,1)S(1)}, bf16[144,512]{1,0:T(8,128)(2,1)S(1)}, u32[]{:S(2)}, u32[]{:S(2)}) collective-permute-start(bf16[144,512]{1,0:T(8,128)(2,1)S(1)} %collective-permute-done.2.refs_0_), channel_id=1, source_target_pairs={{0,224},{32,0},{64,32},{96,64},{128,96},{160,128},{192,160},{224,1... | collective-permute-start | bytes 442376 | tf_op jit(solution)/shard_map/ppermute | solution.py:41
  33.8 7.9 %collective-permute-start.5 = (bf16[144,512]{1,0:T(8,128)(2,1)S(1)}, bf16[144,512]{1,0:T(8,128)(2,1)S(1)}, u32[]{:S(2)}, u32[]{:S(2)}) collective-permute-start(bf16[144,512]{1,0:T(8,128)(2,1)S(1)} %collective-permute-done.3.refs_1_), channel_id=1, source_target_pairs={{0,32},{32,64},{64,96},{96,128},{128,160},{160,192},{192,224},{224... | collective-permute-start | bytes 442376 | tf_op jit(solution)/shard_map/ppermute | solution.py:38
  35.0 6.7 %collective-permute-start.6 = (bf16[144,512]{1,0:T(8,128)(2,1)S(1)}, bf16[144,512]{1,0:T(8,128)(2,1)S(1)}, u32[]{:S(2)}, u32[]{:S(2)}) collective-permute-start(bf16[144,512]{1,0:T(8,128)(2,1)S(1)} %collective-permute-done.4.refs_2_), channel_id=1, source_target_pairs={{0,224},{32,0},{64,32},{96,64},{128,96},{160,128},{192,160},{224,1... | collective-permute-start | bytes 442376 | tf_op jit(solution)/shard_map/ppermute | solution.py:41
  41.7 7.1 %collective-permute-start.7 = (bf16[144,512]{1,0:T(8,128)(2,1)S(1)}, bf16[144,512]{1,0:T(8,128)(2,1)S(1)}, u32[]{:S(2)}, u32[]{:S(2)}) collective-permute-start(bf16[144,512]{1,0:T(8,128)(2,1)S(1)} %collective-permute-done.5.refs_3_), channel_id=1, source_target_pairs={{0,32},{32,64},{64,96},{96,128},{128,160},{160,192},{192,224},{224... | collective-permute-start | bytes 442376 | tf_op jit(solution)/shard_map/ppermute | solution.py:38
  42.8 6.1 %collective-permute-start.8 = (bf16[144,512]{1,0:T(8,128)(2,1)S(1)}, bf16[144,512]{1,0:T(8,128)(2,1)S(1)}, u32[]{:S(2)}, u32[]{:S(2)}) collective-permute-start(bf16[144,512]{1,0:T(8,128)(2,1)S(1)} %collective-permute-done.6.refs_4_), channel_id=1, source_target_pairs={{0,224},{32,0},{64,32},{96,64},{128,96},{160,128},{192,160},{224,1... | collective-permute-start | bytes 442376 | tf_op jit(solution)/shard_map/ppermute | solution.py:41
  48.8 6.4 %collective-permute-start.9 = (bf16[144,512]{1,0:T(8,128)(2,1)S(1)}, bf16[144,512]{1,0:T(8,128)(2,1)S(1)}, u32[]{:S(2)}, u32[]{:S(2)}) collective-permute-start(bf16[144,512]{1,0:T(8,128)(2,1)S(1)} %collective-permute-done.7.refs_5_), channel_id=1, source_target_pairs={{0,32},{32,64},{64,96},{96,128},{128,160},{160,192},{192,224},{224... | collective-permute-start | bytes 442376 | tf_op jit(solution)/shard_map/ppermute | solution.py:38
  60.6 9.3 %copy-start = (f32[3,3,512]{2,1,0:T(4,128)S(1)}, f32[3,3,512]{2,1,0:T(4,128)}, u32[]{:S(2)}) copy-start(f32[3,3,512]{2,1,0:T(4,128)} %taps_ref.3) | copy-start | bytes 55300
  60.6 9.2 %collective-permute-start.10 = (bf16[144,1024]{1,0:T(8,128)(2,1)S(1)}, bf16[144,1024]{1,0:T(8,128)(2,1)S(1)}, u32[]{:S(2)}, u32[]{:S(2)}) collective-permute-start(bf16[144,1024]{1,0:T(8,128)(2,1)S(1)} %get-tuple-element.45), channel_id=1, source_target_pairs={{0,6},{1,7},{2,4},{3,5},{4,2},{5,3},{6,0},{7,1},{8,14},{9,15},{10,... | collective-permute-start | bytes 884744 | tf_op jit(solution)/shard_map/ppermute | solution.py:366
  62.2 27.5 %copy-start.4 = (f32[512]{0:T(512)S(1)}, f32[512]{0:T(512)}, u32[]{:S(2)}) copy-start(f32[512]{0:T(512)} %param.15) | copy-start | bytes 6148
  71.1 18.6 %all-to-all-start = ((f32[32,4,512]{2,1,0:T(4,128)}), f32[32,4,512]{2,1,0:T(4,128)S(1)}, u32[]{:S(2)}, u32[]{:S(2)}) async-start(f32[32,4,512]{2,1,0:T(4,128)} %broadcast_in_dim.13), calls=%async_computation | async-start | bytes 524288 | tf_op jit(solution)/shard_map/all_to_all | solution.py:18
  79.2 8.4 %collective-permute-start.11 = (bf16[144,512]{1,0:T(8,128)(2,1)S(1)}, bf16[144,512]{1,0:T(8,128)(2,1)S(1)}, u32[]{:S(2)}, u32[]{:S(2)}) collective-permute-start(bf16[144,512]{1,0:T(8,128)(2,1)S(1)} %get-tuple-element.57), channel_id=1, source_target_pairs={{0,6},{1,7},{2,4},{3,5},{4,2},{5,3},{6,0},{7,1},{8,14},{9,15},{10,... | collective-permute-start | bytes 442376 | tf_op jit(solution)/shard_map/ppermute | solution.py:390
  90.3 7.2 %collective-permute-start.12 = (bf16[128,512]{1,0:T(8,128)(2,1)S(1)}, bf16[128,512]{1,0:T(8,128)(2,1)S(1)}, u32[]{:S(2)}, u32[]{:S(2)}) collective-permute-start(bf16[128,512]{1,0:T(8,128)(2,1)S(1)} %gate.1.refs_0_), channel_id=1, source_target_pairs={{0,32},{32,64},{64,96},{96,128},{128,160},{160,192},{192,224},{224... | collective-permute-start | bytes 393224 | tf_op jit(solution)/shard_map/ppermute | solution.py:38
  92.1 5.4 %collective-permute-start.16 = (bf16[128,512]{1,0:T(8,128)(2,1)S(1)}, bf16[128,512]{1,0:T(8,128)(2,1)S(1)}, u32[]{:S(2)}, u32[]{:S(2)}) collective-permute-start(bf16[128,512]{1,0:T(8,128)(2,1)S(1)} %gate.1.refs_0_), channel_id=1, source_target_pairs={{0,224},{32,0},{64,32},{96,64},{128,96},{160,128},{192,160},{224,1... | collective-permute-start | bytes 393224 | tf_op jit(solution)/shard_map/ppermute | solution.py:41
  97.4 6.2 %collective-permute-start.13 = (bf16[128,512]{1,0:T(8,128)(2,1)S(1)}, bf16[128,512]{1,0:T(8,128)(2,1)S(1)}, u32[]{:S(2)}, u32[]{:S(2)}) collective-permute-start(bf16[128,512]{1,0:T(8,128)(2,1)S(1)} %collective-permute-done.12.refs_1_), channel_id=1, source_target_pairs={{0,32},{32,64},{64,96},{96,128},{128,160},{160,192},{192,224},{224... | collective-permute-start | bytes 393224 | tf_op jit(solution)/shard_map/ppermute | solution.py:38
  97.4 6.2 %collective-permute-start.17 = (bf16[128,512]{1,0:T(8,128)(2,1)S(1)}, bf16[128,512]{1,0:T(8,128)(2,1)S(1)}, u32[]{:S(2)}, u32[]{:S(2)}) collective-permute-start(bf16[128,512]{1,0:T(8,128)(2,1)S(1)} %collective-permute-done.16.refs_2_), channel_id=1, source_target_pairs={{0,224},{32,0},{64,32},{96,64},{128,96},{160,128},{192,160},{224,1... | collective-permute-start | bytes 393224 | tf_op jit(solution)/shard_map/ppermute | solution.py:41
  103.6 6.2 %collective-permute-start.14 = (bf16[128,512]{1,0:T(8,128)(2,1)S(1)}, bf16[128,512]{1,0:T(8,128)(2,1)S(1)}, u32[]{:S(2)}, u32[]{:S(2)}) collective-permute-start(bf16[128,512]{1,0:T(8,128)(2,1)S(1)} %collective-permute-done.13.refs_3_), channel_id=1, source_target_pairs={{0,32},{32,64},{64,96},{96,128},{128,160},{160,192},{192,224},{224... | collective-permute-start | bytes 393224 | tf_op jit(solution)/shard_map/ppermute | solution.py:38
  103.6 6.3 %collective-permute-start.18 = (bf16[128,512]{1,0:T(8,128)(2,1)S(1)}, bf16[128,512]{1,0:T(8,128)(2,1)S(1)}, u32[]{:S(2)}, u32[]{:S(2)}) collective-permute-start(bf16[128,512]{1,0:T(8,128)(2,1)S(1)} %collective-permute-done.17.refs_4_), channel_id=1, source_target_pairs={{0,224},{32,0},{64,32},{96,64},{128,96},{160,128},{192,160},{224,1... | collective-permute-start | bytes 393224 | tf_op jit(solution)/shard_map/ppermute | solution.py:41
  109.8 6.2 %collective-permute-start.15 = (bf16[128,512]{1,0:T(8,128)(2,1)S(1)}, bf16[128,512]{1,0:T(8,128)(2,1)S(1)}, u32[]{:S(2)}, u32[]{:S(2)}) collective-permute-start(bf16[128,512]{1,0:T(8,128)(2,1)S(1)} %collective-permute-done.14.refs_5_), channel_id=1, source_target_pairs={{0,32},{32,64},{64,96},{96,128},{128,160},{160,192},{192,224},{224... | collective-permute-start | bytes 393224 | tf_op jit(solution)/shard_map/ppermute | solution.py:38
Sparse Core Ops, SparseCore 0:
  9.2 47.6 all-gather.2
  58.7 43.0 all-gather.4
